TPU v7x, 32 devices: a whole 2x2x4 slice. The times are simulated.
32 devices in a mesh: pipe: 4 (over z), expert: 4 (over y, x), dp: 2 (over core).
Axes of the slice: x: 2, y: 2, z: 4, core: 2. Of those that a mesh axis runs over, the one named last changes fastest.
Arguments:
- enter_fwd: bfloat16 [4, 512, 7168], P('pipe', 'expert', 'dp'), may hold values from -6 to 6
- enter_rev: bfloat16 [4, 512, 7168], P('pipe', 'expert', 'dp'), may hold values from -6 to 6
- cot_rev: bfloat16 [4, 512, 7168], P('pipe', 'expert', 'dp'), may hold values from -0.1875 to 0.1875
- gain: bfloat16 [2, 4, 7168], P(None, 'pipe', 'dp'), may hold values from 0.5 to 1.5
- proj_down: bfloat16 [2, 4, 256, 7168], P(None, 'pipe', None, 'dp'), may hold values from -0.0625 to 0.0625
- proj_up: bfloat16 [2, 4, 256, 7168], P(None, 'pipe', None, 'dp'), may hold values from -0.375 to 0.375
- master: float32 [2, 4, 256, 7168], P(None, 'pipe', 'expert', 'dp'), may hold values from -0.125 to 0.125
- moment: bfloat16 [2, 4, 256, 7168], P(None, 'pipe', 'expert', 'dp'), may hold values from -6 to 6
- second: bfloat16 [2, 4, 256, 7168], P(None, 'pipe', 'expert', 'dp'), may hold values from 0.5 to 20
Outputs:
- leave_fwd: bfloat16 [4, 512, 7168], P('pipe', 'expert', 'dp')
- codes: bfloat16 [2, 4, 256, 7168], P(None, 'pipe', 'expert', 'dp')
- scales: float32 [2, 4, 2, 56], P(None, 'pipe', None, 'dp')
All inputs are finite; a program needn't handle non-finite values.
Results may differ from a plain program's by a relative error of at most 0.0047.
The roundings to bfloat16 on the way count: a program that leaves them out, or rounds other values in their place, can miss the bound.
Values may be sent and summed in bfloat16 or wider, within the bound.
No kernel may reach another device: no remote copies, remote signals or barrier semaphores. Data moves between devices by JAX's collectives and lax.ppermute only.
A program may use at most 64 MiB of HBM per device.

v0:
```python
import jax
import jax.numpy as jnp
from jax import lax
from jax.sharding import PartitionSpec as P

D = 7168


def shifted(block, axis, distance):
    devices = range(lax.axis_size(axis))
    route = [(i - distance, i) for i in devices if i - distance in devices]
    return lax.ppermute(block, axis, route)


def from_partner(block, axis, distance):
    count = lax.axis_size(axis)
    route = []
    for low in range(count):
        high = low | 1 << distance
        if high != low and high < count:
            route += [(low, high), (high, low)]
    return lax.ppermute(block, axis, route)


def prepare(rows, gain_row, down):
    scaled = (rows.astype(jnp.float32) * gain_row).astype(jnp.bfloat16)
    squares = jnp.sum(jnp.square(rows.astype(jnp.float32)), axis=-1)
    raw = jnp.einsum("td,rd->tr", scaled, down, preferred_element_type=jnp.float32)
    return (scaled, squares, raw)


def shards(enter_fwd, enter_rev, cot_rev, gain, proj_down, proj_up, master, moment, second):
    fwd_rows = enter_fwd[0]
    back_rows = enter_rev[0]
    back_cot = cot_rev[0]
    own_gain = gain[0, 0].astype(jnp.float32)
    own_down = proj_down[0, 0]
    own_upper = proj_up[0, 0]
    copy_gain = gain[1, 0].astype(jnp.float32)
    copy_down = proj_down[1, 0]
    copy_upper = proj_up[1, 0]
    width_local = fwd_rows.shape[1]
    latent = own_down.shape[0]
    fwd_scaled, fwd_squares, fwd_raw = prepare(fwd_rows, own_gain, own_down)
    back_scaled, back_squares, back_raw = prepare(back_rows, copy_gain, copy_down)
    back_dlat = jnp.einsum("td,rd->tr", back_cot, copy_upper, preferred_element_type=jnp.float32)
    fwd_raw, fwd_squares, back_raw, back_squares, back_dlat = lax.psum(
        (fwd_raw, fwd_squares, back_raw, back_squares, back_dlat), "dp"
    )
    rscale = lax.rsqrt(fwd_squares / D + 1e-06)
    hidden = (fwd_raw * rscale[:, None]).astype(jnp.bfloat16)
    result = (
        fwd_rows.astype(jnp.float32)
        + jnp.dot(hidden, own_upper, preferred_element_type=jnp.float32)
    ).astype(jnp.bfloat16)
    leaving = shifted(result, "pipe", 1)
    back_r = lax.rsqrt(back_squares / D + 1e-06)
    hidden_two = (back_raw * back_r[:, None]).astype(jnp.bfloat16)
    error = (back_dlat * back_r[:, None]).astype(jnp.bfloat16)
    experts = lax.axis_size("expert")
    rows_local = latent // experts
    grad_down = jnp.einsum("tr,td->rd", error, back_scaled, preferred_element_type=jnp.float32)
    grad_up = jnp.einsum("tr,td->rd", hidden_two, back_cot, preferred_element_type=jnp.float32)
    summed = lax.psum_scatter(
        jnp.concatenate([grad_down, grad_up], axis=1).astype(jnp.bfloat16),
        "expert",
        scatter_dimension=0,
        tiled=True,
    ).astype(jnp.float32)
    share = jnp.stack([summed[:, :width_local], summed[:, width_local:]]).astype(jnp.bfloat16)
    levels = lax.axis_size("pipe").bit_length() - 1
    bit_order = list(range(levels))
    for level in bit_order:
        share = from_partner(share, "pipe", level)
    grad = share.astype(jnp.float32)[:, None]
    first = 0.9 * moment.astype(jnp.float32) + 0.1 * grad
    secnd = 0.95 * second.astype(jnp.float32) + 0.05 * grad * grad
    update = first / (1.0 - 0.9**10) / (jnp.sqrt(secnd / (1.0 - 0.95**10)) + 1e-08)
    fresh = master - 0.01 * (update + 0.1 * master)
    col_blocks = width_local // 128
    local_peak = jnp.max(jnp.abs(fresh).reshape(2, rows_local, col_blocks, 128), axis=(1, 3))
    gathered = lax.all_gather(local_peak[None], "expert", axis=0, tiled=True)
    group = 128 // rows_local
    block_peak = jnp.max(gathered.reshape(experts // group, group, 2, col_blocks), axis=1) + 1e-06
    scale_rows = jnp.transpose(block_peak, (1, 0, 2))
    row_block = lax.axis_index("expert") * rows_local // 128
    mine = lax.dynamic_index_in_dim(block_peak, row_block, 0, keepdims=False)
    expanded = jnp.repeat(mine, 128, axis=-1)
    coded = (fresh / expanded[:, None, None, :]).astype(jnp.bfloat16)
    return (leaving[None], coded, scale_rows[:, None])


def solution(mesh):
    in_specs = (
        P("pipe", "expert", "dp"),
        P("pipe", "expert", "dp"),
        P("pipe", "expert", "dp"),
        P(None, "pipe", "dp"),
        P(None, "pipe", None, "dp"),
        P(None, "pipe", None, "dp"),
        P(None, "pipe", "expert", "dp"),
        P(None, "pipe", "expert", "dp"),
        P(None, "pipe", "expert", "dp"),
    )
    out_specs = (
        P("pipe", "expert", "dp"),
        P(None, "pipe", "expert", "dp"),
        P(None, "pipe", None, "dp"),
    )
    return jax.shard_map(shards, mesh=mesh, in_specs=in_specs, out_specs=out_specs, check_vma=False)
```

profile of v0, /device:TPU:8, one launch (start us, length us, event | category | flops | bytes accessed | tf_op | source)
XLA Modules:
  0.0 177.5 jit_solution(3313403401906496017)
XLA Ops:
  7.2 0.0 all-reduce.4.cloned.1.call-start
  7.2 0.9 convert_reduce_fusion
  8.1 3.3 %fusion.21 = f32[128,256]{1,0:T(8,128)} fusion(bf16[2,1,256,3584]{3,2,1,0:T(8,128)(2,1)} %param.13, bf16[1,128,3584]{2,1,0:T(8,128)(2,1)} %param.10, f32[3584]{0:T(1024)S(1)} %get-tuple-element.12), kind=kOutput, calls=%fused_computation.31 | convolution fusion | flops 236257280 | bytes 2897920 | tf_op jit(solution)/shard_map/td,rd->tr/dot_general | solution.py:28
  11.4 2.9 %fusion.26 = f32[128,256]{1,0:T(8,128)} fusion(bf16[2,1,256,3584]{3,2,1,0:T(8,128)(2,1)} %param.13, bf16[1,128,3584]{2,1,0:T(8,128)(2,1)S(1)} %copy-done.2, f32[3584]{0:T(1024)S(1)} %get-tuple-element.13), kind=kOutput, calls=%fused_computation.37 | convolution fusion | flops 236257280 | bytes 2897920 | tf_op jit(solution)/shard_map/td,rd->tr/dot_general | solution.py:28
  14.3 1.4 fusion.23
  15.7 0.0 all-reduce.4.cloned.1.call-update
  15.7 0.0 reduce-scatter.2.cloned.1.call-start
  15.8 0.4 fusion.11
  16.2 2.5 %all-reduce = (f32[128]{0:T(128)S(1)}, f32[128]{0:T(128)S(1)}) all-reduce(f32[128]{0:T(128)S(1)} %get-tuple-element.25, f32[128]{0:T(128)S(1)} %get-tuple-element.26), channel_id=1, replica_groups=mesh['pipe'=4,'expert'=4,'dp'=2] {'dp'}, use_global_device_ids=true, to_apply=%region_2.0 | all-reduce | flops 256 | bytes 2048 | tf_op jit(solution)/shard_map/psum | solution.py:47
  18.7 17.2 %all-reduce.4.cloned.1.call-done = (f32[128,256]{1,0:T(8,128)}, f32[128,256]{1,0:T(8,128)}, f32[128,256]{1,0:T(8,128)}) async-done(((f32[128,256]{1,0:T(8,128)}, f32[128,256]{1,0:T(8,128)}, f32[128,256]{1,0:T(8,128)}), (f32[128,256]{1,0:T(8,128)}, f32[128,256]{1,0:T(8,128)}, f32[128,256]{1,0:T(8,128)})) %all-reduce.4.cloned.1.call-update) | async-done | bytes 393232 | tf_op jit(solution)/shard_map/psum | solution.py:47
  35.9 1.7 convolution_convert_fusion.1
  37.6 0.7 convolution_convert_fusion
  38.4 2.2 %pad_maximum_fusion = bf16[256,7168]{1,0:T(8,128)(2,1)} fusion(bf16[256,3584]{1,0:T(8,128)(2,1)S(1)} %convolution_convert_fusion, bf16[256,3584]{1,0:T(8,128)(2,1)S(1)} %convolution_convert_fusion.1), kind=kLoop, calls=%fused_computation.4 | loop fusion | flops 7340032 | bytes 7340032 | tf_op jit(solution)/shard_map/concatenate | solution.py:65
  40.6 49.4 %reduce-scatter.2.cloned.1.call-done = bf16[64,7168]{1,0:T(8,128)(2,1)} async-done(((bf16[256,7168]{1,0:T(8,128)(2,1)}), bf16[64,7168]{1,0:T(8,128)(2,1)}) %reduce-scatter.2.cloned.1.call-update) | async-done | bytes 917520 | tf_op jit(solution)/shard_map/reduce_scatter | solution.py:64
  90.0 1.4 slice_bitcast_fusion.1
  91.4 0.1 pad_maximum_fusion.1
  91.5 0.6 collective-permute-start.1
  92.1 0.2 copy-done.6
  92.3 0.5 fusion
  92.8 4.1 %collective-permute-start = (bf16[128,3584]{1,0:T(8,128)(2,1)S(1)}, bf16[128,3584]{1,0:T(8,128)(2,1)S(1)}, u32[]{:S(2)}, u32[]{:S(2)}) collective-permute-start(bf16[128,3584]{1,0:T(8,128)(2,1)S(1)} %fusion), channel_id=1, source_target_pairs={{0,8},{8,16},{16,24},{1,9},{9,17},{17,25},{2,10},{10,18},{18,26},{... | collective-permute-start | bytes 2752520 | tf_op jit(solution)/shard_map/ppermute | solution.py:12
  96.9 18.0 %collective-permute-done.1 = bf16[2,64,3584]{2,1,0:T(8,128)(2,1)} collective-permute-done((bf16[2,64,3584]{2,1,0:T(8,128)(2,1)S(1)}, bf16[2,64,3584]{2,1,0:T(8,128)(2,1)}, u32[]{:S(2)}, u32[]{:S(2)}) %collective-permute-start.1) | collective-permute-done | bytes 917536 | tf_op jit(solution)/shard_map/ppermute | solution.py:22
  114.9 2.4 %collective-permute-start.2 = (bf16[2,64,3584]{2,1,0:T(8,128)(2,1)}, bf16[2,64,3584]{2,1,0:T(8,128)(2,1)}, u32[]{:S(2)}, u32[]{:S(2)}) collective-permute-start(bf16[2,64,3584]{2,1,0:T(8,128)(2,1)} %collective-permute-done.1), channel_id=1, source_target_pairs={{0,16},{16,0},{8,24},{24,8},{1,17},{17,1},{9,25},{25,9},{2,18},{18... | collective-permute-start | bytes 2752520 | tf_op jit(solution)/shard_map/ppermute | solution.py:22
  117.3 17.2 %collective-permute-done = bf16[128,3584]{1,0:T(8,128)(2,1)S(1)} collective-permute-done((bf16[128,3584]{1,0:T(8,128)(2,1)S(1)}, bf16[128,3584]{1,0:T(8,128)(2,1)S(1)}, u32[]{:S(2)}, u32[]{:S(2)}) %collective-permute-start) | collective-permute-done | bytes 917536 | tf_op jit(solution)/shard_map/ppermute | solution.py:12
  134.4 0.9 copy-done.3
  135.4 20.3 %collective-permute-done.2 = bf16[2,64,3584]{2,1,0:T(8,128)(2,1)} collective-permute-done((bf16[2,64,3584]{2,1,0:T(8,128)(2,1)}, bf16[2,64,3584]{2,1,0:T(8,128)(2,1)}, u32[]{:S(2)}, u32[]{:S(2)}) %collective-permute-start.2) | collective-permute-done | bytes 917536 | tf_op jit(solution)/shard_map/ppermute | solution.py:22
  155.7 4.1 %abs_reduce_fusion = (f32[2,3584]{1,0:T(2,128)S(1)}, f32[2,1,64,3584]{3,2,0,1:T(8,128)S(1)}) fusion(bf16[2,1,64,3584]{3,2,1,0:T(8,128)(2,1)} %param.17, bf16[2,64,3584]{2,1,0:T(8,128)(2,1)} %collective-permute-done.2, bf16[2,1,64,3584]{3,2,1,0:T(8,128)(2,1)} %param.16, f32[2,1,64,3584]{3,2,1,0:T(8,128)} %param.15), kind=kLoop, calls=%fused_computation.40 | loop fusion | flops 9167872 | bytes 6451200 | tf_op jit(solution)/shard_map/reduce_max | solution.py:81
  159.8 0.1 reduce_max.27
  159.9 8.1 %all-gather.1 = f32[4,2,28]{2,1,0:T(2,128)S(1)} all-gather(f32[1,2,28]{2,1,0:T(2,128)S(1)} %bitcast.106), channel_id=2, replica_groups=mesh['pipe'=4,'expert'=4,'dp'=2] {'expert'}, dimensions={0}, use_global_device_ids=true | all-gather | bytes 1120 | tf_op jit(solution)/shard_map/all_gather | solution.py:82
  168.0 0.1 broadcast_bitcast_fusion
  168.1 0.6 copy.30
  168.6 1.0 fusion.42
  169.7 0.9 copy.40
  (24 shorter events, 0.1 us)
Async XLA Ops:
  7.2 7.2 %copy-start = (bf16[1,128,3584]{2,1,0:T(8,128)(2,1)S(1)}, bf16[1,128,3584]{2,1,0:T(8,128)(2,1)}, u32[]{:S(2)}) copy-start(bf16[1,128,3584]{2,1,0:T(8,128)(2,1)} %param.11) | copy-start | bytes 2752516
  7.2 28.8 %all-reduce.4.cloned.1.call-start = ((), (), s32[]{:S(2)}) async-start(), calls=%async_computation.2 | async-start | bytes 786432 | tf_op jit(solution)/shard_map/psum | solution.py:47
  8.1 3.3 %copy-start.2 = (bf16[1,128,3584]{2,1,0:T(8,128)(2,1)S(1)}, bf16[1,128,3584]{2,1,0:T(8,128)(2,1)}, u32[]{:S(2)}) copy-start(bf16[1,128,3584]{2,1,0:T(8,128)(2,1)} %param.9) | copy-start | bytes 2752516
  8.1 6.2 %copy-start.5 = (bf16[2,1,256,3584]{3,2,1,0:T(8,128)(2,1)S(1)}, bf16[2,1,256,3584]{3,2,1,0:T(8,128)(2,1)}, u32[]{:S(2)}) copy-start(bf16[2,1,256,3584]{3,2,1,0:T(8,128)(2,1)} %param.14) | copy-start | bytes 11010052
  14.3 1.5 copy-start.1
  15.7 74.3 %reduce-scatter.2.cloned.1.call-start = ((), (), s32[]{:S(2)}) async-start(), calls=%async_computation.1 | async-start | bytes 4587520 | tf_op jit(solution)/shard_map/reduce_scatter | solution.py:64
  35.9 1.7 copy-start.8
  40.6 51.5 %copy-start.7 = (f32[128,256]{1,0:T(8,128)S(1)}, f32[128,256]{1,0:T(8,128)}, u32[]{:S(2)}) copy-start(f32[128,256]{1,0:T(8,128)} %get-tuple-element.16) | copy-start | bytes 393220
  90.0 2.3 %copy-start.6 = (bf16[2,1,256,3584]{3,2,1,0:T(8,128)(2,1)S(1)}, bf16[2,1,256,3584]{3,2,1,0:T(8,128)(2,1)}, u32[]{:S(2)}) copy-start(bf16[2,1,256,3584]{3,2,1,0:T(8,128)(2,1)} %param.14) | copy-start | bytes 11010052
  91.5 23.4 %collective-permute-start.1 = (bf16[2,64,3584]{2,1,0:T(8,128)(2,1)S(1)}, bf16[2,64,3584]{2,1,0:T(8,128)(2,1)}, u32[]{:S(2)}, u32[]{:S(2)}) collective-permute-start(bf16[2,64,3584]{2,1,0:T(8,128)(2,1)S(1)} %pad_maximum_fusion.1), channel_id=1, source_target_pairs={{0,8},{8,0},{16,24},{24,16},{1,9},{9,1},{17,25},{25,17},{2,10},{10... | collective-permute-start | bytes 2752520 | tf_op jit(solution)/shard_map/ppermute | solution.py:22
  92.8 41.7 %collective-permute-start = (bf16[128,3584]{1,0:T(8,128)(2,1)S(1)}, bf16[128,3584]{1,0:T(8,128)(2,1)S(1)}, u32[]{:S(2)}, u32[]{:S(2)}) collective-permute-start(bf16[128,3584]{1,0:T(8,128)(2,1)S(1)} %fusion), channel_id=1, source_target_pairs={{0,8},{8,16},{16,24},{1,9},{9,17},{17,25},{2,10},{10,18},{18,26},{... | collective-permute-start | bytes 2752520 | tf_op jit(solution)/shard_map/ppermute | solution.py:12
  114.9 40.8 %collective-permute-start.2 = (bf16[2,64,3584]{2,1,0:T(8,128)(2,1)}, bf16[2,64,3584]{2,1,0:T(8,128)(2,1)}, u32[]{:S(2)}, u32[]{:S(2)}) collective-permute-start(bf16[2,64,3584]{2,1,0:T(8,128)(2,1)} %collective-permute-done.1), channel_id=1, source_target_pairs={{0,16},{16,0},{8,24},{24,8},{1,17},{17,1},{9,25},{25,9},{2,18},{18... | collective-permute-start | bytes 2752520 | tf_op jit(solution)/shard_map/ppermute | solution.py:22
  134.4 0.9 copy-start.3
  159.9 9.8 %copy-start.4 = (bf16[128,3584]{1,0:T(8,128)(2,1)S(1)}, bf16[128,3584]{1,0:T(8,128)(2,1)}, u32[]{:S(2)}) copy-start(bf16[128,3584]{1,0:T(8,128)(2,1)} %copy-done.3) | copy-start | bytes 2752516
Sparse Core Ops, SparseCore 0:
  15.9 20.0 all-reduce.3
  40.7 49.2 reduce-scatter.1
where the time goes:
time: 179 us; the launch traced here: 177 us
  waiting for transfers between devices  122 us (68%)
  between operations  14.2 us (8%)
  blocking collectives  10.5 us (6%)
  matrix products  10.4 us (6%)
  other arithmetic  8.84 us (5%)
  starting transfers between devices  7.17 us (4%)
  local copies, waits for them, and re-layouts  4.19 us (2%)
    reduce_scatter x1, waiting for transfers between devices, shards(): lax.psum_scatter(jnp.concatenate([grad_down, grad_up], axis=1).astype(jnp...  49.4 us
    ppermute x2, waiting for transfers between devices, from_partner(): return lax.ppermute(block, axis, route)  38.3 us
    psum x1, waiting for transfers between devices, shards(): lax.psum((fwd_raw, fwd_squares, back_raw, back_squares, back_dlat), 'dp')  17.2 us
    ppermute x1, waiting for transfers between devices, shifted(): return lax.ppermute(block, axis, route)  17.2 us
    all_gather x1, blocking collectives, shards(): gathered = lax.all_gather(local_peak[None], 'expert', axis=0, tiled=True)  8.06 us
    dot_general x2, matrix products, prepare(): jnp.einsum('td,rd->tr', scaled, down, preferred_element_type=jnp.float32)  6.2 us
    reduce_max x2, other arithmetic, shards(): jnp.max(jnp.abs(fresh).reshape(2, rows_local, col_blocks, 128), axis=(1, 3))  4.14 us
    ppermute x1, starting transfers between devices, shifted(): return lax.ppermute(block, axis, route)  4.1 us
  transfers between devices with their start and end apart: 5, of which 5 were waited for; matrix products, arithmetic and copies ran while one was open for 1% of the time, Pallas kernels for 0%

commit v1 on v0

v1 whole, which is shorter than its diff:
```python
import jax
import jax.numpy as jnp
from jax import lax
from jax.experimental import pallas as pl
from jax.experimental.pallas import tpu as pltpu
from jax.sharding import PartitionSpec as P

D = 7168
LANES = 128
F32 = jnp.float32
BF16 = jnp.bfloat16
BOTH_LAST = (((1,), (1,)), ((), ()))


def exchange(block, axis, offset):
    count = lax.axis_size(axis)
    return lax.ppermute(block, axis, [(i, i ^ offset) for i in range(count)])


def mirrored(block, axis):
    count = lax.axis_size(axis)
    return lax.ppermute(block, axis, [(i, count - 1 - i) for i in range(count)])


def shifted(block, axis):
    count = lax.axis_size(axis)
    return lax.ppermute(block, axis, [(i, i + 1) for i in range(count - 1)])


def halves_of_sum(block, axis):
    count = lax.axis_size(axis)
    offset = 1
    while True:
        other = exchange(block, axis, offset)
        offset *= 2
        if offset >= count:
            return block, other
        block = block + other


def cost(flops, nbytes):
    return pl.CostEstimate(flops=flops, bytes_accessed=nbytes, transcendentals=0)


def folded_squares(rows):
    tokens, width = rows.shape
    total = jnp.zeros((tokens, LANES), F32)
    for at in range(0, width, LANES):
        part = rows[:, at : at + LANES]
        total = total + part * part
    return total


def fwd_latent_kernel(x_ref, g_ref, a_ref, out_ref):
    latent = a_ref.shape[0]

    @pl.when(pl.program_id(0) == 0)
    def _():
        out_ref[...] = jnp.zeros_like(out_ref)

    rows = x_ref[...].astype(F32)
    scaled = (rows * g_ref[...].astype(F32)).astype(BF16)
    out_ref[:, :latent] += lax.dot_general(scaled, a_ref[...], BOTH_LAST, preferred_element_type=F32)
    out_ref[:, latent:] += folded_squares(rows)


def back_latent_kernel(x_ref, c_ref, g_ref, a_ref, b_ref, out_ref):
    latent = a_ref.shape[0]

    @pl.when(pl.program_id(0) == 0)
    def _():
        out_ref[...] = jnp.zeros_like(out_ref)

    rows = x_ref[...].astype(F32)
    scaled = (rows * g_ref[...].astype(F32)).astype(BF16)
    out_ref[:latent] += lax.dot_general(a_ref[...], scaled, BOTH_LAST, preferred_element_type=F32)
    out_ref[latent : 2 * latent] += lax.dot_general(b_ref[...], c_ref[...], BOTH_LAST, preferred_element_type=F32)
    out_ref[2 * latent :] += folded_squares(rows)


def leaving_kernel(own_ref, other_ref, x_ref, b_ref, *rest):
    out_ref, hidden = rest[-2], rest[-1]
    latent = b_ref.shape[0]

    @pl.when(pl.program_id(0) == 0)
    def _():
        total = own_ref[...] + other_ref[...]
        squares = jnp.sum(total[:, latent:], axis=1, keepdims=True)
        hidden[...] = (total[:, :latent] * lax.rsqrt(squares / D + 1e-06)).astype(BF16)

    out_ref[...] = (
        x_ref[...].astype(F32) + jnp.dot(hidden[...], b_ref[...], preferred_element_type=F32)
    ).astype(BF16)


def grad_kernel(experts, own_ref, other_ref, x_ref, g_ref, c_ref, *rest):
    outs, rows_ref = rest[:-1], rest[-1]
    latent = rows_ref.shape[1]
    depth = latent // experts
    me = lax.axis_index("expert")
    squares = own_ref[2 * latent :] + other_ref[2 * latent :]
    rscale = lax.rsqrt(jnp.sum(squares.T, axis=0, keepdims=True) / D + 1e-06)
    rows_ref[0] = (own_ref[latent : 2 * latent] + other_ref[latent : 2 * latent]) * rscale
    rows_ref[1] = (own_ref[:latent] + other_ref[:latent]) * rscale
    scaled = (x_ref[...].astype(F32) * g_ref[...].astype(F32)).astype(BF16)
    cot = c_ref[...]
    for offset in range(experts):
        at = pl.ds(pl.multiple_of((me ^ offset) * depth, depth), depth)
        error = rows_ref[0, at, :].astype(BF16)
        hidden = rows_ref[1, at, :].astype(BF16)
        outs[offset][0] = jnp.dot(error, scaled, preferred_element_type=F32).astype(BF16)
        outs[offset][1] = jnp.dot(hidden, cot, preferred_element_type=F32).astype(BF16)


def share_kernel(*refs):
    total = refs[0][...].astype(F32)
    for ref in refs[1:-1]:
        total = total + ref[...].astype(F32)
    refs[-1][...] = total.astype(BF16)


def update_kernel(share_ref, master_ref, moment_ref, second_ref, *rest):
    fresh_ref, peak_ref = rest[-2:]
    grad = share_ref[...].astype(F32)
    first = 0.9 * moment_ref[...].astype(F32) + 0.1 * grad
    secnd = 0.95 * second_ref[...].astype(F32) + 0.05 * grad * grad
    update = first / (1.0 - 0.9**10) / (jnp.sqrt(secnd / (1.0 - 0.95**10)) + 1e-08)
    weights = master_ref[...]
    fresh = weights - 0.01 * (update + 0.1 * weights)
    fresh_ref[...] = fresh
    peak = jnp.max(jnp.abs(fresh), axis=1, keepdims=True)
    for block in range(peak.shape[-1] // LANES):
        peak_ref[:, block : block + 1] = peak[:, :, block * LANES : (block + 1) * LANES]


def code_kernel(group, fresh_ref, *rest):
    peak_refs, code_ref, scale_ref, wide = rest[:-3], rest[-3], rest[-2], rest[-1]
    chunks, _, per, _ = peak_refs[0].shape
    rows_of = len(peak_refs) // group
    mine = lax.axis_index("expert") // group
    wide[...] = jnp.zeros_like(wide)
    for far in range(rows_of):
        top = peak_refs[far * group][...]
        for ref in peak_refs[far * group + 1 : (far + 1) * group]:
            top = jnp.maximum(top, ref[...])
        for side in range(2):
            for chunk in range(chunks):
                wide[side, chunk * per : (chunk + 1) * per, :] = top[chunk, side]
        where = pl.ds(mine ^ far, 1)
        for side in range(2):
            scale_ref[side, where, :] = (
                jnp.max(wide[side].T, axis=0, keepdims=True)[:, : chunks * per] + 1e-06
            )
        if far == 0:
            for side in range(2):
                scale = jnp.broadcast_to(jnp.max(wide[side], axis=1, keepdims=True), wide.shape[1:]) + 1e-06
                inverse = 1.0 / scale
                for block in range(chunks * per):
                    at = slice(block * LANES, (block + 1) * LANES)
                    code_ref[side, :, at] = (fresh_ref[side, :, at] * inverse[block : block + 1]).astype(BF16)


def place_kernel(in_ref, *rest):
    rest[-1][...] = in_ref[...]


ANY = pl.BlockSpec(memory_space=pl.ANY)


def whole(shape):
    return pl.BlockSpec(shape, lambda *_: (0,) * len(shape))


def shards(enter_fwd, enter_rev, cot_rev, gain, proj_down, proj_up, master, moment, second):
    tokens, width = enter_fwd.shape[1:]
    latent = proj_down.shape[2]
    experts = lax.axis_size("expert")
    depth = latent // experts
    blocks = width // LANES
    steps = 4 if blocks % 4 == 0 else 2
    tile = width // steps
    chunks = steps
    part = width // chunks
    head = tokens * 3 // 4
    tail = tokens - head

    def token_tile(rows):
        return pl.BlockSpec((None, rows, tile), lambda i: (0, 0, i))

    def gain_tile(copy):
        return pl.BlockSpec((None, 1, tile), lambda i: (copy, 0, i))

    def weight_tile(copy):
        return pl.BlockSpec((None, None, latent, tile), lambda i: (copy, 0, 0, i))

    packed = pl.pallas_call(
        fwd_latent_kernel,
        grid=(steps,),
        in_specs=[token_tile(tokens), gain_tile(0), weight_tile(0)],
        out_specs=whole((tokens, latent + LANES)),
        out_shape=jax.ShapeDtypeStruct((tokens, latent + LANES), F32),
        cost_estimate=cost(2 * tokens * latent * width, 2 * (tokens + latent) * width),
        name="fwd_latent",
    )(enter_fwd, gain, proj_down)
    fwd_pair = halves_of_sum(packed, "dp")

    packed = pl.pallas_call(
        back_latent_kernel,
        grid=(steps,),
        in_specs=[token_tile(tokens), token_tile(tokens), gain_tile(1), weight_tile(1), weight_tile(1)],
        out_specs=whole((2 * latent + tokens, tokens)),
        out_shape=jax.ShapeDtypeStruct((2 * latent + tokens, tokens), F32),
        cost_estimate=cost(4 * tokens * latent * width, 4 * (tokens + latent) * width),
        name="back_latent",
    )(enter_rev, cot_rev, gain, proj_down, proj_up)
    back_pair = halves_of_sum(packed, "dp")

    def leaving_rows(start, count, *after):
        at = start // count
        latent_rows = pl.BlockSpec((count, latent + LANES), lambda i: (at, 0))
        return pl.pallas_call(
            leaving_kernel,
            grid=(steps,),
            in_specs=[
                latent_rows,
                latent_rows,
                pl.BlockSpec((None, count, tile), lambda i: (0, at, i)),
                weight_tile(0),
            ]
            + [ANY] * len(after),
            out_specs=pl.BlockSpec((count, tile), lambda i: (0, i)),
            out_shape=jax.ShapeDtypeStruct((count, width), BF16),
            scratch_shapes=[pltpu.VMEM((count, latent), BF16)],
            cost_estimate=cost(2 * count * latent * width, 2 * (2 * count + latent) * width),
            name="leaving",
        )(*fwd_pair, enter_fwd, proj_up, *after)

    left_head = shifted(leaving_rows(0, head), "pipe")

    quarters = jax.ShapeDtypeStruct((2, depth, part), BF16)
    sums = []
    for chunk in range(chunks):
        pieces = pl.pallas_call(
            lambda *refs: grad_kernel(experts, *refs),
            grid=(1,),
            in_specs=[
                whole((2 * latent + tokens, tokens)),
                whole((2 * latent + tokens, tokens)),
                pl.BlockSpec((None, tokens, part), lambda i, c=chunk: (0, 0, c)),
                pl.BlockSpec((None, 1, part), lambda i, c=chunk: (1, 0, c)),
                pl.BlockSpec((None, tokens, part), lambda i, c=chunk: (0, 0, c)),
            ],
            out_specs=[whole((2, depth, part))] * experts,
            out_shape=[quarters] * experts,
            scratch_shapes=[pltpu.VMEM((2, latent, tokens), F32)],
            cost_estimate=cost(4 * tokens * latent * part, 4 * (tokens + latent) * part),
            name="grads",
        )(*back_pair, enter_rev, gain, cot_rev)
        sums.append([pieces[0]] + [exchange(pieces[k], "expert", k) for k in range(1, experts)])

    fresh = peaks = None
    shares = []
    for chunk in range(chunks):
        share = pl.pallas_call(
            share_kernel,
            grid=(1,),
            in_specs=[whole((2, depth, part))] * experts,
            out_specs=whole((2, depth, part)),
            out_shape=quarters,
            cost_estimate=cost(0, 2 * 2 * depth * part * (experts + 1)),
            name="share",
        )(*sums[chunk])
        shares.append(share)
    left_tail = shifted(leaving_rows(head, tail, shares[-1]), "pipe")

    for chunk in range(chunks):
        state = pl.BlockSpec((2, None, depth, part), lambda i, c=chunk: (0, 0, 0, c))
        kept = () if fresh is None else (fresh, peaks)
        fresh, peaks = pl.pallas_call(
            update_kernel,
            grid=(1,),
            in_specs=[whole((2, depth, part)), state, state, state] + [ANY] * len(kept),
            out_specs=[
                pl.BlockSpec((2, depth, part), lambda i, c=chunk: (0, 0, c)),
                pl.BlockSpec((None, 2, part // LANES, LANES), lambda i, c=chunk: (c, 0, 0, 0)),
            ],
            out_shape=[
                jax.ShapeDtypeStruct((2, depth, width), F32),
                jax.ShapeDtypeStruct((chunks, 2, part // LANES, LANES), F32),
            ],
            input_output_aliases={4 + k: k for k in range(len(kept))},
            cost_estimate=cost(20 * 2 * depth * part, 14 * 2 * depth * part),
            name="update",
        )(mirrored(shares[chunk], "pipe"), master, moment, second, *kept)

    peak_rows = [peaks] + [exchange(peaks, "expert", k) for k in range(1, experts)]
    group = LANES // depth
    coded, scales = pl.pallas_call(
        lambda *refs: code_kernel(group, *refs),
        grid=(1,),
        in_specs=[whole((2, depth, width))] + [whole(peaks.shape)] * experts,
        out_specs=[
            pl.BlockSpec((2, None, depth, width), lambda i: (0, 0, 0, 0)),
            pl.BlockSpec((2, None, experts // group, blocks), lambda i: (0, 0, 0, 0)),
        ],
        out_shape=[
            jax.ShapeDtypeStruct((2, 1, depth, width), BF16),
            jax.ShapeDtypeStruct((2, 1, experts // group, blocks), F32),
        ],
        scratch_shapes=[pltpu.VMEM((2, LANES, LANES), F32)],
        cost_estimate=cost(2 * 2 * depth * width, 6 * 2 * depth * width),
        name="codes",
    )(fresh, *peak_rows)

    unit = tail
    placed = None
    for start, rows in ((0, left_head), (head, left_tail)):
        kept = () if placed is None else (placed,)
        placed = pl.pallas_call(
            place_kernel,
            grid=(rows.shape[0] // unit,),
            in_specs=[pl.BlockSpec((unit, width), lambda i: (i, 0))] + [ANY] * len(kept),
            out_specs=pl.BlockSpec((None, unit, width), lambda i, s=start // unit: (0, i + s, 0)),
            out_shape=jax.ShapeDtypeStruct((1, tokens, width), BF16),
            input_output_aliases={1 + k: k for k in range(len(kept))},
            cost_estimate=cost(0, 4 * rows.shape[0] * width),
            name="place",
        )(rows, *kept)
    return (placed, coded, scales)


def solution(mesh):
    in_specs = (
        P("pipe", "expert", "dp"),
        P("pipe", "expert", "dp"),
        P("pipe", "expert", "dp"),
        P(None, "pipe", "dp"),
        P(None, "pipe", None, "dp"),
        P(None, "pipe", None, "dp"),
        P(None, "pipe", "expert", "dp"),
        P(None, "pipe", "expert", "dp"),
        P(None, "pipe", "expert", "dp"),
    )
    out_specs = (
        P("pipe", "expert", "dp"),
        P(None, "pipe", "expert", "dp"),
        P(None, "pipe", None, "dp"),
    )
    return jax.shard_map(shards, mesh=mesh, in_specs=in_specs, out_specs=out_specs, check_vma=False)
```

time: 179 us -> 114 us (0.64)
  waiting for transfers between devices: 122 us -> 18.2 us
  Pallas kernels: 0 us -> 52.1 us
  starting transfers between devices: 7.17 us -> 34.2 us
  between operations: 14.2 us -> 0.76 us
  blocking collectives: 10.5 us -> 0 us
  matrix products: 10.4 us -> 0 us
  other arithmetic: 8.84 us -> 0 us
  local copies, waits for them, and re-layouts: 4.19 us -> 6.99 us
    pallas_call x0 -> x19, Pallas kernels: none -> 52.1 us  [the longest x4 9.99 us: shards(): pl.pallas_call(lambda *refs: grad_kernel(experts, *refs), grid=(1,), in_s...]
    reduce_scatter x1 -> x0, waiting for transfers between devices: 49.4 us -> none  [shards(): lax.psum_scatter(jnp.concatenate([grad_down, grad_up], axis=1).astype(jnp...]
    ppermute x3 -> x23, waiting for transfers between devices: 55.5 us -> 18.2 us  [the longest x4 13 us: mirrored(): return lax.ppermute(block, axis, [(i, count - 1 - i) for i in range(count)])]
    ppermute x3 -> x23, starting transfers between devices: 7.09 us -> 34.2 us  [the longest x17 22.3 us: exchange(): return lax.ppermute(block, axis, [(i, i ^ offset) for i in range(count)])]
    psum x1 -> x0, waiting for transfers between devices: 17.2 us -> none  [shards(): lax.psum((fwd_raw, fwd_squares, back_raw, back_squares, back_dlat), 'dp')]
    dot_general x6 -> x0, matrix products: 10.4 us -> none  [the longest x2 6.2 us: prepare(): jnp.einsum('td,rd->tr', scaled, down, preferred_element_type=jnp.float32)]
    all_gather x1 -> x0, blocking collectives: 8.06 us -> none  [shards(): gathered = lax.all_gather(local_peak[None], 'expert', axis=0, tiled=True)]
    unnamed x22 -> x49, local copies, waits for them, and re-layouts: 2.79 us -> 6.99 us
  transfers between devices with their start and end apart: 5 -> 23, of which waited for: 5 -> 7; matrix products, arithmetic and copies ran while one was open for 1% -> 0% of each run, Pallas kernels for 0% -> 41%
where the time goes in v1:
time: 114 us; the launch traced here: 112 us
  Pallas kernels  52.1 us (46%)
  starting transfers between devices  34.2 us (30%)
  waiting for transfers between devices  18.2 us (16%)
  local copies, waits for them, and re-layouts  6.99 us (6%)
    ppermute x17, starting transfers between devices, exchange(): return lax.ppermute(block, axis, [(i, i ^ offset) for i in range(count)])  22.3 us
    ppermute x4, waiting for transfers between devices, mirrored(): return lax.ppermute(block, axis, [(i, count - 1 - i) for i in range(count)])  13 us
    pallas_call x4, Pallas kernels, shards(): pl.pallas_call(lambda *refs: grad_kernel(experts, *refs), grid=(1,), in_s...  9.99 us
    pallas_call x4, Pallas kernels, shards(): pl.pallas_call(update_kernel, grid=(1,), in_specs=[whole((2, depth, part)...  9.85 us
    pallas_call x4, Pallas kernels, shards(): pl.pallas_call(share_kernel, grid=(1,), in_specs=[whole((2, depth, part))...  8.31 us
    pallas_call x2, Pallas kernels, leaving_rows(): pl.pallas_call(leaving_kernel, grid=(steps,), in_specs=[latent_rows, late...  8.07 us
    ppermute x2, starting transfers between devices, shifted(): return lax.ppermute(block, axis, [(i, i + 1) for i in range(count - 1)])  7.77 us
    unnamed x49, local copies, waits for them, and re-layouts  6.99 us
  transfers between devices with their start and end apart: 23, of which 7 were waited for; matrix products, arithmetic and copies ran while one was open for 0% of the time, Pallas kernels for 41%

profile of v1, /device:TPU:8, one launch (start us, length us, event | category | flops | bytes accessed | tf_op | source)
XLA Modules:
  0.0 112.3 jit_solution(1254205407213256774)
XLA Ops:
  2.0 4.8 %back_latent.1.refs_0_ = f32[640,128]{1,0:T(8,128)} custom-call(bf16[1,128,3584]{2,1,0:T(8,128)(2,1)} %refs_2_.7, bf16[1,128,3584]{2,1,0:T(8,128)(2,1)} %refs_4_.7, bf16[2,1,3584]{2,1,0:T(2,128)(2,1)} %copy.19.g_ref.refs_3_, bf16[2,1,256,3584]{3,2,1,0:T(8,128)(2,1)} %a_ref.3, bf16[2,1,256,3584]{3,2,1,0:T(8,128)(2,1)} %b_ref.5), custom_call_target="tpu_custom_call" | custom-call | flops 469762048 | bytes 5505024 | tf_op jit(solution)/shard_map/back_latent/pallas_call | solution.py:207
  6.8 3.9 %fwd_latent.1.own_ref = f32[128,384]{1,0:T(8,128)} custom-call(bf16[1,128,3584]{2,1,0:T(8,128)(2,1)} %x_ref.7, bf16[2,1,3584]{2,1,0:T(2,128)(2,1)} %copy.19.g_ref.refs_3_, bf16[2,1,256,3584]{3,2,1,0:T(8,128)(2,1)} %a_ref.3), custom_call_target="tpu_custom_call" | custom-call | flops 234881024 | bytes 2752512 | tf_op jit(solution)/shard_map/fwd_latent/pallas_call | solution.py:196
  12.0 2.5 %grads.7 = (bf16[2,64,896]{2,1,0:T(8,128)(2,1)}, bf16[2,64,896]{2,1,0:T(8,128)(2,1)}, bf16[2,64,896]{2,1,0:T(8,128)(2,1)}, bf16[2,64,896]{2,1,0:T(8,128)(2,1)}) custom-call(f32[640,128]{1,0:T(8,128)} %back_latent.1.refs_0_, f32[640,128]{1,0:T(8,128)} %copy-done, bf16[1,128,3584]{2,1,0:T(8,128)(2,1)} %refs_2_.7, bf16[2,1,3584]{2,1,0:T(2,128)(2,1)} %copy.19.g_ref.refs_3_, ...), custom_call_target="tpu_custom_call" | custom-call | flops 117440512 | bytes 1376256 | tf_op jit(solution)/shard_map/grads/pallas_call | solution.py:243
  17.9 2.5 %grads.6 = (bf16[2,64,896]{2,1,0:T(8,128)(2,1)}, bf16[2,64,896]{2,1,0:T(8,128)(2,1)}, bf16[2,64,896]{2,1,0:T(8,128)(2,1)}, bf16[2,64,896]{2,1,0:T(8,128)(2,1)}) custom-call(f32[640,128]{1,0:T(8,128)} %back_latent.1.refs_0_, f32[640,128]{1,0:T(8,128)} %copy-done, bf16[1,128,3584]{2,1,0:T(8,128)(2,1)} %refs_2_.7, bf16[2,1,3584]{2,1,0:T(2,128)(2,1)} %copy.19.g_ref.refs_3_, ...), custom_call_target="tpu_custom_call" | custom-call | flops 117440512 | bytes 1376256 | tf_op jit(solution)/shard_map/grads/pallas_call | solution.py:243
  21.9 1.5 %collective-permute-start.13 = (bf16[2,64,896]{2,1,0:T(8,128)(2,1)}, bf16[2,64,896]{2,1,0:T(8,128)(2,1)S(1)}, u32[]{:S(2)}, u32[]{:S(2)}) collective-permute-start(bf16[2,64,896]{2,1,0:T(8,128)(2,1)} %get-tuple-element.39), channel_id=1, source_target_pairs={{0,4},{2,6},{4,0},{6,2},{1,5},{3,7},{5,1},{7,3},{8,12},{10,14},{12... | collective-permute-start | bytes 688136 | tf_op jit(solution)/shard_map/ppermute | solution.py:17
  23.4 2.1 %collective-permute-start.14 = (bf16[2,64,896]{2,1,0:T(8,128)(2,1)}, bf16[2,64,896]{2,1,0:T(8,128)(2,1)S(1)}, u32[]{:S(2)}, u32[]{:S(2)}) collective-permute-start(bf16[2,64,896]{2,1,0:T(8,128)(2,1)} %get-tuple-element.40), channel_id=1, source_target_pairs={{0,6},{2,4},{4,2},{6,0},{1,7},{3,5},{5,3},{7,1},{8,14},{10,12},{12... | collective-permute-start | bytes 688136 | tf_op jit(solution)/shard_map/ppermute | solution.py:17
  25.6 2.5 %grads.5 = (bf16[2,64,896]{2,1,0:T(8,128)(2,1)}, bf16[2,64,896]{2,1,0:T(8,128)(2,1)}, bf16[2,64,896]{2,1,0:T(8,128)(2,1)}, bf16[2,64,896]{2,1,0:T(8,128)(2,1)}) custom-call(f32[640,128]{1,0:T(8,128)} %back_latent.1.refs_0_, f32[640,128]{1,0:T(8,128)} %copy-done, bf16[1,128,3584]{2,1,0:T(8,128)(2,1)} %refs_2_.7, bf16[2,1,3584]{2,1,0:T(2,128)(2,1)} %copy.19.g_ref.refs_3_, ...), custom_call_target="tpu_custom_call" | custom-call | flops 117440512 | bytes 1376256 | tf_op jit(solution)/shard_map/grads/pallas_call | solution.py:243
  30.0 2.4 %collective-permute-start.8 = (bf16[2,64,896]{2,1,0:T(8,128)(2,1)}, bf16[2,64,896]{2,1,0:T(8,128)(2,1)S(1)}, u32[]{:S(2)}, u32[]{:S(2)}) collective-permute-start(bf16[2,64,896]{2,1,0:T(8,128)(2,1)} %get-tuple-element.34), channel_id=1, source_target_pairs={{0,2},{2,0},{4,6},{6,4},{1,3},{3,1},{5,7},{7,5},{8,10},{10,8},{12,... | collective-permute-start | bytes 688136 | tf_op jit(solution)/shard_map/ppermute | solution.py:17
  32.4 4.2 %leaving.3 = bf16[96,3584]{1,0:T(8,128)(2,1)} custom-call(f32[128,384]{1,0:T(8,128)} %fwd_latent.1.own_ref, f32[128,384]{1,0:T(8,128)} %copy-done.1, bf16[1,128,3584]{2,1,0:T(8,128)(2,1)} %x_ref.7, bf16[2,1,256,3584]{3,2,1,0:T(8,128)(2,1)} %b_ref.5), custom_call_target="tpu_custom_call" | custom-call | flops 176160768 | bytes 3211264 | tf_op jit(solution)/shard_map/leaving/pallas_call | solution.py:221
  36.6 3.5 %collective-permute-start.6 = (bf16[96,3584]{1,0:T(8,128)(2,1)}, bf16[96,3584]{1,0:T(8,128)(2,1)S(1)}, u32[]{:S(2)}, u32[]{:S(2)}) collective-permute-start(bf16[96,3584]{1,0:T(8,128)(2,1)} %leaving.3), channel_id=1, source_target_pairs={{0,8},{8,16},{16,24},{1,9},{9,17},{17,25},{2,10},{10,18},{18,26},{... | collective-permute-start | bytes 2064392 | tf_op jit(solution)/shard_map/ppermute | solution.py:27
  40.1 2.1 %collective-permute-done.13.refs_2_ = bf16[2,64,896]{2,1,0:T(8,128)(2,1)S(1)} collective-permute-done((bf16[2,64,896]{2,1,0:T(8,128)(2,1)}, bf16[2,64,896]{2,1,0:T(8,128)(2,1)S(1)}, u32[]{:S(2)}, u32[]{:S(2)}) %collective-permute-start.13) | collective-permute-done | bytes 229408 | tf_op jit(solution)/shard_map/ppermute | solution.py:17
  42.3 2.3 %collective-permute-start.9 = (bf16[2,64,896]{2,1,0:T(8,128)(2,1)S(1)}, bf16[2,64,896]{2,1,0:T(8,128)(2,1)S(1)}, u32[]{:S(2)}, u32[]{:S(2)}) collective-permute-start(bf16[2,64,896]{2,1,0:T(8,128)(2,1)S(1)} %copy-done.23), channel_id=1, source_target_pairs={{0,4},{2,6},{4,0},{6,2},{1,5},{3,7},{5,1},{7,3},{8,12},{10,14},{12... | collective-permute-start | bytes 688136 | tf_op jit(solution)/shard_map/ppermute | solution.py:17
  44.6 2.5 %grads.4 = (bf16[2,64,896]{2,1,0:T(8,128)(2,1)}, bf16[2,64,896]{2,1,0:T(8,128)(2,1)}, bf16[2,64,896]{2,1,0:T(8,128)(2,1)}, bf16[2,64,896]{2,1,0:T(8,128)(2,1)}) custom-call(f32[640,128]{1,0:T(8,128)} %back_latent.1.refs_0_, f32[640,128]{1,0:T(8,128)} %copy-done, bf16[1,128,3584]{2,1,0:T(8,128)(2,1)} %refs_2_.7, bf16[2,1,3584]{2,1,0:T(2,128)(2,1)} %copy.19.g_ref.refs_3_, ...), custom_call_target="tpu_custom_call" | custom-call | flops 117440512 | bytes 1376256 | tf_op jit(solution)/shard_map/grads/pallas_call | solution.py:243
  47.3 3.3 %collective-permute-start.4 = (bf16[2,64,896]{2,1,0:T(8,128)(2,1)}, bf16[2,64,896]{2,1,0:T(8,128)(2,1)S(1)}, u32[]{:S(2)}, u32[]{:S(2)}) collective-permute-start(bf16[2,64,896]{2,1,0:T(8,128)(2,1)} %get-tuple-element.32), channel_id=1, source_target_pairs={{0,6},{2,4},{4,2},{6,0},{1,7},{3,5},{5,3},{7,1},{8,14},{10,12},{12... | collective-permute-start | bytes 688136 | tf_op jit(solution)/shard_map/ppermute | solution.py:17
  50.6 2.1 %share.7 = bf16[2,64,896]{2,1,0:T(8,128)(2,1)} custom-call(bf16[2,64,896]{2,1,0:T(8,128)(2,1)} %get-tuple-element.41.refs_0_, bf16[2,64,896]{2,1,0:T(8,128)(2,1)} %copy-done.3, bf16[2,64,896]{2,1,0:T(8,128)(2,1)} %copy-done.4, bf16[2,64,896]{2,1,0:T(8,128)(2,1)} %copy-done.6), custom_call_target="tpu_custom_call" | custom-call | bytes 1146880 | tf_op jit(solution)/shard_map/share/pallas_call | solution.py:264
  52.7 1.6 %collective-permute-start.19 = (bf16[2,64,896]{2,1,0:T(8,128)(2,1)}, bf16[2,64,896]{2,1,0:T(8,128)(2,1)S(1)}, u32[]{:S(2)}, u32[]{:S(2)}) collective-permute-start(bf16[2,64,896]{2,1,0:T(8,128)(2,1)} %share.7), channel_id=1, source_target_pairs={{0,24},{8,16},{16,8},{24,0},{1,25},{9,17},{17,9},{25,1},{2,26},{10... | collective-permute-start | bytes 688136 | tf_op jit(solution)/shard_map/ppermute | solution.py:22
  54.4 2.1 %share.6 = bf16[2,64,896]{2,1,0:T(8,128)(2,1)} custom-call(bf16[2,64,896]{2,1,0:T(8,128)(2,1)} %get-tuple-element.37.refs_0_, bf16[2,64,896]{2,1,0:T(8,128)(2,1)} %copy-done.5, bf16[2,64,896]{2,1,0:T(8,128)(2,1)} %copy-done.7, bf16[2,64,896]{2,1,0:T(8,128)(2,1)} %copy-done.8), custom_call_target="tpu_custom_call" | custom-call | bytes 1146880 | tf_op jit(solution)/shard_map/share/pallas_call | solution.py:264
  56.9 2.1 %share.5 = bf16[2,64,896]{2,1,0:T(8,128)(2,1)} custom-call(bf16[2,64,896]{2,1,0:T(8,128)(2,1)} %get-tuple-element.33.refs_0_, bf16[2,64,896]{2,1,0:T(8,128)(2,1)} %copy-done.10, bf16[2,64,896]{2,1,0:T(8,128)(2,1)} %copy-done.12, bf16[2,64,896]{2,1,0:T(8,128)(2,1)} %copy-done.9), custom_call_target="tpu_custom_call" | custom-call | bytes 1146880 | tf_op jit(solution)/shard_map/share/pallas_call | solution.py:264
  59.0 1.6 %collective-permute-start.11 = (bf16[2,64,896]{2,1,0:T(8,128)(2,1)}, bf16[2,64,896]{2,1,0:T(8,128)(2,1)S(1)}, u32[]{:S(2)}, u32[]{:S(2)}) collective-permute-start(bf16[2,64,896]{2,1,0:T(8,128)(2,1)} %share.5), channel_id=1, source_target_pairs={{0,24},{8,16},{16,8},{24,0},{1,25},{9,17},{17,9},{25,1},{2,26},{10... | collective-permute-start | bytes 688136 | tf_op jit(solution)/shard_map/ppermute | solution.py:22
  61.3 2.1 %share.4.rest_0_ = bf16[2,64,896]{2,1,0:T(8,128)(2,1)} custom-call(bf16[2,64,896]{2,1,0:T(8,128)(2,1)} %get-tuple-element.29.refs_0_, bf16[2,64,896]{2,1,0:T(8,128)(2,1)} %copy-done.13, bf16[2,64,896]{2,1,0:T(8,128)(2,1)} %copy-done.14, bf16[2,64,896]{2,1,0:T(8,128)(2,1)} %copy-done.15), custom_call_target="tpu_custom_call" | custom-call | bytes 1146880 | tf_op jit(solution)/shard_map/share/pallas_call | solution.py:264
  63.8 3.9 %leaving.2 = bf16[32,3584]{1,0:T(8,128)(2,1)} custom-call(f32[128,384]{1,0:T(8,128)} %fwd_latent.1.own_ref, f32[128,384]{1,0:T(8,128)} %copy-done.1, bf16[1,128,3584]{2,1,0:T(8,128)(2,1)} %x_ref.7, bf16[2,1,256,3584]{3,2,1,0:T(8,128)(2,1)} %b_ref.5, bf16[2,64,896]{2,1,0:T(8,128)(2,1)} %share.4.rest_0_), custom_call_target="tpu_custom_call" | custom-call | flops 58720256 | bytes 2293760 | tf_op jit(solution)/shard_map/leaving/pallas_call | solution.py:221
  67.7 11.3 %collective-permute-done.19.share_ref = bf16[2,64,896]{2,1,0:T(8,128)(2,1)S(1)} collective-permute-done((bf16[2,64,896]{2,1,0:T(8,128)(2,1)}, bf16[2,64,896]{2,1,0:T(8,128)(2,1)S(1)}, u32[]{:S(2)}, u32[]{:S(2)}) %collective-permute-start.19) | collective-permute-done | bytes 229408 | tf_op jit(solution)/shard_map/ppermute | solution.py:22
  79.0 4.3 %collective-permute-start.5 = (bf16[32,3584]{1,0:T(8,128)(2,1)}, bf16[32,3584]{1,0:T(8,128)(2,1)S(1)}, u32[]{:S(2)}, u32[]{:S(2)}) collective-permute-start(bf16[32,3584]{1,0:T(8,128)(2,1)} %leaving.2), channel_id=1, source_target_pairs={{0,8},{8,16},{16,24},{1,9},{9,17},{17,25},{2,10},{10,18},{18,26},{... | collective-permute-start | bytes 688136 | tf_op jit(solution)/shard_map/ppermute | solution.py:27
  83.3 2.5 %update.4 = (f32[2,64,3584]{2,1,0:T(8,128)}, f32[4,2,7,128]{3,2,1,0:T(8,128)}) custom-call(bf16[2,64,896]{2,1,0:T(8,128)(2,1)} %copy-done.19, f32[2,1,64,3584]{3,2,1,0:T(8,128)} %master_ref.7, bf16[2,1,64,3584]{3,2,1,0:T(8,128)(2,1)} %moment_ref.7, bf16[2,1,64,3584]{3,2,1,0:T(8,128)(2,1)} %second_ref.7), custom_call_target="tpu_custom_call" | custom-call | flops 2293760 | bytes 1605632 | tf_op jit(solution)/shard_map/update/pallas_call | solution.py:279
  86.4 2.5 %update.5 = (f32[2,64,3584]{2,1,0:T(8,128)}, f32[4,2,7,128]{3,2,1,0:T(8,128)}) custom-call(bf16[2,64,896]{2,1,0:T(8,128)(2,1)} %copy-done.16, f32[2,1,64,3584]{3,2,1,0:T(8,128)} %master_ref.7, bf16[2,1,64,3584]{3,2,1,0:T(8,128)(2,1)} %moment_ref.7, bf16[2,1,64,3584]{3,2,1,0:T(8,128)(2,1)} %second_ref.7, ...), custom_call_target="tpu_custom_call", output_to_operand_aliasing={{0}: (4, {}), {1}: (5, {})} | custom-call | flops 2293760 | bytes 1605632 | tf_op jit(solution)/shard_map/update/pallas_call | solution.py:279
  89.6 2.5 %update.6 = (f32[2,64,3584]{2,1,0:T(8,128)}, f32[4,2,7,128]{3,2,1,0:T(8,128)}) custom-call(bf16[2,64,896]{2,1,0:T(8,128)(2,1)} %copy-done.17, f32[2,1,64,3584]{3,2,1,0:T(8,128)} %master_ref.7, bf16[2,1,64,3584]{3,2,1,0:T(8,128)(2,1)} %moment_ref.7, bf16[2,1,64,3584]{3,2,1,0:T(8,128)(2,1)} %second_ref.7, ...), custom_call_target="tpu_custom_call", output_to_operand_aliasing={{0}: (4, {}), {1}: (5, {})} | custom-call | flops 2293760 | bytes 1605632 | tf_op jit(solution)/shard_map/update/pallas_call | solution.py:279
  92.1 1.7 %collective-permute-done.7.share_ref = bf16[2,64,896]{2,1,0:T(8,128)(2,1)S(1)} collective-permute-done((bf16[2,64,896]{2,1,0:T(8,128)(2,1)}, bf16[2,64,896]{2,1,0:T(8,128)(2,1)S(1)}, u32[]{:S(2)}, u32[]{:S(2)}) %collective-permute-start.7) | collective-permute-done | bytes 229408 | tf_op jit(solution)/shard_map/ppermute | solution.py:22
  94.4 2.5 %update.7 = (f32[2,64,3584]{2,1,0:T(8,128)}, f32[4,2,7,128]{3,2,1,0:T(8,128)}) custom-call(bf16[2,64,896]{2,1,0:T(8,128)(2,1)} %copy-done.18, f32[2,1,64,3584]{3,2,1,0:T(8,128)} %master_ref.7, bf16[2,1,64,3584]{3,2,1,0:T(8,128)(2,1)} %moment_ref.7, bf16[2,1,64,3584]{3,2,1,0:T(8,128)(2,1)} %second_ref.7, ...), custom_call_target="tpu_custom_call", output_to_operand_aliasing={{0}: (4, {}), {1}: (5, {})} | custom-call | flops 2293760 | bytes 1605632 | tf_op jit(solution)/shard_map/update/pallas_call | solution.py:279
  97.9 2.4 %collective-permute-start.22 = (f32[4,2,7,128]{3,2,1,0:T(8,128)}, f32[4,2,7,128]{3,2,1,0:T(8,128)S(1)}, u32[]{:S(2)}, u32[]{:S(2)}) collective-permute-start(f32[4,2,7,128]{3,2,1,0:T(8,128)} %get-tuple-element.52.refs_1_), channel_id=1, source_target_pairs={{0,6},{2,4},{4,2},{6,0},{1,7},{3,5},{5,3},{7,1},{8,14},{10,12},{12... | collective-permute-start | bytes 86024 | tf_op jit(solution)/shard_map/ppermute | solution.py:17
  103.6 2.7 %codes.1 = (bf16[2,1,64,3584]{3,2,1,0:T(8,128)(2,1)}, f32[2,1,2,28]{3,2,1,0:T(2,128)}) custom-call(f32[2,64,3584]{2,1,0:T(8,128)} %get-tuple-element.51.refs_0_, f32[4,2,7,128]{3,2,1,0:T(8,128)} %get-tuple-element.52.refs_1_, f32[4,2,7,128]{3,2,1,0:T(8,128)} %copy-done.20, f32[4,2,7,128]{3,2,1,0:T(8,128)} %copy-done.21, f32[4,2,7,128]{3,2,1,0:T(8,128)} %copy-done.22), custom_call_target="tpu_custom_call" | custom-call | flops 917504 | bytes 2752512 | tf_op jit(solution)/shard_map/codes/pallas_call | solution.py:298
  107.1 2.8 %place.2.rest_0_ = bf16[1,128,3584]{2,1,0:T(8,128)(2,1)} custom-call(bf16[96,3584]{1,0:T(8,128)(2,1)} %copy-done.2), custom_call_target="tpu_custom_call" | custom-call | bytes 1376256 | tf_op jit(solution)/shard_map/place/pallas_call | solution.py:319
  110.6 1.6 %place.3 = bf16[1,128,3584]{2,1,0:T(8,128)(2,1)} custom-call(bf16[32,3584]{1,0:T(8,128)(2,1)} %copy-done.11, bf16[1,128,3584]{2,1,0:T(8,128)(2,1)} %place.2.rest_0_), custom_call_target="tpu_custom_call", output_to_operand_aliasing={{}: (1, {})} | custom-call | bytes 458752 | tf_op jit(solution)/shard_map/place/pallas_call | solution.py:319
  (82 shorter events, 19.2 us)
Async XLA Ops:
  6.8 4.4 %collective-permute-start.1 = (f32[640,128]{1,0:T(8,128)}, f32[640,128]{1,0:T(8,128)S(1)}, u32[]{:S(2)}, u32[]{:S(2)}) collective-permute-start(f32[640,128]{1,0:T(8,128)} %back_latent.1.refs_0_), channel_id=1, source_target_pairs={{0,1},{1,0},{2,3},{3,2},{4,5},{5,4},{6,7},{7,6},{8,9},{9,8},{10,11... | collective-permute-start | bytes 983048 | tf_op jit(solution)/shard_map/ppermute | solution.py:17
  10.7 11.2 %collective-permute-start = (f32[128,384]{1,0:T(8,128)}, f32[128,384]{1,0:T(8,128)S(1)}, u32[]{:S(2)}, u32[]{:S(2)}) collective-permute-start(f32[128,384]{1,0:T(8,128)} %fwd_latent.1.own_ref), channel_id=1, source_target_pairs={{0,1},{1,0},{2,3},{3,2},{4,5},{5,4},{6,7},{7,6},{8,9},{9,8},{10,11... | collective-permute-start | bytes 589832 | tf_op jit(solution)/shard_map/ppermute | solution.py:17
  14.4 9.0 %collective-permute-start.16 = (bf16[2,64,896]{2,1,0:T(8,128)(2,1)}, bf16[2,64,896]{2,1,0:T(8,128)(2,1)S(1)}, u32[]{:S(2)}, u32[]{:S(2)}) collective-permute-start(bf16[2,64,896]{2,1,0:T(8,128)(2,1)} %get-tuple-element.42), channel_id=1, source_target_pairs={{0,2},{2,0},{4,6},{6,4},{1,3},{3,1},{5,7},{7,5},{8,10},{10,8},{12,... | collective-permute-start | bytes 688136 | tf_op jit(solution)/shard_map/ppermute | solution.py:17
  15.9 12.6 %collective-permute-start.17 = (bf16[2,64,896]{2,1,0:T(8,128)(2,1)}, bf16[2,64,896]{2,1,0:T(8,128)(2,1)S(1)}, u32[]{:S(2)}, u32[]{:S(2)}) collective-permute-start(bf16[2,64,896]{2,1,0:T(8,128)(2,1)} %get-tuple-element.43), channel_id=1, source_target_pairs={{0,4},{2,6},{4,0},{6,2},{1,5},{3,7},{5,1},{7,3},{8,12},{10,14},{12... | collective-permute-start | bytes 688136 | tf_op jit(solution)/shard_map/ppermute | solution.py:17
  17.4 12.5 %collective-permute-start.18 = (bf16[2,64,896]{2,1,0:T(8,128)(2,1)}, bf16[2,64,896]{2,1,0:T(8,128)(2,1)S(1)}, u32[]{:S(2)}, u32[]{:S(2)}) collective-permute-start(bf16[2,64,896]{2,1,0:T(8,128)(2,1)} %get-tuple-element.44), channel_id=1, source_target_pairs={{0,6},{2,4},{4,2},{6,0},{1,7},{3,5},{5,3},{7,1},{8,14},{10,12},{12... | collective-permute-start | bytes 688136 | tf_op jit(solution)/shard_map/ppermute | solution.py:17
  20.4 16.2 %collective-permute-start.12 = (bf16[2,64,896]{2,1,0:T(8,128)(2,1)}, bf16[2,64,896]{2,1,0:T(8,128)(2,1)S(1)}, u32[]{:S(2)}, u32[]{:S(2)}) collective-permute-start(bf16[2,64,896]{2,1,0:T(8,128)(2,1)} %get-tuple-element.38), channel_id=1, source_target_pairs={{0,2},{2,0},{4,6},{6,4},{1,3},{3,1},{5,7},{7,5},{8,10},{10,8},{12,... | collective-permute-start | bytes 688136 | tf_op jit(solution)/shard_map/ppermute | solution.py:17
  21.9 10.5 %copy-start.1 = (f32[128,384]{1,0:T(8,128)}, f32[128,384]{1,0:T(8,128)S(1)}, u32[]{:S(2)}) copy-start(f32[128,384]{1,0:T(8,128)S(1)} %collective-permute-done.other_ref) | copy-start | bytes 589828
  21.9 20.3 %collective-permute-start.13 = (bf16[2,64,896]{2,1,0:T(8,128)(2,1)}, bf16[2,64,896]{2,1,0:T(8,128)(2,1)S(1)}, u32[]{:S(2)}, u32[]{:S(2)}) collective-permute-start(bf16[2,64,896]{2,1,0:T(8,128)(2,1)} %get-tuple-element.39), channel_id=1, source_target_pairs={{0,4},{2,6},{4,0},{6,2},{1,5},{3,7},{5,1},{7,3},{8,12},{10,14},{12... | collective-permute-start | bytes 688136 | tf_op jit(solution)/shard_map/ppermute | solution.py:17
  23.4 13.1 %copy-start.3 = (bf16[2,64,896]{2,1,0:T(8,128)(2,1)}, bf16[2,64,896]{2,1,0:T(8,128)(2,1)S(1)}, u32[]{:S(2)}) copy-start(bf16[2,64,896]{2,1,0:T(8,128)(2,1)S(1)} %collective-permute-done.16.refs_1_) | copy-start | bytes 688132
  23.4 23.6 %collective-permute-start.14 = (bf16[2,64,896]{2,1,0:T(8,128)(2,1)}, bf16[2,64,896]{2,1,0:T(8,128)(2,1)S(1)}, u32[]{:S(2)}, u32[]{:S(2)}) collective-permute-start(bf16[2,64,896]{2,1,0:T(8,128)(2,1)} %get-tuple-element.40), channel_id=1, source_target_pairs={{0,6},{2,4},{4,2},{6,0},{1,7},{3,5},{5,3},{7,1},{8,14},{10,12},{12... | collective-permute-start | bytes 688136 | tf_op jit(solution)/shard_map/ppermute | solution.py:17
  28.5 8.1 %copy-start.4 = (bf16[2,64,896]{2,1,0:T(8,128)(2,1)}, bf16[2,64,896]{2,1,0:T(8,128)(2,1)S(1)}, u32[]{:S(2)}) copy-start(bf16[2,64,896]{2,1,0:T(8,128)(2,1)S(1)} %collective-permute-done.17.refs_2_) | copy-start | bytes 688132
  28.5 18.6 %collective-permute-start.10 = (bf16[2,64,896]{2,1,0:T(8,128)(2,1)}, bf16[2,64,896]{2,1,0:T(8,128)(2,1)S(1)}, u32[]{:S(2)}, u32[]{:S(2)}) collective-permute-start(bf16[2,64,896]{2,1,0:T(8,128)(2,1)} %get-tuple-element.36), channel_id=1, source_target_pairs={{0,6},{2,4},{4,2},{6,0},{1,7},{3,5},{5,3},{7,1},{8,14},{10,12},{12... | collective-permute-start | bytes 688136 | tf_op jit(solution)/shard_map/ppermute | solution.py:17
  30.0 12.3 %copy-start.23 = (bf16[2,64,896]{2,1,0:T(8,128)(2,1)S(1)}, bf16[2,64,896]{2,1,0:T(8,128)(2,1)}, u32[]{:S(2)}) copy-start(bf16[2,64,896]{2,1,0:T(8,128)(2,1)} %get-tuple-element.35) | copy-start | bytes 688132
  30.0 17.3 %collective-permute-start.8 = (bf16[2,64,896]{2,1,0:T(8,128)(2,1)}, bf16[2,64,896]{2,1,0:T(8,128)(2,1)S(1)}, u32[]{:S(2)}, u32[]{:S(2)}) collective-permute-start(bf16[2,64,896]{2,1,0:T(8,128)(2,1)} %get-tuple-element.34), channel_id=1, source_target_pairs={{0,2},{2,0},{4,6},{6,4},{1,3},{3,1},{5,7},{7,5},{8,10},{10,8},{12,... | collective-permute-start | bytes 688136 | tf_op jit(solution)/shard_map/ppermute | solution.py:17
  36.6 16.1 %copy-start.5 = (bf16[2,64,896]{2,1,0:T(8,128)(2,1)}, bf16[2,64,896]{2,1,0:T(8,128)(2,1)S(1)}, u32[]{:S(2)}) copy-start(bf16[2,64,896]{2,1,0:T(8,128)(2,1)S(1)} %collective-permute-done.12.refs_1_) | copy-start | bytes 688132
  36.6 69.7 %collective-permute-start.6 = (bf16[96,3584]{1,0:T(8,128)(2,1)}, bf16[96,3584]{1,0:T(8,128)(2,1)S(1)}, u32[]{:S(2)}, u32[]{:S(2)}) collective-permute-start(bf16[96,3584]{1,0:T(8,128)(2,1)} %leaving.3), channel_id=1, source_target_pairs={{0,8},{8,16},{16,24},{1,9},{9,17},{17,25},{2,10},{10,18},{18,26},{... | collective-permute-start | bytes 2064392 | tf_op jit(solution)/shard_map/ppermute | solution.py:27
  42.3 10.4 %copy-start.7 = (bf16[2,64,896]{2,1,0:T(8,128)(2,1)}, bf16[2,64,896]{2,1,0:T(8,128)(2,1)S(1)}, u32[]{:S(2)}) copy-start(bf16[2,64,896]{2,1,0:T(8,128)(2,1)S(1)} %collective-permute-done.13.refs_2_) | copy-start | bytes 688132
  42.3 10.4 %collective-permute-start.9 = (bf16[2,64,896]{2,1,0:T(8,128)(2,1)S(1)}, bf16[2,64,896]{2,1,0:T(8,128)(2,1)S(1)}, u32[]{:S(2)}, u32[]{:S(2)}) collective-permute-start(bf16[2,64,896]{2,1,0:T(8,128)(2,1)S(1)} %copy-done.23), channel_id=1, source_target_pairs={{0,4},{2,6},{4,0},{6,2},{1,5},{3,7},{5,1},{7,3},{8,12},{10,14},{12... | collective-permute-start | bytes 688136 | tf_op jit(solution)/shard_map/ppermute | solution.py:17
  47.1 7.3 %copy-start.8 = (bf16[2,64,896]{2,1,0:T(8,128)(2,1)}, bf16[2,64,896]{2,1,0:T(8,128)(2,1)S(1)}, u32[]{:S(2)}) copy-start(bf16[2,64,896]{2,1,0:T(8,128)(2,1)S(1)} %collective-permute-done.14.refs_3_) | copy-start | bytes 688132
  47.1 9.4 %collective-permute-start.2 = (bf16[2,64,896]{2,1,0:T(8,128)(2,1)}, bf16[2,64,896]{2,1,0:T(8,128)(2,1)S(1)}, u32[]{:S(2)}, u32[]{:S(2)}) collective-permute-start(bf16[2,64,896]{2,1,0:T(8,128)(2,1)} %get-tuple-element.30), channel_id=1, source_target_pairs={{0,2},{2,0},{4,6},{6,4},{1,3},{3,1},{5,7},{7,5},{8,10},{10,8},{12,... | collective-permute-start | bytes 688136 | tf_op jit(solution)/shard_map/ppermute | solution.py:17
  47.1 9.8 %copy-start.9 = (bf16[2,64,896]{2,1,0:T(8,128)(2,1)}, bf16[2,64,896]{2,1,0:T(8,128)(2,1)S(1)}, u32[]{:S(2)}) copy-start(bf16[2,64,896]{2,1,0:T(8,128)(2,1)S(1)} %collective-permute-done.10.refs_3_) | copy-start | bytes 688132
  47.2 11.8 %collective-permute-start.3 = (bf16[2,64,896]{2,1,0:T(8,128)(2,1)}, bf16[2,64,896]{2,1,0:T(8,128)(2,1)S(1)}, u32[]{:S(2)}, u32[]{:S(2)}) collective-permute-start(bf16[2,64,896]{2,1,0:T(8,128)(2,1)} %get-tuple-element.31), channel_id=1, source_target_pairs={{0,4},{2,6},{4,0},{6,2},{1,5},{3,7},{5,1},{7,3},{8,12},{10,14},{12... | collective-permute-start | bytes 688136 | tf_op jit(solution)/shard_map/ppermute | solution.py:17
  47.3 9.6 %copy-start.10 = (bf16[2,64,896]{2,1,0:T(8,128)(2,1)}, bf16[2,64,896]{2,1,0:T(8,128)(2,1)S(1)}, u32[]{:S(2)}) copy-start(bf16[2,64,896]{2,1,0:T(8,128)(2,1)S(1)} %collective-permute-done.8.refs_1_) | copy-start | bytes 688132
  47.3 13.3 %collective-permute-start.4 = (bf16[2,64,896]{2,1,0:T(8,128)(2,1)}, bf16[2,64,896]{2,1,0:T(8,128)(2,1)S(1)}, u32[]{:S(2)}, u32[]{:S(2)}) collective-permute-start(bf16[2,64,896]{2,1,0:T(8,128)(2,1)} %get-tuple-element.32), channel_id=1, source_target_pairs={{0,6},{2,4},{4,2},{6,0},{1,7},{3,5},{5,3},{7,1},{8,14},{10,12},{12... | collective-permute-start | bytes 688136 | tf_op jit(solution)/shard_map/ppermute | solution.py:17
  52.7 26.3 %collective-permute-start.19 = (bf16[2,64,896]{2,1,0:T(8,128)(2,1)}, bf16[2,64,896]{2,1,0:T(8,128)(2,1)S(1)}, u32[]{:S(2)}, u32[]{:S(2)}) collective-permute-start(bf16[2,64,896]{2,1,0:T(8,128)(2,1)} %share.7), channel_id=1, source_target_pairs={{0,24},{8,16},{16,8},{24,0},{1,25},{9,17},{17,9},{25,1},{2,26},{10... | collective-permute-start | bytes 688136 | tf_op jit(solution)/shard_map/ppermute | solution.py:22
  56.5 29.3 %collective-permute-start.15 = (bf16[2,64,896]{2,1,0:T(8,128)(2,1)}, bf16[2,64,896]{2,1,0:T(8,128)(2,1)S(1)}, u32[]{:S(2)}, u32[]{:S(2)}) collective-permute-start(bf16[2,64,896]{2,1,0:T(8,128)(2,1)} %share.6), channel_id=1, source_target_pairs={{0,24},{8,16},{16,8},{24,0},{1,25},{9,17},{17,9},{25,1},{2,26},{10... | collective-permute-start | bytes 688136 | tf_op jit(solution)/shard_map/ppermute | solution.py:22
  59.0 29.9 %collective-permute-start.11 = (bf16[2,64,896]{2,1,0:T(8,128)(2,1)}, bf16[2,64,896]{2,1,0:T(8,128)(2,1)S(1)}, u32[]{:S(2)}, u32[]{:S(2)}) collective-permute-start(bf16[2,64,896]{2,1,0:T(8,128)(2,1)} %share.5), channel_id=1, source_target_pairs={{0,24},{8,16},{16,8},{24,0},{1,25},{9,17},{17,9},{25,1},{2,26},{10... | collective-permute-start | bytes 688136 | tf_op jit(solution)/shard_map/ppermute | solution.py:22
  63.3 30.4 %collective-permute-start.7 = (bf16[2,64,896]{2,1,0:T(8,128)(2,1)}, bf16[2,64,896]{2,1,0:T(8,128)(2,1)S(1)}, u32[]{:S(2)}, u32[]{:S(2)}) collective-permute-start(bf16[2,64,896]{2,1,0:T(8,128)(2,1)} %share.4.rest_0_), channel_id=1, source_target_pairs={{0,24},{8,16},{16,8},{24,0},{1,25},{9,17},{17,9},{25,1},{2,26},{10... | collective-permute-start | bytes 688136 | tf_op jit(solution)/shard_map/ppermute | solution.py:22
  79.0 30.9 %collective-permute-start.5 = (bf16[32,3584]{1,0:T(8,128)(2,1)}, bf16[32,3584]{1,0:T(8,128)(2,1)S(1)}, u32[]{:S(2)}, u32[]{:S(2)}) collective-permute-start(bf16[32,3584]{1,0:T(8,128)(2,1)} %leaving.2), channel_id=1, source_target_pairs={{0,8},{8,16},{16,24},{1,9},{9,17},{17,25},{2,10},{10,18},{18,26},{... | collective-permute-start | bytes 688136 | tf_op jit(solution)/shard_map/ppermute | solution.py:27
  96.9 4.1 %collective-permute-start.20 = (f32[4,2,7,128]{3,2,1,0:T(8,128)}, f32[4,2,7,128]{3,2,1,0:T(8,128)S(1)}, u32[]{:S(2)}, u32[]{:S(2)}) collective-permute-start(f32[4,2,7,128]{3,2,1,0:T(8,128)} %get-tuple-element.52.refs_1_), channel_id=1, source_target_pairs={{0,2},{2,0},{4,6},{6,4},{1,3},{3,1},{5,7},{7,5},{8,10},{10,8},{12,... | collective-permute-start | bytes 86024 | tf_op jit(solution)/shard_map/ppermute | solution.py:17
  97.4 4.1 %collective-permute-start.21 = (f32[4,2,7,128]{3,2,1,0:T(8,128)}, f32[4,2,7,128]{3,2,1,0:T(8,128)S(1)}, u32[]{:S(2)}, u32[]{:S(2)}) collective-permute-start(f32[4,2,7,128]{3,2,1,0:T(8,128)} %get-tuple-element.52.refs_1_), channel_id=1, source_target_pairs={{0,4},{2,6},{4,0},{6,2},{1,5},{3,7},{5,1},{7,3},{8,12},{10,14},{12... | collective-permute-start | bytes 86024 | tf_op jit(solution)/shard_map/ppermute | solution.py:17
  97.9 5.0 %collective-permute-start.22 = (f32[4,2,7,128]{3,2,1,0:T(8,128)}, f32[4,2,7,128]{3,2,1,0:T(8,128)S(1)}, u32[]{:S(2)}, u32[]{:S(2)}) collective-permute-start(f32[4,2,7,128]{3,2,1,0:T(8,128)} %get-tuple-element.52.refs_1_), channel_id=1, source_target_pairs={{0,6},{2,4},{4,2},{6,0},{1,7},{3,5},{5,3},{7,1},{8,14},{10,12},{12... | collective-permute-start | bytes 86024 | tf_op jit(solution)/shard_map/ppermute | solution.py:17
  (15 other events, 29.8 us)

commit v2 on v1

--- a/solution.py
+++ b/solution.py
@@ -38,6 +38,9 @@
         block = block + other
 
 
+ROOM = pltpu.CompilerParams(vmem_limit_bytes=16 << 20)
+
+
 def cost(flops, nbytes):
     return pl.CostEstimate(flops=flops, bytes_accessed=nbytes, transcendentals=0)
 
@@ -64,7 +67,8 @@
     out_ref[:, latent:] += folded_squares(rows)
 
 
-def back_latent_kernel(x_ref, c_ref, g_ref, a_ref, b_ref, out_ref):
+def back_latent_kernel(x_ref, c_ref, g_ref, a_ref, b_ref, *rest):
+    out_ref = rest[-1]
     latent = a_ref.shape[0]
 
     @pl.when(pl.program_id(0) == 0)
@@ -94,7 +98,7 @@
 
 
 def grad_kernel(experts, own_ref, other_ref, x_ref, g_ref, c_ref, *rest):
-    outs, rows_ref = rest[:-1], rest[-1]
+    outs, rows_ref = rest[-1 - experts : -1], rest[-1]
     latent = rows_ref.shape[1]
     depth = latent // experts
     me = lax.axis_index("expert")
@@ -112,9 +116,9 @@
         outs[offset][1] = jnp.dot(hidden, cot, preferred_element_type=F32).astype(BF16)
 
 
-def share_kernel(*refs):
+def share_kernel(experts, *refs):
     total = refs[0][...].astype(F32)
-    for ref in refs[1:-1]:
+    for ref in refs[1:experts]:
         total = total + ref[...].astype(F32)
     refs[-1][...] = total.astype(BF16)
 
@@ -199,6 +203,7 @@
         in_specs=[token_tile(tokens), gain_tile(0), weight_tile(0)],
         out_specs=whole((tokens, latent + LANES)),
         out_shape=jax.ShapeDtypeStruct((tokens, latent + LANES), F32),
+        compiler_params=ROOM,
         cost_estimate=cost(2 * tokens * latent * width, 2 * (tokens + latent) * width),
         name="fwd_latent",
     )(enter_fwd, gain, proj_down)
@@ -207,12 +212,13 @@
     packed = pl.pallas_call(
         back_latent_kernel,
         grid=(steps,),
-        in_specs=[token_tile(tokens), token_tile(tokens), gain_tile(1), weight_tile(1), weight_tile(1)],
+        in_specs=[token_tile(tokens), token_tile(tokens), gain_tile(1), weight_tile(1), weight_tile(1), ANY],
         out_specs=whole((2 * latent + tokens, tokens)),
         out_shape=jax.ShapeDtypeStruct((2 * latent + tokens, tokens), F32),
+        compiler_params=ROOM,
         cost_estimate=cost(4 * tokens * latent * width, 4 * (tokens + latent) * width),
         name="back_latent",
-    )(enter_rev, cot_rev, gain, proj_down, proj_up)
+    )(enter_rev, cot_rev, gain, proj_down, proj_up, packed)
     back_pair = halves_of_sum(packed, "dp")
 
     def leaving_rows(start, count, *after):
@@ -231,46 +237,55 @@
             out_specs=pl.BlockSpec((count, tile), lambda i: (0, i)),
             out_shape=jax.ShapeDtypeStruct((count, width), BF16),
             scratch_shapes=[pltpu.VMEM((count, latent), BF16)],
-            cost_estimate=cost(2 * count * latent * width, 2 * (2 * count + latent) * width),
+            compiler_params=ROOM,
+        cost_estimate=cost(2 * count * latent * width, 2 * (2 * count + latent) * width),
             name="leaving",
         )(*fwd_pair, enter_fwd, proj_up, *after)
 
-    left_head = shifted(leaving_rows(0, head), "pipe")
+    first_rows = leaving_rows(0, head)
+    left_head = shifted(first_rows, "pipe")
 
     quarters = jax.ShapeDtypeStruct((2, depth, part), BF16)
-    sums = []
-    for chunk in range(chunks):
-        pieces = pl.pallas_call(
+
+    def grads(chunk, *after):
+        return pl.pallas_call(
             lambda *refs: grad_kernel(experts, *refs),
             grid=(1,),
             in_specs=[
                 whole((2 * latent + tokens, tokens)),
                 whole((2 * latent + tokens, tokens)),
-                pl.BlockSpec((None, tokens, part), lambda i, c=chunk: (0, 0, c)),
-                pl.BlockSpec((None, 1, part), lambda i, c=chunk: (1, 0, c)),
-                pl.BlockSpec((None, tokens, part), lambda i, c=chunk: (0, 0, c)),
-            ],
+                pl.BlockSpec((None, tokens, part), lambda i: (0, 0, chunk)),
+                pl.BlockSpec((None, 1, part), lambda i: (1, 0, chunk)),
+                pl.BlockSpec((None, tokens, part), lambda i: (0, 0, chunk)),
+            ]
+            + [ANY] * len(after),
             out_specs=[whole((2, depth, part))] * experts,
             out_shape=[quarters] * experts,
             scratch_shapes=[pltpu.VMEM((2, latent, tokens), F32)],
+            compiler_params=ROOM,
             cost_estimate=cost(4 * tokens * latent * part, 4 * (tokens + latent) * part),
             name="grads",
-        )(*back_pair, enter_rev, gain, cot_rev)
-        sums.append([pieces[0]] + [exchange(pieces[k], "expert", k) for k in range(1, experts)])
-
-    fresh = peaks = None
-    shares = []
-    for chunk in range(chunks):
-        share = pl.pallas_call(
-            share_kernel,
+        )(*back_pair, enter_rev, gain, cot_rev, *after)
+
+    def summed(pieces, *after):
+        others = [exchange(pieces[k], "expert", k) for k in range(1, experts)]
+        return pl.pallas_call(
+            lambda *refs: share_kernel(experts, *refs),
             grid=(1,),
-            in_specs=[whole((2, depth, part))] * experts,
+            in_specs=[whole((2, depth, part))] * experts + [ANY] * len(after),
             out_specs=whole((2, depth, part)),
             out_shape=quarters,
+            compiler_params=ROOM,
             cost_estimate=cost(0, 2 * 2 * depth * part * (experts + 1)),
             name="share",
-        )(*sums[chunk])
-        shares.append(share)
+        )(pieces[0], *others, *after)
+
+    shares, arrived = [], [left_head]
+    for chunk in range(chunks):
+        pieces = grads(chunk, first_rows, *shares[-2:-1])
+        shares.append(summed(pieces, *arrived[chunk - 1 : chunk]))
+        arrived.append(mirrored(shares[-1], "pipe"))
+    fresh = peaks = None
     left_tail = shifted(leaving_rows(head, tail, shares[-1]), "pipe")
 
     for chunk in range(chunks):
@@ -289,9 +304,10 @@
                 jax.ShapeDtypeStruct((chunks, 2, part // LANES, LANES), F32),
             ],
             input_output_aliases={4 + k: k for k in range(len(kept))},
-            cost_estimate=cost(20 * 2 * depth * part, 14 * 2 * depth * part),
+            compiler_params=ROOM,
+        cost_estimate=cost(20 * 2 * depth * part, 14 * 2 * depth * part),
             name="update",
-        )(mirrored(shares[chunk], "pipe"), master, moment, second, *kept)
+        )(arrived[1 + chunk], master, moment, second, *kept)
 
     peak_rows = [peaks] + [exchange(peaks, "expert", k) for k in range(1, experts)]
     group = LANES // depth
@@ -308,6 +324,7 @@
             jax.ShapeDtypeStruct((2, 1, experts // group, blocks), F32),
         ],
         scratch_shapes=[pltpu.VMEM((2, LANES, LANES), F32)],
+        compiler_params=ROOM,
         cost_estimate=cost(2 * 2 * depth * width, 6 * 2 * depth * width),
         name="codes",
     )(fresh, *peak_rows)
@@ -323,7 +340,8 @@
             out_specs=pl.BlockSpec((None, unit, width), lambda i, s=start // unit: (0, i + s, 0)),
             out_shape=jax.ShapeDtypeStruct((1, tokens, width), BF16),
             input_output_aliases={1 + k: k for k in range(len(kept))},
-            cost_estimate=cost(0, 4 * rows.shape[0] * width),
+            compiler_params=ROOM,
+        cost_estimate=cost(0, 4 * rows.shape[0] * width),
             name="place",
         )(rows, *kept)
     return (placed, coded, scales)

time: 114 us -> 94.7 us (0.83)
  the two profiles are of different devices: /device:TPU:8 before, /device:TPU:0 now
where the time goes in v2:
time: 94.7 us; the launch traced here: 94.3 us
  starting transfers between devices  47.5 us (50%)
  waiting for transfers between devices  22.7 us (24%)
  Pallas kernels  15.4 us (16%)
  local copies, waits for them, and re-layouts  7.92 us (8%)
    ppermute x17, waiting for transfers between devices, exchange(): return lax.ppermute(block, axis, [(i, i ^ offset) for i in range(count)])  20.8 us
    ppermute x17, starting transfers between devices, exchange(): return lax.ppermute(block, axis, [(i, i ^ offset) for i in range(count)])  20.2 us
    ppermute x2, starting transfers between devices, shifted(): return lax.ppermute(block, axis, [(i, i + 1) for i in range(count - 1)])  18.8 us
    ppermute x4, starting transfers between devices, mirrored(): return lax.ppermute(block, axis, [(i, count - 1 - i) for i in range(count)])  8.55 us
    unnamed x23, local copies, waits for them, and re-layouts  7.92 us
    pallas_call x4, Pallas kernels, shards(): pl.pallas_call(update_kernel, grid=(1,), in_specs=[whole((2, depth, part)...  3.13 us
    pallas_call x2, Pallas kernels, leaving_rows(): pl.pallas_call(leaving_kernel, grid=(steps,), in_specs=[latent_rows, late...  2.49 us
    pallas_call x1, Pallas kernels, shards(): pl.pallas_call(back_latent_kernel, grid=(steps,), in_specs=[token_tile(to...  2.26 us
  transfers between devices with their start and end apart: 23, of which 10 were waited for; matrix products, arithmetic and copies ran while one was open for 0% of the time, Pallas kernels for 11%

profile of v2, /device:TPU:0, one launch (start us, length us, event | category | flops | bytes accessed | tf_op | source)
XLA Modules:
  0.0 94.3 jit_solution(9889584063767517111)
XLA Ops:
  1.4 2.0 %copy-done.5 = bf16[2,1,256,3584]{3,2,1,0:T(8,128)(2,1)S(1)} copy-done((bf16[2,1,256,3584]{3,2,1,0:T(8,128)(2,1)S(1)}, bf16[2,1,256,3584]{3,2,1,0:T(8,128)(2,1)}, u32[]{:S(2)}) %copy-start.5) | copy-done | bytes 3670040
  3.4 1.2 %copy-done.9 = bf16[1,128,3584]{2,1,0:T(8,128)(2,1)S(1)} copy-done((bf16[1,128,3584]{2,1,0:T(8,128)(2,1)S(1)}, bf16[1,128,3584]{2,1,0:T(8,128)(2,1)}, u32[]{:S(2)}) %copy-start.9) | copy-done | bytes 917528
  4.6 1.5 %fwd_latent.1.rest_0_.own_ref = f32[128,384]{1,0:T(8,128)S(1)} custom-call(bf16[1,128,3584]{2,1,0:T(8,128)(2,1)S(1)} %copy-done.9, bf16[2,1,3584]{2,1,0:T(2,128)(2,1)S(1)} %copy.19.g_ref.refs_3_, bf16[2,1,256,3584]{3,2,1,0:T(8,128)(2,1)S(1)} %copy-done.5), custom_call_target="tpu_custom_call" | custom-call | flops 234881024 | bytes 2752512 | tf_op jit(solution)/shard_map/fwd_latent/pallas_call | solution.py:200
  8.1 2.0 %copy-done.6 = bf16[2,1,256,3584]{3,2,1,0:T(8,128)(2,1)S(1)} copy-done((bf16[2,1,256,3584]{3,2,1,0:T(8,128)(2,1)S(1)}, bf16[2,1,256,3584]{3,2,1,0:T(8,128)(2,1)}, u32[]{:S(2)}) %copy-start.6) | copy-done | bytes 3670040
  10.1 2.3 %back_latent.1.refs_0_ = f32[640,128]{1,0:T(8,128)S(1)} custom-call(bf16[1,128,3584]{2,1,0:T(8,128)(2,1)S(1)} %copy-done.2, bf16[1,128,3584]{2,1,0:T(8,128)(2,1)S(1)} %copy-done.3, bf16[2,1,3584]{2,1,0:T(2,128)(2,1)S(1)} %copy.19.g_ref.refs_3_, bf16[2,1,256,3584]{3,2,1,0:T(8,128)(2,1)S(1)} %copy-done.6, bf16[2,1,256,3584]{3,2,1,0:T(8,128)(2,1)S(1)} %copy-done, ...), custom_call_target="tpu_custom_call" | custom-call | flops 469762048 | bytes 5505024 | tf_op jit(solution)/shard_map/back_latent/pallas_call | solution.py:212
  13.0 1.5 %collective-permute-done.other_ref = f32[128,384]{1,0:T(8,128)S(1)} collective-permute-done((f32[128,384]{1,0:T(8,128)S(1)}, f32[128,384]{1,0:T(8,128)S(1)}, u32[]{:S(2)}, u32[]{:S(2)}) %collective-permute-start) | collective-permute-done | bytes 196640 | tf_op jit(solution)/shard_map/ppermute | solution.py:17
  14.4 1.3 %leaving.2.refs_5_ = bf16[96,3584]{1,0:T(8,128)(2,1)S(1)} custom-call(f32[128,384]{1,0:T(8,128)S(1)} %fwd_latent.1.rest_0_.own_ref, f32[128,384]{1,0:T(8,128)S(1)} %collective-permute-done.other_ref, bf16[1,128,3584]{2,1,0:T(8,128)(2,1)S(1)} %copy-done.10, bf16[2,1,256,3584]{3,2,1,0:T(8,128)(2,1)S(1)} %copy-done), custom_call_target="tpu_custom_call" | custom-call | flops 176160768 | bytes 3211264 | tf_op jit(solution)/shard_map/leaving/pallas_call | solution.py:227
  15.8 4.9 %collective-permute-start.5 = (bf16[96,3584]{1,0:T(8,128)(2,1)S(1)}, bf16[96,3584]{1,0:T(8,128)(2,1)S(1)}, u32[]{:S(2)}, u32[]{:S(2)}) collective-permute-start(bf16[96,3584]{1,0:T(8,128)(2,1)S(1)} %leaving.2.refs_5_), channel_id=1, source_target_pairs={{0,8},{8,16},{16,24},{1,9},{9,17},{17,25},{2,10},{10,18},{18,26},{... | collective-permute-start | bytes 2064392 | tf_op jit(solution)/shard_map/ppermute | solution.py:27
  21.2 1.6 %collective-permute-start.12 = (bf16[2,64,896]{2,1,0:T(8,128)(2,1)S(1)}, bf16[2,64,896]{2,1,0:T(8,128)(2,1)S(1)}, u32[]{:S(2)}, u32[]{:S(2)}) collective-permute-start(bf16[2,64,896]{2,1,0:T(8,128)(2,1)S(1)} %get-tuple-element.38), channel_id=1, source_target_pairs={{0,2},{2,0},{4,6},{6,4},{1,3},{3,1},{5,7},{7,5},{8,10},{10,8},{12,... | collective-permute-start | bytes 688136 | tf_op jit(solution)/shard_map/ppermute | solution.py:17
  22.8 1.5 %collective-permute-start.13 = (bf16[2,64,896]{2,1,0:T(8,128)(2,1)S(1)}, bf16[2,64,896]{2,1,0:T(8,128)(2,1)S(1)}, u32[]{:S(2)}, u32[]{:S(2)}) collective-permute-start(bf16[2,64,896]{2,1,0:T(8,128)(2,1)S(1)} %get-tuple-element.39), channel_id=1, source_target_pairs={{0,4},{2,6},{4,0},{6,2},{1,5},{3,7},{5,1},{7,3},{8,12},{10,14},{12... | collective-permute-start | bytes 688136 | tf_op jit(solution)/shard_map/ppermute | solution.py:17
  25.3 1.6 %collective-permute-start.2 = (bf16[2,64,896]{2,1,0:T(8,128)(2,1)S(1)}, bf16[2,64,896]{2,1,0:T(8,128)(2,1)S(1)}, u32[]{:S(2)}, u32[]{:S(2)}) collective-permute-start(bf16[2,64,896]{2,1,0:T(8,128)(2,1)S(1)} %get-tuple-element.30), channel_id=1, source_target_pairs={{0,2},{2,0},{4,6},{6,4},{1,3},{3,1},{5,7},{7,5},{8,10},{10,8},{12,... | collective-permute-start | bytes 688136 | tf_op jit(solution)/shard_map/ppermute | solution.py:17
  26.9 2.9 %collective-permute-done.12.refs_1_ = bf16[2,64,896]{2,1,0:T(8,128)(2,1)S(1)} collective-permute-done((bf16[2,64,896]{2,1,0:T(8,128)(2,1)S(1)}, bf16[2,64,896]{2,1,0:T(8,128)(2,1)S(1)}, u32[]{:S(2)}, u32[]{:S(2)}) %collective-permute-start.12) | collective-permute-done | bytes 229408 | tf_op jit(solution)/shard_map/ppermute | solution.py:17
  29.8 1.5 %collective-permute-start.3 = (bf16[2,64,896]{2,1,0:T(8,128)(2,1)S(1)}, bf16[2,64,896]{2,1,0:T(8,128)(2,1)S(1)}, u32[]{:S(2)}, u32[]{:S(2)}) collective-permute-start(bf16[2,64,896]{2,1,0:T(8,128)(2,1)S(1)} %get-tuple-element.31), channel_id=1, source_target_pairs={{0,4},{2,6},{4,0},{6,2},{1,5},{3,7},{5,1},{7,3},{8,12},{10,14},{12... | collective-permute-start | bytes 688136 | tf_op jit(solution)/shard_map/ppermute | solution.py:17
  31.3 3.6 %collective-permute-done.13.refs_2_ = bf16[2,64,896]{2,1,0:T(8,128)(2,1)S(1)} collective-permute-done((bf16[2,64,896]{2,1,0:T(8,128)(2,1)S(1)}, bf16[2,64,896]{2,1,0:T(8,128)(2,1)S(1)}, u32[]{:S(2)}, u32[]{:S(2)}) %collective-permute-start.13) | collective-permute-done | bytes 229408 | tf_op jit(solution)/shard_map/ppermute | solution.py:17
  35.9 2.0 %collective-permute-start.18 = (bf16[2,64,896]{2,1,0:T(8,128)(2,1)S(1)}, bf16[2,64,896]{2,1,0:T(8,128)(2,1)S(1)}, u32[]{:S(2)}, u32[]{:S(2)}) collective-permute-start(bf16[2,64,896]{2,1,0:T(8,128)(2,1)S(1)} %share.6.refs_6_), channel_id=1, source_target_pairs={{0,24},{8,16},{16,8},{24,0},{1,25},{9,17},{17,9},{25,1},{2,26},{10... | collective-permute-start | bytes 688136 | tf_op jit(solution)/shard_map/ppermute | solution.py:22
  38.5 1.2 %collective-permute-done.2.refs_1_ = bf16[2,64,896]{2,1,0:T(8,128)(2,1)S(1)} collective-permute-done((bf16[2,64,896]{2,1,0:T(8,128)(2,1)S(1)}, bf16[2,64,896]{2,1,0:T(8,128)(2,1)S(1)}, u32[]{:S(2)}, u32[]{:S(2)}) %collective-permute-start.2) | collective-permute-done | bytes 229408 | tf_op jit(solution)/shard_map/ppermute | solution.py:17
  39.7 1.7 %collective-permute-start.15 = (bf16[2,64,896]{2,1,0:T(8,128)(2,1)S(1)}, bf16[2,64,896]{2,1,0:T(8,128)(2,1)S(1)}, u32[]{:S(2)}, u32[]{:S(2)}) collective-permute-start(bf16[2,64,896]{2,1,0:T(8,128)(2,1)S(1)} %get-tuple-element.42), channel_id=1, source_target_pairs={{0,2},{2,0},{4,6},{6,4},{1,3},{3,1},{5,7},{7,5},{8,10},{10,8},{12,... | collective-permute-start | bytes 688136 | tf_op jit(solution)/shard_map/ppermute | solution.py:17
  41.4 2.3 %collective-permute-done.3.refs_2_ = bf16[2,64,896]{2,1,0:T(8,128)(2,1)S(1)} collective-permute-done((bf16[2,64,896]{2,1,0:T(8,128)(2,1)S(1)}, bf16[2,64,896]{2,1,0:T(8,128)(2,1)S(1)}, u32[]{:S(2)}, u32[]{:S(2)}) %collective-permute-start.3) | collective-permute-done | bytes 229408 | tf_op jit(solution)/shard_map/ppermute | solution.py:17
  43.7 1.7 %collective-permute-start.16 = (bf16[2,64,896]{2,1,0:T(8,128)(2,1)S(1)}, bf16[2,64,896]{2,1,0:T(8,128)(2,1)S(1)}, u32[]{:S(2)}, u32[]{:S(2)}) collective-permute-start(bf16[2,64,896]{2,1,0:T(8,128)(2,1)S(1)} %get-tuple-element.43), channel_id=1, source_target_pairs={{0,4},{2,6},{4,0},{6,2},{1,5},{3,7},{5,1},{7,3},{8,12},{10,14},{12... | collective-permute-start | bytes 688136 | tf_op jit(solution)/shard_map/ppermute | solution.py:17
  45.6 1.4 %collective-permute-start.17 = (bf16[2,64,896]{2,1,0:T(8,128)(2,1)S(1)}, bf16[2,64,896]{2,1,0:T(8,128)(2,1)S(1)}, u32[]{:S(2)}, u32[]{:S(2)}) collective-permute-start(bf16[2,64,896]{2,1,0:T(8,128)(2,1)S(1)} %get-tuple-element.44), channel_id=1, source_target_pairs={{0,6},{2,4},{4,2},{6,0},{1,7},{3,5},{5,3},{7,1},{8,14},{10,12},{12... | collective-permute-start | bytes 688136 | tf_op jit(solution)/shard_map/ppermute | solution.py:17
  47.7 1.4 %collective-permute-start.6 = (bf16[2,64,896]{2,1,0:T(8,128)(2,1)S(1)}, bf16[2,64,896]{2,1,0:T(8,128)(2,1)S(1)}, u32[]{:S(2)}, u32[]{:S(2)}) collective-permute-start(bf16[2,64,896]{2,1,0:T(8,128)(2,1)S(1)} %get-tuple-element.34), channel_id=1, source_target_pairs={{0,2},{2,0},{4,6},{6,4},{1,3},{3,1},{5,7},{7,5},{8,10},{10,8},{12,... | collective-permute-start | bytes 688136 | tf_op jit(solution)/shard_map/ppermute | solution.py:17
  50.4 1.6 %collective-permute-start.8 = (bf16[2,64,896]{2,1,0:T(8,128)(2,1)S(1)}, bf16[2,64,896]{2,1,0:T(8,128)(2,1)S(1)}, u32[]{:S(2)}, u32[]{:S(2)}) collective-permute-start(bf16[2,64,896]{2,1,0:T(8,128)(2,1)S(1)} %get-tuple-element.36), channel_id=1, source_target_pairs={{0,6},{2,4},{4,2},{6,0},{1,7},{3,5},{5,3},{7,1},{8,14},{10,12},{12... | collective-permute-start | bytes 688136 | tf_op jit(solution)/shard_map/ppermute | solution.py:17
  51.9 4.5 %collective-permute-done.16.refs_2_ = bf16[2,64,896]{2,1,0:T(8,128)(2,1)S(1)} collective-permute-done((bf16[2,64,896]{2,1,0:T(8,128)(2,1)S(1)}, bf16[2,64,896]{2,1,0:T(8,128)(2,1)S(1)}, u32[]{:S(2)}, u32[]{:S(2)}) %collective-permute-start.16) | collective-permute-done | bytes 229408 | tf_op jit(solution)/shard_map/ppermute | solution.py:17
  56.5 2.6 %collective-permute-start.9 = (bf16[2,64,896]{2,1,0:T(8,128)(2,1)S(1)}, bf16[2,64,896]{2,1,0:T(8,128)(2,1)S(1)}, u32[]{:S(2)}, u32[]{:S(2)}) collective-permute-start(bf16[2,64,896]{2,1,0:T(8,128)(2,1)S(1)} %share.4.refs_6_), channel_id=1, source_target_pairs={{0,24},{8,16},{16,8},{24,0},{1,25},{9,17},{17,9},{25,1},{2,26},{10... | collective-permute-start | bytes 688136 | tf_op jit(solution)/shard_map/ppermute | solution.py:22
  59.1 1.3 %collective-permute-start.19 = (bf16[2,64,896]{2,1,0:T(8,128)(2,1)S(1)}, bf16[2,64,896]{2,1,0:T(8,128)(2,1)S(1)}, u32[]{:S(2)}, u32[]{:S(2)}) collective-permute-start(bf16[2,64,896]{2,1,0:T(8,128)(2,1)S(1)} %share.7), channel_id=1, source_target_pairs={{0,24},{8,16},{16,8},{24,0},{1,25},{9,17},{17,9},{25,1},{2,26},{10... | collective-permute-start | bytes 688136 | tf_op jit(solution)/shard_map/ppermute | solution.py:22
  60.5 4.1 %collective-permute-done.7.refs_2_ = bf16[2,64,896]{2,1,0:T(8,128)(2,1)S(1)} collective-permute-done((bf16[2,64,896]{2,1,0:T(8,128)(2,1)S(1)}, bf16[2,64,896]{2,1,0:T(8,128)(2,1)S(1)}, u32[]{:S(2)}, u32[]{:S(2)}) %collective-permute-start.7) | collective-permute-done | bytes 229408 | tf_op jit(solution)/shard_map/ppermute | solution.py:17
  64.5 1.9 %collective-permute-done.9.refs_4_.share_ref = bf16[2,64,896]{2,1,0:T(8,128)(2,1)S(1)} collective-permute-done((bf16[2,64,896]{2,1,0:T(8,128)(2,1)S(1)}, bf16[2,64,896]{2,1,0:T(8,128)(2,1)S(1)}, u32[]{:S(2)}, u32[]{:S(2)}) %collective-permute-start.9) | collective-permute-done | bytes 229408 | tf_op jit(solution)/shard_map/ppermute | solution.py:22
  66.6 2.6 %collective-permute-start.11 = (bf16[2,64,896]{2,1,0:T(8,128)(2,1)S(1)}, bf16[2,64,896]{2,1,0:T(8,128)(2,1)S(1)}, u32[]{:S(2)}, u32[]{:S(2)}) collective-permute-start(bf16[2,64,896]{2,1,0:T(8,128)(2,1)S(1)} %share.5.rest_0_), channel_id=1, source_target_pairs={{0,24},{8,16},{16,8},{24,0},{1,25},{9,17},{17,9},{25,1},{2,26},{10... | collective-permute-start | bytes 688136 | tf_op jit(solution)/shard_map/ppermute | solution.py:22
  70.3 13.9 %collective-permute-start.10 = (bf16[32,3584]{1,0:T(8,128)(2,1)S(1)}, bf16[32,3584]{1,0:T(8,128)(2,1)S(1)}, u32[]{:S(2)}, u32[]{:S(2)}) collective-permute-start(bf16[32,3584]{1,0:T(8,128)(2,1)S(1)} %leaving.3), channel_id=1, source_target_pairs={{0,8},{8,16},{16,24},{1,9},{9,17},{17,25},{2,10},{10,18},{18,26},{... | collective-permute-start | bytes 688136 | tf_op jit(solution)/shard_map/ppermute | solution.py:27
  87.5 1.3 %collective-permute-start.22 = (f32[4,2,7,128]{3,2,1,0:T(8,128)S(1)}, f32[4,2,7,128]{3,2,1,0:T(8,128)S(1)}, u32[]{:S(2)}, u32[]{:S(2)}) collective-permute-start(f32[4,2,7,128]{3,2,1,0:T(8,128)S(1)} %get-tuple-element.52.refs_1_), channel_id=1, source_target_pairs={{0,6},{2,4},{4,2},{6,0},{1,7},{3,5},{5,3},{7,1},{8,14},{10,12},{12... | collective-permute-start | bytes 86024 | tf_op jit(solution)/shard_map/ppermute | solution.py:17
  88.8 2.2 %collective-permute-start.20 = (f32[4,2,7,128]{3,2,1,0:T(8,128)S(1)}, f32[4,2,7,128]{3,2,1,0:T(8,128)S(1)}, u32[]{:S(2)}, u32[]{:S(2)}) collective-permute-start(f32[4,2,7,128]{3,2,1,0:T(8,128)S(1)} %get-tuple-element.52.refs_1_), channel_id=1, source_target_pairs={{0,2},{2,0},{4,6},{6,4},{1,3},{3,1},{5,7},{7,5},{8,10},{10,8},{12,... | collective-permute-start | bytes 86024 | tf_op jit(solution)/shard_map/ppermute | solution.py:17
  91.0 1.4 %place.2.rest_0_ = bf16[1,128,3584]{2,1,0:T(8,128)(2,1)} custom-call(bf16[96,3584]{1,0:T(8,128)(2,1)S(1)} %collective-permute-done.5.refs_4_.in_ref), custom_call_target="tpu_custom_call" | custom-call | bytes 1376256 | tf_op jit(solution)/shard_map/place/pallas_call | solution.py:336
  (56 shorter events, 14.9 us)
Async XLA Ops:
  1.4 2.0 %copy-start.5 = (bf16[2,1,256,3584]{3,2,1,0:T(8,128)(2,1)S(1)}, bf16[2,1,256,3584]{3,2,1,0:T(8,128)(2,1)}, u32[]{:S(2)}) copy-start(bf16[2,1,256,3584]{3,2,1,0:T(8,128)(2,1)} %a_ref.3) | copy-start | bytes 11010052
  4.6 2.0 %copy-start = (bf16[2,1,256,3584]{3,2,1,0:T(8,128)(2,1)S(1)}, bf16[2,1,256,3584]{3,2,1,0:T(8,128)(2,1)}, u32[]{:S(2)}) copy-start(bf16[2,1,256,3584]{3,2,1,0:T(8,128)(2,1)} %b_ref.5) | copy-start | bytes 11010052
  4.6 2.3 %copy-start.2 = (bf16[1,128,3584]{2,1,0:T(8,128)(2,1)S(1)}, bf16[1,128,3584]{2,1,0:T(8,128)(2,1)}, u32[]{:S(2)}) copy-start(bf16[1,128,3584]{2,1,0:T(8,128)(2,1)} %refs_2_.7) | copy-start | bytes 2752516
  8.1 2.0 %copy-start.6 = (bf16[2,1,256,3584]{3,2,1,0:T(8,128)(2,1)S(1)}, bf16[2,1,256,3584]{3,2,1,0:T(8,128)(2,1)}, u32[]{:S(2)}) copy-start(bf16[2,1,256,3584]{3,2,1,0:T(8,128)(2,1)} %a_ref.3) | copy-start | bytes 11010052
  10.1 4.3 %copy-start.10 = (bf16[1,128,3584]{2,1,0:T(8,128)(2,1)S(1)}, bf16[1,128,3584]{2,1,0:T(8,128)(2,1)}, u32[]{:S(2)}) copy-start(bf16[1,128,3584]{2,1,0:T(8,128)(2,1)} %x_ref.7) | copy-start | bytes 2752516
  12.4 8.3 %copy-start.4 = (bf16[1,128,3584]{2,1,0:T(8,128)(2,1)S(1)}, bf16[1,128,3584]{2,1,0:T(8,128)(2,1)}, u32[]{:S(2)}) copy-start(bf16[1,128,3584]{2,1,0:T(8,128)(2,1)} %refs_4_.7) | copy-start | bytes 2752516
  12.4 8.3 %collective-permute-start.1 = (f32[640,128]{1,0:T(8,128)S(1)}, f32[640,128]{1,0:T(8,128)S(1)}, u32[]{:S(2)}, u32[]{:S(2)}) collective-permute-start(f32[640,128]{1,0:T(8,128)S(1)} %back_latent.1.refs_0_), channel_id=1, source_target_pairs={{0,1},{1,0},{2,3},{3,2},{4,5},{5,4},{6,7},{7,6},{8,9},{9,8},{10,11... | collective-permute-start | bytes 983048 | tf_op jit(solution)/shard_map/ppermute | solution.py:17
  12.9 1.5 %collective-permute-start = (f32[128,384]{1,0:T(8,128)S(1)}, f32[128,384]{1,0:T(8,128)S(1)}, u32[]{:S(2)}, u32[]{:S(2)}) collective-permute-start(f32[128,384]{1,0:T(8,128)S(1)} %fwd_latent.1.rest_0_.own_ref), channel_id=1, source_target_pairs={{0,1},{1,0},{2,3},{3,2},{4,5},{5,4},{6,7},{7,6},{8,9},{9,8},{10,11... | collective-permute-start | bytes 589832 | tf_op jit(solution)/shard_map/ppermute | solution.py:17
  15.8 31.2 %collective-permute-start.5 = (bf16[96,3584]{1,0:T(8,128)(2,1)S(1)}, bf16[96,3584]{1,0:T(8,128)(2,1)S(1)}, u32[]{:S(2)}, u32[]{:S(2)}) collective-permute-start(bf16[96,3584]{1,0:T(8,128)(2,1)S(1)} %leaving.2.refs_5_), channel_id=1, source_target_pairs={{0,8},{8,16},{16,24},{1,9},{9,17},{17,25},{2,10},{10,18},{18,26},{... | collective-permute-start | bytes 2064392 | tf_op jit(solution)/shard_map/ppermute | solution.py:27
  21.2 8.6 %collective-permute-start.12 = (bf16[2,64,896]{2,1,0:T(8,128)(2,1)S(1)}, bf16[2,64,896]{2,1,0:T(8,128)(2,1)S(1)}, u32[]{:S(2)}, u32[]{:S(2)}) collective-permute-start(bf16[2,64,896]{2,1,0:T(8,128)(2,1)S(1)} %get-tuple-element.38), channel_id=1, source_target_pairs={{0,2},{2,0},{4,6},{6,4},{1,3},{3,1},{5,7},{7,5},{8,10},{10,8},{12,... | collective-permute-start | bytes 688136 | tf_op jit(solution)/shard_map/ppermute | solution.py:17
  22.8 12.1 %collective-permute-start.13 = (bf16[2,64,896]{2,1,0:T(8,128)(2,1)S(1)}, bf16[2,64,896]{2,1,0:T(8,128)(2,1)S(1)}, u32[]{:S(2)}, u32[]{:S(2)}) collective-permute-start(bf16[2,64,896]{2,1,0:T(8,128)(2,1)S(1)} %get-tuple-element.39), channel_id=1, source_target_pairs={{0,4},{2,6},{4,0},{6,2},{1,5},{3,7},{5,1},{7,3},{8,12},{10,14},{12... | collective-permute-start | bytes 688136 | tf_op jit(solution)/shard_map/ppermute | solution.py:17
  24.3 11.4 %collective-permute-start.14 = (bf16[2,64,896]{2,1,0:T(8,128)(2,1)S(1)}, bf16[2,64,896]{2,1,0:T(8,128)(2,1)S(1)}, u32[]{:S(2)}, u32[]{:S(2)}) collective-permute-start(bf16[2,64,896]{2,1,0:T(8,128)(2,1)S(1)} %get-tuple-element.40), channel_id=1, source_target_pairs={{0,6},{2,4},{4,2},{6,0},{1,7},{3,5},{5,3},{7,1},{8,14},{10,12},{12... | collective-permute-start | bytes 688136 | tf_op jit(solution)/shard_map/ppermute | solution.py:17
  25.3 14.3 %collective-permute-start.2 = (bf16[2,64,896]{2,1,0:T(8,128)(2,1)S(1)}, bf16[2,64,896]{2,1,0:T(8,128)(2,1)S(1)}, u32[]{:S(2)}, u32[]{:S(2)}) collective-permute-start(bf16[2,64,896]{2,1,0:T(8,128)(2,1)S(1)} %get-tuple-element.30), channel_id=1, source_target_pairs={{0,2},{2,0},{4,6},{6,4},{1,3},{3,1},{5,7},{7,5},{8,10},{10,8},{12,... | collective-permute-start | bytes 688136 | tf_op jit(solution)/shard_map/ppermute | solution.py:17
  29.8 13.9 %collective-permute-start.3 = (bf16[2,64,896]{2,1,0:T(8,128)(2,1)S(1)}, bf16[2,64,896]{2,1,0:T(8,128)(2,1)S(1)}, u32[]{:S(2)}, u32[]{:S(2)}) collective-permute-start(bf16[2,64,896]{2,1,0:T(8,128)(2,1)S(1)} %get-tuple-element.31), channel_id=1, source_target_pairs={{0,4},{2,6},{4,0},{6,2},{1,5},{3,7},{5,1},{7,3},{8,12},{10,14},{12... | collective-permute-start | bytes 688136 | tf_op jit(solution)/shard_map/ppermute | solution.py:17
  34.9 10.6 %collective-permute-start.4 = (bf16[2,64,896]{2,1,0:T(8,128)(2,1)S(1)}, bf16[2,64,896]{2,1,0:T(8,128)(2,1)S(1)}, u32[]{:S(2)}, u32[]{:S(2)}) collective-permute-start(bf16[2,64,896]{2,1,0:T(8,128)(2,1)S(1)} %get-tuple-element.32), channel_id=1, source_target_pairs={{0,6},{2,4},{4,2},{6,0},{1,7},{3,5},{5,3},{7,1},{8,14},{10,12},{12... | collective-permute-start | bytes 688136 | tf_op jit(solution)/shard_map/ppermute | solution.py:17
  35.9 13.3 %collective-permute-start.18 = (bf16[2,64,896]{2,1,0:T(8,128)(2,1)S(1)}, bf16[2,64,896]{2,1,0:T(8,128)(2,1)S(1)}, u32[]{:S(2)}, u32[]{:S(2)}) collective-permute-start(bf16[2,64,896]{2,1,0:T(8,128)(2,1)S(1)} %share.6.refs_6_), channel_id=1, source_target_pairs={{0,24},{8,16},{16,8},{24,0},{1,25},{9,17},{17,9},{25,1},{2,26},{10... | collective-permute-start | bytes 688136 | tf_op jit(solution)/shard_map/ppermute | solution.py:22
  39.7 10.7 %collective-permute-start.15 = (bf16[2,64,896]{2,1,0:T(8,128)(2,1)S(1)}, bf16[2,64,896]{2,1,0:T(8,128)(2,1)S(1)}, u32[]{:S(2)}, u32[]{:S(2)}) collective-permute-start(bf16[2,64,896]{2,1,0:T(8,128)(2,1)S(1)} %get-tuple-element.42), channel_id=1, source_target_pairs={{0,2},{2,0},{4,6},{6,4},{1,3},{3,1},{5,7},{7,5},{8,10},{10,8},{12,... | collective-permute-start | bytes 688136 | tf_op jit(solution)/shard_map/ppermute | solution.py:17
  43.7 12.8 %collective-permute-start.16 = (bf16[2,64,896]{2,1,0:T(8,128)(2,1)S(1)}, bf16[2,64,896]{2,1,0:T(8,128)(2,1)S(1)}, u32[]{:S(2)}, u32[]{:S(2)}) collective-permute-start(bf16[2,64,896]{2,1,0:T(8,128)(2,1)S(1)} %get-tuple-element.43), channel_id=1, source_target_pairs={{0,4},{2,6},{4,0},{6,2},{1,5},{3,7},{5,1},{7,3},{8,12},{10,14},{12... | collective-permute-start | bytes 688136 | tf_op jit(solution)/shard_map/ppermute | solution.py:17
  45.6 13.4 %collective-permute-start.17 = (bf16[2,64,896]{2,1,0:T(8,128)(2,1)S(1)}, bf16[2,64,896]{2,1,0:T(8,128)(2,1)S(1)}, u32[]{:S(2)}, u32[]{:S(2)}) collective-permute-start(bf16[2,64,896]{2,1,0:T(8,128)(2,1)S(1)} %get-tuple-element.44), channel_id=1, source_target_pairs={{0,6},{2,4},{4,2},{6,0},{1,7},{3,5},{5,3},{7,1},{8,14},{10,12},{12... | collective-permute-start | bytes 688136 | tf_op jit(solution)/shard_map/ppermute | solution.py:17
  47.7 12.8 %collective-permute-start.6 = (bf16[2,64,896]{2,1,0:T(8,128)(2,1)S(1)}, bf16[2,64,896]{2,1,0:T(8,128)(2,1)S(1)}, u32[]{:S(2)}, u32[]{:S(2)}) collective-permute-start(bf16[2,64,896]{2,1,0:T(8,128)(2,1)S(1)} %get-tuple-element.34), channel_id=1, source_target_pairs={{0,2},{2,0},{4,6},{6,4},{1,3},{3,1},{5,7},{7,5},{8,10},{10,8},{12,... | collective-permute-start | bytes 688136 | tf_op jit(solution)/shard_map/ppermute | solution.py:17
  49.1 15.4 %collective-permute-start.7 = (bf16[2,64,896]{2,1,0:T(8,128)(2,1)S(1)}, bf16[2,64,896]{2,1,0:T(8,128)(2,1)S(1)}, u32[]{:S(2)}, u32[]{:S(2)}) collective-permute-start(bf16[2,64,896]{2,1,0:T(8,128)(2,1)S(1)} %get-tuple-element.35), channel_id=1, source_target_pairs={{0,4},{2,6},{4,0},{6,2},{1,5},{3,7},{5,1},{7,3},{8,12},{10,14},{12... | collective-permute-start | bytes 688136 | tf_op jit(solution)/shard_map/ppermute | solution.py:17
  50.4 14.2 %collective-permute-start.8 = (bf16[2,64,896]{2,1,0:T(8,128)(2,1)S(1)}, bf16[2,64,896]{2,1,0:T(8,128)(2,1)S(1)}, u32[]{:S(2)}, u32[]{:S(2)}) collective-permute-start(bf16[2,64,896]{2,1,0:T(8,128)(2,1)S(1)} %get-tuple-element.36), channel_id=1, source_target_pairs={{0,6},{2,4},{4,2},{6,0},{1,7},{3,5},{5,3},{7,1},{8,14},{10,12},{12... | collective-permute-start | bytes 688136 | tf_op jit(solution)/shard_map/ppermute | solution.py:17
  56.5 9.9 %collective-permute-start.9 = (bf16[2,64,896]{2,1,0:T(8,128)(2,1)S(1)}, bf16[2,64,896]{2,1,0:T(8,128)(2,1)S(1)}, u32[]{:S(2)}, u32[]{:S(2)}) collective-permute-start(bf16[2,64,896]{2,1,0:T(8,128)(2,1)S(1)} %share.4.refs_6_), channel_id=1, source_target_pairs={{0,24},{8,16},{16,8},{24,0},{1,25},{9,17},{17,9},{25,1},{2,26},{10... | collective-permute-start | bytes 688136 | tf_op jit(solution)/shard_map/ppermute | solution.py:22
  59.1 26.7 %collective-permute-start.19 = (bf16[2,64,896]{2,1,0:T(8,128)(2,1)S(1)}, bf16[2,64,896]{2,1,0:T(8,128)(2,1)S(1)}, u32[]{:S(2)}, u32[]{:S(2)}) collective-permute-start(bf16[2,64,896]{2,1,0:T(8,128)(2,1)S(1)} %share.7), channel_id=1, source_target_pairs={{0,24},{8,16},{16,8},{24,0},{1,25},{9,17},{17,9},{25,1},{2,26},{10... | collective-permute-start | bytes 688136 | tf_op jit(solution)/shard_map/ppermute | solution.py:22
  66.5 17.8 %copy-start.1 = (f32[2,1,64,3584]{3,2,1,0:T(8,128)S(1)}, f32[2,1,64,3584]{3,2,1,0:T(8,128)}, u32[]{:S(2)}) copy-start(f32[2,1,64,3584]{3,2,1,0:T(8,128)} %master_ref.7) | copy-start | bytes 5505028
  66.5 17.8 %copy-start.7 = (bf16[2,1,64,3584]{3,2,1,0:T(8,128)(2,1)S(1)}, bf16[2,1,64,3584]{3,2,1,0:T(8,128)(2,1)}, u32[]{:S(2)}) copy-start(bf16[2,1,64,3584]{3,2,1,0:T(8,128)(2,1)} %moment_ref.7) | copy-start | bytes 2752516
  66.5 17.8 %copy-start.8 = (bf16[2,1,64,3584]{3,2,1,0:T(8,128)(2,1)S(1)}, bf16[2,1,64,3584]{3,2,1,0:T(8,128)(2,1)}, u32[]{:S(2)}) copy-start(bf16[2,1,64,3584]{3,2,1,0:T(8,128)(2,1)} %second_ref.7) | copy-start | bytes 2752516
  66.6 20.1 %collective-permute-start.11 = (bf16[2,64,896]{2,1,0:T(8,128)(2,1)S(1)}, bf16[2,64,896]{2,1,0:T(8,128)(2,1)S(1)}, u32[]{:S(2)}, u32[]{:S(2)}) collective-permute-start(bf16[2,64,896]{2,1,0:T(8,128)(2,1)S(1)} %share.5.rest_0_), channel_id=1, source_target_pairs={{0,24},{8,16},{16,8},{24,0},{1,25},{9,17},{17,9},{25,1},{2,26},{10... | collective-permute-start | bytes 688136 | tf_op jit(solution)/shard_map/ppermute | solution.py:22
  70.3 22.1 %collective-permute-start.10 = (bf16[32,3584]{1,0:T(8,128)(2,1)S(1)}, bf16[32,3584]{1,0:T(8,128)(2,1)S(1)}, u32[]{:S(2)}, u32[]{:S(2)}) collective-permute-start(bf16[32,3584]{1,0:T(8,128)(2,1)S(1)} %leaving.3), channel_id=1, source_target_pairs={{0,8},{8,16},{16,24},{1,9},{9,17},{17,25},{2,10},{10,18},{18,26},{... | collective-permute-start | bytes 688136 | tf_op jit(solution)/shard_map/ppermute | solution.py:27
  87.5 5.7 %collective-permute-start.22 = (f32[4,2,7,128]{3,2,1,0:T(8,128)S(1)}, f32[4,2,7,128]{3,2,1,0:T(8,128)S(1)}, u32[]{:S(2)}, u32[]{:S(2)}) collective-permute-start(f32[4,2,7,128]{3,2,1,0:T(8,128)S(1)} %get-tuple-element.52.refs_1_), channel_id=1, source_target_pairs={{0,6},{2,4},{4,2},{6,0},{1,7},{3,5},{5,3},{7,1},{8,14},{10,12},{12... | collective-permute-start | bytes 86024 | tf_op jit(solution)/shard_map/ppermute | solution.py:17
  88.8 4.4 %collective-permute-start.21 = (f32[4,2,7,128]{3,2,1,0:T(8,128)S(1)}, f32[4,2,7,128]{3,2,1,0:T(8,128)S(1)}, u32[]{:S(2)}, u32[]{:S(2)}) collective-permute-start(f32[4,2,7,128]{3,2,1,0:T(8,128)S(1)} %get-tuple-element.52.refs_1_), channel_id=1, source_target_pairs={{0,4},{2,6},{4,0},{6,2},{1,5},{3,7},{5,1},{7,3},{8,12},{10,14},{12... | collective-permute-start | bytes 86024 | tf_op jit(solution)/shard_map/ppermute | solution.py:17
  88.8 4.4 %collective-permute-start.20 = (f32[4,2,7,128]{3,2,1,0:T(8,128)S(1)}, f32[4,2,7,128]{3,2,1,0:T(8,128)S(1)}, u32[]{:S(2)}, u32[]{:S(2)}) collective-permute-start(f32[4,2,7,128]{3,2,1,0:T(8,128)S(1)} %get-tuple-element.52.refs_1_), channel_id=1, source_target_pairs={{0,2},{2,0},{4,6},{6,4},{1,3},{3,1},{5,7},{7,5},{8,10},{10,8},{12,... | collective-permute-start | bytes 86024 | tf_op jit(solution)/shard_map/ppermute | solution.py:17
  (2 other events, 2.4 us)

commit v3 on v1

v3 whole, which is shorter than its diff:
```python
import jax
import jax.numpy as jnp
from jax import lax
from jax.experimental import pallas as pl
from jax.experimental.pallas import tpu as pltpu
from jax.sharding import PartitionSpec as P

D = 7168
LANES = 128
F32 = jnp.float32
BF16 = jnp.bfloat16
BOTH_LAST = (((1,), (1,)), ((), ()))


def exchange(block, axis, offset):
    count = lax.axis_size(axis)
    return lax.ppermute(block, axis, [(i, i ^ offset) for i in range(count)])


def mirrored(block, axis):
    count = lax.axis_size(axis)
    return lax.ppermute(block, axis, [(i, count - 1 - i) for i in range(count)])


def shifted(block, axis):
    count = lax.axis_size(axis)
    return lax.ppermute(block, axis, [(i, i + 1) for i in range(count - 1)])


def halves_of_sum(block, axis):
    count = lax.axis_size(axis)
    offset = 1
    while True:
        other = exchange(block, axis, offset)
        offset *= 2
        if offset >= count:
            return block, other
        block = block + other


ROOM = pltpu.CompilerParams(vmem_limit_bytes=16 << 20)


def cost(flops, nbytes):
    return pl.CostEstimate(flops=flops, bytes_accessed=nbytes, transcendentals=0)


def folded_squares(rows):
    tokens, width = rows.shape
    total = jnp.zeros((tokens, LANES), F32)
    for at in range(0, width, LANES):
        part = rows[:, at : at + LANES]
        total = total + part * part
    return total


def latent_kernel(tiles, x1, a1, x2, c2, a2, b2, gain_ref, out_ref, vx1, va1, vx2, vc2, va2, vb2, sems):
    tokens, width = vx1.shape
    latent = va1.shape[0]
    tile = width // tiles
    jobs = []
    for names in (((x1, vx1), (a1, va1)), ((x2, vx2), (a2, va2)), ((c2, vc2), (b2, vb2))):
        for at in range(tiles):
            cols = pl.ds(at * tile, tile)
            jobs.append([])
            for src, dst in names:
                copy = pltpu.make_async_copy(
                    src.at[:, cols], dst.at[:, cols], sems.at[2 * len(jobs) - 2 + len(jobs[-1])]
                )
                copy.start()
                jobs[-1].append(copy)
    gains = gain_ref[...].astype(F32)

    def product(job, left, right):
        total = None
        squares = jnp.zeros((tokens, LANES), F32)
        for at in range(tiles):
            for copy in jobs[job * tiles + at]:
                copy.wait()
            cols = slice(at * tile, (at + 1) * tile)
            one, two, folded = left(cols), right(cols), None
            if job < 2:
                rows = (vx1, vx2)[job][:, cols].astype(F32)
                squares += folded_squares(rows)
                scaled = (rows * gains[job : job + 1, cols]).astype(BF16)
                one = scaled if one is None else one
                two = scaled if two is None else two
            term = lax.dot_general(one, two, BOTH_LAST, preferred_element_type=F32)
            total = term if total is None else total + term
        return total, squares

    raw, squares = product(0, lambda c: None, lambda c: va1[:, c])
    base = 2 * latent + tokens
    for at in range(latent // LANES):
        out_ref[base + at * tokens : base + (at + 1) * tokens] = raw[:, at * LANES : (at + 1) * LANES]
    out_ref[base + (latent // LANES) * tokens :] = squares
    raw, squares = product(1, lambda c: va2[:, c], lambda c: None)
    out_ref[:latent] = raw
    out_ref[2 * latent : base] = squares
    out_ref[latent : 2 * latent], _ = product(2, lambda c: vb2[:, c], lambda c: vc2[:, c])


def leaving_kernel(own_ref, other_ref, x_ref, b_ref, out_ref, hidden):
    latent = b_ref.shape[0]
    tokens = x_ref.shape[0]

    @pl.when(pl.program_id(0) == 0)
    def _():
        base = own_ref.shape[0] - tokens
        squares = jnp.sum(own_ref[base:] + other_ref[base:], axis=1, keepdims=True)
        rscale = lax.rsqrt(squares / D + 1e-06)
        base -= (latent // LANES) * tokens
        for at in range(latent // LANES):
            rows = slice(base + at * tokens, base + (at + 1) * tokens)
            hidden[:, at * LANES : (at + 1) * LANES] = ((own_ref[rows] + other_ref[rows]) * rscale).astype(BF16)

    out_ref[...] = (
        x_ref[...].astype(F32) + jnp.dot(hidden[...], b_ref[...], preferred_element_type=F32)
    ).astype(BF16)


def grad_kernel(orders, own_ref, other_ref, x_ref, g_ref, c_ref, *rest):
    (down_keep, up_keep, down_send, up_send), rows_ref = rest[-5:-1], rest[-1]
    latent = rows_ref.shape[0]
    experts = len(orders[0])
    depth = latent // experts
    me = lax.axis_index("expert")
    squares = own_ref[2 * latent : 2 * latent + LANES] + other_ref[2 * latent : 2 * latent + LANES]
    rscale = lax.rsqrt(jnp.sum(squares.T, axis=0, keepdims=True) / D + 1e-06)
    scaled = (x_ref[...].astype(F32) * g_ref[1:2].astype(F32)).astype(BF16)
    for base, order, right, keep, send in (
        (latent, orders[0], scaled, down_keep, down_send),
        (0, orders[1], c_ref[...], up_keep, up_send),
    ):
        rows_ref[...] = (own_ref[base : base + latent] + other_ref[base : base + latent]) * rscale
        for half, out in enumerate((keep, send)):
            some = order[half * experts // 2 : (half + 1) * experts // 2]
            left = jnp.concatenate(
                [rows_ref[pl.ds(pl.multiple_of((me ^ offset) * depth, depth), depth), :] for offset in some]
            )
            out[...] = jnp.dot(left.astype(BF16), right, preferred_element_type=F32).astype(BF16)


def fold_kernel(down_keep, down_in, up_keep, up_in, *rest):
    outs = rest[-4:]
    for keep, more, kept, send in ((down_keep, down_in, outs[0], outs[2]), (up_keep, up_in, outs[1], outs[3])):
        total = keep[...].astype(F32) + more[...].astype(F32)
        half = total.shape[0] // 2
        kept[...] = total[:half]
        send[...] = total[half:].astype(BF16)


def share_kernel(down_keep, down_in, up_keep, up_in, *rest):
    out_ref = rest[-1]
    out_ref[0] = (down_keep[...].astype(F32) + down_in[...].astype(F32)).astype(BF16)
    out_ref[1] = (up_keep[...].astype(F32) + up_in[...].astype(F32)).astype(BF16)


def update_kernel(share_ref, master_ref, moment_ref, second_ref, *rest):
    fresh_ref, peak_ref = rest[-2:]
    grad = share_ref[...].astype(F32)
    first = 0.9 * moment_ref[...].astype(F32) + 0.1 * grad
    secnd = 0.95 * second_ref[...].astype(F32) + 0.05 * grad * grad
    update = first / (1.0 - 0.9**10) / (jnp.sqrt(secnd / (1.0 - 0.95**10)) + 1e-08)
    weights = master_ref[...]
    fresh = weights - 0.01 * (update + 0.1 * weights)
    fresh_ref[...] = fresh
    peak = jnp.max(jnp.abs(fresh), axis=1, keepdims=True)
    for block in range(peak.shape[-1] // LANES):
        peak_ref[:, block : block + 1] = peak[:, :, block * LANES : (block + 1) * LANES]


def code_kernel(group, fresh_ref, *rest):
    peak_refs, code_ref, scale_ref, wide = rest[:-3], rest[-3], rest[-2], rest[-1]
    chunks, _, per, _ = peak_refs[0].shape
    rows_of = len(peak_refs) // group
    mine = lax.axis_index("expert") // group
    wide[...] = jnp.zeros_like(wide)
    for far in range(rows_of):
        top = peak_refs[far * group][...]
        for ref in peak_refs[far * group + 1 : (far + 1) * group]:
            top = jnp.maximum(top, ref[...])
        for side in range(2):
            for chunk in range(chunks):
                wide[side, chunk * per : (chunk + 1) * per, :] = top[chunk, side]
        where = pl.ds(mine ^ far, 1)
        for side in range(2):
            scale_ref[side, where, :] = (
                jnp.max(wide[side].T, axis=0, keepdims=True)[:, : chunks * per] + 1e-06
            )
        if far == 0:
            for side in range(2):
                scale = jnp.broadcast_to(jnp.max(wide[side], axis=1, keepdims=True), wide.shape[1:]) + 1e-06
                inverse = 1.0 / scale
                for block in range(chunks * per):
                    at = slice(block * LANES, (block + 1) * LANES)
                    code_ref[side, :, at] = (fresh_ref[side, :, at] * inverse[block : block + 1]).astype(BF16)


ANY = pl.BlockSpec(memory_space=pl.ANY)


def whole(shape):
    return pl.BlockSpec(shape, lambda *_: (0,) * len(shape))


def shards(enter_fwd, enter_rev, cot_rev, gain, proj_down, proj_up, master, moment, second):
    tokens, width = enter_fwd.shape[1:]
    latent = proj_down.shape[2]
    experts = lax.axis_size("expert")
    depth = latent // experts
    blocks = width // LANES
    tiles = 4 if blocks % 4 == 0 else 2
    tile = width // tiles
    chunks = 2
    part = width // chunks
    gains = gain.reshape(2, width)

    def streamed(array):
        return pltpu.with_memory_space_constraint(array, pltpu.HBM)

    pack_rows = 2 * latent + tokens + (latent // LANES + 1) * tokens
    packed = pl.pallas_call(
        lambda x1, x2, c2, down, up, *refs: latent_kernel(
            tiles, x1.at[0], down.at[0, 0], x2.at[0], c2.at[0], down.at[1, 0], up.at[1, 0], *refs
        ),
        in_specs=[ANY] * 5 + [pl.BlockSpec(memory_space=pltpu.VMEM)],
        out_specs=pl.BlockSpec(memory_space=pltpu.VMEM),
        out_shape=jax.ShapeDtypeStruct((pack_rows, LANES), F32),
        scratch_shapes=[
            pltpu.VMEM((tokens, width), BF16),
            pltpu.VMEM((latent, width), BF16),
            pltpu.VMEM((tokens, width), BF16),
            pltpu.VMEM((tokens, width), BF16),
            pltpu.VMEM((latent, width), BF16),
            pltpu.VMEM((latent, width), BF16),
            pltpu.SemaphoreType.DMA((6 * tiles,)),
        ],
        compiler_params=ROOM,
        cost_estimate=cost(6 * tokens * latent * width, 6 * (tokens + latent) * width),
        name="latents",
    )(streamed(enter_fwd), streamed(enter_rev), streamed(cot_rev), streamed(proj_down), streamed(proj_up), gains)
    pair = halves_of_sum(packed, "dp")

    first_rows = pl.pallas_call(
        leaving_kernel,
        grid=(tiles,),
        in_specs=[
            whole((pack_rows, LANES)),
            whole((pack_rows, LANES)),
            pl.BlockSpec((None, tokens, tile), lambda i: (0, 0, i)),
            pl.BlockSpec((None, None, latent, tile), lambda i: (0, 0, 0, i)),
        ],
        out_specs=pl.BlockSpec((tokens, tile), lambda i: (0, i)),
        out_shape=jax.ShapeDtypeStruct((tokens, width), BF16),
        scratch_shapes=[pltpu.VMEM((tokens, latent), BF16)],
        compiler_params=ROOM,
        cost_estimate=cost(2 * tokens * latent * width, 2 * (2 * tokens + latent) * width),
        name="leaving",
    )(*pair, enter_fwd, proj_up)
    left = shifted(first_rows, "pipe")

    levels = experts.bit_length() - 1
    orders = [[sum((i >> k & 1) << (levels - 1 - k) for k in range(levels)) for i in range(experts)], list(range(experts))]

    def split(kernel, rows, keep_type, name, *operands, specs=None, scratch=(), flops=0):
        return pl.pallas_call(
            kernel,
            grid=(1,),
            in_specs=[whole(o.shape) for o in operands] if specs is None else specs,
            out_specs=[whole((rows, part))] * 4,
            out_shape=[jax.ShapeDtypeStruct((rows, part), t) for t in (keep_type, keep_type, BF16, BF16)],
            scratch_shapes=scratch,
            compiler_params=ROOM,
            cost_estimate=cost(flops, 12 * rows * part),
            name=name,
        )(*operands)

    def columns(rows, chunk):
        return pl.BlockSpec((None, rows, part), lambda i: (0, 0, chunk))

    arrived = []
    last = share = first_rows
    for chunk in range(chunks):
        down, up, down_out, up_out = split(
            lambda *refs: grad_kernel(orders, *refs),
            latent // 2,
            BF16,
            "grads",
            *pair,
            enter_rev,
            gains,
            cot_rev,
            last,
            share,
            specs=[
                whole((pack_rows, LANES)),
                whole((pack_rows, LANES)),
                columns(tokens, chunk),
                pl.BlockSpec((2, part), lambda i, c=chunk: (0, c)),
                columns(tokens, chunk),
                ANY,
                ANY,
            ],
            scratch=[pltpu.VMEM((latent, tokens), F32)],
            flops=4 * tokens * latent * part,
        )
        for level in range(levels):
            down_in = exchange(down_out, "expert", 1 << level)
            up_in = exchange(up_out, "expert", 1 << (levels - 1 - level))
            if level < levels - 1:
                down, up, down_out, up_out = split(
                    fold_kernel,
                    latent >> (level + 2),
                    F32,
                    "fold",
                    down,
                    down_in,
                    up,
                    up_in,


                )
        share = pl.pallas_call(
            share_kernel,
            grid=(1,),
            in_specs=[whole((depth, part))] * 4 + [ANY] * len(arrived),
            out_specs=whole((2, depth, part)),
            out_shape=jax.ShapeDtypeStruct((2, depth, part), BF16),
            compiler_params=ROOM,
            cost_estimate=cost(0, 16 * depth * part),
            name="share",
        )(down, down_in, up, up_in, *arrived)
        arrived = arrived + [mirrored(share, "pipe")]
        last = left if chunk == 0 else share

    fresh = peaks = None
    for chunk in range(chunks):
        state = pl.BlockSpec((2, None, depth, part), lambda i, c=chunk: (0, 0, 0, c))
        kept = () if fresh is None else (fresh, peaks)
        fresh, peaks = pl.pallas_call(
            update_kernel,
            grid=(1,),
            in_specs=[whole((2, depth, part)), state, state, state] + [ANY] * len(kept),
            out_specs=[
                pl.BlockSpec((2, depth, part), lambda i, c=chunk: (0, 0, c)),
                pl.BlockSpec((None, 2, part // LANES, LANES), lambda i, c=chunk: (c, 0, 0, 0)),
            ],
            out_shape=[
                jax.ShapeDtypeStruct((2, depth, width), F32),
                jax.ShapeDtypeStruct((chunks, 2, part // LANES, LANES), F32),
            ],
            input_output_aliases={4 + k: k for k in range(len(kept))},
            compiler_params=ROOM,
        cost_estimate=cost(20 * 2 * depth * part, 14 * 2 * depth * part),
            name="update",
        )(arrived[chunk], master, moment, second, *kept)

    peak_rows = [peaks] + [exchange(peaks, "expert", k) for k in range(1, experts)]
    group = LANES // depth
    coded, scales = pl.pallas_call(
        lambda *refs: code_kernel(group, *refs),
        grid=(1,),
        in_specs=[whole((2, depth, width))] + [whole(peaks.shape)] * experts,
        out_specs=[
            pl.BlockSpec((2, None, depth, width), lambda i: (0, 0, 0, 0)),
            pl.BlockSpec((2, None, experts // group, blocks), lambda i: (0, 0, 0, 0)),
        ],
        out_shape=[
            jax.ShapeDtypeStruct((2, 1, depth, width), BF16),
            jax.ShapeDtypeStruct((2, 1, experts // group, blocks), F32),
        ],
        scratch_shapes=[pltpu.VMEM((2, LANES, LANES), F32)],
        compiler_params=ROOM,
        cost_estimate=cost(2 * 2 * depth * width, 6 * 2 * depth * width),
        name="codes",
    )(fresh, *peak_rows)

    return (left[None], coded, scales)


def solution(mesh):
    in_specs = (
        P("pipe", "expert", "dp"),
        P("pipe", "expert", "dp"),
        P("pipe", "expert", "dp"),
        P(None, "pipe", "dp"),
        P(None, "pipe", None, "dp"),
        P(None, "pipe", None, "dp"),
        P(None, "pipe", "expert", "dp"),
        P(None, "pipe", "expert", "dp"),
        P(None, "pipe", "expert", "dp"),
    )
    out_specs = (
        P("pipe", "expert", "dp"),
        P(None, "pipe", "expert", "dp"),
        P(None, "pipe", None, "dp"),
    )
    return jax.shard_map(shards, mesh=mesh, in_specs=in_specs, out_specs=out_specs, check_vma=False)
```

time: 114 us -> 90.2 us (0.79); the launches traced: 112 us -> 89.9 us
  Pallas kernels: 52.1 us -> 11.9 us
  waiting for transfers between devices: 18.2 us -> 56.3 us
  starting transfers between devices: 34.2 us -> 19.3 us
  local copies, waits for them, and re-layouts: 6.99 us -> 1.67 us
    pallas_call x14 -> x8, Pallas kernels: 39.6 us -> 9.11 us  [the longest x1 5.64 us: shards(): pl.pallas_call(lambda x1, x2, c2, down, up, *refs: latent_kernel(tiles, x...]
    ppermute x17 -> x12, waiting for transfers between devices: 5.2 us -> 28.6 us  [exchange(): return lax.ppermute(block, axis, [(i, i ^ offset) for i in range(count)])]
    ppermute x4 -> x2, waiting for transfers between devices: 13 us -> 27.7 us  [mirrored(): return lax.ppermute(block, axis, [(i, count - 1 - i) for i in range(count)])]
    ppermute x17 -> x12, starting transfers between devices: 22.3 us -> 12.6 us  [exchange(): return lax.ppermute(block, axis, [(i, i ^ offset) for i in range(count)])]
    pallas_call x4 -> x2, Pallas kernels: 9.85 us -> 1.65 us  [shards(): pl.pallas_call(update_kernel, grid=(1,), in_specs=[whole((2, depth, part)...]
    unnamed x49 -> x19, local copies, waits for them, and re-layouts: 6.99 us -> 1.67 us
    ppermute x2 -> x1, starting transfers between devices: 7.77 us -> 3.49 us  [shifted(): return lax.ppermute(block, axis, [(i, i + 1) for i in range(count - 1)])]
    pallas_call x1, Pallas kernels: 2.72 us -> 1.17 us  [shards(): pl.pallas_call(lambda *refs: code_kernel(group, *refs), grid=(1,), in_spe...]
  transfers between devices with their start and end apart: 23 -> 15, of which waited for: 7 -> 12; matrix products, arithmetic and copies ran while one was open for 0% -> 0% of each run, Pallas kernels for 41% -> 2%
where the time goes in v3:
time: 90.2 us; the launch traced here: 89.9 us
  waiting for transfers between devices  56.3 us (62%)
  starting transfers between devices  19.3 us (21%)
  Pallas kernels  11.9 us (13%)
  local copies, waits for them, and re-layouts  1.67 us (2%)
    ppermute x12, waiting for transfers between devices, exchange(): return lax.ppermute(block, axis, [(i, i ^ offset) for i in range(count)])  28.6 us
    ppermute x2, waiting for transfers between devices, mirrored(): return lax.ppermute(block, axis, [(i, count - 1 - i) for i in range(count)])  27.7 us
    ppermute x12, starting transfers between devices, exchange(): return lax.ppermute(block, axis, [(i, i ^ offset) for i in range(count)])  12.6 us
    pallas_call x1, Pallas kernels, shards(): pl.pallas_call(lambda x1, x2, c2, down, up, *refs: latent_kernel(tiles, x...  5.64 us
    ppermute x1, starting transfers between devices, shifted(): return lax.ppermute(block, axis, [(i, i + 1) for i in range(count - 1)])  3.49 us
    ppermute x2, starting transfers between devices, mirrored(): return lax.ppermute(block, axis, [(i, count - 1 - i) for i in range(count)])  3.22 us
    pallas_call x4, Pallas kernels, split(): pl.pallas_call(kernel, grid=(1,), in_specs=[whole(o.shape) for o in opera...  1.91 us
  transfers between devices with their start and end apart: 15, of which 12 were waited for; matrix products, arithmetic and copies ran while one was open for 0% of the time, Pallas kernels for 2%

profile of v3, /device:TPU:8, one launch (start us, length us, event | category | flops | bytes accessed | tf_op | source)
XLA Modules:
  0.0 89.9 jit_solution(17155718891861399050)
XLA Ops:
  0.6 0.7 copy-done.7
  1.4 5.6 %latents.1.own_ref.refs_0_ = f32[1024,128]{1,0:T(8,128)S(1)} custom-call(bf16[1,128,3584]{2,1,0:T(8,128)(2,1)} %x_ref.1, bf16[1,128,3584]{2,1,0:T(8,128)(2,1)} %refs_2_.3, bf16[1,128,3584]{2,1,0:T(8,128)(2,1)} %refs_4_.3, bf16[2,1,256,3584]{3,2,1,0:T(8,128)(2,1)} %down.1, bf16[2,1,256,3584]{3,2,1,0:T(8,128)(2,1)} %b_ref.1, bf16[2,3584]{1,0:T(2,128)(2,1)S(1)} %bitcast.3), custom_call_target="tpu_custom_call" | custom-call | flops 704643072 | bytes 8257536 | tf_op jit(solution)/shard_map/latents/pallas_call | solution.py:223
  7.1 1.9 %collective-permute-done.other_ref.refs_1_ = f32[1024,128]{1,0:T(8,128)S(1)} collective-permute-done((f32[1024,128]{1,0:T(8,128)S(1)}, f32[1024,128]{1,0:T(8,128)S(1)}, u32[]{:S(2)}, u32[]{:S(2)}) %collective-permute-start) | collective-permute-done | bytes 524320 | tf_op jit(solution)/shard_map/ppermute | solution.py:17
  9.0 1.4 %leaving.1.refs_5_.refs_6_ = bf16[128,3584]{1,0:T(8,128)(2,1)S(1)} custom-call(f32[1024,128]{1,0:T(8,128)S(1)} %latents.1.own_ref.refs_0_, f32[1024,128]{1,0:T(8,128)S(1)} %collective-permute-done.other_ref.refs_1_, bf16[1,128,3584]{2,1,0:T(8,128)(2,1)S(1)} %copy-done.4, bf16[2,1,256,3584]{3,2,1,0:T(8,128)(2,1)S(1)} %copy-done), custom_call_target="tpu_custom_call" | custom-call | flops 234881024 | bytes 3670016 | tf_op jit(solution)/shard_map/leaving/pallas_call | solution.py:245
  10.4 3.5 %collective-permute-start.1 = (bf16[128,3584]{1,0:T(8,128)(2,1)S(1)}, bf16[128,3584]{1,0:T(8,128)(2,1)S(1)}, u32[]{:S(2)}, u32[]{:S(2)}) collective-permute-start(bf16[128,3584]{1,0:T(8,128)(2,1)S(1)} %leaving.1.refs_5_.refs_6_), channel_id=1, source_target_pairs={{0,8},{8,16},{16,24},{1,9},{9,17},{17,25},{2,10},{10,18},{18,26},{... | collective-permute-start | bytes 2752520 | tf_op jit(solution)/shard_map/ppermute | solution.py:27
  14.0 0.8 grads.2
  14.7 1.6 %collective-permute-start.2 = (bf16[128,1792]{1,0:T(8,128)(2,1)S(1)}, bf16[128,1792]{1,0:T(8,128)(2,1)S(1)}, u32[]{:S(2)}, u32[]{:S(2)}) collective-permute-start(bf16[128,1792]{1,0:T(8,128)(2,1)S(1)} %get-tuple-element.26), channel_id=1, source_target_pairs={{0,2},{2,0},{4,6},{6,4},{1,3},{3,1},{5,7},{7,5},{8,10},{10,8},{12,... | collective-permute-start | bytes 1376264 | tf_op jit(solution)/shard_map/ppermute | solution.py:17
  16.3 1.5 %collective-permute-start.3 = (bf16[128,1792]{1,0:T(8,128)(2,1)S(1)}, bf16[128,1792]{1,0:T(8,128)(2,1)S(1)}, u32[]{:S(2)}, u32[]{:S(2)}) collective-permute-start(bf16[128,1792]{1,0:T(8,128)(2,1)S(1)} %get-tuple-element.28), channel_id=1, source_target_pairs={{0,4},{2,6},{4,0},{6,2},{1,5},{3,7},{5,1},{7,3},{8,12},{10,14},{12... | collective-permute-start | bytes 1376264 | tf_op jit(solution)/shard_map/ppermute | solution.py:17
  17.8 9.3 %collective-permute-done.2.down_in = bf16[128,1792]{1,0:T(8,128)(2,1)S(1)} collective-permute-done((bf16[128,1792]{1,0:T(8,128)(2,1)S(1)}, bf16[128,1792]{1,0:T(8,128)(2,1)S(1)}, u32[]{:S(2)}, u32[]{:S(2)}) %collective-permute-start.2) | collective-permute-done | bytes 458784 | tf_op jit(solution)/shard_map/ppermute | solution.py:17
  27.1 1.2 %collective-permute-done.3.up_in = bf16[128,1792]{1,0:T(8,128)(2,1)S(1)} collective-permute-done((bf16[128,1792]{1,0:T(8,128)(2,1)S(1)}, bf16[128,1792]{1,0:T(8,128)(2,1)S(1)}, u32[]{:S(2)}, u32[]{:S(2)}) %collective-permute-start.3) | collective-permute-done | bytes 458784 | tf_op jit(solution)/shard_map/ppermute | solution.py:17
  28.5 1.6 %collective-permute-start.4 = (bf16[64,1792]{1,0:T(8,128)(2,1)S(1)}, bf16[64,1792]{1,0:T(8,128)(2,1)S(1)}, u32[]{:S(2)}, u32[]{:S(2)}) collective-permute-start(bf16[64,1792]{1,0:T(8,128)(2,1)S(1)} %get-tuple-element.30), channel_id=1, source_target_pairs={{0,4},{2,6},{4,0},{6,2},{1,5},{3,7},{5,1},{7,3},{8,12},{10,14},{12... | collective-permute-start | bytes 688136 | tf_op jit(solution)/shard_map/ppermute | solution.py:17
  30.6 4.1 %collective-permute-done.4.down_in = bf16[64,1792]{1,0:T(8,128)(2,1)S(1)} collective-permute-done((bf16[64,1792]{1,0:T(8,128)(2,1)S(1)}, bf16[64,1792]{1,0:T(8,128)(2,1)S(1)}, u32[]{:S(2)}, u32[]{:S(2)}) %collective-permute-start.4) | collective-permute-done | bytes 229408 | tf_op jit(solution)/shard_map/ppermute | solution.py:17
  34.7 1.4 %collective-permute-done.5.up_in = bf16[64,1792]{1,0:T(8,128)(2,1)S(1)} collective-permute-done((bf16[64,1792]{1,0:T(8,128)(2,1)S(1)}, bf16[64,1792]{1,0:T(8,128)(2,1)S(1)}, u32[]{:S(2)}, u32[]{:S(2)}) %collective-permute-start.5) | collective-permute-done | bytes 229408 | tf_op jit(solution)/shard_map/ppermute | solution.py:17
  36.2 0.8 grads.3
  36.9 0.6 collective-permute-start.6
  37.5 1.0 %collective-permute-start.7 = (bf16[128,1792]{1,0:T(8,128)(2,1)S(1)}, bf16[128,1792]{1,0:T(8,128)(2,1)S(1)}, u32[]{:S(2)}, u32[]{:S(2)}) collective-permute-start(bf16[128,1792]{1,0:T(8,128)(2,1)S(1)} %get-tuple-element.36), channel_id=1, source_target_pairs={{0,4},{2,6},{4,0},{6,2},{1,5},{3,7},{5,1},{7,3},{8,12},{10,14},{12... | collective-permute-start | bytes 1376264 | tf_op jit(solution)/shard_map/ppermute | solution.py:17
  38.6 1.6 %collective-permute-start.10 = (bf16[2,64,1792]{2,1,0:T(8,128)(2,1)S(1)}, bf16[2,64,1792]{2,1,0:T(8,128)(2,1)S(1)}, u32[]{:S(2)}, u32[]{:S(2)}) collective-permute-start(bf16[2,64,1792]{2,1,0:T(8,128)(2,1)S(1)} %share.2.refs_6_), channel_id=1, source_target_pairs={{0,24},{8,16},{16,8},{24,0},{1,25},{9,17},{17,9},{25,1},{2,26},{10... | collective-permute-start | bytes 1376264 | tf_op jit(solution)/shard_map/ppermute | solution.py:22
  40.1 7.1 %collective-permute-done.6.down_in = bf16[128,1792]{1,0:T(8,128)(2,1)S(1)} collective-permute-done((bf16[128,1792]{1,0:T(8,128)(2,1)S(1)}, bf16[128,1792]{1,0:T(8,128)(2,1)S(1)}, u32[]{:S(2)}, u32[]{:S(2)}) %collective-permute-start.6) | collective-permute-done | bytes 458784 | tf_op jit(solution)/shard_map/ppermute | solution.py:17
  47.3 1.2 %collective-permute-done.7.up_in = bf16[128,1792]{1,0:T(8,128)(2,1)S(1)} collective-permute-done((bf16[128,1792]{1,0:T(8,128)(2,1)S(1)}, bf16[128,1792]{1,0:T(8,128)(2,1)S(1)}, u32[]{:S(2)}, u32[]{:S(2)}) %collective-permute-start.7) | collective-permute-done | bytes 458784 | tf_op jit(solution)/shard_map/ppermute | solution.py:17
  48.7 1.6 %collective-permute-start.8 = (bf16[64,1792]{1,0:T(8,128)(2,1)S(1)}, bf16[64,1792]{1,0:T(8,128)(2,1)S(1)}, u32[]{:S(2)}, u32[]{:S(2)}) collective-permute-start(bf16[64,1792]{1,0:T(8,128)(2,1)S(1)} %get-tuple-element.38), channel_id=1, source_target_pairs={{0,4},{2,6},{4,0},{6,2},{1,5},{3,7},{5,1},{7,3},{8,12},{10,14},{12... | collective-permute-start | bytes 688136 | tf_op jit(solution)/shard_map/ppermute | solution.py:17
  50.3 0.5 collective-permute-start.9
  50.8 18.6 %collective-permute-done.10.rest_0_.share_ref = bf16[2,64,1792]{2,1,0:T(8,128)(2,1)S(1)} collective-permute-done((bf16[2,64,1792]{2,1,0:T(8,128)(2,1)S(1)}, bf16[2,64,1792]{2,1,0:T(8,128)(2,1)S(1)}, u32[]{:S(2)}, u32[]{:S(2)}) %collective-permute-start.10) | collective-permute-done | bytes 458784 | tf_op jit(solution)/shard_map/ppermute | solution.py:22
  69.5 1.6 %collective-permute-start.11 = (bf16[2,64,1792]{2,1,0:T(8,128)(2,1)S(1)}, bf16[2,64,1792]{2,1,0:T(8,128)(2,1)S(1)}, u32[]{:S(2)}, u32[]{:S(2)}) collective-permute-start(bf16[2,64,1792]{2,1,0:T(8,128)(2,1)S(1)} %share.3), channel_id=1, source_target_pairs={{0,24},{8,16},{16,8},{24,0},{1,25},{9,17},{17,9},{25,1},{2,26},{10... | collective-permute-start | bytes 1376264 | tf_op jit(solution)/shard_map/ppermute | solution.py:22
  71.1 0.8 update.2
  72.0 9.1 %collective-permute-done.11.share_ref = bf16[2,64,1792]{2,1,0:T(8,128)(2,1)S(1)} collective-permute-done((bf16[2,64,1792]{2,1,0:T(8,128)(2,1)S(1)}, bf16[2,64,1792]{2,1,0:T(8,128)(2,1)S(1)}, u32[]{:S(2)}, u32[]{:S(2)}) %collective-permute-start.11) | collective-permute-done | bytes 458784 | tf_op jit(solution)/shard_map/ppermute | solution.py:22
  81.1 0.8 update.3
  81.9 0.6 collective-permute-start.12
  83.0 2.4 %collective-permute-start.14 = (f32[2,2,14,128]{3,2,1,0:T(8,128)S(1)}, f32[2,2,14,128]{3,2,1,0:T(8,128)S(1)}, u32[]{:S(2)}, u32[]{:S(2)}) collective-permute-start(f32[2,2,14,128]{3,2,1,0:T(8,128)S(1)} %get-tuple-element.44.refs_1_), channel_id=1, source_target_pairs={{0,6},{2,4},{4,2},{6,0},{1,7},{3,5},{5,3},{7,1},{8,14},{10,12},{12... | collective-permute-start | bytes 86024 | tf_op jit(solution)/shard_map/ppermute | solution.py:17
  85.9 0.6 collective-permute-done.13.refs_3_
  86.4 1.4 %collective-permute-done.14.refs_4_ = f32[2,2,14,128]{3,2,1,0:T(8,128)S(1)} collective-permute-done((f32[2,2,14,128]{3,2,1,0:T(8,128)S(1)}, f32[2,2,14,128]{3,2,1,0:T(8,128)S(1)}, u32[]{:S(2)}, u32[]{:S(2)}) %collective-permute-start.14) | collective-permute-done | bytes 28704 | tf_op jit(solution)/shard_map/ppermute | solution.py:17
  87.8 1.2 %codes.1 = (bf16[2,1,64,3584]{3,2,1,0:T(8,128)(2,1)}, f32[2,1,2,28]{3,2,1,0:T(2,128)}) custom-call(f32[2,64,3584]{2,1,0:T(8,128)S(1)} %get-tuple-element.43.refs_0_, f32[2,2,14,128]{3,2,1,0:T(8,128)S(1)} %get-tuple-element.44.refs_1_, f32[2,2,14,128]{3,2,1,0:T(8,128)S(1)} %collective-permute-done.12.refs_2_, ...), custom_call_target="tpu_custom_call" | custom-call | flops 917504 | bytes 2752512 | tf_op jit(solution)/shard_map/codes/pallas_call | solution.py:361
  89.0 0.9 %copy.17 = bf16[1,128,3584]{2,1,0:T(8,128)(2,1)} copy(bf16[1,128,3584]{2,1,0:T(8,128)(2,1)S(1)} %bitcast.2) | data formatting | bytes 1835008
  (28 shorter events, 2.1 us)
Async XLA Ops:
  0.6 0.7 copy-start.7
  1.3 7.7 %copy-start = (bf16[2,1,256,3584]{3,2,1,0:T(8,128)(2,1)S(1)}, bf16[2,1,256,3584]{3,2,1,0:T(8,128)(2,1)}, u32[]{:S(2)}) copy-start(bf16[2,1,256,3584]{3,2,1,0:T(8,128)(2,1)} %b_ref.1) | copy-start | bytes 11010052
  1.3 7.7 %copy-start.4 = (bf16[1,128,3584]{2,1,0:T(8,128)(2,1)S(1)}, bf16[1,128,3584]{2,1,0:T(8,128)(2,1)}, u32[]{:S(2)}) copy-start(bf16[1,128,3584]{2,1,0:T(8,128)(2,1)} %x_ref.1) | copy-start | bytes 2752516
  7.0 6.9 %copy-start.1 = (bf16[1,128,3584]{2,1,0:T(8,128)(2,1)S(1)}, bf16[1,128,3584]{2,1,0:T(8,128)(2,1)}, u32[]{:S(2)}) copy-start(bf16[1,128,3584]{2,1,0:T(8,128)(2,1)} %refs_2_.3) | copy-start | bytes 2752516
  7.0 6.9 %copy-start.2 = (bf16[1,128,3584]{2,1,0:T(8,128)(2,1)S(1)}, bf16[1,128,3584]{2,1,0:T(8,128)(2,1)}, u32[]{:S(2)}) copy-start(bf16[1,128,3584]{2,1,0:T(8,128)(2,1)} %refs_4_.3) | copy-start | bytes 2752516
  7.0 6.9 %copy-start.8 = (bf16[2,1,3584]{2,0,1:T(2,128)(2,1)S(1)}, bf16[2,1,3584]{2,0,1:T(2,128)(2,1)}, u32[]{:S(2)}) copy-start(bf16[2,1,3584]{2,0,1:T(2,128)(2,1)} %param.12) | copy-start | bytes 43012
  7.0 2.0 %collective-permute-start = (f32[1024,128]{1,0:T(8,128)S(1)}, f32[1024,128]{1,0:T(8,128)S(1)}, u32[]{:S(2)}, u32[]{:S(2)}) collective-permute-start(f32[1024,128]{1,0:T(8,128)S(1)} %latents.1.own_ref.refs_0_), channel_id=1, source_target_pairs={{0,1},{1,0},{2,3},{3,2},{4,5},{5,4},{6,7},{7,6},{8,9},{9,8},{10,11... | collective-permute-start | bytes 1572872 | tf_op jit(solution)/shard_map/ppermute | solution.py:17
  10.4 25.7 %collective-permute-start.1 = (bf16[128,3584]{1,0:T(8,128)(2,1)S(1)}, bf16[128,3584]{1,0:T(8,128)(2,1)S(1)}, u32[]{:S(2)}, u32[]{:S(2)}) collective-permute-start(bf16[128,3584]{1,0:T(8,128)(2,1)S(1)} %leaving.1.refs_5_.refs_6_), channel_id=1, source_target_pairs={{0,8},{8,16},{16,24},{1,9},{9,17},{17,25},{2,10},{10,18},{18,26},{... | collective-permute-start | bytes 2752520 | tf_op jit(solution)/shard_map/ppermute | solution.py:27
  14.7 12.3 %collective-permute-start.2 = (bf16[128,1792]{1,0:T(8,128)(2,1)S(1)}, bf16[128,1792]{1,0:T(8,128)(2,1)S(1)}, u32[]{:S(2)}, u32[]{:S(2)}) collective-permute-start(bf16[128,1792]{1,0:T(8,128)(2,1)S(1)} %get-tuple-element.26), channel_id=1, source_target_pairs={{0,2},{2,0},{4,6},{6,4},{1,3},{3,1},{5,7},{7,5},{8,10},{10,8},{12,... | collective-permute-start | bytes 1376264 | tf_op jit(solution)/shard_map/ppermute | solution.py:17
  16.3 12.0 %collective-permute-start.3 = (bf16[128,1792]{1,0:T(8,128)(2,1)S(1)}, bf16[128,1792]{1,0:T(8,128)(2,1)S(1)}, u32[]{:S(2)}, u32[]{:S(2)}) collective-permute-start(bf16[128,1792]{1,0:T(8,128)(2,1)S(1)} %get-tuple-element.28), channel_id=1, source_target_pairs={{0,4},{2,6},{4,0},{6,2},{1,5},{3,7},{5,1},{7,3},{8,12},{10,14},{12... | collective-permute-start | bytes 1376264 | tf_op jit(solution)/shard_map/ppermute | solution.py:17
  28.5 6.2 %collective-permute-start.4 = (bf16[64,1792]{1,0:T(8,128)(2,1)S(1)}, bf16[64,1792]{1,0:T(8,128)(2,1)S(1)}, u32[]{:S(2)}, u32[]{:S(2)}) collective-permute-start(bf16[64,1792]{1,0:T(8,128)(2,1)S(1)} %get-tuple-element.30), channel_id=1, source_target_pairs={{0,4},{2,6},{4,0},{6,2},{1,5},{3,7},{5,1},{7,3},{8,12},{10,14},{12... | collective-permute-start | bytes 688136 | tf_op jit(solution)/shard_map/ppermute | solution.py:17
  30.1 6.0 %collective-permute-start.5 = (bf16[64,1792]{1,0:T(8,128)(2,1)S(1)}, bf16[64,1792]{1,0:T(8,128)(2,1)S(1)}, u32[]{:S(2)}, u32[]{:S(2)}) collective-permute-start(bf16[64,1792]{1,0:T(8,128)(2,1)S(1)} %get-tuple-element.32), channel_id=1, source_target_pairs={{0,2},{2,0},{4,6},{6,4},{1,3},{3,1},{5,7},{7,5},{8,10},{10,8},{12,... | collective-permute-start | bytes 688136 | tf_op jit(solution)/shard_map/ppermute | solution.py:17
  36.9 10.3 %collective-permute-start.6 = (bf16[128,1792]{1,0:T(8,128)(2,1)S(1)}, bf16[128,1792]{1,0:T(8,128)(2,1)S(1)}, u32[]{:S(2)}, u32[]{:S(2)}) collective-permute-start(bf16[128,1792]{1,0:T(8,128)(2,1)S(1)} %get-tuple-element.34), channel_id=1, source_target_pairs={{0,2},{2,0},{4,6},{6,4},{1,3},{3,1},{5,7},{7,5},{8,10},{10,8},{12,... | collective-permute-start | bytes 1376264 | tf_op jit(solution)/shard_map/ppermute | solution.py:17
  37.5 10.9 %collective-permute-start.7 = (bf16[128,1792]{1,0:T(8,128)(2,1)S(1)}, bf16[128,1792]{1,0:T(8,128)(2,1)S(1)}, u32[]{:S(2)}, u32[]{:S(2)}) collective-permute-start(bf16[128,1792]{1,0:T(8,128)(2,1)S(1)} %get-tuple-element.36), channel_id=1, source_target_pairs={{0,4},{2,6},{4,0},{6,2},{1,5},{3,7},{5,1},{7,3},{8,12},{10,14},{12... | collective-permute-start | bytes 1376264 | tf_op jit(solution)/shard_map/ppermute | solution.py:17
  38.6 30.8 %collective-permute-start.10 = (bf16[2,64,1792]{2,1,0:T(8,128)(2,1)S(1)}, bf16[2,64,1792]{2,1,0:T(8,128)(2,1)S(1)}, u32[]{:S(2)}, u32[]{:S(2)}) collective-permute-start(bf16[2,64,1792]{2,1,0:T(8,128)(2,1)S(1)} %share.2.refs_6_), channel_id=1, source_target_pairs={{0,24},{8,16},{16,8},{24,0},{1,25},{9,17},{17,9},{25,1},{2,26},{10... | collective-permute-start | bytes 1376264 | tf_op jit(solution)/shard_map/ppermute | solution.py:22
  48.5 22.6 %copy-start.3 = (f32[2,1,64,3584]{3,2,1,0:T(8,128)S(1)}, f32[2,1,64,3584]{3,2,1,0:T(8,128)}, u32[]{:S(2)}) copy-start(f32[2,1,64,3584]{3,2,1,0:T(8,128)} %master_ref.3) | copy-start | bytes 5505028
  48.5 22.6 %copy-start.5 = (bf16[2,1,64,3584]{3,2,1,0:T(8,128)(2,1)S(1)}, bf16[2,1,64,3584]{3,2,1,0:T(8,128)(2,1)}, u32[]{:S(2)}) copy-start(bf16[2,1,64,3584]{3,2,1,0:T(8,128)(2,1)} %moment_ref.3) | copy-start | bytes 2752516
  48.5 22.6 %copy-start.6 = (bf16[2,1,64,3584]{3,2,1,0:T(8,128)(2,1)S(1)}, bf16[2,1,64,3584]{3,2,1,0:T(8,128)(2,1)}, u32[]{:S(2)}) copy-start(bf16[2,1,64,3584]{3,2,1,0:T(8,128)(2,1)} %second_ref.3) | copy-start | bytes 2752516
  48.7 20.7 %collective-permute-start.8 = (bf16[64,1792]{1,0:T(8,128)(2,1)S(1)}, bf16[64,1792]{1,0:T(8,128)(2,1)S(1)}, u32[]{:S(2)}, u32[]{:S(2)}) collective-permute-start(bf16[64,1792]{1,0:T(8,128)(2,1)S(1)} %get-tuple-element.38), channel_id=1, source_target_pairs={{0,4},{2,6},{4,0},{6,2},{1,5},{3,7},{5,1},{7,3},{8,12},{10,14},{12... | collective-permute-start | bytes 688136 | tf_op jit(solution)/shard_map/ppermute | solution.py:17
  50.3 19.1 %collective-permute-start.9 = (bf16[64,1792]{1,0:T(8,128)(2,1)S(1)}, bf16[64,1792]{1,0:T(8,128)(2,1)S(1)}, u32[]{:S(2)}, u32[]{:S(2)}) collective-permute-start(bf16[64,1792]{1,0:T(8,128)(2,1)S(1)} %get-tuple-element.40), channel_id=1, source_target_pairs={{0,2},{2,0},{4,6},{6,4},{1,3},{3,1},{5,7},{7,5},{8,10},{10,8},{12,... | collective-permute-start | bytes 688136 | tf_op jit(solution)/shard_map/ppermute | solution.py:17
  69.5 11.6 %collective-permute-start.11 = (bf16[2,64,1792]{2,1,0:T(8,128)(2,1)S(1)}, bf16[2,64,1792]{2,1,0:T(8,128)(2,1)S(1)}, u32[]{:S(2)}, u32[]{:S(2)}) collective-permute-start(bf16[2,64,1792]{2,1,0:T(8,128)(2,1)S(1)} %share.3), channel_id=1, source_target_pairs={{0,24},{8,16},{16,8},{24,0},{1,25},{9,17},{17,9},{25,1},{2,26},{10... | collective-permute-start | bytes 1376264 | tf_op jit(solution)/shard_map/ppermute | solution.py:22
  81.9 4.0 %collective-permute-start.12 = (f32[2,2,14,128]{3,2,1,0:T(8,128)S(1)}, f32[2,2,14,128]{3,2,1,0:T(8,128)S(1)}, u32[]{:S(2)}, u32[]{:S(2)}) collective-permute-start(f32[2,2,14,128]{3,2,1,0:T(8,128)S(1)} %get-tuple-element.44.refs_1_), channel_id=1, source_target_pairs={{0,2},{2,0},{4,6},{6,4},{1,3},{3,1},{5,7},{7,5},{8,10},{10,8},{12,... | collective-permute-start | bytes 86024 | tf_op jit(solution)/shard_map/ppermute | solution.py:17
  82.5 3.9 %collective-permute-start.13 = (f32[2,2,14,128]{3,2,1,0:T(8,128)S(1)}, f32[2,2,14,128]{3,2,1,0:T(8,128)S(1)}, u32[]{:S(2)}, u32[]{:S(2)}) collective-permute-start(f32[2,2,14,128]{3,2,1,0:T(8,128)S(1)} %get-tuple-element.44.refs_1_), channel_id=1, source_target_pairs={{0,4},{2,6},{4,0},{6,2},{1,5},{3,7},{5,1},{7,3},{8,12},{10,14},{12... | collective-permute-start | bytes 86024 | tf_op jit(solution)/shard_map/ppermute | solution.py:17
  83.0 4.8 %collective-permute-start.14 = (f32[2,2,14,128]{3,2,1,0:T(8,128)S(1)}, f32[2,2,14,128]{3,2,1,0:T(8,128)S(1)}, u32[]{:S(2)}, u32[]{:S(2)}) collective-permute-start(f32[2,2,14,128]{3,2,1,0:T(8,128)S(1)} %get-tuple-element.44.refs_1_), channel_id=1, source_target_pairs={{0,6},{2,4},{4,2},{6,0},{1,7},{3,5},{5,3},{7,1},{8,14},{10,12},{12... | collective-permute-start | bytes 86024 | tf_op jit(solution)/shard_map/ppermute | solution.py:17

commit v4 on v3

v4 whole, which is shorter than its diff:
```python
import jax
import jax.numpy as jnp
from jax import lax
from jax.experimental import pallas as pl
from jax.experimental.pallas import tpu as pltpu
from jax.sharding import PartitionSpec as P

D = 7168
LANES = 128
F32 = jnp.float32
BF16 = jnp.bfloat16
BOTH_LAST = (((1,), (1,)), ((), ()))


def exchange(block, axis, offset):
    count = lax.axis_size(axis)
    return lax.ppermute(block, axis, [(i, i ^ offset) for i in range(count)])


def mirrored(block, axis):
    count = lax.axis_size(axis)
    return lax.ppermute(block, axis, [(i, count - 1 - i) for i in range(count)])


def shifted(block, axis):
    count = lax.axis_size(axis)
    return lax.ppermute(block, axis, [(i, (i + 1) % count) for i in range(count)])


def halves_of_sum(block, axis):
    count = lax.axis_size(axis)
    offset = 1
    while True:
        other = exchange(block, axis, offset)
        offset *= 2
        if offset >= count:
            return block, other
        block = block + other


ROOM = pltpu.CompilerParams(vmem_limit_bytes=16 << 20)


def cost(flops, nbytes):
    return pl.CostEstimate(flops=flops, bytes_accessed=nbytes, transcendentals=0)


def folded_squares(rows):
    tokens, width = rows.shape
    total = jnp.zeros((tokens, LANES), F32)
    for at in range(0, width, LANES):
        part = rows[:, at : at + LANES]
        total = total + part * part
    return total


def latent_kernel(tiles, x1, a1, x2, c2, a2, b2, gain, out_ref, vx1, va1, vx2, vc2, va2, vb2, vgain, sems):
    tokens, width = vx1.shape
    latent = va1.shape[0]
    tile = width // tiles
    jobs = [[pltpu.make_async_copy(gain, vgain, sems.at[6 * tiles])]]
    for names in (((x1, vx1), (a1, va1)), ((x2, vx2), (a2, va2)), ((c2, vc2), (b2, vb2))):
        for at in range(tiles):
            cols = pl.ds(at * tile, tile)
            sem = 2 * (len(jobs) - 1)
            jobs.append(
                [pltpu.make_async_copy(s.at[:, cols], d.at[:, cols], sems.at[sem + k]) for k, (s, d) in enumerate(names)]
            )
    ahead = 4
    for job in jobs[:ahead]:
        for copy in job:
            copy.start()

    def arrive(at):
        for copy in jobs[at]:
            copy.wait()
        if at + ahead < len(jobs):
            for copy in jobs[at + ahead]:
                copy.start()

    arrive(0)
    gains = vgain[...].astype(F32)

    def product(job, left, right):
        total = None
        squares = jnp.zeros((tokens, LANES), F32)
        for at in range(tiles):
            arrive(1 + job * tiles + at)
            cols = slice(at * tile, (at + 1) * tile)
            one, two = left(cols), right(cols)
            if job < 2:
                rows = (vx1, vx2)[job][:, cols].astype(F32)
                squares += folded_squares(rows)
                scaled = (rows * gains[job : job + 1, cols]).astype(BF16)
                one = scaled if one is None else one
                two = scaled if two is None else two
            term = lax.dot_general(one, two, BOTH_LAST, preferred_element_type=F32)
            total = term if total is None else total + term
        return total, squares

    raw, squares = product(0, lambda c: None, lambda c: va1[:, c])
    base = 2 * latent + tokens
    for at in range(latent // LANES):
        out_ref[base + at * tokens : base + (at + 1) * tokens] = raw[:, at * LANES : (at + 1) * LANES]
    out_ref[base + (latent // LANES) * tokens :] = squares
    raw, squares = product(1, lambda c: va2[:, c], lambda c: None)
    out_ref[:latent] = raw
    out_ref[2 * latent : base] = squares
    out_ref[latent : 2 * latent], _ = product(2, lambda c: vb2[:, c], lambda c: vc2[:, c])


def leaving_kernel(start, own_ref, other_ref, x_ref, b_ref, *rest):
    out_ref = rest[-1]
    latent = b_ref.shape[0]
    count = out_ref.shape[0]
    tokens = x_ref.shape[0]

    def summed(at):
        rows = slice(at + start, at + start + count)
        return own_ref[rows] + other_ref[rows]

    base = own_ref.shape[0] - tokens
    rscale = lax.rsqrt(jnp.sum(summed(base), axis=1, keepdims=True) / D + 1e-06)
    base -= (latent // LANES) * tokens
    hidden = jnp.concatenate([summed(base + at * tokens) * rscale for at in range(latent // LANES)], axis=1).astype(BF16)
    last = lax.axis_index("pipe") == lax.axis_size("pipe") - 1
    width = out_ref.shape[1]
    step = width // (4 if width % 512 == 0 else 2)
    for at in range(0, width, step):
        cols = slice(at, at + step)
        rows = x_ref[start : start + count, cols].astype(F32)
        rows += jnp.dot(hidden, b_ref[:, cols], preferred_element_type=F32)
        out_ref[:, cols] = jnp.where(last, 0.0, rows).astype(BF16)


def grad_kernel(experts, own_ref, other_ref, x_ref, g_ref, c_ref, *rest):
    outs, rows_ref = rest[-1 - experts : -1], rest[-1]
    latent = rows_ref.shape[1]
    depth = latent // experts
    me = lax.axis_index("expert")
    squares = own_ref[2 * latent : 2 * latent + LANES] + other_ref[2 * latent : 2 * latent + LANES]
    rscale = lax.rsqrt(jnp.sum(squares.T, axis=0, keepdims=True) / D + 1e-06)
    rows_ref[0] = (own_ref[latent : 2 * latent] + other_ref[latent : 2 * latent]) * rscale
    rows_ref[1] = (own_ref[:latent] + other_ref[:latent]) * rscale
    scaled = (x_ref[...].astype(F32) * g_ref[1:2].astype(F32)).astype(BF16)
    for side, right in enumerate((scaled, c_ref[...])):
        left = jnp.concatenate(
            [rows_ref[side, pl.ds(pl.multiple_of((me ^ k) * depth, depth), depth), :] for k in range(experts)]
        )
        both = jnp.dot(left.astype(BF16), right, preferred_element_type=F32).astype(BF16)
        for k in range(experts):
            outs[k][side] = both[k * depth : (k + 1) * depth]


def share_kernel(experts, *refs):
    total = refs[0][...].astype(F32)
    for ref in refs[1:experts]:
        total = total + ref[...].astype(F32)
    refs[-1][...] = total.astype(BF16)


def update_kernel(share_ref, master_ref, moment_ref, second_ref, *rest):
    fresh_ref, peak_ref = rest[-2:]
    grad = share_ref[...].astype(F32)
    first = 0.9 * moment_ref[...].astype(F32) + 0.1 * grad
    secnd = 0.95 * second_ref[...].astype(F32) + 0.05 * grad * grad
    update = first / (1.0 - 0.9**10) / (jnp.sqrt(secnd / (1.0 - 0.95**10)) + 1e-08)
    weights = master_ref[...]
    fresh = weights - 0.01 * (update + 0.1 * weights)
    fresh_ref[...] = fresh
    peak = jnp.max(jnp.abs(fresh), axis=1, keepdims=True)
    for block in range(peak.shape[-1] // LANES):
        peak_ref[:, block : block + 1] = peak[:, :, block * LANES : (block + 1) * LANES]


def code_kernel(group, fresh_ref, *rest):
    peak_refs, code_ref, scale_ref, wide = rest[:-3], rest[-3], rest[-2], rest[-1]
    chunks, _, per, _ = peak_refs[0].shape
    mine = lax.axis_index("expert") // group
    wide[...] = jnp.zeros_like(wide)
    for far, top in enumerate(peak_refs):
        for side in range(2):
            for chunk in range(chunks):
                wide[side, chunk * per : (chunk + 1) * per, :] = top[chunk, side]
        where = pl.ds(mine ^ far, 1)
        for side in range(2):
            scale_ref[side, where, :] = (
                jnp.max(wide[side].T, axis=0, keepdims=True)[:, : chunks * per] + 1e-06
            )
        if far == 0:
            for side in range(2):
                scale = jnp.broadcast_to(jnp.max(wide[side], axis=1, keepdims=True), wide.shape[1:]) + 1e-06
                inverse = 1.0 / scale
                for block in range(chunks * per):
                    at = slice(block * LANES, (block + 1) * LANES)
                    code_ref[side, :, at] = (fresh_ref[side, :, at] * inverse[block : block + 1]).astype(BF16)


def place_kernel(start, in_ref, *rest):
    out_ref, sem = rest[-2:]
    copy = pltpu.make_async_copy(in_ref, out_ref.at[0, pl.ds(start, in_ref.shape[0])], sem)
    copy.start()
    copy.wait()


ANY = pl.BlockSpec(memory_space=pl.ANY)


def whole(shape):
    return pl.BlockSpec(shape, lambda *_: (0,) * len(shape))


def shards(enter_fwd, enter_rev, cot_rev, gain, proj_down, proj_up, master, moment, second):
    tokens, width = enter_fwd.shape[1:]
    latent = proj_down.shape[2]
    experts = lax.axis_size("expert")
    depth = latent // experts
    blocks = width // LANES
    tiles = 4 if blocks % 4 == 0 else 2
    tile = width // tiles
    chunks = tiles
    part = width // chunks
    gains = gain.reshape(2, width)

    def streamed(array):
        return pltpu.with_memory_space_constraint(array, pltpu.HBM)

    pack_rows = 2 * latent + tokens + (latent // LANES + 1) * tokens
    packed = pl.pallas_call(
        lambda x1, x2, c2, down, up, *refs: latent_kernel(
            tiles, x1.at[0], down.at[0, 0], x2.at[0], c2.at[0], down.at[1, 0], up.at[1, 0], *refs
        ),
        in_specs=[ANY] * 6,
        out_specs=pl.BlockSpec(memory_space=pltpu.VMEM),
        out_shape=jax.ShapeDtypeStruct((pack_rows, LANES), F32),
        scratch_shapes=[
            pltpu.VMEM((tokens, width), BF16),
            pltpu.VMEM((latent, width), BF16),
            pltpu.VMEM((tokens, width), BF16),
            pltpu.VMEM((tokens, width), BF16),
            pltpu.VMEM((latent, width), BF16),
            pltpu.VMEM((latent, width), BF16),
            pltpu.VMEM((2, width), BF16),
            pltpu.SemaphoreType.DMA((6 * tiles + 1,)),
        ],
        compiler_params=ROOM,
        cost_estimate=cost(6 * tokens * latent * width, 6 * (tokens + latent) * width),
        name="latents",
    )(streamed(enter_fwd), streamed(enter_rev), streamed(cot_rev), streamed(proj_down), streamed(proj_up), streamed(gains))
    pair = halves_of_sum(packed, "dp")

    def leaving(start, count, *after):
        return pl.pallas_call(
            lambda *refs: leaving_kernel(start, *refs),
            grid=(1,),
            in_specs=[
                whole((pack_rows, LANES)),
                whole((pack_rows, LANES)),
                pl.BlockSpec((None, tokens, width), lambda i: (0, 0, 0)),
                pl.BlockSpec((None, None, latent, width), lambda i: (0, 0, 0, 0)),
            ]
            + [ANY] * len(after),
            out_specs=whole((count, width)),
            out_shape=jax.ShapeDtypeStruct((count, width), BF16),
            compiler_params=ROOM,
            cost_estimate=cost(2 * count * latent * width, 2 * (2 * count + latent) * width),
            name="leaving",
        )(*pair, enter_fwd, proj_up, *after)

    head = tokens * 5 // 8
    first_rows = leaving(0, head)
    left_head = shifted(first_rows, "pipe")

    def grads(chunk, *after):
        def columns():
            return pl.BlockSpec((None, tokens, part), lambda i: (0, 0, chunk))

        return pl.pallas_call(
            lambda *refs: grad_kernel(experts, *refs),
            grid=(1,),
            in_specs=[
                whole((pack_rows, LANES)),
                whole((pack_rows, LANES)),
                columns(),
                pl.BlockSpec((2, part), lambda i: (0, chunk)),
                columns(),
            ]
            + [ANY] * len(after),
            out_specs=[whole((2, depth, part))] * experts,
            out_shape=[jax.ShapeDtypeStruct((2, depth, part), BF16)] * experts,
            scratch_shapes=[pltpu.VMEM((2, latent, tokens), F32)],
            compiler_params=ROOM,
            cost_estimate=cost(4 * tokens * latent * part, 4 * (tokens + latent) * part),
            name="grads",
        )(*pair, enter_rev, gains, cot_rev, *after)

    def summed(own, others, *after):
        return pl.pallas_call(
            lambda *refs: share_kernel(experts, *refs),
            grid=(1,),
            in_specs=[whole((2, depth, part))] * experts + [ANY] * len(after),
            out_specs=whole((2, depth, part)),
            out_shape=jax.ShapeDtypeStruct((2, depth, part), BF16),
            compiler_params=ROOM,
            cost_estimate=cost(0, 4 * depth * part * (experts + 1)),
            name="share",
        )(own, *others, *after)

    shares, arrived, others = [], [], []
    for chunk in range(chunks):
        after = [first_rows, *shares[-2:-1], *([own] if chunk == 1 else [])]
        own, *pieces = grads(chunk, *after)
        others.append([exchange(piece, "expert", 1 + k) for k, piece in enumerate(pieces)])
        after = [left_head] if chunk == 1 else arrived[chunk - 2 : chunk - 1] if chunk else []
        shares.append(summed(own, others[-1], *after))
        arrived.append(mirrored(shares[-1], "pipe"))
    left_tail = shifted(leaving(head, tokens - head, shares[-1]), "pipe")

    def place(start, rows, *kept):
        return pl.pallas_call(
            lambda *refs: place_kernel(start, *refs),
            in_specs=[ANY] * (1 + len(kept)),
            out_specs=ANY,
            out_shape=jax.ShapeDtypeStruct((1, tokens, width), BF16),
            scratch_shapes=[pltpu.SemaphoreType.DMA],
            input_output_aliases={1 + k: k for k in range(len(kept))},
            compiler_params=ROOM,
            cost_estimate=cost(0, 4 * rows.shape[0] * width),
            name="place",
        )(rows, *kept)

    placed = place(0, left_head)

    fresh = peaks = None
    for chunk in range(chunks):
        state = pl.BlockSpec((2, None, depth, part), lambda i, c=chunk: (0, 0, 0, c))
        kept = () if fresh is None else (fresh, peaks)
        after = (placed,) if chunk == 2 else ()
        fresh, peaks = pl.pallas_call(
            update_kernel,
            grid=(1,),
            in_specs=[whole((2, depth, part)), state, state, state] + [ANY] * (len(kept) + len(after)),
            out_specs=[
                pl.BlockSpec((2, depth, part), lambda i, c=chunk: (0, 0, c)),
                pl.BlockSpec((None, 2, part // LANES, LANES), lambda i, c=chunk: (c, 0, 0, 0)),
            ],
            out_shape=[
                jax.ShapeDtypeStruct((2, depth, width), F32),
                jax.ShapeDtypeStruct((chunks, 2, part // LANES, LANES), F32),
            ],
            input_output_aliases={4 + k: k for k in range(len(kept))},
            compiler_params=ROOM,
            cost_estimate=cost(20 * 2 * depth * part, 14 * 2 * depth * part),
            name="update",
        )(arrived[chunk], master, moment, second, *kept, *after)

    group = LANES // depth
    for level in range(group.bit_length() - 1):
        peaks = jnp.maximum(peaks, exchange(peaks, "expert", 1 << level))
    peak_rows = [peaks] + [exchange(peaks, "expert", k * group) for k in range(1, experts // group)]
    coded, scales = pl.pallas_call(
        lambda *refs: code_kernel(group, *refs),
        grid=(1,),
        in_specs=[whole((2, depth, width))] + [whole(peaks.shape)] * len(peak_rows),
        out_specs=[
            pl.BlockSpec((2, None, depth, width), lambda i: (0, 0, 0, 0)),
            pl.BlockSpec((2, None, experts // group, blocks), lambda i: (0, 0, 0, 0)),
        ],
        out_shape=[
            jax.ShapeDtypeStruct((2, 1, depth, width), BF16),
            jax.ShapeDtypeStruct((2, 1, experts // group, blocks), F32),
        ],
        scratch_shapes=[pltpu.VMEM((2, LANES, LANES), F32)],
        compiler_params=ROOM,
        cost_estimate=cost(2 * 2 * depth * width, 6 * 2 * depth * width),
        name="codes",
    )(fresh, *peak_rows)

    return (place(head, left_tail, placed), coded, scales)


def solution(mesh):
    in_specs = (
        P("pipe", "expert", "dp"),
        P("pipe", "expert", "dp"),
        P("pipe", "expert", "dp"),
        P(None, "pipe", "dp"),
        P(None, "pipe", None, "dp"),
        P(None, "pipe", None, "dp"),
        P(None, "pipe", "expert", "dp"),
        P(None, "pipe", "expert", "dp"),
        P(None, "pipe", "expert", "dp"),
    )
    out_specs = (
        P("pipe", "expert", "dp"),
        P(None, "pipe", "expert", "dp"),
        P(None, "pipe", None, "dp"),
    )
    return jax.shard_map(shards, mesh=mesh, in_specs=in_specs, out_specs=out_specs, check_vma=False)
```

time: 90.2 us -> 87.3 us (0.968)
  waiting for transfers between devices: 56.3 us -> 44.5 us
  starting transfers between devices: 19.3 us -> 26.3 us
  Pallas kernels: 11.9 us -> 15.5 us
  local copies, waits for them, and re-layouts: 1.67 us -> 0.05 us
    ppermute x2 -> x4, waiting for transfers between devices: 27.7 us -> 16 us  [mirrored(): return lax.ppermute(block, axis, [(i, count - 1 - i) for i in range(count)])]
    ppermute x12 -> x15, starting transfers between devices: 12.6 us -> 17.7 us  [exchange(): return lax.ppermute(block, axis, [(i, i ^ offset) for i in range(count)])]
    ppermute x2 -> x4, starting transfers between devices: 3.22 us -> 5.37 us  [mirrored(): return lax.ppermute(block, axis, [(i, count - 1 - i) for i in range(count)])]
    unnamed x19 -> x18, local copies, waits for them, and re-layouts: 1.67 us -> 0.05 us
    pallas_call x7 -> x12, Pallas kernels: 3.48 us -> 4.91 us  [the longest x4 1.98 us: grads(): pl.pallas_call(lambda *refs: grad_kernel(experts, *refs), grid=(1,), in_s...]
    pallas_call x2 -> x4, Pallas kernels: 1.65 us -> 3.02 us  [shards(): pl.pallas_call(update_kernel, grid=(1,), in_specs=[whole((2, depth, part)...]
    ppermute x1 -> x2, starting transfers between devices: 3.49 us -> 3.24 us  [shifted(): lax.ppermute(block, axis, [(i, (i + 1) % count) for i in range(count)])]
    ppermute x12 -> x15, waiting for transfers between devices: 28.6 us -> 28.5 us  [exchange(): return lax.ppermute(block, axis, [(i, i ^ offset) for i in range(count)])]
  transfers between devices with their start and end apart: 15 -> 21, of which waited for: 12 -> 13; matrix products, arithmetic and copies ran while one was open for 0% -> 0% of each run, Pallas kernels for 2% -> 9%
where the time goes in v4:
time: 87.3 us; the launch traced here: 87.2 us
  waiting for transfers between devices  44.5 us (51%)
  starting transfers between devices  26.3 us (30%)
  Pallas kernels  15.5 us (18%)
    ppermute x15, waiting for transfers between devices, exchange(): return lax.ppermute(block, axis, [(i, i ^ offset) for i in range(count)])  28.5 us
    ppermute x15, starting transfers between devices, exchange(): return lax.ppermute(block, axis, [(i, i ^ offset) for i in range(count)])  17.7 us
    ppermute x4, waiting for transfers between devices, mirrored(): return lax.ppermute(block, axis, [(i, count - 1 - i) for i in range(count)])  16 us
    pallas_call x1, Pallas kernels, shards(): pl.pallas_call(lambda x1, x2, c2, down, up, *refs: latent_kernel(tiles, x...  6.41 us
    ppermute x4, starting transfers between devices, mirrored(): return lax.ppermute(block, axis, [(i, count - 1 - i) for i in range(count)])  5.37 us
    ppermute x2, starting transfers between devices, shifted(): lax.ppermute(block, axis, [(i, (i + 1) % count) for i in range(count)])  3.24 us
    pallas_call x4, Pallas kernels, shards(): pl.pallas_call(update_kernel, grid=(1,), in_specs=[whole((2, depth, part)...  3.02 us
    pallas_call x4, Pallas kernels, grads(): pl.pallas_call(lambda *refs: grad_kernel(experts, *refs), grid=(1,), in_s...  1.98 us
  transfers between devices with their start and end apart: 21, of which 13 were waited for; matrix products, arithmetic and copies ran while one was open for 0% of the time, Pallas kernels for 9%

profile of v4, /device:TPU:8, one launch (start us, length us, event | category | flops | bytes accessed | tf_op | source)
XLA Modules:
  0.0 87.2 jit_solution(4354022830516557487)
XLA Ops:
  0.7 6.4 %latents.1.refs_0_ = f32[1024,128]{1,0:T(8,128)S(1)} custom-call(bf16[1,128,3584]{2,1,0:T(8,128)(2,1)} %refs_2_.10, bf16[1,128,3584]{2,1,0:T(8,128)(2,1)} %refs_2_.11, bf16[1,128,3584]{2,1,0:T(8,128)(2,1)} %refs_4_.7, bf16[2,1,256,3584]{3,2,1,0:T(8,128)(2,1)} %down.1, bf16[2,1,256,3584]{3,2,1,0:T(8,128)(2,1)} %refs_3_.3, bf16[2,3584]{1,0:T(2,128)(2,1)} %bitcast.1), custom_call_target="tpu_custom_call" | custom-call | flops 704643072 | bytes 8257536 | tf_op jit(solution)/shard_map/latents/pallas_call | solution.py:229
  7.2 1.9 %collective-permute-done.refs_1_ = f32[1024,128]{1,0:T(8,128)S(1)} collective-permute-done((f32[1024,128]{1,0:T(8,128)S(1)}, f32[1024,128]{1,0:T(8,128)S(1)}, u32[]{:S(2)}, u32[]{:S(2)}) %collective-permute-start) | collective-permute-done | bytes 524320 | tf_op jit(solution)/shard_map/ppermute | solution.py:17
  9.6 1.6 %collective-permute-start.4 = (bf16[80,3584]{1,0:T(8,128)(2,1)S(1)}, bf16[80,3584]{1,0:T(8,128)(2,1)S(1)}, u32[]{:S(2)}, u32[]{:S(2)}) collective-permute-start(bf16[80,3584]{1,0:T(8,128)(2,1)S(1)} %leaving.2.refs_5_), channel_id=1, source_target_pairs={{0,8},{8,16},{16,24},{24,0},{1,9},{9,17},{17,25},{25,1},{2,10},{10... | collective-permute-start | bytes 1720328 | tf_op jit(solution)/shard_map/ppermute | solution.py:27
  12.2 1.6 %collective-permute-start.1 = (bf16[2,64,896]{2,1,0:T(8,128)(2,1)S(1)}, bf16[2,64,896]{2,1,0:T(8,128)(2,1)S(1)}, u32[]{:S(2)}, u32[]{:S(2)}) collective-permute-start(bf16[2,64,896]{2,1,0:T(8,128)(2,1)S(1)} %get-tuple-element.31), channel_id=1, source_target_pairs={{0,2},{2,0},{4,6},{6,4},{1,3},{3,1},{5,7},{7,5},{8,10},{10,8},{12,... | collective-permute-start | bytes 688136 | tf_op jit(solution)/shard_map/ppermute | solution.py:17
  13.8 1.5 %collective-permute-start.2 = (bf16[2,64,896]{2,1,0:T(8,128)(2,1)S(1)}, bf16[2,64,896]{2,1,0:T(8,128)(2,1)S(1)}, u32[]{:S(2)}, u32[]{:S(2)}) collective-permute-start(bf16[2,64,896]{2,1,0:T(8,128)(2,1)S(1)} %get-tuple-element.32), channel_id=1, source_target_pairs={{0,4},{2,6},{4,0},{6,2},{1,5},{3,7},{5,1},{7,3},{8,12},{10,14},{12... | collective-permute-start | bytes 688136 | tf_op jit(solution)/shard_map/ppermute | solution.py:17
  15.8 1.5 %collective-permute-start.11 = (bf16[2,64,896]{2,1,0:T(8,128)(2,1)S(1)}, bf16[2,64,896]{2,1,0:T(8,128)(2,1)S(1)}, u32[]{:S(2)}, u32[]{:S(2)}) collective-permute-start(bf16[2,64,896]{2,1,0:T(8,128)(2,1)S(1)} %get-tuple-element.38), channel_id=1, source_target_pairs={{0,2},{2,0},{4,6},{6,4},{1,3},{3,1},{5,7},{7,5},{8,10},{10,8},{12,... | collective-permute-start | bytes 688136 | tf_op jit(solution)/shard_map/ppermute | solution.py:17
  17.2 3.5 %collective-permute-done.1.refs_1_ = bf16[2,64,896]{2,1,0:T(8,128)(2,1)S(1)} collective-permute-done((bf16[2,64,896]{2,1,0:T(8,128)(2,1)S(1)}, bf16[2,64,896]{2,1,0:T(8,128)(2,1)S(1)}, u32[]{:S(2)}, u32[]{:S(2)}) %collective-permute-start.1) | collective-permute-done | bytes 229408 | tf_op jit(solution)/shard_map/ppermute | solution.py:17
  20.7 1.5 %collective-permute-start.12 = (bf16[2,64,896]{2,1,0:T(8,128)(2,1)S(1)}, bf16[2,64,896]{2,1,0:T(8,128)(2,1)S(1)}, u32[]{:S(2)}, u32[]{:S(2)}) collective-permute-start(bf16[2,64,896]{2,1,0:T(8,128)(2,1)S(1)} %get-tuple-element.39), channel_id=1, source_target_pairs={{0,4},{2,6},{4,0},{6,2},{1,5},{3,7},{5,1},{7,3},{8,12},{10,14},{12... | collective-permute-start | bytes 688136 | tf_op jit(solution)/shard_map/ppermute | solution.py:17
  22.3 3.6 %collective-permute-done.2.refs_2_ = bf16[2,64,896]{2,1,0:T(8,128)(2,1)S(1)} collective-permute-done((bf16[2,64,896]{2,1,0:T(8,128)(2,1)S(1)}, bf16[2,64,896]{2,1,0:T(8,128)(2,1)S(1)}, u32[]{:S(2)}, u32[]{:S(2)}) %collective-permute-start.2) | collective-permute-done | bytes 229408 | tf_op jit(solution)/shard_map/ppermute | solution.py:17
  25.9 0.8 collective-permute-start.13
  26.8 1.6 %collective-permute-start.8 = (bf16[2,64,896]{2,1,0:T(8,128)(2,1)S(1)}, bf16[2,64,896]{2,1,0:T(8,128)(2,1)S(1)}, u32[]{:S(2)}, u32[]{:S(2)}) collective-permute-start(bf16[2,64,896]{2,1,0:T(8,128)(2,1)S(1)} %share.4.refs_6_), channel_id=1, source_target_pairs={{0,24},{8,16},{16,8},{24,0},{1,25},{9,17},{17,9},{25,1},{2,26},{10... | collective-permute-start | bytes 688136 | tf_op jit(solution)/shard_map/ppermute | solution.py:22
  28.9 3.2 %collective-permute-start.5 = (bf16[2,64,896]{2,1,0:T(8,128)(2,1)S(1)}, bf16[2,64,896]{2,1,0:T(8,128)(2,1)S(1)}, u32[]{:S(2)}, u32[]{:S(2)}) collective-permute-start(bf16[2,64,896]{2,1,0:T(8,128)(2,1)S(1)} %get-tuple-element.35), channel_id=1, source_target_pairs={{0,2},{2,0},{4,6},{6,4},{1,3},{3,1},{5,7},{7,5},{8,10},{10,8},{12,... | collective-permute-start | bytes 688136 | tf_op jit(solution)/shard_map/ppermute | solution.py:17
  32.2 3.4 %collective-permute-done.12.refs_2_ = bf16[2,64,896]{2,1,0:T(8,128)(2,1)S(1)} collective-permute-done((bf16[2,64,896]{2,1,0:T(8,128)(2,1)S(1)}, bf16[2,64,896]{2,1,0:T(8,128)(2,1)S(1)}, u32[]{:S(2)}, u32[]{:S(2)}) %collective-permute-start.12) | collective-permute-done | bytes 229408 | tf_op jit(solution)/shard_map/ppermute | solution.py:17
  35.6 0.8 collective-permute-start.7
  36.7 1.6 %collective-permute-start.17 = (bf16[2,64,896]{2,1,0:T(8,128)(2,1)S(1)}, bf16[2,64,896]{2,1,0:T(8,128)(2,1)S(1)}, u32[]{:S(2)}, u32[]{:S(2)}) collective-permute-start(bf16[2,64,896]{2,1,0:T(8,128)(2,1)S(1)} %share.6.refs_6_), channel_id=1, source_target_pairs={{0,24},{8,16},{16,8},{24,0},{1,25},{9,17},{17,9},{25,1},{2,26},{10... | collective-permute-start | bytes 688136 | tf_op jit(solution)/shard_map/ppermute | solution.py:22
  38.8 3.2 %collective-permute-start.14 = (bf16[2,64,896]{2,1,0:T(8,128)(2,1)S(1)}, bf16[2,64,896]{2,1,0:T(8,128)(2,1)S(1)}, u32[]{:S(2)}, u32[]{:S(2)}) collective-permute-start(bf16[2,64,896]{2,1,0:T(8,128)(2,1)S(1)} %get-tuple-element.42), channel_id=1, source_target_pairs={{0,2},{2,0},{4,6},{6,4},{1,3},{3,1},{5,7},{7,5},{8,10},{10,8},{12,... | collective-permute-start | bytes 688136 | tf_op jit(solution)/shard_map/ppermute | solution.py:17
  42.0 0.8 collective-permute-start.15
  42.8 2.5 %collective-permute-done.6.refs_2_ = bf16[2,64,896]{2,1,0:T(8,128)(2,1)S(1)} collective-permute-done((bf16[2,64,896]{2,1,0:T(8,128)(2,1)S(1)}, bf16[2,64,896]{2,1,0:T(8,128)(2,1)S(1)}, u32[]{:S(2)}, u32[]{:S(2)}) %collective-permute-start.6) | collective-permute-done | bytes 229408 | tf_op jit(solution)/shard_map/ppermute | solution.py:17
  47.0 1.6 %collective-permute-start.9 = (bf16[48,3584]{1,0:T(8,128)(2,1)S(1)}, bf16[48,3584]{1,0:T(8,128)(2,1)S(1)}, u32[]{:S(2)}, u32[]{:S(2)}) collective-permute-start(bf16[48,3584]{1,0:T(8,128)(2,1)S(1)} %leaving.3), channel_id=1, source_target_pairs={{0,8},{8,16},{16,24},{24,0},{1,9},{9,17},{17,25},{25,1},{2,10},{10... | collective-permute-start | bytes 1032200 | tf_op jit(solution)/shard_map/ppermute | solution.py:27
  48.6 2.5 %collective-permute-done.14.refs_1_ = bf16[2,64,896]{2,1,0:T(8,128)(2,1)S(1)} collective-permute-done((bf16[2,64,896]{2,1,0:T(8,128)(2,1)S(1)}, bf16[2,64,896]{2,1,0:T(8,128)(2,1)S(1)}, u32[]{:S(2)}, u32[]{:S(2)}) %collective-permute-start.14) | collective-permute-done | bytes 229408 | tf_op jit(solution)/shard_map/ppermute | solution.py:17
  51.2 4.1 %collective-permute-done.15.refs_2_ = bf16[2,64,896]{2,1,0:T(8,128)(2,1)S(1)} collective-permute-done((bf16[2,64,896]{2,1,0:T(8,128)(2,1)S(1)}, bf16[2,64,896]{2,1,0:T(8,128)(2,1)S(1)}, u32[]{:S(2)}, u32[]{:S(2)}) %collective-permute-start.15) | collective-permute-done | bytes 229408 | tf_op jit(solution)/shard_map/ppermute | solution.py:17
  55.4 1.6 %collective-permute-start.18 = (bf16[2,64,896]{2,1,0:T(8,128)(2,1)S(1)}, bf16[2,64,896]{2,1,0:T(8,128)(2,1)S(1)}, u32[]{:S(2)}, u32[]{:S(2)}) collective-permute-start(bf16[2,64,896]{2,1,0:T(8,128)(2,1)S(1)} %share.7), channel_id=1, source_target_pairs={{0,24},{8,16},{16,8},{24,0},{1,25},{9,17},{17,9},{25,1},{2,26},{10... | collective-permute-start | bytes 688136 | tf_op jit(solution)/shard_map/ppermute | solution.py:22
  57.5 0.8 update.4
  58.2 0.8 place.2.refs_1_.rest_2_
  59.1 0.8 update.5
  59.8 12.8 %collective-permute-done.18.share_ref = bf16[2,64,896]{2,1,0:T(8,128)(2,1)S(1)} collective-permute-done((bf16[2,64,896]{2,1,0:T(8,128)(2,1)S(1)}, bf16[2,64,896]{2,1,0:T(8,128)(2,1)S(1)}, u32[]{:S(2)}, u32[]{:S(2)}) %collective-permute-start.18) | collective-permute-done | bytes 229408 | tf_op jit(solution)/shard_map/ppermute | solution.py:22
  72.6 0.8 update.6
  73.4 3.2 %collective-permute-done.10.share_ref = bf16[2,64,896]{2,1,0:T(8,128)(2,1)S(1)} collective-permute-done((bf16[2,64,896]{2,1,0:T(8,128)(2,1)S(1)}, bf16[2,64,896]{2,1,0:T(8,128)(2,1)S(1)}, u32[]{:S(2)}, u32[]{:S(2)}) %collective-permute-start.10) | collective-permute-done | bytes 229408 | tf_op jit(solution)/shard_map/ppermute | solution.py:22
  77.3 1.5 %collective-permute-start.19 = (f32[4,2,7,128]{3,2,1,0:T(8,128)S(1)}, f32[4,2,7,128]{3,2,1,0:T(8,128)S(1)}, u32[]{:S(2)}, u32[]{:S(2)}) collective-permute-start(f32[4,2,7,128]{3,2,1,0:T(8,128)S(1)} %get-tuple-element.52), channel_id=1, source_target_pairs={{0,2},{2,0},{4,6},{6,4},{1,3},{3,1},{5,7},{7,5},{8,10},{10,8},{12,... | collective-permute-start | bytes 86024 | tf_op jit(solution)/shard_map/ppermute | solution.py:17
  78.9 2.5 %collective-permute-done.19 = f32[4,2,7,128]{3,2,1,0:T(8,128)S(1)} collective-permute-done((f32[4,2,7,128]{3,2,1,0:T(8,128)S(1)}, f32[4,2,7,128]{3,2,1,0:T(8,128)S(1)}, u32[]{:S(2)}, u32[]{:S(2)}) %collective-permute-start.19) | collective-permute-done | bytes 28704 | tf_op jit(solution)/shard_map/ppermute | solution.py:17
  81.3 3.9 %collective-permute-done.20.refs_2_ = f32[4,2,7,128]{3,2,1,0:T(8,128)S(1)} collective-permute-done((f32[4,2,7,128]{3,2,1,0:T(8,128)S(1)}, f32[4,2,7,128]{3,2,1,0:T(8,128)S(1)}, u32[]{:S(2)}, u32[]{:S(2)}) %collective-permute-start.20) | collective-permute-done | bytes 28704 | tf_op jit(solution)/shard_map/ppermute | solution.py:17
  85.2 1.2 %codes.1 = (bf16[2,1,64,3584]{3,2,1,0:T(8,128)(2,1)}, f32[2,1,2,28]{3,2,1,0:T(2,128)}) custom-call(f32[2,64,3584]{2,1,0:T(8,128)S(1)} %get-tuple-element.51.refs_0_, f32[4,2,7,128]{3,2,1,0:T(8,128)S(1)} %max.3.refs_1_, f32[4,2,7,128]{3,2,1,0:T(8,128)S(1)} %collective-permute-done.20.refs_2_), custom_call_target="tpu_custom_call" | custom-call | flops 917504 | bytes 2752512 | tf_op jit(solution)/shard_map/codes/pallas_call | solution.py:361
  (47 shorter events, 7.2 us)
Async XLA Ops:
  0.6 8.4 %copy-start = (bf16[2,1,256,3584]{3,2,1,0:T(8,128)(2,1)S(1)}, bf16[2,1,256,3584]{3,2,1,0:T(8,128)(2,1)}, u32[]{:S(2)}) copy-start(bf16[2,1,256,3584]{3,2,1,0:T(8,128)(2,1)} %refs_3_.3) | copy-start | bytes 11010052
  0.6 8.4 %copy-start.6 = (bf16[1,128,3584]{2,1,0:T(8,128)(2,1)S(1)}, bf16[1,128,3584]{2,1,0:T(8,128)(2,1)}, u32[]{:S(2)}) copy-start(bf16[1,128,3584]{2,1,0:T(8,128)(2,1)} %refs_2_.10) | copy-start | bytes 2752516
  7.1 4.1 %copy-start.2 = (bf16[1,128,3584]{2,1,0:T(8,128)(2,1)S(1)}, bf16[1,128,3584]{2,1,0:T(8,128)(2,1)}, u32[]{:S(2)}) copy-start(bf16[1,128,3584]{2,1,0:T(8,128)(2,1)} %refs_2_.11) | copy-start | bytes 2752516
  7.1 4.1 %copy-start.3 = (bf16[1,128,3584]{2,1,0:T(8,128)(2,1)S(1)}, bf16[1,128,3584]{2,1,0:T(8,128)(2,1)}, u32[]{:S(2)}) copy-start(bf16[1,128,3584]{2,1,0:T(8,128)(2,1)} %refs_4_.7) | copy-start | bytes 2752516
  7.1 4.1 %copy-start.8 = (bf16[2,1,3584]{2,0,1:T(2,128)(2,1)S(1)}, bf16[2,1,3584]{2,0,1:T(2,128)(2,1)}, u32[]{:S(2)}) copy-start(bf16[2,1,3584]{2,0,1:T(2,128)(2,1)} %param.12) | copy-start | bytes 43012
  7.1 2.0 %collective-permute-start = (f32[1024,128]{1,0:T(8,128)S(1)}, f32[1024,128]{1,0:T(8,128)S(1)}, u32[]{:S(2)}, u32[]{:S(2)}) collective-permute-start(f32[1024,128]{1,0:T(8,128)S(1)} %latents.1.refs_0_), channel_id=1, source_target_pairs={{0,1},{1,0},{2,3},{3,2},{4,5},{5,4},{6,7},{7,6},{8,9},{9,8},{10,11... | collective-permute-start | bytes 1572872 | tf_op jit(solution)/shard_map/ppermute | solution.py:17
  9.6 17.1 %collective-permute-start.4 = (bf16[80,3584]{1,0:T(8,128)(2,1)S(1)}, bf16[80,3584]{1,0:T(8,128)(2,1)S(1)}, u32[]{:S(2)}, u32[]{:S(2)}) collective-permute-start(bf16[80,3584]{1,0:T(8,128)(2,1)S(1)} %leaving.2.refs_5_), channel_id=1, source_target_pairs={{0,8},{8,16},{16,24},{24,0},{1,9},{9,17},{17,25},{25,1},{2,10},{10... | collective-permute-start | bytes 1720328 | tf_op jit(solution)/shard_map/ppermute | solution.py:27
  12.2 8.6 %collective-permute-start.1 = (bf16[2,64,896]{2,1,0:T(8,128)(2,1)S(1)}, bf16[2,64,896]{2,1,0:T(8,128)(2,1)S(1)}, u32[]{:S(2)}, u32[]{:S(2)}) collective-permute-start(bf16[2,64,896]{2,1,0:T(8,128)(2,1)S(1)} %get-tuple-element.31), channel_id=1, source_target_pairs={{0,2},{2,0},{4,6},{6,4},{1,3},{3,1},{5,7},{7,5},{8,10},{10,8},{12,... | collective-permute-start | bytes 688136 | tf_op jit(solution)/shard_map/ppermute | solution.py:17
  13.8 12.1 %collective-permute-start.2 = (bf16[2,64,896]{2,1,0:T(8,128)(2,1)S(1)}, bf16[2,64,896]{2,1,0:T(8,128)(2,1)S(1)}, u32[]{:S(2)}, u32[]{:S(2)}) collective-permute-start(bf16[2,64,896]{2,1,0:T(8,128)(2,1)S(1)} %get-tuple-element.32), channel_id=1, source_target_pairs={{0,4},{2,6},{4,0},{6,2},{1,5},{3,7},{5,1},{7,3},{8,12},{10,14},{12... | collective-permute-start | bytes 688136 | tf_op jit(solution)/shard_map/ppermute | solution.py:17
  15.3 11.4 %collective-permute-start.3 = (bf16[2,64,896]{2,1,0:T(8,128)(2,1)S(1)}, bf16[2,64,896]{2,1,0:T(8,128)(2,1)S(1)}, u32[]{:S(2)}, u32[]{:S(2)}) collective-permute-start(bf16[2,64,896]{2,1,0:T(8,128)(2,1)S(1)} %get-tuple-element.33), channel_id=1, source_target_pairs={{0,6},{2,4},{4,2},{6,0},{1,7},{3,5},{5,3},{7,1},{8,14},{10,12},{12... | collective-permute-start | bytes 688136 | tf_op jit(solution)/shard_map/ppermute | solution.py:17
  15.8 16.4 %collective-permute-start.11 = (bf16[2,64,896]{2,1,0:T(8,128)(2,1)S(1)}, bf16[2,64,896]{2,1,0:T(8,128)(2,1)S(1)}, u32[]{:S(2)}, u32[]{:S(2)}) collective-permute-start(bf16[2,64,896]{2,1,0:T(8,128)(2,1)S(1)} %get-tuple-element.38), channel_id=1, source_target_pairs={{0,2},{2,0},{4,6},{6,4},{1,3},{3,1},{5,7},{7,5},{8,10},{10,8},{12,... | collective-permute-start | bytes 688136 | tf_op jit(solution)/shard_map/ppermute | solution.py:17
  20.7 14.8 %collective-permute-start.12 = (bf16[2,64,896]{2,1,0:T(8,128)(2,1)S(1)}, bf16[2,64,896]{2,1,0:T(8,128)(2,1)S(1)}, u32[]{:S(2)}, u32[]{:S(2)}) collective-permute-start(bf16[2,64,896]{2,1,0:T(8,128)(2,1)S(1)} %get-tuple-element.39), channel_id=1, source_target_pairs={{0,4},{2,6},{4,0},{6,2},{1,5},{3,7},{5,1},{7,3},{8,12},{10,14},{12... | collective-permute-start | bytes 688136 | tf_op jit(solution)/shard_map/ppermute | solution.py:17
  25.9 10.7 %collective-permute-start.13 = (bf16[2,64,896]{2,1,0:T(8,128)(2,1)S(1)}, bf16[2,64,896]{2,1,0:T(8,128)(2,1)S(1)}, u32[]{:S(2)}, u32[]{:S(2)}) collective-permute-start(bf16[2,64,896]{2,1,0:T(8,128)(2,1)S(1)} %get-tuple-element.40), channel_id=1, source_target_pairs={{0,6},{2,4},{4,2},{6,0},{1,7},{3,5},{5,3},{7,1},{8,14},{10,12},{12... | collective-permute-start | bytes 688136 | tf_op jit(solution)/shard_map/ppermute | solution.py:17
  26.8 12.0 %collective-permute-start.8 = (bf16[2,64,896]{2,1,0:T(8,128)(2,1)S(1)}, bf16[2,64,896]{2,1,0:T(8,128)(2,1)S(1)}, u32[]{:S(2)}, u32[]{:S(2)}) collective-permute-start(bf16[2,64,896]{2,1,0:T(8,128)(2,1)S(1)} %share.4.refs_6_), channel_id=1, source_target_pairs={{0,24},{8,16},{16,8},{24,0},{1,25},{9,17},{17,9},{25,1},{2,26},{10... | collective-permute-start | bytes 688136 | tf_op jit(solution)/shard_map/ppermute | solution.py:22
  28.9 13.1 %collective-permute-start.5 = (bf16[2,64,896]{2,1,0:T(8,128)(2,1)S(1)}, bf16[2,64,896]{2,1,0:T(8,128)(2,1)S(1)}, u32[]{:S(2)}, u32[]{:S(2)}) collective-permute-start(bf16[2,64,896]{2,1,0:T(8,128)(2,1)S(1)} %get-tuple-element.35), channel_id=1, source_target_pairs={{0,2},{2,0},{4,6},{6,4},{1,3},{3,1},{5,7},{7,5},{8,10},{10,8},{12,... | collective-permute-start | bytes 688136 | tf_op jit(solution)/shard_map/ppermute | solution.py:17
  32.2 13.2 %collective-permute-start.6 = (bf16[2,64,896]{2,1,0:T(8,128)(2,1)S(1)}, bf16[2,64,896]{2,1,0:T(8,128)(2,1)S(1)}, u32[]{:S(2)}, u32[]{:S(2)}) collective-permute-start(bf16[2,64,896]{2,1,0:T(8,128)(2,1)S(1)} %get-tuple-element.36), channel_id=1, source_target_pairs={{0,4},{2,6},{4,0},{6,2},{1,5},{3,7},{5,1},{7,3},{8,12},{10,14},{12... | collective-permute-start | bytes 688136 | tf_op jit(solution)/shard_map/ppermute | solution.py:17
  35.6 10.9 %collective-permute-start.7 = (bf16[2,64,896]{2,1,0:T(8,128)(2,1)S(1)}, bf16[2,64,896]{2,1,0:T(8,128)(2,1)S(1)}, u32[]{:S(2)}, u32[]{:S(2)}) collective-permute-start(bf16[2,64,896]{2,1,0:T(8,128)(2,1)S(1)} %get-tuple-element.37), channel_id=1, source_target_pairs={{0,6},{2,4},{4,2},{6,0},{1,7},{3,5},{5,3},{7,1},{8,14},{10,12},{12... | collective-permute-start | bytes 688136 | tf_op jit(solution)/shard_map/ppermute | solution.py:17
  36.7 12.0 %collective-permute-start.17 = (bf16[2,64,896]{2,1,0:T(8,128)(2,1)S(1)}, bf16[2,64,896]{2,1,0:T(8,128)(2,1)S(1)}, u32[]{:S(2)}, u32[]{:S(2)}) collective-permute-start(bf16[2,64,896]{2,1,0:T(8,128)(2,1)S(1)} %share.6.refs_6_), channel_id=1, source_target_pairs={{0,24},{8,16},{16,8},{24,0},{1,25},{9,17},{17,9},{25,1},{2,26},{10... | collective-permute-start | bytes 688136 | tf_op jit(solution)/shard_map/ppermute | solution.py:22
  38.8 12.4 %collective-permute-start.14 = (bf16[2,64,896]{2,1,0:T(8,128)(2,1)S(1)}, bf16[2,64,896]{2,1,0:T(8,128)(2,1)S(1)}, u32[]{:S(2)}, u32[]{:S(2)}) collective-permute-start(bf16[2,64,896]{2,1,0:T(8,128)(2,1)S(1)} %get-tuple-element.42), channel_id=1, source_target_pairs={{0,2},{2,0},{4,6},{6,4},{1,3},{3,1},{5,7},{7,5},{8,10},{10,8},{12,... | collective-permute-start | bytes 688136 | tf_op jit(solution)/shard_map/ppermute | solution.py:17
  42.0 13.2 %collective-permute-start.15 = (bf16[2,64,896]{2,1,0:T(8,128)(2,1)S(1)}, bf16[2,64,896]{2,1,0:T(8,128)(2,1)S(1)}, u32[]{:S(2)}, u32[]{:S(2)}) collective-permute-start(bf16[2,64,896]{2,1,0:T(8,128)(2,1)S(1)} %get-tuple-element.43), channel_id=1, source_target_pairs={{0,4},{2,6},{4,0},{6,2},{1,5},{3,7},{5,1},{7,3},{8,12},{10,14},{12... | collective-permute-start | bytes 688136 | tf_op jit(solution)/shard_map/ppermute | solution.py:17
  45.4 9.9 %collective-permute-start.16 = (bf16[2,64,896]{2,1,0:T(8,128)(2,1)S(1)}, bf16[2,64,896]{2,1,0:T(8,128)(2,1)S(1)}, u32[]{:S(2)}, u32[]{:S(2)}) collective-permute-start(bf16[2,64,896]{2,1,0:T(8,128)(2,1)S(1)} %get-tuple-element.44), channel_id=1, source_target_pairs={{0,6},{2,4},{4,2},{6,0},{1,7},{3,5},{5,3},{7,1},{8,14},{10,12},{12... | collective-permute-start | bytes 688136 | tf_op jit(solution)/shard_map/ppermute | solution.py:17
  46.5 10.9 %copy-start.1 = (f32[2,1,64,3584]{3,2,1,0:T(8,128)S(1)}, f32[2,1,64,3584]{3,2,1,0:T(8,128)}, u32[]{:S(2)}) copy-start(f32[2,1,64,3584]{3,2,1,0:T(8,128)} %master_ref.7) | copy-start | bytes 5505028
  46.6 10.9 %copy-start.5 = (bf16[2,1,64,3584]{3,2,1,0:T(8,128)(2,1)S(1)}, bf16[2,1,64,3584]{3,2,1,0:T(8,128)(2,1)}, u32[]{:S(2)}) copy-start(bf16[2,1,64,3584]{3,2,1,0:T(8,128)(2,1)} %second_ref.7) | copy-start | bytes 2752516
  47.0 10.5 %copy-start.4 = (bf16[2,1,64,3584]{3,2,1,0:T(8,128)(2,1)S(1)}, bf16[2,1,64,3584]{3,2,1,0:T(8,128)(2,1)}, u32[]{:S(2)}) copy-start(bf16[2,1,64,3584]{3,2,1,0:T(8,128)(2,1)} %moment_ref.7) | copy-start | bytes 2752516
  47.0 39.4 %collective-permute-start.9 = (bf16[48,3584]{1,0:T(8,128)(2,1)S(1)}, bf16[48,3584]{1,0:T(8,128)(2,1)S(1)}, u32[]{:S(2)}, u32[]{:S(2)}) collective-permute-start(bf16[48,3584]{1,0:T(8,128)(2,1)S(1)} %leaving.3), channel_id=1, source_target_pairs={{0,8},{8,16},{16,24},{24,0},{1,9},{9,17},{17,25},{25,1},{2,10},{10... | collective-permute-start | bytes 1032200 | tf_op jit(solution)/shard_map/ppermute | solution.py:27
  55.4 17.2 %collective-permute-start.18 = (bf16[2,64,896]{2,1,0:T(8,128)(2,1)S(1)}, bf16[2,64,896]{2,1,0:T(8,128)(2,1)S(1)}, u32[]{:S(2)}, u32[]{:S(2)}) collective-permute-start(bf16[2,64,896]{2,1,0:T(8,128)(2,1)S(1)} %share.7), channel_id=1, source_target_pairs={{0,24},{8,16},{16,8},{24,0},{1,25},{9,17},{17,9},{25,1},{2,26},{10... | collective-permute-start | bytes 688136 | tf_op jit(solution)/shard_map/ppermute | solution.py:22
  57.0 19.6 %collective-permute-start.10 = (bf16[2,64,896]{2,1,0:T(8,128)(2,1)S(1)}, bf16[2,64,896]{2,1,0:T(8,128)(2,1)S(1)}, u32[]{:S(2)}, u32[]{:S(2)}) collective-permute-start(bf16[2,64,896]{2,1,0:T(8,128)(2,1)S(1)} %share.5.refs_4_), channel_id=1, source_target_pairs={{0,24},{8,16},{16,8},{24,0},{1,25},{9,17},{17,9},{25,1},{2,26},{10... | collective-permute-start | bytes 688136 | tf_op jit(solution)/shard_map/ppermute | solution.py:22
  59.1 13.6 %copy-start.7 = (bf16[1,128,3584]{2,1,0:T(8,128)(2,1)S(1)}, bf16[1,128,3584]{2,1,0:T(8,128)(2,1)}, u32[]{:S(2)}) copy-start(bf16[1,128,3584]{2,1,0:T(8,128)(2,1)} %place.2.refs_1_.rest_2_) | copy-start | bytes 2752516
  77.3 4.0 %collective-permute-start.19 = (f32[4,2,7,128]{3,2,1,0:T(8,128)S(1)}, f32[4,2,7,128]{3,2,1,0:T(8,128)S(1)}, u32[]{:S(2)}, u32[]{:S(2)}) collective-permute-start(f32[4,2,7,128]{3,2,1,0:T(8,128)S(1)} %get-tuple-element.52), channel_id=1, source_target_pairs={{0,2},{2,0},{4,6},{6,4},{1,3},{3,1},{5,7},{7,5},{8,10},{10,8},{12,... | collective-permute-start | bytes 86024 | tf_op jit(solution)/shard_map/ppermute | solution.py:17
  81.3 3.9 %collective-permute-start.20 = (f32[4,2,7,128]{3,2,1,0:T(8,128)S(1)}, f32[4,2,7,128]{3,2,1,0:T(8,128)S(1)}, u32[]{:S(2)}, u32[]{:S(2)}) collective-permute-start(f32[4,2,7,128]{3,2,1,0:T(8,128)S(1)} %max.3.refs_1_), channel_id=1, source_target_pairs={{0,4},{2,6},{4,0},{6,2},{1,5},{3,7},{5,1},{7,3},{8,12},{10,14},{12... | collective-permute-start | bytes 86024 | tf_op jit(solution)/shard_map/ppermute | solution.py:17

commit v5 on v4

v5 whole, which is shorter than its diff:
```python
import jax
import jax.numpy as jnp
from jax import lax
from jax.experimental import pallas as pl
from jax.experimental.pallas import tpu as pltpu
from jax.sharding import PartitionSpec as P

D = 7168
LANES = 128
F32 = jnp.float32
BF16 = jnp.bfloat16
BOTH_LAST = (((1,), (1,)), ((), ()))
ROOM = pltpu.CompilerParams(vmem_limit_bytes=16 << 20)
ANY = pl.BlockSpec(memory_space=pl.ANY)
VMEM = pl.BlockSpec(memory_space=pltpu.VMEM)


def exchange(block, axis, offset):
    count = lax.axis_size(axis)
    return lax.ppermute(block, axis, [(i, i ^ offset) for i in range(count)])


def mirrored(block, axis):
    count = lax.axis_size(axis)
    return lax.ppermute(block, axis, [(i, count - 1 - i) for i in range(count)])


def turned(block, axis):
    count = lax.axis_size(axis)
    return lax.ppermute(block, axis, [(i, (i + 1) % count) for i in range(count)])


def halves_of_sum(block, axis):
    count = lax.axis_size(axis)
    offset = 1
    while True:
        other = exchange(block, axis, offset)
        offset *= 2
        if offset >= count:
            return block, other
        block = block + other


def shape(dims, dtype):
    return jax.ShapeDtypeStruct(dims, dtype)


def call(kernel, name, outs, *operands, read, scratch=(), flops=0):
    many = isinstance(outs, list)
    nbytes = sum(o.size * o.dtype.itemsize for o in operands[:read])
    return pl.pallas_call(
        kernel,
        in_specs=[VMEM] * read + [ANY] * (len(operands) - read),
        out_specs=[VMEM] * len(outs) if many else VMEM,
        out_shape=outs,
        scratch_shapes=list(scratch),
        compiler_params=ROOM,
        cost_estimate=pl.CostEstimate(flops=flops, bytes_accessed=nbytes, transcendentals=0),
        name=name,
    )(*operands)


def folded_squares(rows):
    tokens, width = rows.shape
    total = jnp.zeros((tokens, LANES), F32)
    for at in range(0, width, LANES):
        part = rows[:, at : at + LANES]
        total = total + part * part
    return total


def latent_kernel(tiles, x1, x2, c2, down, up, gain, out_ref, vx1, scaled2, vc2, va1, vx2, va2, vb2, vgain, sems):
    tokens, width = vx1.shape
    latent = va1.shape[0]
    tile = width // tiles
    pairs = (
        ((x1.at[0], vx1), (down.at[0, 0], va1)),
        ((x2.at[0], vx2), (down.at[1, 0], va2)),
        ((c2.at[0], vc2), (up.at[1, 0], vb2)),
    )
    jobs = [[pltpu.make_async_copy(gain, vgain, sems.at[6 * tiles])]]
    for pair in pairs:
        for at in range(tiles):
            cols = pl.ds(at * tile, tile)
            sem = 2 * (len(jobs) - 1)
            jobs.append(
                [pltpu.make_async_copy(s.at[:, cols], d.at[:, cols], sems.at[sem + k]) for k, (s, d) in enumerate(pair)]
            )
    for job in jobs:
        for copy in job:
            copy.start()

    def arrive(at):
        for copy in jobs[at]:
            copy.wait()

    arrive(0)
    gains = vgain[...].astype(F32)

    def product(job):
        total = None
        squares = jnp.zeros((tokens, LANES), F32)
        for at in range(tiles):
            arrive(1 + job * tiles + at)
            cols = slice(at * tile, (at + 1) * tile)
            if job < 2:
                rows = (vx1, vx2)[job][:, cols].astype(F32)
                squares += folded_squares(rows)
                right = (rows * gains[job : job + 1, cols]).astype(BF16)
            if job == 0:
                left, right = right, va1[:, cols]
            elif job == 1:
                scaled2[:, cols] = right
                left = va2[:, cols]
            else:
                left, right = vb2[:, cols], vc2[:, cols]
            term = lax.dot_general(left, right, BOTH_LAST, preferred_element_type=F32)
            total = term if total is None else total + term
        return total, squares

    raw, squares = product(0)
    base = 2 * latent + tokens
    for at in range(latent // LANES):
        out_ref[base + at * tokens : base + (at + 1) * tokens] = raw[:, at * LANES : (at + 1) * LANES]
    out_ref[base + (latent // LANES) * tokens :] = squares
    raw, squares = product(1)
    out_ref[:latent] = raw
    out_ref[2 * latent : base] = squares
    out_ref[latent : 2 * latent], _ = product(2)


def fetch_kernel(in_ref, *rest):
    out_ref, sem = rest[-2:]
    copy = pltpu.make_async_copy(in_ref.at[0, 0], out_ref, sem)
    copy.start()
    copy.wait()


def leaving_kernel(start, own_ref, other_ref, x_ref, b_ref, *rest):
    out_ref = rest[-1]
    latent = b_ref.shape[0]
    count, width = out_ref.shape
    tokens = x_ref.shape[0]

    def summed(at):
        rows = slice(at + start, at + start + count)
        return own_ref[rows] + other_ref[rows]

    base = own_ref.shape[0] - tokens
    rscale = lax.rsqrt(jnp.sum(summed(base), axis=1, keepdims=True) / D + 1e-06)
    base -= (latent // LANES) * tokens
    hidden = jnp.concatenate([summed(base + at * tokens) * rscale for at in range(latent // LANES)], axis=1).astype(BF16)
    last = lax.axis_index("pipe") == lax.axis_size("pipe") - 1
    step = width // (4 if width % (4 * LANES) == 0 else 2)
    for at in range(0, width, step):
        cols = slice(at, at + step)
        rows = x_ref[start : start + count, cols].astype(F32)
        rows += jnp.dot(hidden, b_ref[:, cols], preferred_element_type=F32)
        out_ref[:, cols] = jnp.where(last, 0.0, rows).astype(BF16)


def grad_kernel(experts, start, own_ref, other_ref, x_ref, c_ref, *rest):
    outs, rows_ref = rest[-1 - experts : -1], rest[-1]
    latent = rows_ref.shape[1]
    depth = latent // experts
    cols = slice(start, start + outs[0].shape[2])
    me = lax.axis_index("expert")
    squares = own_ref[2 * latent : 2 * latent + LANES] + other_ref[2 * latent : 2 * latent + LANES]
    rscale = lax.rsqrt(jnp.sum(squares.T, axis=0, keepdims=True) / D + 1e-06)
    rows_ref[0] = (own_ref[latent : 2 * latent] + other_ref[latent : 2 * latent]) * rscale
    rows_ref[1] = (own_ref[:latent] + other_ref[:latent]) * rscale
    for side, right in enumerate((x_ref[:, cols], c_ref[:, cols])):
        left = jnp.concatenate(
            [rows_ref[side, pl.ds(pl.multiple_of((me ^ k) * depth, depth), depth), :] for k in range(experts)]
        )
        both = jnp.dot(left.astype(BF16), right, preferred_element_type=F32).astype(BF16)
        for k in range(experts):
            outs[k][side] = both[k * depth : (k + 1) * depth]


def share_kernel(experts, *refs):
    total = refs[0][...].astype(F32)
    for ref in refs[1:experts]:
        total = total + ref[...].astype(F32)
    refs[-1][...] = total.astype(BF16)


def update_kernel(start, share_ref, master_ref, moment_ref, second_ref, *rest):
    fresh_ref, peak_ref, wide = rest[-3:]
    cols = slice(start, start + share_ref.shape[2])
    grad = share_ref[...].astype(F32)
    first = 0.9 * moment_ref[:, 0, :, cols].astype(F32) + 0.1 * grad
    secnd = 0.95 * second_ref[:, 0, :, cols].astype(F32) + 0.05 * grad * grad
    update = first / (1.0 - 0.9**10) / (jnp.sqrt(secnd / (1.0 - 0.95**10)) + 1e-08)
    weights = master_ref[:, 0, :, cols]
    fresh = weights - 0.01 * (update + 0.1 * weights)
    fresh_ref[...] = fresh
    peak_ref[...] = jnp.zeros_like(peak_ref) if start == 0 else rest[0][...]
    wide[...] = jnp.zeros_like(wide)
    for side in range(2):
        peak = jnp.max(jnp.abs(fresh[side]), axis=0, keepdims=True)
        for at in range(0, peak.shape[1], LANES):
            block = (start + at) // LANES
            wide[side, block : block + 1, :] = peak[:, at : at + LANES]
        peak_ref[side : side + 1, :] = jnp.maximum(
            peak_ref[side : side + 1, :], jnp.max(wide[side].T, axis=0, keepdims=True)
        )


def code_kernel(group, peak_refs, fresh_refs, code_ref, scale_ref):
    blocks = scale_ref.shape[3]
    mine = lax.axis_index("expert") // group
    for far, ref in enumerate(peak_refs):
        for side in range(2):
            scale_ref[side, 0, pl.ds(mine ^ far, 1), :] = ref[side : side + 1, :blocks] + 1e-06
    column = (1.0 / (peak_refs[0][...] + 1e-06)).T
    for side in range(2):
        inverse = jnp.broadcast_to(column[:, side : side + 1], (LANES, LANES))
        block = 0
        for ref in fresh_refs:
            for at in range(0, ref.shape[2], LANES):
                code_ref[side, 0, :, block * LANES : (block + 1) * LANES] = (
                    ref[side, :, at : at + LANES] * inverse[block : block + 1]
                ).astype(BF16)
                block += 1


def place_kernel(start, in_ref, *rest):
    out_ref, sem = rest[-2:]
    copy = pltpu.make_async_copy(in_ref, out_ref.at[0, pl.ds(start, in_ref.shape[0])], sem)
    copy.start()
    copy.wait()


def shards(enter_fwd, enter_rev, cot_rev, gain, proj_down, proj_up, master, moment, second):
    tokens, width = enter_fwd.shape[1:]
    latent = proj_down.shape[2]
    experts = lax.axis_size("expert")
    depth = latent // experts
    blocks = width // LANES
    tiles = 2
    weights = [8, 8, 7, 5]
    edges = [blocks * sum(weights[:k]) // sum(weights) * LANES for k in range(len(weights) + 1)]
    chunks = list(zip(edges[:-1], edges[1:]))

    def streamed(array):
        return pltpu.with_memory_space_constraint(array, pltpu.HBM)

    pack_rows = 2 * latent + tokens + (latent // LANES + 1) * tokens
    held = pltpu.VMEM((tokens, width), BF16)
    packed, rows1, scaled2, cot2 = pl.pallas_call(
        lambda *refs: latent_kernel(tiles, *refs),
        in_specs=[ANY] * 6,
        out_specs=[VMEM] * 4,
        out_shape=[pltpu.VMEM((pack_rows, LANES), F32), held, held, held],
        scratch_shapes=[
            pltpu.VMEM((latent, width), BF16),
            pltpu.VMEM((tokens, width), BF16),
            pltpu.VMEM((latent, width), BF16),
            pltpu.VMEM((latent, width), BF16),
            pltpu.VMEM((2, width), BF16),
            pltpu.SemaphoreType.DMA((6 * tiles + 1,)),
        ],
        compiler_params=ROOM,
        cost_estimate=pl.CostEstimate(
            flops=6 * tokens * latent * width, bytes_accessed=6 * (tokens + latent) * width, transcendentals=0
        ),
        name="latents",
    )(*(streamed(a) for a in (enter_fwd, enter_rev, cot_rev, proj_down, proj_up, gain.reshape(2, width))))
    own_up = pl.pallas_call(
        fetch_kernel,
        in_specs=[ANY] * 2,
        out_specs=VMEM,
        out_shape=pltpu.VMEM((latent, width), BF16),
        scratch_shapes=[pltpu.SemaphoreType.DMA],
        compiler_params=ROOM,
        cost_estimate=pl.CostEstimate(flops=0, bytes_accessed=2 * latent * width, transcendentals=0),
        name="fetch",
    )(streamed(proj_up), packed)
    pair = halves_of_sum(packed, "dp")

    def leaving(start, count, *after):
        return call(
            lambda *refs: leaving_kernel(start, *refs),
            "leaving",
            shape((count, width), BF16),
            *pair,
            rows1,
            own_up,
            *after,
            read=4,
            flops=2 * count * latent * width,
        )

    def grads(chunk, *after):
        start, stop = chunks[chunk]
        return call(
            lambda *refs: grad_kernel(experts, start, *refs),
            "grads",
            [shape((2, depth, stop - start), BF16)] * experts,
            *pair,
            scaled2,
            cot2,
            *after,
            read=4,
            scratch=[pltpu.VMEM((2, latent, tokens), F32)],
            flops=4 * tokens * latent * (stop - start),
        )

    head = 128
    first_rows = leaving(0, head)
    left_head = turned(first_rows, "pipe")
    first = grads(0, first_rows)
    shares, arrived, others = [], [], []
    for chunk in range(len(chunks)):
        own, *pieces = grads(chunk, *shares[-2:-1], *others[-1][:1]) if chunk else first
        others.append([exchange(piece, "expert", 1 + k) for k, piece in enumerate(pieces)])
        after = [left_head] if chunk == 1 else arrived[chunk - 2 : chunk - 1] if chunk > 1 else []
        shares.append(
            call(
                lambda *refs: share_kernel(experts, *refs),
                "share",
                shape(own.shape, BF16),
                own,
                *others[-1],
                *shares[-1:],
                *after,
                read=experts,
            )
        )
        arrived.append(mirrored(shares[-1], "pipe"))
    left_tail = None

    def place(start, rows, *kept):
        return pl.pallas_call(
            lambda *refs: place_kernel(start, *refs),
            in_specs=[ANY] * (1 + len(kept)),
            out_specs=ANY,
            out_shape=shape((1, tokens, width), BF16),
            scratch_shapes=[pltpu.SemaphoreType.DMA],
            input_output_aliases={1 + k: k for k in range(len(kept))},
            compiler_params=ROOM,
            cost_estimate=pl.CostEstimate(flops=0, bytes_accessed=4 * rows.shape[0] * width, transcendentals=0),
            name="place",
        )(rows, *kept)

    placed = place(0, left_head)

    fresh, peaks = [], None
    for chunk, (start, stop) in enumerate(chunks):
        kept = () if peaks is None else (peaks,)
        after = (placed,) if chunk == len(chunks) - 1 else ()
        some, peaks = call(
            lambda *refs: update_kernel(start, *refs),
            "update",
            [shape((2, depth, stop - start), F32), shape((8, LANES), F32)],
            arrived[chunk],
            master,
            moment,
            second,
            *kept,
            *after,
            read=4 + len(kept),
            scratch=[pltpu.VMEM((2, LANES, LANES), F32)],
            flops=40 * depth * (stop - start),
        )
        fresh.append(some)

    group = LANES // depth
    for level in range(group.bit_length() - 1):
        peaks = jnp.maximum(peaks, exchange(peaks, "expert", 1 << level))
    peak_rows = [peaks] + [exchange(peaks, "expert", k * group) for k in range(1, experts // group)]
    count = len(peak_rows)
    coded, scales = call(
        lambda *refs: code_kernel(group, refs[:count], refs[count:-2], *refs[-2:]),
        "codes",
        [shape((2, 1, depth, width), BF16), shape((2, 1, experts // group, blocks), F32)],
        *peak_rows,
        *fresh,
        read=count + len(fresh),
        flops=4 * depth * width,
    )
    return (placed, coded, scales)


def solution(mesh):
    in_specs = (
        P("pipe", "expert", "dp"),
        P("pipe", "expert", "dp"),
        P("pipe", "expert", "dp"),
        P(None, "pipe", "dp"),
        P(None, "pipe", None, "dp"),
        P(None, "pipe", None, "dp"),
        P(None, "pipe", "expert", "dp"),
        P(None, "pipe", "expert", "dp"),
        P(None, "pipe", "expert", "dp"),
    )
    out_specs = (
        P("pipe", "expert", "dp"),
        P(None, "pipe", "expert", "dp"),
        P(None, "pipe", None, "dp"),
    )
    return jax.shard_map(shards, mesh=mesh, in_specs=in_specs, out_specs=out_specs, check_vma=False)
```

time: 87.3 us -> 80 us (0.916)
  waiting for transfers between devices: 44.5 us -> 35.5 us
  starting transfers between devices: 26.3 us -> 29.6 us
  Pallas kernels: 15.5 us -> 13.8 us
    ppermute x4, waiting for transfers between devices: 16 us -> 10.8 us  [mirrored(): return lax.ppermute(block, axis, [(i, count - 1 - i) for i in range(count)])]
    ppermute x15, starting transfers between devices: 17.7 us -> 22.4 us  [exchange(): return lax.ppermute(block, axis, [(i, i ^ offset) for i in range(count)])]
    ppermute x15, waiting for transfers between devices: 28.5 us -> 24.8 us  [exchange(): return lax.ppermute(block, axis, [(i, i ^ offset) for i in range(count)])]
    ppermute x2 -> x1, starting transfers between devices: 3.24 us -> 1.62 us  [turned(): lax.ppermute(block, axis, [(i, (i + 1) % count) for i in range(count)])]
    pallas_call x16, Pallas kernels: 14 us -> 12.8 us  [the longest x14 6.24 us: call(): pl.pallas_call(kernel, in_specs=[VMEM] * read + [ANY] * (len(operands) -...]
  transfers between devices with their start and end apart: 21 -> 20, of which waited for: 13 -> 13; matrix products, arithmetic and copies ran while one was open for 0% -> 0% of each run, Pallas kernels for 9% -> 8%
where the time goes in v5:
time: 80 us; the launch traced here: 79.7 us
  waiting for transfers between devices  35.5 us (44%)
  starting transfers between devices  29.6 us (37%)
  Pallas kernels  13.8 us (17%)
  between operations  0.8 us (1%)
    ppermute x15, waiting for transfers between devices, exchange(): return lax.ppermute(block, axis, [(i, i ^ offset) for i in range(count)])  24.8 us
    ppermute x15, starting transfers between devices, exchange(): return lax.ppermute(block, axis, [(i, i ^ offset) for i in range(count)])  22.4 us
    ppermute x4, waiting for transfers between devices, mirrored(): return lax.ppermute(block, axis, [(i, count - 1 - i) for i in range(count)])  10.8 us
    pallas_call x14, Pallas kernels, call(): pl.pallas_call(kernel, in_specs=[VMEM] * read + [ANY] * (len(operands) -...  6.24 us
    ppermute x4, starting transfers between devices, mirrored(): return lax.ppermute(block, axis, [(i, count - 1 - i) for i in range(count)])  5.62 us
    pallas_call x1, Pallas kernels, shards(): pl.pallas_call(lambda *refs: latent_kernel(tiles, *refs), in_specs=[ANY]...  5.09 us
    ppermute x1, starting transfers between devices, turned(): lax.ppermute(block, axis, [(i, (i + 1) % count) for i in range(count)])  1.62 us
  transfers between devices with their start and end apart: 20, of which 13 were waited for; matrix products, arithmetic and copies ran while one was open for 0% of the time, Pallas kernels for 8%

profile of v5, /device:TPU:8, one launch (start us, length us, event | category | flops | bytes accessed | tf_op | source)
XLA Modules:
  0.0 79.7 jit_solution(14964251364485777779)
XLA Ops:
  0.6 5.1 %latents.1 = (f32[1024,128]{1,0:T(8,128)S(1)}, bf16[128,3584]{1,0:T(8,128)(2,1)S(1)}, bf16[128,3584]{1,0:T(8,128)(2,1)S(1)}, bf16[128,3584]{1,0:T(8,128)(2,1)S(1)}) custom-call(bf16[1,128,3584]{2,1,0:T(8,128)(2,1)} %refs_0_.1, bf16[1,128,3584]{2,1,0:T(8,128)(2,1)} %refs_1_.5, bf16[1,128,3584]{2,1,0:T(8,128)(2,1)} %refs_2_.5, ...), custom_call_target="tpu_custom_call" | custom-call | flops 704643072 | bytes 8257536 | tf_op jit(solution)/shard_map/latents/pallas_call | solution.py:251
  5.8 1.5 %fetch.1.refs_3_ = bf16[256,3584]{1,0:T(8,128)(2,1)S(1)} custom-call(bf16[2,1,256,3584]{3,2,1,0:T(8,128)(2,1)} %in_ref.1, f32[1024,128]{1,0:T(8,128)S(1)} %get-tuple-element.33.rest_0_.refs_0_), custom_call_target="tpu_custom_call" | custom-call | bytes 1835008 | tf_op jit(solution)/shard_map/fetch/pallas_call | solution.py:270
  8.2 1.6 %collective-permute-start.1 = (bf16[128,3584]{1,0:T(8,128)(2,1)S(1)}, bf16[128,3584]{1,0:T(8,128)(2,1)S(1)}, u32[]{:S(2)}, u32[]{:S(2)}) collective-permute-start(bf16[128,3584]{1,0:T(8,128)(2,1)S(1)} %leaving.1.refs_4_), channel_id=1, source_target_pairs={{0,8},{8,16},{16,24},{24,0},{1,9},{9,17},{17,25},{25,1},{2,10},{10... | collective-permute-start | bytes 2752520 | tf_op jit(solution)/shard_map/ppermute | solution.py:30
  10.4 1.6 %collective-permute-start.2 = (bf16[2,64,1024]{2,1,0:T(8,128)(2,1)S(1)}, bf16[2,64,1024]{2,1,0:T(8,128)(2,1)S(1)}, u32[]{:S(2)}, u32[]{:S(2)}) collective-permute-start(bf16[2,64,1024]{2,1,0:T(8,128)(2,1)S(1)} %get-tuple-element.37), channel_id=1, source_target_pairs={{0,2},{2,0},{4,6},{6,4},{1,3},{3,1},{5,7},{7,5},{8,10},{10,8},{12,... | collective-permute-start | bytes 786440 | tf_op jit(solution)/shard_map/ppermute | solution.py:20
  11.9 1.5 %collective-permute-start.6 = (bf16[2,64,1024]{2,1,0:T(8,128)(2,1)S(1)}, bf16[2,64,1024]{2,1,0:T(8,128)(2,1)S(1)}, u32[]{:S(2)}, u32[]{:S(2)}) collective-permute-start(bf16[2,64,1024]{2,1,0:T(8,128)(2,1)S(1)} %get-tuple-element.43), channel_id=1, source_target_pairs={{0,4},{2,6},{4,0},{6,2},{1,5},{3,7},{5,1},{7,3},{8,12},{10,14},{12... | collective-permute-start | bytes 786440 | tf_op jit(solution)/shard_map/ppermute | solution.py:20
  13.9 5.7 %collective-permute-done.2.refs_4_.refs_1_ = bf16[2,64,1024]{2,1,0:T(8,128)(2,1)S(1)} collective-permute-done((bf16[2,64,1024]{2,1,0:T(8,128)(2,1)S(1)}, bf16[2,64,1024]{2,1,0:T(8,128)(2,1)S(1)}, u32[]{:S(2)}, u32[]{:S(2)}) %collective-permute-start.2) | collective-permute-done | bytes 262176 | tf_op jit(solution)/shard_map/ppermute | solution.py:20
  20.2 1.6 %collective-permute-start.3 = (bf16[2,64,1024]{2,1,0:T(8,128)(2,1)S(1)}, bf16[2,64,1024]{2,1,0:T(8,128)(2,1)S(1)}, u32[]{:S(2)}, u32[]{:S(2)}) collective-permute-start(bf16[2,64,1024]{2,1,0:T(8,128)(2,1)S(1)} %get-tuple-element.39), channel_id=1, source_target_pairs={{0,2},{2,0},{4,6},{6,4},{1,3},{3,1},{5,7},{7,5},{8,10},{10,8},{12,... | collective-permute-start | bytes 786440 | tf_op jit(solution)/shard_map/ppermute | solution.py:20
  21.7 1.5 %collective-permute-start.4 = (bf16[2,64,1024]{2,1,0:T(8,128)(2,1)S(1)}, bf16[2,64,1024]{2,1,0:T(8,128)(2,1)S(1)}, u32[]{:S(2)}, u32[]{:S(2)}) collective-permute-start(bf16[2,64,1024]{2,1,0:T(8,128)(2,1)S(1)} %get-tuple-element.40), channel_id=1, source_target_pairs={{0,4},{2,6},{4,0},{6,2},{1,5},{3,7},{5,1},{7,3},{8,12},{10,14},{12... | collective-permute-start | bytes 786440 | tf_op jit(solution)/shard_map/ppermute | solution.py:20
  23.2 2.2 %collective-permute-done.6.refs_2_ = bf16[2,64,1024]{2,1,0:T(8,128)(2,1)S(1)} collective-permute-done((bf16[2,64,1024]{2,1,0:T(8,128)(2,1)S(1)}, bf16[2,64,1024]{2,1,0:T(8,128)(2,1)S(1)}, u32[]{:S(2)}, u32[]{:S(2)}) %collective-permute-start.6) | collective-permute-done | bytes 262176 | tf_op jit(solution)/shard_map/ppermute | solution.py:20
  26.4 1.6 %collective-permute-start.14 = (bf16[2,64,1024]{2,1,0:T(8,128)(2,1)S(1)}, bf16[2,64,1024]{2,1,0:T(8,128)(2,1)S(1)}, u32[]{:S(2)}, u32[]{:S(2)}) collective-permute-start(bf16[2,64,1024]{2,1,0:T(8,128)(2,1)S(1)} %share.4.refs_4_), channel_id=1, source_target_pairs={{0,24},{8,16},{16,8},{24,0},{1,25},{9,17},{17,9},{25,1},{2,26},{10... | collective-permute-start | bytes 786440 | tf_op jit(solution)/shard_map/ppermute | solution.py:25
  28.0 2.9 %collective-permute-done.3.refs_1_.refs_5_ = bf16[2,64,1024]{2,1,0:T(8,128)(2,1)S(1)} collective-permute-done((bf16[2,64,1024]{2,1,0:T(8,128)(2,1)S(1)}, bf16[2,64,1024]{2,1,0:T(8,128)(2,1)S(1)}, u32[]{:S(2)}, u32[]{:S(2)}) %collective-permute-start.3) | collective-permute-done | bytes 262176 | tf_op jit(solution)/shard_map/ppermute | solution.py:20
  31.4 1.6 %collective-permute-start.8 = (bf16[2,64,896]{2,1,0:T(8,128)(2,1)S(1)}, bf16[2,64,896]{2,1,0:T(8,128)(2,1)S(1)}, u32[]{:S(2)}, u32[]{:S(2)}) collective-permute-start(bf16[2,64,896]{2,1,0:T(8,128)(2,1)S(1)} %get-tuple-element.45), channel_id=1, source_target_pairs={{0,2},{2,0},{4,6},{6,4},{1,3},{3,1},{5,7},{7,5},{8,10},{10,8},{12,... | collective-permute-start | bytes 688136 | tf_op jit(solution)/shard_map/ppermute | solution.py:20
  33.0 2.6 %collective-permute-done.4.refs_2_ = bf16[2,64,1024]{2,1,0:T(8,128)(2,1)S(1)} collective-permute-done((bf16[2,64,1024]{2,1,0:T(8,128)(2,1)S(1)}, bf16[2,64,1024]{2,1,0:T(8,128)(2,1)S(1)}, u32[]{:S(2)}, u32[]{:S(2)}) %collective-permute-start.4) | collective-permute-done | bytes 262176 | tf_op jit(solution)/shard_map/ppermute | solution.py:20
  35.6 2.4 %collective-permute-start.12 = (bf16[2,64,896]{2,1,0:T(8,128)(2,1)S(1)}, bf16[2,64,896]{2,1,0:T(8,128)(2,1)S(1)}, u32[]{:S(2)}, u32[]{:S(2)}) collective-permute-start(bf16[2,64,896]{2,1,0:T(8,128)(2,1)S(1)} %get-tuple-element.51), channel_id=1, source_target_pairs={{0,4},{2,6},{4,0},{6,2},{1,5},{3,7},{5,1},{7,3},{8,12},{10,14},{12... | collective-permute-start | bytes 688136 | tf_op jit(solution)/shard_map/ppermute | solution.py:20
  38.0 0.9 %collective-permute-start.13 = (bf16[2,64,896]{2,1,0:T(8,128)(2,1)S(1)}, bf16[2,64,896]{2,1,0:T(8,128)(2,1)S(1)}, u32[]{:S(2)}, u32[]{:S(2)}) collective-permute-start(bf16[2,64,896]{2,1,0:T(8,128)(2,1)S(1)} %get-tuple-element.52), channel_id=1, source_target_pairs={{0,6},{2,4},{4,2},{6,0},{1,7},{3,5},{5,3},{7,1},{8,14},{10,12},{12... | collective-permute-start | bytes 688136 | tf_op jit(solution)/shard_map/ppermute | solution.py:20
  39.1 1.6 %collective-permute-start.15 = (bf16[2,64,1024]{2,1,0:T(8,128)(2,1)S(1)}, bf16[2,64,1024]{2,1,0:T(8,128)(2,1)S(1)}, u32[]{:S(2)}, u32[]{:S(2)}) collective-permute-start(bf16[2,64,1024]{2,1,0:T(8,128)(2,1)S(1)} %share.5.refs_4_), channel_id=1, source_target_pairs={{0,24},{8,16},{16,8},{24,0},{1,25},{9,17},{17,9},{25,1},{2,26},{10... | collective-permute-start | bytes 786440 | tf_op jit(solution)/shard_map/ppermute | solution.py:25
  40.8 0.8 %collective-permute-done.8.refs_5_.refs_1_ = bf16[2,64,896]{2,1,0:T(8,128)(2,1)S(1)} collective-permute-done((bf16[2,64,896]{2,1,0:T(8,128)(2,1)S(1)}, bf16[2,64,896]{2,1,0:T(8,128)(2,1)S(1)}, u32[]{:S(2)}, u32[]{:S(2)}) %collective-permute-start.8) | collective-permute-done | bytes 229408 | tf_op jit(solution)/shard_map/ppermute | solution.py:20
  42.0 1.5 %collective-permute-start.10 = (bf16[2,64,640]{2,1,0:T(8,128)(2,1)S(1)}, bf16[2,64,640]{2,1,0:T(8,128)(2,1)S(1)}, u32[]{:S(2)}, u32[]{:S(2)}) collective-permute-start(bf16[2,64,640]{2,1,0:T(8,128)(2,1)S(1)} %get-tuple-element.48), channel_id=1, source_target_pairs={{0,4},{2,6},{4,0},{6,2},{1,5},{3,7},{5,1},{7,3},{8,12},{10,14},{12... | collective-permute-start | bytes 491528 | tf_op jit(solution)/shard_map/ppermute | solution.py:20
  43.5 4.9 %collective-permute-done.14.refs_5_.refs_0_ = bf16[2,64,1024]{2,1,0:T(8,128)(2,1)S(1)} collective-permute-done((bf16[2,64,1024]{2,1,0:T(8,128)(2,1)S(1)}, bf16[2,64,1024]{2,1,0:T(8,128)(2,1)S(1)}, u32[]{:S(2)}, u32[]{:S(2)}) %collective-permute-start.14) | collective-permute-done | bytes 262176 | tf_op jit(solution)/shard_map/ppermute | solution.py:25
  48.5 4.9 %collective-permute-start.11 = (bf16[2,64,640]{2,1,0:T(8,128)(2,1)S(1)}, bf16[2,64,640]{2,1,0:T(8,128)(2,1)S(1)}, u32[]{:S(2)}, u32[]{:S(2)}) collective-permute-start(bf16[2,64,640]{2,1,0:T(8,128)(2,1)S(1)} %get-tuple-element.49), channel_id=1, source_target_pairs={{0,6},{2,4},{4,2},{6,0},{1,7},{3,5},{5,3},{7,1},{8,14},{10,12},{12... | collective-permute-start | bytes 491528 | tf_op jit(solution)/shard_map/ppermute | solution.py:20
  54.0 1.5 %collective-permute-start.17 = (bf16[2,64,896]{2,1,0:T(8,128)(2,1)S(1)}, bf16[2,64,896]{2,1,0:T(8,128)(2,1)S(1)}, u32[]{:S(2)}, u32[]{:S(2)}) collective-permute-start(bf16[2,64,896]{2,1,0:T(8,128)(2,1)S(1)} %share.6.refs_4_), channel_id=1, source_target_pairs={{0,24},{8,16},{16,8},{24,0},{1,25},{9,17},{17,9},{25,1},{2,26},{10... | collective-permute-start | bytes 688136 | tf_op jit(solution)/shard_map/ppermute | solution.py:25
  55.5 2.8 %collective-permute-done.11.refs_3_ = bf16[2,64,640]{2,1,0:T(8,128)(2,1)S(1)} collective-permute-done((bf16[2,64,640]{2,1,0:T(8,128)(2,1)S(1)}, bf16[2,64,640]{2,1,0:T(8,128)(2,1)S(1)}, u32[]{:S(2)}, u32[]{:S(2)}) %collective-permute-start.11) | collective-permute-done | bytes 163872 | tf_op jit(solution)/shard_map/ppermute | solution.py:20
  58.4 3.0 %collective-permute-done.9.refs_1_ = bf16[2,64,640]{2,1,0:T(8,128)(2,1)S(1)} collective-permute-done((bf16[2,64,640]{2,1,0:T(8,128)(2,1)S(1)}, bf16[2,64,640]{2,1,0:T(8,128)(2,1)S(1)}, u32[]{:S(2)}, u32[]{:S(2)}) %collective-permute-start.9) | collective-permute-done | bytes 163872 | tf_op jit(solution)/shard_map/ppermute | solution.py:20
  61.5 0.8 %collective-permute-start.16 = (bf16[2,64,640]{2,1,0:T(8,128)(2,1)S(1)}, bf16[2,64,640]{2,1,0:T(8,128)(2,1)S(1)}, u32[]{:S(2)}, u32[]{:S(2)}) collective-permute-start(bf16[2,64,640]{2,1,0:T(8,128)(2,1)S(1)} %share.7), channel_id=1, source_target_pairs={{0,24},{8,16},{16,8},{24,0},{1,25},{9,17},{17,9},{25,1},{2,26},{10... | collective-permute-start | bytes 491528 | tf_op jit(solution)/shard_map/ppermute | solution.py:25
  62.9 0.9 %place.1.refs_5_ = bf16[1,128,3584]{2,1,0:T(8,128)(2,1)} custom-call(bf16[128,3584]{1,0:T(8,128)(2,1)S(1)} %collective-permute-done.1.refs_0_.refs_5_), custom_call_target="tpu_custom_call" | custom-call | bytes 1835008 | tf_op jit(solution)/shard_map/place/pallas_call | solution.py:335
  64.5 2.9 %collective-permute-done.17.refs_0_ = bf16[2,64,896]{2,1,0:T(8,128)(2,1)S(1)} collective-permute-done((bf16[2,64,896]{2,1,0:T(8,128)(2,1)S(1)}, bf16[2,64,896]{2,1,0:T(8,128)(2,1)S(1)}, u32[]{:S(2)}, u32[]{:S(2)}) %collective-permute-start.17) | collective-permute-done | bytes 229408 | tf_op jit(solution)/shard_map/ppermute | solution.py:25
  68.0 2.9 %collective-permute-done.16.refs_0_ = bf16[2,64,640]{2,1,0:T(8,128)(2,1)S(1)} collective-permute-done((bf16[2,64,640]{2,1,0:T(8,128)(2,1)S(1)}, bf16[2,64,640]{2,1,0:T(8,128)(2,1)S(1)}, u32[]{:S(2)}, u32[]{:S(2)}) %collective-permute-start.16) | collective-permute-done | bytes 163872 | tf_op jit(solution)/shard_map/ppermute | solution.py:25
  71.3 1.6 %collective-permute-start.18 = (f32[8,128]{1,0:T(8,128)S(1)}, f32[8,128]{1,0:T(8,128)S(1)}, u32[]{:S(2)}, u32[]{:S(2)}) collective-permute-start(f32[8,128]{1,0:T(8,128)S(1)} %get-tuple-element.56), channel_id=1, source_target_pairs={{0,2},{2,0},{4,6},{6,4},{1,3},{3,1},{5,7},{7,5},{8,10},{10,8},{12,... | collective-permute-start | bytes 12296 | tf_op jit(solution)/shard_map/ppermute | solution.py:20
  72.8 2.1 %collective-permute-done.18 = f32[8,128]{1,0:T(8,128)S(1)} collective-permute-done((f32[8,128]{1,0:T(8,128)S(1)}, f32[8,128]{1,0:T(8,128)S(1)}, u32[]{:S(2)}, u32[]{:S(2)}) %collective-permute-start.18) | collective-permute-done | bytes 4128 | tf_op jit(solution)/shard_map/ppermute | solution.py:20
  74.9 1.5 %collective-permute-start.19 = (f32[8,128]{1,0:T(8,128)S(1)}, f32[8,128]{1,0:T(8,128)S(1)}, u32[]{:S(2)}, u32[]{:S(2)}) collective-permute-start(f32[8,128]{1,0:T(8,128)S(1)} %max.3.refs_0_), channel_id=1, source_target_pairs={{0,4},{2,6},{4,0},{6,2},{1,5},{3,7},{5,1},{7,3},{8,12},{10,14},{12... | collective-permute-start | bytes 12296 | tf_op jit(solution)/shard_map/ppermute | solution.py:20
  76.4 2.1 %collective-permute-done.19.refs_1_ = f32[8,128]{1,0:T(8,128)S(1)} collective-permute-done((f32[8,128]{1,0:T(8,128)S(1)}, f32[8,128]{1,0:T(8,128)S(1)}, u32[]{:S(2)}, u32[]{:S(2)}) %collective-permute-start.19) | collective-permute-done | bytes 4128 | tf_op jit(solution)/shard_map/ppermute | solution.py:20
  78.5 1.2 %codes.1 = (bf16[2,1,64,3584]{3,2,1,0:T(8,128)(2,1)}, f32[2,1,2,28]{3,2,1,0:T(2,128)}) custom-call(f32[8,128]{1,0:T(8,128)S(1)} %max.3.refs_0_, f32[8,128]{1,0:T(8,128)S(1)} %collective-permute-done.19.refs_1_, f32[2,64,1024]{2,1,0:T(8,128)S(1)} %get-tuple-element.57.refs_2_, f32[2,64,1024]{2,1,0:T(8,128)S(1)} %get-tuple-element.58.refs_3_, ...), custom_call_target="tpu_custom_call" | custom-call | flops 917504 | bytes 1843200 | tf_op jit(solution)/shard_map/codes/pallas_call | solution.py:51
  (34 shorter events, 7.3 us)
Async XLA Ops:
  5.7 2.0 %collective-permute-start = (f32[1024,128]{1,0:T(8,128)S(1)}, f32[1024,128]{1,0:T(8,128)S(1)}, u32[]{:S(2)}, u32[]{:S(2)}) collective-permute-start(f32[1024,128]{1,0:T(8,128)S(1)} %get-tuple-element.33.rest_0_.refs_0_), channel_id=1, source_target_pairs={{0,1},{1,0},{2,3},{3,2},{4,5},{5,4},{6,7},{7,6},{8,9},{9,8},{10,11... | collective-permute-start | bytes 1572872 | tf_op jit(solution)/shard_map/ppermute | solution.py:20
  8.2 30.8 %collective-permute-start.1 = (bf16[128,3584]{1,0:T(8,128)(2,1)S(1)}, bf16[128,3584]{1,0:T(8,128)(2,1)S(1)}, u32[]{:S(2)}, u32[]{:S(2)}) collective-permute-start(bf16[128,3584]{1,0:T(8,128)(2,1)S(1)} %leaving.1.refs_4_), channel_id=1, source_target_pairs={{0,8},{8,16},{16,24},{24,0},{1,9},{9,17},{17,25},{25,1},{2,10},{10... | collective-permute-start | bytes 2752520 | tf_op jit(solution)/shard_map/ppermute | solution.py:30
  10.4 9.3 %collective-permute-start.2 = (bf16[2,64,1024]{2,1,0:T(8,128)(2,1)S(1)}, bf16[2,64,1024]{2,1,0:T(8,128)(2,1)S(1)}, u32[]{:S(2)}, u32[]{:S(2)}) collective-permute-start(bf16[2,64,1024]{2,1,0:T(8,128)(2,1)S(1)} %get-tuple-element.37), channel_id=1, source_target_pairs={{0,2},{2,0},{4,6},{6,4},{1,3},{3,1},{5,7},{7,5},{8,10},{10,8},{12,... | collective-permute-start | bytes 786440 | tf_op jit(solution)/shard_map/ppermute | solution.py:20
  11.9 13.6 %collective-permute-start.6 = (bf16[2,64,1024]{2,1,0:T(8,128)(2,1)S(1)}, bf16[2,64,1024]{2,1,0:T(8,128)(2,1)S(1)}, u32[]{:S(2)}, u32[]{:S(2)}) collective-permute-start(bf16[2,64,1024]{2,1,0:T(8,128)(2,1)S(1)} %get-tuple-element.43), channel_id=1, source_target_pairs={{0,4},{2,6},{4,0},{6,2},{1,5},{3,7},{5,1},{7,3},{8,12},{10,14},{12... | collective-permute-start | bytes 786440 | tf_op jit(solution)/shard_map/ppermute | solution.py:20
  13.5 12.8 %collective-permute-start.7 = (bf16[2,64,1024]{2,1,0:T(8,128)(2,1)S(1)}, bf16[2,64,1024]{2,1,0:T(8,128)(2,1)S(1)}, u32[]{:S(2)}, u32[]{:S(2)}) collective-permute-start(bf16[2,64,1024]{2,1,0:T(8,128)(2,1)S(1)} %get-tuple-element.44), channel_id=1, source_target_pairs={{0,6},{2,4},{4,2},{6,0},{1,7},{3,5},{5,3},{7,1},{8,14},{10,12},{12... | collective-permute-start | bytes 786440 | tf_op jit(solution)/shard_map/ppermute | solution.py:20
  20.2 10.7 %collective-permute-start.3 = (bf16[2,64,1024]{2,1,0:T(8,128)(2,1)S(1)}, bf16[2,64,1024]{2,1,0:T(8,128)(2,1)S(1)}, u32[]{:S(2)}, u32[]{:S(2)}) collective-permute-start(bf16[2,64,1024]{2,1,0:T(8,128)(2,1)S(1)} %get-tuple-element.39), channel_id=1, source_target_pairs={{0,2},{2,0},{4,6},{6,4},{1,3},{3,1},{5,7},{7,5},{8,10},{10,8},{12,... | collective-permute-start | bytes 786440 | tf_op jit(solution)/shard_map/ppermute | solution.py:20
  21.7 13.9 %collective-permute-start.4 = (bf16[2,64,1024]{2,1,0:T(8,128)(2,1)S(1)}, bf16[2,64,1024]{2,1,0:T(8,128)(2,1)S(1)}, u32[]{:S(2)}, u32[]{:S(2)}) collective-permute-start(bf16[2,64,1024]{2,1,0:T(8,128)(2,1)S(1)} %get-tuple-element.40), channel_id=1, source_target_pairs={{0,4},{2,6},{4,0},{6,2},{1,5},{3,7},{5,1},{7,3},{8,12},{10,14},{12... | collective-permute-start | bytes 786440 | tf_op jit(solution)/shard_map/ppermute | solution.py:20
  25.5 12.5 %collective-permute-start.5 = (bf16[2,64,1024]{2,1,0:T(8,128)(2,1)S(1)}, bf16[2,64,1024]{2,1,0:T(8,128)(2,1)S(1)}, u32[]{:S(2)}, u32[]{:S(2)}) collective-permute-start(bf16[2,64,1024]{2,1,0:T(8,128)(2,1)S(1)} %get-tuple-element.41), channel_id=1, source_target_pairs={{0,6},{2,4},{4,2},{6,0},{1,7},{3,5},{5,3},{7,1},{8,14},{10,12},{12... | collective-permute-start | bytes 786440 | tf_op jit(solution)/shard_map/ppermute | solution.py:20
  26.4 22.1 %collective-permute-start.14 = (bf16[2,64,1024]{2,1,0:T(8,128)(2,1)S(1)}, bf16[2,64,1024]{2,1,0:T(8,128)(2,1)S(1)}, u32[]{:S(2)}, u32[]{:S(2)}) collective-permute-start(bf16[2,64,1024]{2,1,0:T(8,128)(2,1)S(1)} %share.4.refs_4_), channel_id=1, source_target_pairs={{0,24},{8,16},{16,8},{24,0},{1,25},{9,17},{17,9},{25,1},{2,26},{10... | collective-permute-start | bytes 786440 | tf_op jit(solution)/shard_map/ppermute | solution.py:25
  31.4 10.2 %collective-permute-start.8 = (bf16[2,64,896]{2,1,0:T(8,128)(2,1)S(1)}, bf16[2,64,896]{2,1,0:T(8,128)(2,1)S(1)}, u32[]{:S(2)}, u32[]{:S(2)}) collective-permute-start(bf16[2,64,896]{2,1,0:T(8,128)(2,1)S(1)} %get-tuple-element.45), channel_id=1, source_target_pairs={{0,2},{2,0},{4,6},{6,4},{1,3},{3,1},{5,7},{7,5},{8,10},{10,8},{12,... | collective-permute-start | bytes 688136 | tf_op jit(solution)/shard_map/ppermute | solution.py:20
  35.6 17.8 %collective-permute-start.12 = (bf16[2,64,896]{2,1,0:T(8,128)(2,1)S(1)}, bf16[2,64,896]{2,1,0:T(8,128)(2,1)S(1)}, u32[]{:S(2)}, u32[]{:S(2)}) collective-permute-start(bf16[2,64,896]{2,1,0:T(8,128)(2,1)S(1)} %get-tuple-element.51), channel_id=1, source_target_pairs={{0,4},{2,6},{4,0},{6,2},{1,5},{3,7},{5,1},{7,3},{8,12},{10,14},{12... | collective-permute-start | bytes 688136 | tf_op jit(solution)/shard_map/ppermute | solution.py:20
  38.0 15.9 %collective-permute-start.13 = (bf16[2,64,896]{2,1,0:T(8,128)(2,1)S(1)}, bf16[2,64,896]{2,1,0:T(8,128)(2,1)S(1)}, u32[]{:S(2)}, u32[]{:S(2)}) collective-permute-start(bf16[2,64,896]{2,1,0:T(8,128)(2,1)S(1)} %get-tuple-element.52), channel_id=1, source_target_pairs={{0,6},{2,4},{4,2},{6,0},{1,7},{3,5},{5,3},{7,1},{8,14},{10,12},{12... | collective-permute-start | bytes 688136 | tf_op jit(solution)/shard_map/ppermute | solution.py:20
  39.1 23.2 %copy-start = (f32[2,1,64,3584]{3,2,1,0:T(8,128)S(1)}, f32[2,1,64,3584]{3,2,1,0:T(8,128)}, u32[]{:S(2)}) copy-start(f32[2,1,64,3584]{3,2,1,0:T(8,128)} %refs_1_.9) | copy-start | bytes 5505028
  39.1 23.2 %copy-start.1 = (bf16[2,1,64,3584]{3,2,1,0:T(8,128)(2,1)S(1)}, bf16[2,1,64,3584]{3,2,1,0:T(8,128)(2,1)}, u32[]{:S(2)}) copy-start(bf16[2,1,64,3584]{3,2,1,0:T(8,128)(2,1)} %refs_2_.9) | copy-start | bytes 2752516
  39.1 23.2 %copy-start.2 = (bf16[2,1,64,3584]{3,2,1,0:T(8,128)(2,1)S(1)}, bf16[2,1,64,3584]{3,2,1,0:T(8,128)(2,1)}, u32[]{:S(2)}) copy-start(bf16[2,1,64,3584]{3,2,1,0:T(8,128)(2,1)} %refs_3_.9) | copy-start | bytes 2752516
  39.1 22.3 %collective-permute-start.15 = (bf16[2,64,1024]{2,1,0:T(8,128)(2,1)S(1)}, bf16[2,64,1024]{2,1,0:T(8,128)(2,1)S(1)}, u32[]{:S(2)}, u32[]{:S(2)}) collective-permute-start(bf16[2,64,1024]{2,1,0:T(8,128)(2,1)S(1)} %share.5.refs_4_), channel_id=1, source_target_pairs={{0,24},{8,16},{16,8},{24,0},{1,25},{9,17},{17,9},{25,1},{2,26},{10... | collective-permute-start | bytes 786440 | tf_op jit(solution)/shard_map/ppermute | solution.py:25
  42.0 13.5 %collective-permute-start.10 = (bf16[2,64,640]{2,1,0:T(8,128)(2,1)S(1)}, bf16[2,64,640]{2,1,0:T(8,128)(2,1)S(1)}, u32[]{:S(2)}, u32[]{:S(2)}) collective-permute-start(bf16[2,64,640]{2,1,0:T(8,128)(2,1)S(1)} %get-tuple-element.48), channel_id=1, source_target_pairs={{0,4},{2,6},{4,0},{6,2},{1,5},{3,7},{5,1},{7,3},{8,12},{10,14},{12... | collective-permute-start | bytes 491528 | tf_op jit(solution)/shard_map/ppermute | solution.py:20
  48.5 9.9 %collective-permute-start.11 = (bf16[2,64,640]{2,1,0:T(8,128)(2,1)S(1)}, bf16[2,64,640]{2,1,0:T(8,128)(2,1)S(1)}, u32[]{:S(2)}, u32[]{:S(2)}) collective-permute-start(bf16[2,64,640]{2,1,0:T(8,128)(2,1)S(1)} %get-tuple-element.49), channel_id=1, source_target_pairs={{0,6},{2,4},{4,2},{6,0},{1,7},{3,5},{5,3},{7,1},{8,14},{10,12},{12... | collective-permute-start | bytes 491528 | tf_op jit(solution)/shard_map/ppermute | solution.py:20
  53.4 8.0 %collective-permute-start.9 = (bf16[2,64,640]{2,1,0:T(8,128)(2,1)S(1)}, bf16[2,64,640]{2,1,0:T(8,128)(2,1)S(1)}, u32[]{:S(2)}, u32[]{:S(2)}) collective-permute-start(bf16[2,64,640]{2,1,0:T(8,128)(2,1)S(1)} %get-tuple-element.47), channel_id=1, source_target_pairs={{0,2},{2,0},{4,6},{6,4},{1,3},{3,1},{5,7},{7,5},{8,10},{10,8},{12,... | collective-permute-start | bytes 491528 | tf_op jit(solution)/shard_map/ppermute | solution.py:20
  54.0 13.4 %collective-permute-start.17 = (bf16[2,64,896]{2,1,0:T(8,128)(2,1)S(1)}, bf16[2,64,896]{2,1,0:T(8,128)(2,1)S(1)}, u32[]{:S(2)}, u32[]{:S(2)}) collective-permute-start(bf16[2,64,896]{2,1,0:T(8,128)(2,1)S(1)} %share.6.refs_4_), channel_id=1, source_target_pairs={{0,24},{8,16},{16,8},{24,0},{1,25},{9,17},{17,9},{25,1},{2,26},{10... | collective-permute-start | bytes 688136 | tf_op jit(solution)/shard_map/ppermute | solution.py:25
  61.5 9.3 %collective-permute-start.16 = (bf16[2,64,640]{2,1,0:T(8,128)(2,1)S(1)}, bf16[2,64,640]{2,1,0:T(8,128)(2,1)S(1)}, u32[]{:S(2)}, u32[]{:S(2)}) collective-permute-start(bf16[2,64,640]{2,1,0:T(8,128)(2,1)S(1)} %share.7), channel_id=1, source_target_pairs={{0,24},{8,16},{16,8},{24,0},{1,25},{9,17},{17,9},{25,1},{2,26},{10... | collective-permute-start | bytes 491528 | tf_op jit(solution)/shard_map/ppermute | solution.py:25
  63.9 7.0 %copy-start.3 = (bf16[1,128,3584]{2,1,0:T(8,128)(2,1)S(1)}, bf16[1,128,3584]{2,1,0:T(8,128)(2,1)}, u32[]{:S(2)}) copy-start(bf16[1,128,3584]{2,1,0:T(8,128)(2,1)} %place.1.refs_5_) | copy-start | bytes 2752516
  71.3 3.7 %collective-permute-start.18 = (f32[8,128]{1,0:T(8,128)S(1)}, f32[8,128]{1,0:T(8,128)S(1)}, u32[]{:S(2)}, u32[]{:S(2)}) collective-permute-start(f32[8,128]{1,0:T(8,128)S(1)} %get-tuple-element.56), channel_id=1, source_target_pairs={{0,2},{2,0},{4,6},{6,4},{1,3},{3,1},{5,7},{7,5},{8,10},{10,8},{12,... | collective-permute-start | bytes 12296 | tf_op jit(solution)/shard_map/ppermute | solution.py:20
  74.9 3.6 %collective-permute-start.19 = (f32[8,128]{1,0:T(8,128)S(1)}, f32[8,128]{1,0:T(8,128)S(1)}, u32[]{:S(2)}, u32[]{:S(2)}) collective-permute-start(f32[8,128]{1,0:T(8,128)S(1)} %max.3.refs_0_), channel_id=1, source_target_pairs={{0,4},{2,6},{4,0},{6,2},{1,5},{3,7},{5,1},{7,3},{8,12},{10,14},{12... | collective-permute-start | bytes 12296 | tf_op jit(solution)/shard_map/ppermute | solution.py:20

commit v6 on v5

--- a/solution.py
+++ b/solution.py
@@ -73,60 +73,53 @@
     tokens, width = vx1.shape
     latent = va1.shape[0]
     tile = width // tiles
-    pairs = (
+    groups = (
         ((x1.at[0], vx1), (down.at[0, 0], va1)),
         ((x2.at[0], vx2), (down.at[1, 0], va2)),
         ((c2.at[0], vc2), (up.at[1, 0], vb2)),
     )
-    jobs = [[pltpu.make_async_copy(gain, vgain, sems.at[6 * tiles])]]
-    for pair in pairs:
+
+    def copies(job, at):
+        cols = pl.ds(at * tile, tile)
+        return [
+            pltpu.make_async_copy(src.at[:, cols], dst.at[:, cols], sems.at[job, k, at])
+            for k, (src, dst) in enumerate(groups[job])
+        ]
+
+    whole_gain = pltpu.make_async_copy(gain, vgain, sems.at[len(groups), 0, 0])
+    whole_gain.start()
+    for job in range(len(groups)):
         for at in range(tiles):
-            cols = pl.ds(at * tile, tile)
-            sem = 2 * (len(jobs) - 1)
-            jobs.append(
-                [pltpu.make_async_copy(s.at[:, cols], d.at[:, cols], sems.at[sem + k]) for k, (s, d) in enumerate(pair)]
+            for copy in copies(job, at):
+                copy.start()
+    base = 2 * latent + tokens
+    out_ref[...] = jnp.zeros_like(out_ref)
+    whole_gain.wait()
+
+    def step(job, at):
+        for copy in copies(job, at):
+            copy.wait()
+        cols = pl.ds(pl.multiple_of(at * tile, LANES), tile)
+        if job < 2:
+            rows = (vx1, vx2)[job][:, cols].astype(F32)
+            right = (rows * vgain[job : job + 1, cols].astype(F32)).astype(BF16)
+            squares = folded_squares(rows)
+        if job == 0:
+            raw = lax.dot_general(right, va1[:, cols], BOTH_LAST, preferred_element_type=F32)
+            for piece in range(latent // LANES):
+                out_ref[base + piece * tokens : base + (piece + 1) * tokens] += raw[:, piece * LANES : (piece + 1) * LANES]
+            out_ref[base + (latent // LANES) * tokens :] += squares
+        elif job == 1:
+            scaled2[:, cols] = right
+            out_ref[:latent] += lax.dot_general(va2[:, cols], right, BOTH_LAST, preferred_element_type=F32)
+            out_ref[2 * latent : base] += squares
+        else:
+            out_ref[latent : 2 * latent] += lax.dot_general(
+                vb2[:, cols], vc2[:, cols], BOTH_LAST, preferred_element_type=F32
             )
-    for job in jobs:
-        for copy in job:
-            copy.start()
-
-    def arrive(at):
-        for copy in jobs[at]:
-            copy.wait()
-
-    arrive(0)
-    gains = vgain[...].astype(F32)
-
-    def product(job):
-        total = None
-        squares = jnp.zeros((tokens, LANES), F32)
-        for at in range(tiles):
-            arrive(1 + job * tiles + at)
-            cols = slice(at * tile, (at + 1) * tile)
-            if job < 2:
-                rows = (vx1, vx2)[job][:, cols].astype(F32)
-                squares += folded_squares(rows)
-                right = (rows * gains[job : job + 1, cols]).astype(BF16)
-            if job == 0:
-                left, right = right, va1[:, cols]
-            elif job == 1:
-                scaled2[:, cols] = right
-                left = va2[:, cols]
-            else:
-                left, right = vb2[:, cols], vc2[:, cols]
-            term = lax.dot_general(left, right, BOTH_LAST, preferred_element_type=F32)
-            total = term if total is None else total + term
-        return total, squares
-
-    raw, squares = product(0)
-    base = 2 * latent + tokens
-    for at in range(latent // LANES):
-        out_ref[base + at * tokens : base + (at + 1) * tokens] = raw[:, at * LANES : (at + 1) * LANES]
-    out_ref[base + (latent // LANES) * tokens :] = squares
-    raw, squares = product(1)
-    out_ref[:latent] = raw
-    out_ref[2 * latent : base] = squares
-    out_ref[latent : 2 * latent], _ = product(2)
+
+    for job in range(len(groups)):
+        lax.fori_loop(0, tiles, lambda at, _, job=job: step(job, at) or 0, 0)
 
 
 def fetch_kernel(in_ref, *rest):
@@ -210,10 +203,15 @@
 def code_kernel(group, peak_refs, fresh_refs, code_ref, scale_ref):
     blocks = scale_ref.shape[3]
     mine = lax.axis_index("expert") // group
-    for far, ref in enumerate(peak_refs):
+    tops = []
+    for far in range(len(peak_refs) // group):
+        top = peak_refs[far * group][...]
+        for ref in peak_refs[far * group + 1 : (far + 1) * group]:
+            top = jnp.maximum(top, ref[...])
+        tops.append(top + 1e-06)
         for side in range(2):
-            scale_ref[side, 0, pl.ds(mine ^ far, 1), :] = ref[side : side + 1, :blocks] + 1e-06
-    column = (1.0 / (peak_refs[0][...] + 1e-06)).T
+            scale_ref[side, 0, pl.ds(mine ^ far, 1), :] = tops[far][side : side + 1, :blocks]
+    column = (1.0 / tops[0]).T
     for side in range(2):
         inverse = jnp.broadcast_to(column[:, side : side + 1], (LANES, LANES))
         block = 0
@@ -259,7 +257,7 @@
             pltpu.VMEM((latent, width), BF16),
             pltpu.VMEM((latent, width), BF16),
             pltpu.VMEM((2, width), BF16),
-            pltpu.SemaphoreType.DMA((6 * tiles + 1,)),
+            pltpu.SemaphoreType.DMA((4, 2, tiles)),
         ],
         compiler_params=ROOM,
         cost_estimate=pl.CostEstimate(
@@ -367,9 +365,7 @@
         fresh.append(some)
 
     group = LANES // depth
-    for level in range(group.bit_length() - 1):
-        peaks = jnp.maximum(peaks, exchange(peaks, "expert", 1 << level))
-    peak_rows = [peaks] + [exchange(peaks, "expert", k * group) for k in range(1, experts // group)]
+    peak_rows = [peaks] + [exchange(peaks, "expert", k) for k in range(1, experts)]
     count = len(peak_rows)
     coded, scales = call(
         lambda *refs: code_kernel(group, refs[:count], refs[count:-2], *refs[-2:]),

time: 80 us -> 79.3 us (level)
  Pallas kernels: 13.8 us -> 12.8 us
    pallas_call x1, Pallas kernels: 5.09 us -> 4.13 us  [shards(): pl.pallas_call(lambda *refs: latent_kernel(tiles, *refs), in_specs=[ANY]...]
    ppermute x15 -> x16, starting transfers between devices: 22.4 us -> 22.9 us  [exchange(): return lax.ppermute(block, axis, [(i, i ^ offset) for i in range(count)])]
    ppermute x15 -> x16, waiting for transfers between devices: 24.8 us -> 24.6 us  [exchange(): return lax.ppermute(block, axis, [(i, i ^ offset) for i in range(count)])]
  transfers between devices with their start and end apart: 20 -> 21, of which waited for: 13 -> 14; matrix products, arithmetic and copies ran while one was open for 0% -> 0% of each run, Pallas kernels for 8% -> 8%
where the time goes in v6:
time: 79.3 us; the launch traced here: 79.1 us
  waiting for transfers between devices  35.3 us (45%)
  starting transfers between devices  30.1 us (38%)
  Pallas kernels  12.8 us (16%)
  between operations  0.8 us (1%)
    ppermute x16, waiting for transfers between devices, exchange(): return lax.ppermute(block, axis, [(i, i ^ offset) for i in range(count)])  24.6 us
    ppermute x16, starting transfers between devices, exchange(): return lax.ppermute(block, axis, [(i, i ^ offset) for i in range(count)])  22.9 us
    ppermute x4, waiting for transfers between devices, mirrored(): return lax.ppermute(block, axis, [(i, count - 1 - i) for i in range(count)])  10.7 us
    pallas_call x14, Pallas kernels, call(): pl.pallas_call(kernel, in_specs=[VMEM] * read + [ANY] * (len(operands) -...  6.25 us
    ppermute x4, starting transfers between devices, mirrored(): return lax.ppermute(block, axis, [(i, count - 1 - i) for i in range(count)])  5.62 us
    pallas_call x1, Pallas kernels, shards(): pl.pallas_call(lambda *refs: latent_kernel(tiles, *refs), in_specs=[ANY]...  4.13 us
    ppermute x1, starting transfers between devices, turned(): lax.ppermute(block, axis, [(i, (i + 1) % count) for i in range(count)])  1.63 us
  transfers between devices with their start and end apart: 21, of which 14 were waited for; matrix products, arithmetic and copies ran while one was open for 0% of the time, Pallas kernels for 8%

profile of v6, /device:TPU:8, one launch (start us, length us, event | category | flops | bytes accessed | tf_op | source)
XLA Modules:
  0.0 79.1 jit_solution(16364601389324489943)
XLA Ops:
  0.6 4.1 %latents.1 = (f32[1024,128]{1,0:T(8,128)S(1)}, bf16[128,3584]{1,0:T(8,128)(2,1)S(1)}, bf16[128,3584]{1,0:T(8,128)(2,1)S(1)}, bf16[128,3584]{1,0:T(8,128)(2,1)S(1)}) custom-call(bf16[1,128,3584]{2,1,0:T(8,128)(2,1)} %refs_0_.1, bf16[1,128,3584]{2,1,0:T(8,128)(2,1)} %refs_1_.5, bf16[1,128,3584]{2,1,0:T(8,128)(2,1)} %refs_2_.5, ...), custom_call_target="tpu_custom_call" | custom-call | flops 704643072 | bytes 8257536 | tf_op jit(solution)/shard_map/latents/pallas_call | solution.py:249
  4.9 1.5 %fetch.1.refs_3_ = bf16[256,3584]{1,0:T(8,128)(2,1)S(1)} custom-call(bf16[2,1,256,3584]{3,2,1,0:T(8,128)(2,1)} %in_ref.1, f32[1024,128]{1,0:T(8,128)S(1)} %get-tuple-element.33.rest_0_.refs_0_), custom_call_target="tpu_custom_call" | custom-call | bytes 1835008 | tf_op jit(solution)/shard_map/fetch/pallas_call | solution.py:268
  7.3 1.6 %collective-permute-start.1 = (bf16[128,3584]{1,0:T(8,128)(2,1)S(1)}, bf16[128,3584]{1,0:T(8,128)(2,1)S(1)}, u32[]{:S(2)}, u32[]{:S(2)}) collective-permute-start(bf16[128,3584]{1,0:T(8,128)(2,1)S(1)} %leaving.1.refs_4_), channel_id=1, source_target_pairs={{0,8},{8,16},{16,24},{24,0},{1,9},{9,17},{17,25},{25,1},{2,10},{10... | collective-permute-start | bytes 2752520 | tf_op jit(solution)/shard_map/ppermute | solution.py:30
  9.4 1.6 %collective-permute-start.2 = (bf16[2,64,1024]{2,1,0:T(8,128)(2,1)S(1)}, bf16[2,64,1024]{2,1,0:T(8,128)(2,1)S(1)}, u32[]{:S(2)}, u32[]{:S(2)}) collective-permute-start(bf16[2,64,1024]{2,1,0:T(8,128)(2,1)S(1)} %get-tuple-element.37), channel_id=1, source_target_pairs={{0,2},{2,0},{4,6},{6,4},{1,3},{3,1},{5,7},{7,5},{8,10},{10,8},{12,... | collective-permute-start | bytes 786440 | tf_op jit(solution)/shard_map/ppermute | solution.py:20
  11.0 1.5 %collective-permute-start.6 = (bf16[2,64,1024]{2,1,0:T(8,128)(2,1)S(1)}, bf16[2,64,1024]{2,1,0:T(8,128)(2,1)S(1)}, u32[]{:S(2)}, u32[]{:S(2)}) collective-permute-start(bf16[2,64,1024]{2,1,0:T(8,128)(2,1)S(1)} %get-tuple-element.43), channel_id=1, source_target_pairs={{0,4},{2,6},{4,0},{6,2},{1,5},{3,7},{5,1},{7,3},{8,12},{10,14},{12... | collective-permute-start | bytes 786440 | tf_op jit(solution)/shard_map/ppermute | solution.py:20
  13.0 5.7 %collective-permute-done.2.refs_4_.refs_1_ = bf16[2,64,1024]{2,1,0:T(8,128)(2,1)S(1)} collective-permute-done((bf16[2,64,1024]{2,1,0:T(8,128)(2,1)S(1)}, bf16[2,64,1024]{2,1,0:T(8,128)(2,1)S(1)}, u32[]{:S(2)}, u32[]{:S(2)}) %collective-permute-start.2) | collective-permute-done | bytes 262176 | tf_op jit(solution)/shard_map/ppermute | solution.py:20
  19.2 1.6 %collective-permute-start.3 = (bf16[2,64,1024]{2,1,0:T(8,128)(2,1)S(1)}, bf16[2,64,1024]{2,1,0:T(8,128)(2,1)S(1)}, u32[]{:S(2)}, u32[]{:S(2)}) collective-permute-start(bf16[2,64,1024]{2,1,0:T(8,128)(2,1)S(1)} %get-tuple-element.39), channel_id=1, source_target_pairs={{0,2},{2,0},{4,6},{6,4},{1,3},{3,1},{5,7},{7,5},{8,10},{10,8},{12,... | collective-permute-start | bytes 786440 | tf_op jit(solution)/shard_map/ppermute | solution.py:20
  20.8 1.5 %collective-permute-start.4 = (bf16[2,64,1024]{2,1,0:T(8,128)(2,1)S(1)}, bf16[2,64,1024]{2,1,0:T(8,128)(2,1)S(1)}, u32[]{:S(2)}, u32[]{:S(2)}) collective-permute-start(bf16[2,64,1024]{2,1,0:T(8,128)(2,1)S(1)} %get-tuple-element.40), channel_id=1, source_target_pairs={{0,4},{2,6},{4,0},{6,2},{1,5},{3,7},{5,1},{7,3},{8,12},{10,14},{12... | collective-permute-start | bytes 786440 | tf_op jit(solution)/shard_map/ppermute | solution.py:20
  22.3 2.2 %collective-permute-done.6.refs_2_ = bf16[2,64,1024]{2,1,0:T(8,128)(2,1)S(1)} collective-permute-done((bf16[2,64,1024]{2,1,0:T(8,128)(2,1)S(1)}, bf16[2,64,1024]{2,1,0:T(8,128)(2,1)S(1)}, u32[]{:S(2)}, u32[]{:S(2)}) %collective-permute-start.6) | collective-permute-done | bytes 262176 | tf_op jit(solution)/shard_map/ppermute | solution.py:20
  25.5 1.6 %collective-permute-start.14 = (bf16[2,64,1024]{2,1,0:T(8,128)(2,1)S(1)}, bf16[2,64,1024]{2,1,0:T(8,128)(2,1)S(1)}, u32[]{:S(2)}, u32[]{:S(2)}) collective-permute-start(bf16[2,64,1024]{2,1,0:T(8,128)(2,1)S(1)} %share.4.refs_4_), channel_id=1, source_target_pairs={{0,24},{8,16},{16,8},{24,0},{1,25},{9,17},{17,9},{25,1},{2,26},{10... | collective-permute-start | bytes 786440 | tf_op jit(solution)/shard_map/ppermute | solution.py:25
  27.1 2.9 %collective-permute-done.3.refs_1_.refs_5_ = bf16[2,64,1024]{2,1,0:T(8,128)(2,1)S(1)} collective-permute-done((bf16[2,64,1024]{2,1,0:T(8,128)(2,1)S(1)}, bf16[2,64,1024]{2,1,0:T(8,128)(2,1)S(1)}, u32[]{:S(2)}, u32[]{:S(2)}) %collective-permute-start.3) | collective-permute-done | bytes 262176 | tf_op jit(solution)/shard_map/ppermute | solution.py:20
  30.5 1.6 %collective-permute-start.8 = (bf16[2,64,896]{2,1,0:T(8,128)(2,1)S(1)}, bf16[2,64,896]{2,1,0:T(8,128)(2,1)S(1)}, u32[]{:S(2)}, u32[]{:S(2)}) collective-permute-start(bf16[2,64,896]{2,1,0:T(8,128)(2,1)S(1)} %get-tuple-element.45), channel_id=1, source_target_pairs={{0,2},{2,0},{4,6},{6,4},{1,3},{3,1},{5,7},{7,5},{8,10},{10,8},{12,... | collective-permute-start | bytes 688136 | tf_op jit(solution)/shard_map/ppermute | solution.py:20
  32.0 2.6 %collective-permute-done.4.refs_2_ = bf16[2,64,1024]{2,1,0:T(8,128)(2,1)S(1)} collective-permute-done((bf16[2,64,1024]{2,1,0:T(8,128)(2,1)S(1)}, bf16[2,64,1024]{2,1,0:T(8,128)(2,1)S(1)}, u32[]{:S(2)}, u32[]{:S(2)}) %collective-permute-start.4) | collective-permute-done | bytes 262176 | tf_op jit(solution)/shard_map/ppermute | solution.py:20
  34.7 2.4 %collective-permute-start.12 = (bf16[2,64,896]{2,1,0:T(8,128)(2,1)S(1)}, bf16[2,64,896]{2,1,0:T(8,128)(2,1)S(1)}, u32[]{:S(2)}, u32[]{:S(2)}) collective-permute-start(bf16[2,64,896]{2,1,0:T(8,128)(2,1)S(1)} %get-tuple-element.51), channel_id=1, source_target_pairs={{0,4},{2,6},{4,0},{6,2},{1,5},{3,7},{5,1},{7,3},{8,12},{10,14},{12... | collective-permute-start | bytes 688136 | tf_op jit(solution)/shard_map/ppermute | solution.py:20
  37.1 0.9 %collective-permute-start.13 = (bf16[2,64,896]{2,1,0:T(8,128)(2,1)S(1)}, bf16[2,64,896]{2,1,0:T(8,128)(2,1)S(1)}, u32[]{:S(2)}, u32[]{:S(2)}) collective-permute-start(bf16[2,64,896]{2,1,0:T(8,128)(2,1)S(1)} %get-tuple-element.52), channel_id=1, source_target_pairs={{0,6},{2,4},{4,2},{6,0},{1,7},{3,5},{5,3},{7,1},{8,14},{10,12},{12... | collective-permute-start | bytes 688136 | tf_op jit(solution)/shard_map/ppermute | solution.py:20
  38.2 1.6 %collective-permute-start.15 = (bf16[2,64,1024]{2,1,0:T(8,128)(2,1)S(1)}, bf16[2,64,1024]{2,1,0:T(8,128)(2,1)S(1)}, u32[]{:S(2)}, u32[]{:S(2)}) collective-permute-start(bf16[2,64,1024]{2,1,0:T(8,128)(2,1)S(1)} %share.5.refs_4_), channel_id=1, source_target_pairs={{0,24},{8,16},{16,8},{24,0},{1,25},{9,17},{17,9},{25,1},{2,26},{10... | collective-permute-start | bytes 786440 | tf_op jit(solution)/shard_map/ppermute | solution.py:25
  39.8 0.8 %collective-permute-done.8.refs_5_.refs_1_ = bf16[2,64,896]{2,1,0:T(8,128)(2,1)S(1)} collective-permute-done((bf16[2,64,896]{2,1,0:T(8,128)(2,1)S(1)}, bf16[2,64,896]{2,1,0:T(8,128)(2,1)S(1)}, u32[]{:S(2)}, u32[]{:S(2)}) %collective-permute-start.8) | collective-permute-done | bytes 229408 | tf_op jit(solution)/shard_map/ppermute | solution.py:20
  41.1 1.5 %collective-permute-start.10 = (bf16[2,64,640]{2,1,0:T(8,128)(2,1)S(1)}, bf16[2,64,640]{2,1,0:T(8,128)(2,1)S(1)}, u32[]{:S(2)}, u32[]{:S(2)}) collective-permute-start(bf16[2,64,640]{2,1,0:T(8,128)(2,1)S(1)} %get-tuple-element.48), channel_id=1, source_target_pairs={{0,4},{2,6},{4,0},{6,2},{1,5},{3,7},{5,1},{7,3},{8,12},{10,14},{12... | collective-permute-start | bytes 491528 | tf_op jit(solution)/shard_map/ppermute | solution.py:20
  42.6 4.9 %collective-permute-done.14.refs_5_.refs_0_ = bf16[2,64,1024]{2,1,0:T(8,128)(2,1)S(1)} collective-permute-done((bf16[2,64,1024]{2,1,0:T(8,128)(2,1)S(1)}, bf16[2,64,1024]{2,1,0:T(8,128)(2,1)S(1)}, u32[]{:S(2)}, u32[]{:S(2)}) %collective-permute-start.14) | collective-permute-done | bytes 262176 | tf_op jit(solution)/shard_map/ppermute | solution.py:25
  47.5 4.9 %collective-permute-start.11 = (bf16[2,64,640]{2,1,0:T(8,128)(2,1)S(1)}, bf16[2,64,640]{2,1,0:T(8,128)(2,1)S(1)}, u32[]{:S(2)}, u32[]{:S(2)}) collective-permute-start(bf16[2,64,640]{2,1,0:T(8,128)(2,1)S(1)} %get-tuple-element.49), channel_id=1, source_target_pairs={{0,6},{2,4},{4,2},{6,0},{1,7},{3,5},{5,3},{7,1},{8,14},{10,12},{12... | collective-permute-start | bytes 491528 | tf_op jit(solution)/shard_map/ppermute | solution.py:20
  53.1 1.5 %collective-permute-start.17 = (bf16[2,64,896]{2,1,0:T(8,128)(2,1)S(1)}, bf16[2,64,896]{2,1,0:T(8,128)(2,1)S(1)}, u32[]{:S(2)}, u32[]{:S(2)}) collective-permute-start(bf16[2,64,896]{2,1,0:T(8,128)(2,1)S(1)} %share.6.refs_4_), channel_id=1, source_target_pairs={{0,24},{8,16},{16,8},{24,0},{1,25},{9,17},{17,9},{25,1},{2,26},{10... | collective-permute-start | bytes 688136 | tf_op jit(solution)/shard_map/ppermute | solution.py:25
  54.6 2.8 %collective-permute-done.11.refs_3_ = bf16[2,64,640]{2,1,0:T(8,128)(2,1)S(1)} collective-permute-done((bf16[2,64,640]{2,1,0:T(8,128)(2,1)S(1)}, bf16[2,64,640]{2,1,0:T(8,128)(2,1)S(1)}, u32[]{:S(2)}, u32[]{:S(2)}) %collective-permute-start.11) | collective-permute-done | bytes 163872 | tf_op jit(solution)/shard_map/ppermute | solution.py:20
  57.4 3.0 %collective-permute-done.9.refs_1_ = bf16[2,64,640]{2,1,0:T(8,128)(2,1)S(1)} collective-permute-done((bf16[2,64,640]{2,1,0:T(8,128)(2,1)S(1)}, bf16[2,64,640]{2,1,0:T(8,128)(2,1)S(1)}, u32[]{:S(2)}, u32[]{:S(2)}) %collective-permute-start.9) | collective-permute-done | bytes 163872 | tf_op jit(solution)/shard_map/ppermute | solution.py:20
  60.6 0.8 %collective-permute-start.16 = (bf16[2,64,640]{2,1,0:T(8,128)(2,1)S(1)}, bf16[2,64,640]{2,1,0:T(8,128)(2,1)S(1)}, u32[]{:S(2)}, u32[]{:S(2)}) collective-permute-start(bf16[2,64,640]{2,1,0:T(8,128)(2,1)S(1)} %share.7), channel_id=1, source_target_pairs={{0,24},{8,16},{16,8},{24,0},{1,25},{9,17},{17,9},{25,1},{2,26},{10... | collective-permute-start | bytes 491528 | tf_op jit(solution)/shard_map/ppermute | solution.py:25
  62.0 0.9 %place.1.refs_5_ = bf16[1,128,3584]{2,1,0:T(8,128)(2,1)} custom-call(bf16[128,3584]{1,0:T(8,128)(2,1)S(1)} %collective-permute-done.1.refs_0_.refs_5_), custom_call_target="tpu_custom_call" | custom-call | bytes 1835008 | tf_op jit(solution)/shard_map/place/pallas_call | solution.py:333
  63.5 2.9 %collective-permute-done.17.refs_0_ = bf16[2,64,896]{2,1,0:T(8,128)(2,1)S(1)} collective-permute-done((bf16[2,64,896]{2,1,0:T(8,128)(2,1)S(1)}, bf16[2,64,896]{2,1,0:T(8,128)(2,1)S(1)}, u32[]{:S(2)}, u32[]{:S(2)}) %collective-permute-start.17) | collective-permute-done | bytes 229408 | tf_op jit(solution)/shard_map/ppermute | solution.py:25
  67.0 2.9 %collective-permute-done.16.refs_0_ = bf16[2,64,640]{2,1,0:T(8,128)(2,1)S(1)} collective-permute-done((bf16[2,64,640]{2,1,0:T(8,128)(2,1)S(1)}, bf16[2,64,640]{2,1,0:T(8,128)(2,1)S(1)}, u32[]{:S(2)}, u32[]{:S(2)}) %collective-permute-start.16) | collective-permute-done | bytes 163872 | tf_op jit(solution)/shard_map/ppermute | solution.py:25
  70.3 1.6 %collective-permute-start.18 = (f32[8,128]{1,0:T(8,128)S(1)}, f32[8,128]{1,0:T(8,128)S(1)}, u32[]{:S(2)}, u32[]{:S(2)}) collective-permute-start(f32[8,128]{1,0:T(8,128)S(1)} %get-tuple-element.56.refs_0_), channel_id=1, source_target_pairs={{0,2},{2,0},{4,6},{6,4},{1,3},{3,1},{5,7},{7,5},{8,10},{10,8},{12,... | collective-permute-start | bytes 12296 | tf_op jit(solution)/shard_map/ppermute | solution.py:20
  71.9 1.5 %collective-permute-start.19 = (f32[8,128]{1,0:T(8,128)S(1)}, f32[8,128]{1,0:T(8,128)S(1)}, u32[]{:S(2)}, u32[]{:S(2)}) collective-permute-start(f32[8,128]{1,0:T(8,128)S(1)} %get-tuple-element.56.refs_0_), channel_id=1, source_target_pairs={{0,4},{2,6},{4,0},{6,2},{1,5},{3,7},{5,1},{7,3},{8,12},{10,14},{12... | collective-permute-start | bytes 12296 | tf_op jit(solution)/shard_map/ppermute | solution.py:20
  74.0 1.5 %collective-permute-done.19.refs_2_ = f32[8,128]{1,0:T(8,128)S(1)} collective-permute-done((f32[8,128]{1,0:T(8,128)S(1)}, f32[8,128]{1,0:T(8,128)S(1)}, u32[]{:S(2)}, u32[]{:S(2)}) %collective-permute-start.19) | collective-permute-done | bytes 4128 | tf_op jit(solution)/shard_map/ppermute | solution.py:20
  75.5 2.4 %collective-permute-done.20.refs_3_ = f32[8,128]{1,0:T(8,128)S(1)} collective-permute-done((f32[8,128]{1,0:T(8,128)S(1)}, f32[8,128]{1,0:T(8,128)S(1)}, u32[]{:S(2)}, u32[]{:S(2)}) %collective-permute-start.20) | collective-permute-done | bytes 4128 | tf_op jit(solution)/shard_map/ppermute | solution.py:20
  77.9 1.2 %codes.1 = (bf16[2,1,64,3584]{3,2,1,0:T(8,128)(2,1)}, f32[2,1,2,28]{3,2,1,0:T(2,128)}) custom-call(f32[8,128]{1,0:T(8,128)S(1)} %get-tuple-element.56.refs_0_, f32[8,128]{1,0:T(8,128)S(1)} %collective-permute-done.18.refs_1_, f32[8,128]{1,0:T(8,128)S(1)} %collective-permute-done.19.refs_2_, f32[8,128]{1,0:T(8,128)S(1)} %collective-permute-done.20.refs_3_, ...), custom_call_target="tpu_custom_call" | custom-call | flops 917504 | bytes 1851392 | tf_op jit(solution)/shard_map/codes/pallas_call | solution.py:51
  (35 shorter events, 8.0 us)
Async XLA Ops:
  4.8 2.0 %collective-permute-start = (f32[1024,128]{1,0:T(8,128)S(1)}, f32[1024,128]{1,0:T(8,128)S(1)}, u32[]{:S(2)}, u32[]{:S(2)}) collective-permute-start(f32[1024,128]{1,0:T(8,128)S(1)} %get-tuple-element.33.rest_0_.refs_0_), channel_id=1, source_target_pairs={{0,1},{1,0},{2,3},{3,2},{4,5},{5,4},{6,7},{7,6},{8,9},{9,8},{10,11... | collective-permute-start | bytes 1572872 | tf_op jit(solution)/shard_map/ppermute | solution.py:20
  7.3 30.8 %collective-permute-start.1 = (bf16[128,3584]{1,0:T(8,128)(2,1)S(1)}, bf16[128,3584]{1,0:T(8,128)(2,1)S(1)}, u32[]{:S(2)}, u32[]{:S(2)}) collective-permute-start(bf16[128,3584]{1,0:T(8,128)(2,1)S(1)} %leaving.1.refs_4_), channel_id=1, source_target_pairs={{0,8},{8,16},{16,24},{24,0},{1,9},{9,17},{17,25},{25,1},{2,10},{10... | collective-permute-start | bytes 2752520 | tf_op jit(solution)/shard_map/ppermute | solution.py:30
  9.4 9.3 %collective-permute-start.2 = (bf16[2,64,1024]{2,1,0:T(8,128)(2,1)S(1)}, bf16[2,64,1024]{2,1,0:T(8,128)(2,1)S(1)}, u32[]{:S(2)}, u32[]{:S(2)}) collective-permute-start(bf16[2,64,1024]{2,1,0:T(8,128)(2,1)S(1)} %get-tuple-element.37), channel_id=1, source_target_pairs={{0,2},{2,0},{4,6},{6,4},{1,3},{3,1},{5,7},{7,5},{8,10},{10,8},{12,... | collective-permute-start | bytes 786440 | tf_op jit(solution)/shard_map/ppermute | solution.py:20
  11.0 13.5 %collective-permute-start.6 = (bf16[2,64,1024]{2,1,0:T(8,128)(2,1)S(1)}, bf16[2,64,1024]{2,1,0:T(8,128)(2,1)S(1)}, u32[]{:S(2)}, u32[]{:S(2)}) collective-permute-start(bf16[2,64,1024]{2,1,0:T(8,128)(2,1)S(1)} %get-tuple-element.43), channel_id=1, source_target_pairs={{0,4},{2,6},{4,0},{6,2},{1,5},{3,7},{5,1},{7,3},{8,12},{10,14},{12... | collective-permute-start | bytes 786440 | tf_op jit(solution)/shard_map/ppermute | solution.py:20
  12.5 12.8 %collective-permute-start.7 = (bf16[2,64,1024]{2,1,0:T(8,128)(2,1)S(1)}, bf16[2,64,1024]{2,1,0:T(8,128)(2,1)S(1)}, u32[]{:S(2)}, u32[]{:S(2)}) collective-permute-start(bf16[2,64,1024]{2,1,0:T(8,128)(2,1)S(1)} %get-tuple-element.44), channel_id=1, source_target_pairs={{0,6},{2,4},{4,2},{6,0},{1,7},{3,5},{5,3},{7,1},{8,14},{10,12},{12... | collective-permute-start | bytes 786440 | tf_op jit(solution)/shard_map/ppermute | solution.py:20
  19.2 10.7 %collective-permute-start.3 = (bf16[2,64,1024]{2,1,0:T(8,128)(2,1)S(1)}, bf16[2,64,1024]{2,1,0:T(8,128)(2,1)S(1)}, u32[]{:S(2)}, u32[]{:S(2)}) collective-permute-start(bf16[2,64,1024]{2,1,0:T(8,128)(2,1)S(1)} %get-tuple-element.39), channel_id=1, source_target_pairs={{0,2},{2,0},{4,6},{6,4},{1,3},{3,1},{5,7},{7,5},{8,10},{10,8},{12,... | collective-permute-start | bytes 786440 | tf_op jit(solution)/shard_map/ppermute | solution.py:20
  20.8 13.9 %collective-permute-start.4 = (bf16[2,64,1024]{2,1,0:T(8,128)(2,1)S(1)}, bf16[2,64,1024]{2,1,0:T(8,128)(2,1)S(1)}, u32[]{:S(2)}, u32[]{:S(2)}) collective-permute-start(bf16[2,64,1024]{2,1,0:T(8,128)(2,1)S(1)} %get-tuple-element.40), channel_id=1, source_target_pairs={{0,4},{2,6},{4,0},{6,2},{1,5},{3,7},{5,1},{7,3},{8,12},{10,14},{12... | collective-permute-start | bytes 786440 | tf_op jit(solution)/shard_map/ppermute | solution.py:20
  24.5 12.6 %collective-permute-start.5 = (bf16[2,64,1024]{2,1,0:T(8,128)(2,1)S(1)}, bf16[2,64,1024]{2,1,0:T(8,128)(2,1)S(1)}, u32[]{:S(2)}, u32[]{:S(2)}) collective-permute-start(bf16[2,64,1024]{2,1,0:T(8,128)(2,1)S(1)} %get-tuple-element.41), channel_id=1, source_target_pairs={{0,6},{2,4},{4,2},{6,0},{1,7},{3,5},{5,3},{7,1},{8,14},{10,12},{12... | collective-permute-start | bytes 786440 | tf_op jit(solution)/shard_map/ppermute | solution.py:20
  25.5 22.0 %collective-permute-start.14 = (bf16[2,64,1024]{2,1,0:T(8,128)(2,1)S(1)}, bf16[2,64,1024]{2,1,0:T(8,128)(2,1)S(1)}, u32[]{:S(2)}, u32[]{:S(2)}) collective-permute-start(bf16[2,64,1024]{2,1,0:T(8,128)(2,1)S(1)} %share.4.refs_4_), channel_id=1, source_target_pairs={{0,24},{8,16},{16,8},{24,0},{1,25},{9,17},{17,9},{25,1},{2,26},{10... | collective-permute-start | bytes 786440 | tf_op jit(solution)/shard_map/ppermute | solution.py:25
  30.5 10.2 %collective-permute-start.8 = (bf16[2,64,896]{2,1,0:T(8,128)(2,1)S(1)}, bf16[2,64,896]{2,1,0:T(8,128)(2,1)S(1)}, u32[]{:S(2)}, u32[]{:S(2)}) collective-permute-start(bf16[2,64,896]{2,1,0:T(8,128)(2,1)S(1)} %get-tuple-element.45), channel_id=1, source_target_pairs={{0,2},{2,0},{4,6},{6,4},{1,3},{3,1},{5,7},{7,5},{8,10},{10,8},{12,... | collective-permute-start | bytes 688136 | tf_op jit(solution)/shard_map/ppermute | solution.py:20
  34.7 17.7 %collective-permute-start.12 = (bf16[2,64,896]{2,1,0:T(8,128)(2,1)S(1)}, bf16[2,64,896]{2,1,0:T(8,128)(2,1)S(1)}, u32[]{:S(2)}, u32[]{:S(2)}) collective-permute-start(bf16[2,64,896]{2,1,0:T(8,128)(2,1)S(1)} %get-tuple-element.51), channel_id=1, source_target_pairs={{0,4},{2,6},{4,0},{6,2},{1,5},{3,7},{5,1},{7,3},{8,12},{10,14},{12... | collective-permute-start | bytes 688136 | tf_op jit(solution)/shard_map/ppermute | solution.py:20
  37.1 15.9 %collective-permute-start.13 = (bf16[2,64,896]{2,1,0:T(8,128)(2,1)S(1)}, bf16[2,64,896]{2,1,0:T(8,128)(2,1)S(1)}, u32[]{:S(2)}, u32[]{:S(2)}) collective-permute-start(bf16[2,64,896]{2,1,0:T(8,128)(2,1)S(1)} %get-tuple-element.52), channel_id=1, source_target_pairs={{0,6},{2,4},{4,2},{6,0},{1,7},{3,5},{5,3},{7,1},{8,14},{10,12},{12... | collective-permute-start | bytes 688136 | tf_op jit(solution)/shard_map/ppermute | solution.py:20
  38.1 23.2 %copy-start = (f32[2,1,64,3584]{3,2,1,0:T(8,128)S(1)}, f32[2,1,64,3584]{3,2,1,0:T(8,128)}, u32[]{:S(2)}) copy-start(f32[2,1,64,3584]{3,2,1,0:T(8,128)} %refs_1_.9) | copy-start | bytes 5505028
  38.2 23.2 %copy-start.1 = (bf16[2,1,64,3584]{3,2,1,0:T(8,128)(2,1)S(1)}, bf16[2,1,64,3584]{3,2,1,0:T(8,128)(2,1)}, u32[]{:S(2)}) copy-start(bf16[2,1,64,3584]{3,2,1,0:T(8,128)(2,1)} %refs_2_.9) | copy-start | bytes 2752516
  38.2 23.2 %copy-start.2 = (bf16[2,1,64,3584]{3,2,1,0:T(8,128)(2,1)S(1)}, bf16[2,1,64,3584]{3,2,1,0:T(8,128)(2,1)}, u32[]{:S(2)}) copy-start(bf16[2,1,64,3584]{3,2,1,0:T(8,128)(2,1)} %refs_3_.9) | copy-start | bytes 2752516
  38.2 22.3 %collective-permute-start.15 = (bf16[2,64,1024]{2,1,0:T(8,128)(2,1)S(1)}, bf16[2,64,1024]{2,1,0:T(8,128)(2,1)S(1)}, u32[]{:S(2)}, u32[]{:S(2)}) collective-permute-start(bf16[2,64,1024]{2,1,0:T(8,128)(2,1)S(1)} %share.5.refs_4_), channel_id=1, source_target_pairs={{0,24},{8,16},{16,8},{24,0},{1,25},{9,17},{17,9},{25,1},{2,26},{10... | collective-permute-start | bytes 786440 | tf_op jit(solution)/shard_map/ppermute | solution.py:25
  41.1 13.5 %collective-permute-start.10 = (bf16[2,64,640]{2,1,0:T(8,128)(2,1)S(1)}, bf16[2,64,640]{2,1,0:T(8,128)(2,1)S(1)}, u32[]{:S(2)}, u32[]{:S(2)}) collective-permute-start(bf16[2,64,640]{2,1,0:T(8,128)(2,1)S(1)} %get-tuple-element.48), channel_id=1, source_target_pairs={{0,4},{2,6},{4,0},{6,2},{1,5},{3,7},{5,1},{7,3},{8,12},{10,14},{12... | collective-permute-start | bytes 491528 | tf_op jit(solution)/shard_map/ppermute | solution.py:20
  47.5 9.9 %collective-permute-start.11 = (bf16[2,64,640]{2,1,0:T(8,128)(2,1)S(1)}, bf16[2,64,640]{2,1,0:T(8,128)(2,1)S(1)}, u32[]{:S(2)}, u32[]{:S(2)}) collective-permute-start(bf16[2,64,640]{2,1,0:T(8,128)(2,1)S(1)} %get-tuple-element.49), channel_id=1, source_target_pairs={{0,6},{2,4},{4,2},{6,0},{1,7},{3,5},{5,3},{7,1},{8,14},{10,12},{12... | collective-permute-start | bytes 491528 | tf_op jit(solution)/shard_map/ppermute | solution.py:20
  52.4 8.0 %collective-permute-start.9 = (bf16[2,64,640]{2,1,0:T(8,128)(2,1)S(1)}, bf16[2,64,640]{2,1,0:T(8,128)(2,1)S(1)}, u32[]{:S(2)}, u32[]{:S(2)}) collective-permute-start(bf16[2,64,640]{2,1,0:T(8,128)(2,1)S(1)} %get-tuple-element.47), channel_id=1, source_target_pairs={{0,2},{2,0},{4,6},{6,4},{1,3},{3,1},{5,7},{7,5},{8,10},{10,8},{12,... | collective-permute-start | bytes 491528 | tf_op jit(solution)/shard_map/ppermute | solution.py:20
  53.1 13.4 %collective-permute-start.17 = (bf16[2,64,896]{2,1,0:T(8,128)(2,1)S(1)}, bf16[2,64,896]{2,1,0:T(8,128)(2,1)S(1)}, u32[]{:S(2)}, u32[]{:S(2)}) collective-permute-start(bf16[2,64,896]{2,1,0:T(8,128)(2,1)S(1)} %share.6.refs_4_), channel_id=1, source_target_pairs={{0,24},{8,16},{16,8},{24,0},{1,25},{9,17},{17,9},{25,1},{2,26},{10... | collective-permute-start | bytes 688136 | tf_op jit(solution)/shard_map/ppermute | solution.py:25
  60.6 9.3 %collective-permute-start.16 = (bf16[2,64,640]{2,1,0:T(8,128)(2,1)S(1)}, bf16[2,64,640]{2,1,0:T(8,128)(2,1)S(1)}, u32[]{:S(2)}, u32[]{:S(2)}) collective-permute-start(bf16[2,64,640]{2,1,0:T(8,128)(2,1)S(1)} %share.7), channel_id=1, source_target_pairs={{0,24},{8,16},{16,8},{24,0},{1,25},{9,17},{17,9},{25,1},{2,26},{10... | collective-permute-start | bytes 491528 | tf_op jit(solution)/shard_map/ppermute | solution.py:25
  62.9 6.9 %copy-start.3 = (bf16[1,128,3584]{2,1,0:T(8,128)(2,1)S(1)}, bf16[1,128,3584]{2,1,0:T(8,128)(2,1)}, u32[]{:S(2)}) copy-start(bf16[1,128,3584]{2,1,0:T(8,128)(2,1)} %place.1.refs_5_) | copy-start | bytes 2752516
  70.3 3.7 %collective-permute-start.18 = (f32[8,128]{1,0:T(8,128)S(1)}, f32[8,128]{1,0:T(8,128)S(1)}, u32[]{:S(2)}, u32[]{:S(2)}) collective-permute-start(f32[8,128]{1,0:T(8,128)S(1)} %get-tuple-element.56.refs_0_), channel_id=1, source_target_pairs={{0,2},{2,0},{4,6},{6,4},{1,3},{3,1},{5,7},{7,5},{8,10},{10,8},{12,... | collective-permute-start | bytes 12296 | tf_op jit(solution)/shard_map/ppermute | solution.py:20
  71.9 3.6 %collective-permute-start.19 = (f32[8,128]{1,0:T(8,128)S(1)}, f32[8,128]{1,0:T(8,128)S(1)}, u32[]{:S(2)}, u32[]{:S(2)}) collective-permute-start(f32[8,128]{1,0:T(8,128)S(1)} %get-tuple-element.56.refs_0_), channel_id=1, source_target_pairs={{0,4},{2,6},{4,0},{6,2},{1,5},{3,7},{5,1},{7,3},{8,12},{10,14},{12... | collective-permute-start | bytes 12296 | tf_op jit(solution)/shard_map/ppermute | solution.py:20
  73.4 4.5 %collective-permute-start.20 = (f32[8,128]{1,0:T(8,128)S(1)}, f32[8,128]{1,0:T(8,128)S(1)}, u32[]{:S(2)}, u32[]{:S(2)}) collective-permute-start(f32[8,128]{1,0:T(8,128)S(1)} %get-tuple-element.56.refs_0_), channel_id=1, source_target_pairs={{0,6},{2,4},{4,2},{6,0},{1,7},{3,5},{5,3},{7,1},{8,14},{10,12},{12... | collective-permute-start | bytes 12296 | tf_op jit(solution)/shard_map/ppermute | solution.py:20

commit v7 on v6

--- a/solution.py
+++ b/solution.py
@@ -200,18 +200,16 @@
         )
 
 
-def code_kernel(group, peak_refs, fresh_refs, code_ref, scale_ref):
-    blocks = scale_ref.shape[3]
-    mine = lax.axis_index("expert") // group
-    tops = []
-    for far in range(len(peak_refs) // group):
-        top = peak_refs[far * group][...]
-        for ref in peak_refs[far * group + 1 : (far + 1) * group]:
-            top = jnp.maximum(top, ref[...])
-        tops.append(top + 1e-06)
-        for side in range(2):
-            scale_ref[side, 0, pl.ds(mine ^ far, 1), :] = tops[far][side : side + 1, :blocks]
-    column = (1.0 / tops[0]).T
+def merged(refs):
+    top = refs[0][...]
+    for ref in refs[1:]:
+        top = jnp.maximum(top, ref[...])
+    return top + 1e-06
+
+
+def code_kernel(group, *refs):
+    peak_refs, fresh_refs, code_ref = refs[:group], refs[group:-1], refs[-1]
+    column = (1.0 / merged(peak_refs)).T
     for side in range(2):
         inverse = jnp.broadcast_to(column[:, side : side + 1], (LANES, LANES))
         block = 0
@@ -223,6 +221,16 @@
                 block += 1
 
 
+def scale_kernel(group, experts, *refs):
+    peak_refs, scale_ref = refs[:experts], refs[-1]
+    blocks = scale_ref.shape[3]
+    mine = lax.axis_index("expert") // group
+    for far in range(len(peak_refs) // group):
+        top = merged(peak_refs[far * group : (far + 1) * group])
+        for side in range(2):
+            scale_ref[side, 0, pl.ds(mine ^ far, 1), :] = top[side : side + 1, :blocks]
+
+
 def place_kernel(start, in_ref, *rest):
     out_ref, sem = rest[-2:]
     copy = pltpu.make_async_copy(in_ref, out_ref.at[0, pl.ds(start, in_ref.shape[0])], sem)
@@ -237,7 +245,7 @@
     depth = latent // experts
     blocks = width // LANES
     tiles = 2
-    weights = [8, 8, 7, 5]
+    weights = [8, 7, 7, 6]
     edges = [blocks * sum(weights[:k]) // sum(weights) * LANES for k in range(len(weights) + 1)]
     chunks = list(zip(edges[:-1], edges[1:]))
 
@@ -305,7 +313,7 @@
             flops=4 * tokens * latent * (stop - start),
         )
 
-    head = 128
+    head = 112
     first_rows = leaving(0, head)
     left_head = turned(first_rows, "pipe")
     first = grads(0, first_rows)
@@ -321,18 +329,17 @@
                 shape(own.shape, BF16),
                 own,
                 *others[-1],
-                *shares[-1:],
                 *after,
                 read=experts,
             )
         )
         arrived.append(mirrored(shares[-1], "pipe"))
-    left_tail = None
-
-    def place(start, rows, *kept):
+    left_tail = turned(leaving(head, tokens - head, arrived[-2]), "pipe")
+
+    def place(start, rows, kept=(), after=()):
         return pl.pallas_call(
             lambda *refs: place_kernel(start, *refs),
-            in_specs=[ANY] * (1 + len(kept)),
+            in_specs=[ANY] * (1 + len(kept) + len(after)),
             out_specs=ANY,
             out_shape=shape((1, tokens, width), BF16),
             scratch_shapes=[pltpu.SemaphoreType.DMA],
@@ -340,7 +347,7 @@
             compiler_params=ROOM,
             cost_estimate=pl.CostEstimate(flops=0, bytes_accessed=4 * rows.shape[0] * width, transcendentals=0),
             name="place",
-        )(rows, *kept)
+        )(rows, *kept, *after)
 
     placed = place(0, left_head)
 
@@ -366,17 +373,24 @@
 
     group = LANES // depth
     peak_rows = [peaks] + [exchange(peaks, "expert", k) for k in range(1, experts)]
-    count = len(peak_rows)
-    coded, scales = call(
-        lambda *refs: code_kernel(group, refs[:count], refs[count:-2], *refs[-2:]),
+    coded = call(
+        lambda *refs: code_kernel(group, *refs),
         "codes",
-        [shape((2, 1, depth, width), BF16), shape((2, 1, experts // group, blocks), F32)],
-        *peak_rows,
+        shape((2, 1, depth, width), BF16),
+        *peak_rows[:group],
         *fresh,
-        read=count + len(fresh),
+        read=group + len(fresh),
         flops=4 * depth * width,
     )
-    return (placed, coded, scales)
+    scales = call(
+        lambda *refs: scale_kernel(group, experts, *refs),
+        "scales",
+        shape((2, 1, experts // group, blocks), F32),
+        *peak_rows,
+        coded,
+        read=experts,
+    )
+    return (place(head, left_tail, (placed,), (coded,)), coded, scales)
 
 
 def solution(mesh):

time: 79.3 us -> 82 us (1.034)
  the two profiles are of different devices: /device:TPU:8 before, /device:TPU:0 now
where the time goes in v7:
time: 82 us; the launch traced here: 81.7 us
  starting transfers between devices  45.7 us (56%)
  waiting for transfers between devices  18.4 us (22%)
  Pallas kernels  14.4 us (18%)
  local copies, waits for them, and re-layouts  2.46 us (3%)
    ppermute x16, starting transfers between devices, exchange(): return lax.ppermute(block, axis, [(i, i ^ offset) for i in range(count)])  20.7 us
    ppermute x16, waiting for transfers between devices, exchange(): return lax.ppermute(block, axis, [(i, i ^ offset) for i in range(count)])  18.4 us
    ppermute x2, starting transfers between devices, turned(): lax.ppermute(block, axis, [(i, (i + 1) % count) for i in range(count)])  15.2 us
    ppermute x4, starting transfers between devices, mirrored(): return lax.ppermute(block, axis, [(i, count - 1 - i) for i in range(count)])  9.79 us
    pallas_call x16, Pallas kernels, call(): pl.pallas_call(kernel, in_specs=[VMEM] * read + [ANY] * (len(operands) -...  7.24 us
    pallas_call x1, Pallas kernels, shards(): pl.pallas_call(lambda *refs: latent_kernel(tiles, *refs), in_specs=[ANY]...  4.12 us
    unnamed x12, local copies, waits for them, and re-layouts  2.46 us
  transfers between devices with their start and end apart: 22, of which 10 were waited for; matrix products, arithmetic and copies ran while one was open for 0% of the time, Pallas kernels for 11%

profile of v7, /device:TPU:0, one launch (start us, length us, event | category | flops | bytes accessed | tf_op | source)
XLA Modules:
  0.0 81.7 jit_solution(11342528632513420407)
XLA Ops:
  0.6 4.1 %latents.1 = (f32[1024,128]{1,0:T(8,128)S(1)}, bf16[128,3584]{1,0:T(8,128)(2,1)S(1)}, bf16[128,3584]{1,0:T(8,128)(2,1)S(1)}, bf16[128,3584]{1,0:T(8,128)(2,1)S(1)}) custom-call(bf16[1,128,3584]{2,1,0:T(8,128)(2,1)} %refs_0_.1, bf16[1,128,3584]{2,1,0:T(8,128)(2,1)} %refs_1_.5, bf16[1,128,3584]{2,1,0:T(8,128)(2,1)} %refs_2_.5, ...), custom_call_target="tpu_custom_call" | custom-call | flops 704643072 | bytes 8257536 | tf_op jit(solution)/shard_map/latents/pallas_call | solution.py:257
  5.3 1.5 %fetch.1.refs_3_ = bf16[256,3584]{1,0:T(8,128)(2,1)S(1)} custom-call(bf16[2,1,256,3584]{3,2,1,0:T(8,128)(2,1)} %in_ref.1, f32[1024,128]{1,0:T(8,128)S(1)} %get-tuple-element.31.rest_0_.refs_0_), custom_call_target="tpu_custom_call" | custom-call | bytes 1835008 | tf_op jit(solution)/shard_map/fetch/pallas_call | solution.py:276
  7.3 3.0 %collective-permute-start.11 = (bf16[112,3584]{1,0:T(8,128)(2,1)S(1)}, bf16[112,3584]{1,0:T(8,128)(2,1)S(1)}, u32[]{:S(2)}, u32[]{:S(2)}) collective-permute-start(bf16[112,3584]{1,0:T(8,128)(2,1)S(1)} %leaving.2.refs_4_), channel_id=1, source_target_pairs={{0,8},{8,16},{16,24},{24,0},{1,9},{9,17},{17,25},{25,1},{2,10},{10... | collective-permute-start | bytes 2408456 | tf_op jit(solution)/shard_map/ppermute | solution.py:30
  10.9 1.6 %collective-permute-start.1 = (bf16[2,64,1024]{2,1,0:T(8,128)(2,1)S(1)}, bf16[2,64,1024]{2,1,0:T(8,128)(2,1)S(1)}, u32[]{:S(2)}, u32[]{:S(2)}) collective-permute-start(bf16[2,64,1024]{2,1,0:T(8,128)(2,1)S(1)} %get-tuple-element.36), channel_id=1, source_target_pairs={{0,2},{2,0},{4,6},{6,4},{1,3},{3,1},{5,7},{7,5},{8,10},{10,8},{12,... | collective-permute-start | bytes 786440 | tf_op jit(solution)/shard_map/ppermute | solution.py:20
  12.4 1.5 %collective-permute-start.2 = (bf16[2,64,1024]{2,1,0:T(8,128)(2,1)S(1)}, bf16[2,64,1024]{2,1,0:T(8,128)(2,1)S(1)}, u32[]{:S(2)}, u32[]{:S(2)}) collective-permute-start(bf16[2,64,1024]{2,1,0:T(8,128)(2,1)S(1)} %get-tuple-element.37), channel_id=1, source_target_pairs={{0,4},{2,6},{4,0},{6,2},{1,5},{3,7},{5,1},{7,3},{8,12},{10,14},{12... | collective-permute-start | bytes 786440 | tf_op jit(solution)/shard_map/ppermute | solution.py:20
  14.4 5.7 %collective-permute-done.1.refs_1_.refs_4_ = bf16[2,64,1024]{2,1,0:T(8,128)(2,1)S(1)} collective-permute-done((bf16[2,64,1024]{2,1,0:T(8,128)(2,1)S(1)}, bf16[2,64,1024]{2,1,0:T(8,128)(2,1)S(1)}, u32[]{:S(2)}, u32[]{:S(2)}) %collective-permute-start.1) | collective-permute-done | bytes 262176 | tf_op jit(solution)/shard_map/ppermute | solution.py:20
  20.6 1.6 %collective-permute-start.4 = (bf16[2,64,896]{2,1,0:T(8,128)(2,1)S(1)}, bf16[2,64,896]{2,1,0:T(8,128)(2,1)S(1)}, u32[]{:S(2)}, u32[]{:S(2)}) collective-permute-start(bf16[2,64,896]{2,1,0:T(8,128)(2,1)S(1)} %get-tuple-element.39), channel_id=1, source_target_pairs={{0,2},{2,0},{4,6},{6,4},{1,3},{3,1},{5,7},{7,5},{8,10},{10,8},{12,... | collective-permute-start | bytes 688136 | tf_op jit(solution)/shard_map/ppermute | solution.py:20
  22.2 1.5 %collective-permute-start.12 = (bf16[2,64,896]{2,1,0:T(8,128)(2,1)S(1)}, bf16[2,64,896]{2,1,0:T(8,128)(2,1)S(1)}, u32[]{:S(2)}, u32[]{:S(2)}) collective-permute-start(bf16[2,64,896]{2,1,0:T(8,128)(2,1)S(1)} %get-tuple-element.45), channel_id=1, source_target_pairs={{0,4},{2,6},{4,0},{6,2},{1,5},{3,7},{5,1},{7,3},{8,12},{10,14},{12... | collective-permute-start | bytes 688136 | tf_op jit(solution)/shard_map/ppermute | solution.py:20
  23.7 2.3 %collective-permute-done.2.refs_2_ = bf16[2,64,1024]{2,1,0:T(8,128)(2,1)S(1)} collective-permute-done((bf16[2,64,1024]{2,1,0:T(8,128)(2,1)S(1)}, bf16[2,64,1024]{2,1,0:T(8,128)(2,1)S(1)}, u32[]{:S(2)}, u32[]{:S(2)}) %collective-permute-start.2) | collective-permute-done | bytes 262176 | tf_op jit(solution)/shard_map/ppermute | solution.py:20
  25.9 0.8 collective-permute-start.13
  26.9 2.5 %collective-permute-start.8 = (bf16[2,64,1024]{2,1,0:T(8,128)(2,1)S(1)}, bf16[2,64,1024]{2,1,0:T(8,128)(2,1)S(1)}, u32[]{:S(2)}, u32[]{:S(2)}) collective-permute-start(bf16[2,64,1024]{2,1,0:T(8,128)(2,1)S(1)} %share.4.refs_4_), channel_id=1, source_target_pairs={{0,24},{8,16},{16,8},{24,0},{1,25},{9,17},{17,9},{25,1},{2,26},{10... | collective-permute-start | bytes 786440 | tf_op jit(solution)/shard_map/ppermute | solution.py:25
  29.4 1.3 %collective-permute-done.4.refs_5_.refs_1_ = bf16[2,64,896]{2,1,0:T(8,128)(2,1)S(1)} collective-permute-done((bf16[2,64,896]{2,1,0:T(8,128)(2,1)S(1)}, bf16[2,64,896]{2,1,0:T(8,128)(2,1)S(1)}, u32[]{:S(2)}, u32[]{:S(2)}) %collective-permute-start.4) | collective-permute-done | bytes 229408 | tf_op jit(solution)/shard_map/ppermute | solution.py:20
  31.2 1.8 %collective-permute-start.5 = (bf16[2,64,896]{2,1,0:T(8,128)(2,1)S(1)}, bf16[2,64,896]{2,1,0:T(8,128)(2,1)S(1)}, u32[]{:S(2)}, u32[]{:S(2)}) collective-permute-start(bf16[2,64,896]{2,1,0:T(8,128)(2,1)S(1)} %get-tuple-element.41), channel_id=1, source_target_pairs={{0,2},{2,0},{4,6},{6,4},{1,3},{3,1},{5,7},{7,5},{8,10},{10,8},{12,... | collective-permute-start | bytes 688136 | tf_op jit(solution)/shard_map/ppermute | solution.py:20
  33.0 1.7 %collective-permute-done.12.refs_2_ = bf16[2,64,896]{2,1,0:T(8,128)(2,1)S(1)} collective-permute-done((bf16[2,64,896]{2,1,0:T(8,128)(2,1)S(1)}, bf16[2,64,896]{2,1,0:T(8,128)(2,1)S(1)}, u32[]{:S(2)}, u32[]{:S(2)}) %collective-permute-start.12) | collective-permute-done | bytes 229408 | tf_op jit(solution)/shard_map/ppermute | solution.py:20
  34.7 1.7 %collective-permute-start.6 = (bf16[2,64,896]{2,1,0:T(8,128)(2,1)S(1)}, bf16[2,64,896]{2,1,0:T(8,128)(2,1)S(1)}, u32[]{:S(2)}, u32[]{:S(2)}) collective-permute-start(bf16[2,64,896]{2,1,0:T(8,128)(2,1)S(1)} %get-tuple-element.42), channel_id=1, source_target_pairs={{0,4},{2,6},{4,0},{6,2},{1,5},{3,7},{5,1},{7,3},{8,12},{10,14},{12... | collective-permute-start | bytes 688136 | tf_op jit(solution)/shard_map/ppermute | solution.py:20
  36.6 1.4 %collective-permute-start.7 = (bf16[2,64,896]{2,1,0:T(8,128)(2,1)S(1)}, bf16[2,64,896]{2,1,0:T(8,128)(2,1)S(1)}, u32[]{:S(2)}, u32[]{:S(2)}) collective-permute-start(bf16[2,64,896]{2,1,0:T(8,128)(2,1)S(1)} %get-tuple-element.43), channel_id=1, source_target_pairs={{0,6},{2,4},{4,2},{6,0},{1,7},{3,5},{5,3},{7,1},{8,14},{10,12},{12... | collective-permute-start | bytes 688136 | tf_op jit(solution)/shard_map/ppermute | solution.py:20
  38.2 2.3 %collective-permute-start.17 = (bf16[2,64,896]{2,1,0:T(8,128)(2,1)S(1)}, bf16[2,64,896]{2,1,0:T(8,128)(2,1)S(1)}, u32[]{:S(2)}, u32[]{:S(2)}) collective-permute-start(bf16[2,64,896]{2,1,0:T(8,128)(2,1)S(1)} %share.6.refs_4_), channel_id=1, source_target_pairs={{0,24},{8,16},{16,8},{24,0},{1,25},{9,17},{17,9},{25,1},{2,26},{10... | collective-permute-start | bytes 688136 | tf_op jit(solution)/shard_map/ppermute | solution.py:25
  40.5 0.9 %collective-permute-done.5.refs_1_.refs_5_ = bf16[2,64,896]{2,1,0:T(8,128)(2,1)S(1)} collective-permute-done((bf16[2,64,896]{2,1,0:T(8,128)(2,1)S(1)}, bf16[2,64,896]{2,1,0:T(8,128)(2,1)S(1)}, u32[]{:S(2)}, u32[]{:S(2)}) %collective-permute-start.5) | collective-permute-done | bytes 229408 | tf_op jit(solution)/shard_map/ppermute | solution.py:20
  42.6 1.5 %collective-permute-start.15 = (bf16[2,64,768]{2,1,0:T(8,128)(2,1)S(1)}, bf16[2,64,768]{2,1,0:T(8,128)(2,1)S(1)}, u32[]{:S(2)}, u32[]{:S(2)}) collective-permute-start(bf16[2,64,768]{2,1,0:T(8,128)(2,1)S(1)} %get-tuple-element.49), channel_id=1, source_target_pairs={{0,4},{2,6},{4,0},{6,2},{1,5},{3,7},{5,1},{7,3},{8,12},{10,14},{12... | collective-permute-start | bytes 589832 | tf_op jit(solution)/shard_map/ppermute | solution.py:20
  44.1 1.7 %collective-permute-done.6.refs_2_ = bf16[2,64,896]{2,1,0:T(8,128)(2,1)S(1)} collective-permute-done((bf16[2,64,896]{2,1,0:T(8,128)(2,1)S(1)}, bf16[2,64,896]{2,1,0:T(8,128)(2,1)S(1)}, u32[]{:S(2)}, u32[]{:S(2)}) %collective-permute-start.6) | collective-permute-done | bytes 229408 | tf_op jit(solution)/shard_map/ppermute | solution.py:20
  45.8 2.0 %collective-permute-start.16 = (bf16[2,64,768]{2,1,0:T(8,128)(2,1)S(1)}, bf16[2,64,768]{2,1,0:T(8,128)(2,1)S(1)}, u32[]{:S(2)}, u32[]{:S(2)}) collective-permute-start(bf16[2,64,768]{2,1,0:T(8,128)(2,1)S(1)} %get-tuple-element.50), channel_id=1, source_target_pairs={{0,6},{2,4},{4,2},{6,0},{1,7},{3,5},{5,3},{7,1},{8,14},{10,12},{12... | collective-permute-start | bytes 589832 | tf_op jit(solution)/shard_map/ppermute | solution.py:20
  47.9 2.6 %collective-permute-start.9 = (bf16[2,64,896]{2,1,0:T(8,128)(2,1)S(1)}, bf16[2,64,896]{2,1,0:T(8,128)(2,1)S(1)}, u32[]{:S(2)}, u32[]{:S(2)}) collective-permute-start(bf16[2,64,896]{2,1,0:T(8,128)(2,1)S(1)} %share.5), channel_id=1, source_target_pairs={{0,24},{8,16},{16,8},{24,0},{1,25},{9,17},{17,9},{25,1},{2,26},{10... | collective-permute-start | bytes 688136 | tf_op jit(solution)/shard_map/ppermute | solution.py:25
  50.5 3.6 %collective-permute-done.15.refs_2_ = bf16[2,64,768]{2,1,0:T(8,128)(2,1)S(1)} collective-permute-done((bf16[2,64,768]{2,1,0:T(8,128)(2,1)S(1)}, bf16[2,64,768]{2,1,0:T(8,128)(2,1)S(1)}, u32[]{:S(2)}, u32[]{:S(2)}) %collective-permute-start.15) | collective-permute-done | bytes 196640 | tf_op jit(solution)/shard_map/ppermute | solution.py:20
  54.3 2.4 %collective-permute-start.18 = (bf16[2,64,768]{2,1,0:T(8,128)(2,1)S(1)}, bf16[2,64,768]{2,1,0:T(8,128)(2,1)S(1)}, u32[]{:S(2)}, u32[]{:S(2)}) collective-permute-start(bf16[2,64,768]{2,1,0:T(8,128)(2,1)S(1)} %share.7), channel_id=1, source_target_pairs={{0,24},{8,16},{16,8},{24,0},{1,25},{9,17},{17,9},{25,1},{2,26},{10... | collective-permute-start | bytes 589832 | tf_op jit(solution)/shard_map/ppermute | solution.py:25
  57.0 12.2 %collective-permute-start.10 = (bf16[16,3584]{1,0:T(8,128)(2,1)S(1)}, bf16[16,3584]{1,0:T(8,128)(2,1)S(1)}, u32[]{:S(2)}, u32[]{:S(2)}) collective-permute-start(bf16[16,3584]{1,0:T(8,128)(2,1)S(1)} %leaving.3), channel_id=1, source_target_pairs={{0,8},{8,16},{16,24},{24,0},{1,9},{9,17},{17,25},{25,1},{2,10},{10... | collective-permute-start | bytes 344072 | tf_op jit(solution)/shard_map/ppermute | solution.py:30
  69.8 0.9 %place.2.refs_5_.refs_1_ = bf16[1,128,3584]{2,1,0:T(8,128)(2,1)} custom-call(bf16[112,3584]{1,0:T(8,128)(2,1)S(1)} %collective-permute-done.11.refs_0_.refs_4_), custom_call_target="tpu_custom_call" | custom-call | bytes 1605632 | tf_op jit(solution)/shard_map/place/pallas_call | solution.py:340
  72.4 1.6 %collective-permute-start.19 = (f32[8,128]{1,0:T(8,128)S(1)}, f32[8,128]{1,0:T(8,128)S(1)}, u32[]{:S(2)}, u32[]{:S(2)}) collective-permute-start(f32[8,128]{1,0:T(8,128)S(1)} %get-tuple-element.54.refs_0_), channel_id=1, source_target_pairs={{0,2},{2,0},{4,6},{6,4},{1,3},{3,1},{5,7},{7,5},{8,10},{10,8},{12,... | collective-permute-start | bytes 12296 | tf_op jit(solution)/shard_map/ppermute | solution.py:20
  73.9 1.5 %collective-permute-start.20 = (f32[8,128]{1,0:T(8,128)S(1)}, f32[8,128]{1,0:T(8,128)S(1)}, u32[]{:S(2)}, u32[]{:S(2)}) collective-permute-start(f32[8,128]{1,0:T(8,128)S(1)} %get-tuple-element.54.refs_0_), channel_id=1, source_target_pairs={{0,4},{2,6},{4,0},{6,2},{1,5},{3,7},{5,1},{7,3},{8,12},{10,14},{12... | collective-permute-start | bytes 12296 | tf_op jit(solution)/shard_map/ppermute | solution.py:20
  76.1 1.2 %codes.1.refs_2_.refs_4_ = bf16[2,1,64,3584]{3,2,1,0:T(8,128)(2,1)} custom-call(f32[8,128]{1,0:T(8,128)S(1)} %get-tuple-element.54.refs_0_, f32[8,128]{1,0:T(8,128)S(1)} %collective-permute-done.19.refs_1_, f32[2,64,1024]{2,1,0:T(8,128)S(1)} %get-tuple-element.55.refs_2_, f32[2,64,896]{2,1,0:T(8,128)S(1)} %get-tuple-element.56.refs_3_, ...), custom_call_target="tpu_custom_call" | custom-call | flops 917504 | bytes 1843200 | tf_op jit(solution)/shard_map/codes/pallas_call | solution.py:51
  77.3 1.2 %copy-done.4 = bf16[2,1,64,3584]{3,2,1,0:T(8,128)(2,1)S(1)} copy-done((bf16[2,1,64,3584]{3,2,1,0:T(8,128)(2,1)S(1)}, bf16[2,1,64,3584]{3,2,1,0:T(8,128)(2,1)}, u32[]{:S(2)}) %copy-start.4) | copy-done | bytes 917528
  79.1 0.9 %collective-permute-done.21.refs_3_ = f32[8,128]{1,0:T(8,128)S(1)} collective-permute-done((f32[8,128]{1,0:T(8,128)S(1)}, f32[8,128]{1,0:T(8,128)S(1)}, u32[]{:S(2)}, u32[]{:S(2)}) %collective-permute-start.21) | collective-permute-done | bytes 4128 | tf_op jit(solution)/shard_map/ppermute | solution.py:20
  80.0 1.2 %copy-done.5 = bf16[2,1,64,3584]{3,2,1,0:T(8,128)(2,1)S(1)} copy-done((bf16[2,1,64,3584]{3,2,1,0:T(8,128)(2,1)S(1)}, bf16[2,1,64,3584]{3,2,1,0:T(8,128)(2,1)}, u32[]{:S(2)}) %copy-start.5) | copy-done | bytes 917528
  (44 shorter events, 9.4 us)
Async XLA Ops:
  4.8 2.1 %collective-permute-start = (f32[1024,128]{1,0:T(8,128)S(1)}, f32[1024,128]{1,0:T(8,128)S(1)}, u32[]{:S(2)}, u32[]{:S(2)}) collective-permute-start(f32[1024,128]{1,0:T(8,128)S(1)} %get-tuple-element.31.rest_0_.refs_0_), channel_id=1, source_target_pairs={{0,1},{1,0},{2,3},{3,2},{4,5},{5,4},{6,7},{7,6},{8,9},{9,8},{10,11... | collective-permute-start | bytes 1572872 | tf_op jit(solution)/shard_map/ppermute | solution.py:20
  7.3 30.7 %collective-permute-start.11 = (bf16[112,3584]{1,0:T(8,128)(2,1)S(1)}, bf16[112,3584]{1,0:T(8,128)(2,1)S(1)}, u32[]{:S(2)}, u32[]{:S(2)}) collective-permute-start(bf16[112,3584]{1,0:T(8,128)(2,1)S(1)} %leaving.2.refs_4_), channel_id=1, source_target_pairs={{0,8},{8,16},{16,24},{24,0},{1,9},{9,17},{17,25},{25,1},{2,10},{10... | collective-permute-start | bytes 2408456 | tf_op jit(solution)/shard_map/ppermute | solution.py:30
  10.9 9.3 %collective-permute-start.1 = (bf16[2,64,1024]{2,1,0:T(8,128)(2,1)S(1)}, bf16[2,64,1024]{2,1,0:T(8,128)(2,1)S(1)}, u32[]{:S(2)}, u32[]{:S(2)}) collective-permute-start(bf16[2,64,1024]{2,1,0:T(8,128)(2,1)S(1)} %get-tuple-element.36), channel_id=1, source_target_pairs={{0,2},{2,0},{4,6},{6,4},{1,3},{3,1},{5,7},{7,5},{8,10},{10,8},{12,... | collective-permute-start | bytes 786440 | tf_op jit(solution)/shard_map/ppermute | solution.py:20
  12.4 13.5 %collective-permute-start.2 = (bf16[2,64,1024]{2,1,0:T(8,128)(2,1)S(1)}, bf16[2,64,1024]{2,1,0:T(8,128)(2,1)S(1)}, u32[]{:S(2)}, u32[]{:S(2)}) collective-permute-start(bf16[2,64,1024]{2,1,0:T(8,128)(2,1)S(1)} %get-tuple-element.37), channel_id=1, source_target_pairs={{0,4},{2,6},{4,0},{6,2},{1,5},{3,7},{5,1},{7,3},{8,12},{10,14},{12... | collective-permute-start | bytes 786440 | tf_op jit(solution)/shard_map/ppermute | solution.py:20
  13.9 12.8 %collective-permute-start.3 = (bf16[2,64,1024]{2,1,0:T(8,128)(2,1)S(1)}, bf16[2,64,1024]{2,1,0:T(8,128)(2,1)S(1)}, u32[]{:S(2)}, u32[]{:S(2)}) collective-permute-start(bf16[2,64,1024]{2,1,0:T(8,128)(2,1)S(1)} %get-tuple-element.38), channel_id=1, source_target_pairs={{0,6},{2,4},{4,2},{6,0},{1,7},{3,5},{5,3},{7,1},{8,14},{10,12},{12... | collective-permute-start | bytes 786440 | tf_op jit(solution)/shard_map/ppermute | solution.py:20
  20.6 10.1 %collective-permute-start.4 = (bf16[2,64,896]{2,1,0:T(8,128)(2,1)S(1)}, bf16[2,64,896]{2,1,0:T(8,128)(2,1)S(1)}, u32[]{:S(2)}, u32[]{:S(2)}) collective-permute-start(bf16[2,64,896]{2,1,0:T(8,128)(2,1)S(1)} %get-tuple-element.39), channel_id=1, source_target_pairs={{0,2},{2,0},{4,6},{6,4},{1,3},{3,1},{5,7},{7,5},{8,10},{10,8},{12,... | collective-permute-start | bytes 688136 | tf_op jit(solution)/shard_map/ppermute | solution.py:20
  22.2 12.5 %collective-permute-start.12 = (bf16[2,64,896]{2,1,0:T(8,128)(2,1)S(1)}, bf16[2,64,896]{2,1,0:T(8,128)(2,1)S(1)}, u32[]{:S(2)}, u32[]{:S(2)}) collective-permute-start(bf16[2,64,896]{2,1,0:T(8,128)(2,1)S(1)} %get-tuple-element.45), channel_id=1, source_target_pairs={{0,4},{2,6},{4,0},{6,2},{1,5},{3,7},{5,1},{7,3},{8,12},{10,14},{12... | collective-permute-start | bytes 688136 | tf_op jit(solution)/shard_map/ppermute | solution.py:20
  25.9 10.7 %collective-permute-start.13 = (bf16[2,64,896]{2,1,0:T(8,128)(2,1)S(1)}, bf16[2,64,896]{2,1,0:T(8,128)(2,1)S(1)}, u32[]{:S(2)}, u32[]{:S(2)}) collective-permute-start(bf16[2,64,896]{2,1,0:T(8,128)(2,1)S(1)} %get-tuple-element.46), channel_id=1, source_target_pairs={{0,6},{2,4},{4,2},{6,0},{1,7},{3,5},{5,3},{7,1},{8,14},{10,12},{12... | collective-permute-start | bytes 688136 | tf_op jit(solution)/shard_map/ppermute | solution.py:20
  26.9 15.7 %collective-permute-start.8 = (bf16[2,64,1024]{2,1,0:T(8,128)(2,1)S(1)}, bf16[2,64,1024]{2,1,0:T(8,128)(2,1)S(1)}, u32[]{:S(2)}, u32[]{:S(2)}) collective-permute-start(bf16[2,64,1024]{2,1,0:T(8,128)(2,1)S(1)} %share.4.refs_4_), channel_id=1, source_target_pairs={{0,24},{8,16},{16,8},{24,0},{1,25},{9,17},{17,9},{25,1},{2,26},{10... | collective-permute-start | bytes 786440 | tf_op jit(solution)/shard_map/ppermute | solution.py:25
  31.2 10.2 %collective-permute-start.5 = (bf16[2,64,896]{2,1,0:T(8,128)(2,1)S(1)}, bf16[2,64,896]{2,1,0:T(8,128)(2,1)S(1)}, u32[]{:S(2)}, u32[]{:S(2)}) collective-permute-start(bf16[2,64,896]{2,1,0:T(8,128)(2,1)S(1)} %get-tuple-element.41), channel_id=1, source_target_pairs={{0,2},{2,0},{4,6},{6,4},{1,3},{3,1},{5,7},{7,5},{8,10},{10,8},{12,... | collective-permute-start | bytes 688136 | tf_op jit(solution)/shard_map/ppermute | solution.py:20
  34.7 11.1 %collective-permute-start.6 = (bf16[2,64,896]{2,1,0:T(8,128)(2,1)S(1)}, bf16[2,64,896]{2,1,0:T(8,128)(2,1)S(1)}, u32[]{:S(2)}, u32[]{:S(2)}) collective-permute-start(bf16[2,64,896]{2,1,0:T(8,128)(2,1)S(1)} %get-tuple-element.42), channel_id=1, source_target_pairs={{0,4},{2,6},{4,0},{6,2},{1,5},{3,7},{5,1},{7,3},{8,12},{10,14},{12... | collective-permute-start | bytes 688136 | tf_op jit(solution)/shard_map/ppermute | solution.py:20
  36.6 11.2 %collective-permute-start.7 = (bf16[2,64,896]{2,1,0:T(8,128)(2,1)S(1)}, bf16[2,64,896]{2,1,0:T(8,128)(2,1)S(1)}, u32[]{:S(2)}, u32[]{:S(2)}) collective-permute-start(bf16[2,64,896]{2,1,0:T(8,128)(2,1)S(1)} %get-tuple-element.43), channel_id=1, source_target_pairs={{0,6},{2,4},{4,2},{6,0},{1,7},{3,5},{5,3},{7,1},{8,14},{10,12},{12... | collective-permute-start | bytes 688136 | tf_op jit(solution)/shard_map/ppermute | solution.py:20
  38.2 16.0 %collective-permute-start.17 = (bf16[2,64,896]{2,1,0:T(8,128)(2,1)S(1)}, bf16[2,64,896]{2,1,0:T(8,128)(2,1)S(1)}, u32[]{:S(2)}, u32[]{:S(2)}) collective-permute-start(bf16[2,64,896]{2,1,0:T(8,128)(2,1)S(1)} %share.6.refs_4_), channel_id=1, source_target_pairs={{0,24},{8,16},{16,8},{24,0},{1,25},{9,17},{17,9},{25,1},{2,26},{10... | collective-permute-start | bytes 688136 | tf_op jit(solution)/shard_map/ppermute | solution.py:25
  41.8 27.4 %copy-start = (f32[2,1,64,3584]{3,2,1,0:T(8,128)S(1)}, f32[2,1,64,3584]{3,2,1,0:T(8,128)}, u32[]{:S(2)}) copy-start(f32[2,1,64,3584]{3,2,1,0:T(8,128)} %refs_1_.9) | copy-start | bytes 5505028
  41.8 27.4 %copy-start.1 = (bf16[2,1,64,3584]{3,2,1,0:T(8,128)(2,1)S(1)}, bf16[2,1,64,3584]{3,2,1,0:T(8,128)(2,1)}, u32[]{:S(2)}) copy-start(bf16[2,1,64,3584]{3,2,1,0:T(8,128)(2,1)} %refs_2_.9) | copy-start | bytes 2752516
  41.9 27.4 %copy-start.2 = (bf16[2,1,64,3584]{3,2,1,0:T(8,128)(2,1)S(1)}, bf16[2,1,64,3584]{3,2,1,0:T(8,128)(2,1)}, u32[]{:S(2)}) copy-start(bf16[2,1,64,3584]{3,2,1,0:T(8,128)(2,1)} %refs_3_.9) | copy-start | bytes 2752516
  41.9 8.7 %collective-permute-start.14 = (bf16[2,64,768]{2,1,0:T(8,128)(2,1)S(1)}, bf16[2,64,768]{2,1,0:T(8,128)(2,1)S(1)}, u32[]{:S(2)}, u32[]{:S(2)}) collective-permute-start(bf16[2,64,768]{2,1,0:T(8,128)(2,1)S(1)} %get-tuple-element.48), channel_id=1, source_target_pairs={{0,2},{2,0},{4,6},{6,4},{1,3},{3,1},{5,7},{7,5},{8,10},{10,8},{12,... | collective-permute-start | bytes 589832 | tf_op jit(solution)/shard_map/ppermute | solution.py:20
  42.6 11.5 %collective-permute-start.15 = (bf16[2,64,768]{2,1,0:T(8,128)(2,1)S(1)}, bf16[2,64,768]{2,1,0:T(8,128)(2,1)S(1)}, u32[]{:S(2)}, u32[]{:S(2)}) collective-permute-start(bf16[2,64,768]{2,1,0:T(8,128)(2,1)S(1)} %get-tuple-element.49), channel_id=1, source_target_pairs={{0,4},{2,6},{4,0},{6,2},{1,5},{3,7},{5,1},{7,3},{8,12},{10,14},{12... | collective-permute-start | bytes 589832 | tf_op jit(solution)/shard_map/ppermute | solution.py:20
  45.8 8.4 %collective-permute-start.16 = (bf16[2,64,768]{2,1,0:T(8,128)(2,1)S(1)}, bf16[2,64,768]{2,1,0:T(8,128)(2,1)S(1)}, u32[]{:S(2)}, u32[]{:S(2)}) collective-permute-start(bf16[2,64,768]{2,1,0:T(8,128)(2,1)S(1)} %get-tuple-element.50), channel_id=1, source_target_pairs={{0,6},{2,4},{4,2},{6,0},{1,7},{3,5},{5,3},{7,1},{8,14},{10,12},{12... | collective-permute-start | bytes 589832 | tf_op jit(solution)/shard_map/ppermute | solution.py:20
  47.9 8.7 %collective-permute-start.9 = (bf16[2,64,896]{2,1,0:T(8,128)(2,1)S(1)}, bf16[2,64,896]{2,1,0:T(8,128)(2,1)S(1)}, u32[]{:S(2)}, u32[]{:S(2)}) collective-permute-start(bf16[2,64,896]{2,1,0:T(8,128)(2,1)S(1)} %share.5), channel_id=1, source_target_pairs={{0,24},{8,16},{16,8},{24,0},{1,25},{9,17},{17,9},{25,1},{2,26},{10... | collective-permute-start | bytes 688136 | tf_op jit(solution)/shard_map/ppermute | solution.py:25
  54.3 17.6 %collective-permute-start.18 = (bf16[2,64,768]{2,1,0:T(8,128)(2,1)S(1)}, bf16[2,64,768]{2,1,0:T(8,128)(2,1)S(1)}, u32[]{:S(2)}, u32[]{:S(2)}) collective-permute-start(bf16[2,64,768]{2,1,0:T(8,128)(2,1)S(1)} %share.7), channel_id=1, source_target_pairs={{0,24},{8,16},{16,8},{24,0},{1,25},{9,17},{17,9},{25,1},{2,26},{10... | collective-permute-start | bytes 589832 | tf_op jit(solution)/shard_map/ppermute | solution.py:25
  57.0 20.2 %collective-permute-start.10 = (bf16[16,3584]{1,0:T(8,128)(2,1)S(1)}, bf16[16,3584]{1,0:T(8,128)(2,1)S(1)}, u32[]{:S(2)}, u32[]{:S(2)}) collective-permute-start(bf16[16,3584]{1,0:T(8,128)(2,1)S(1)} %leaving.3), channel_id=1, source_target_pairs={{0,8},{8,16},{16,24},{24,0},{1,9},{9,17},{17,25},{25,1},{2,10},{10... | collective-permute-start | bytes 344072 | tf_op jit(solution)/shard_map/ppermute | solution.py:30
  70.7 1.2 %copy-start.3 = (bf16[1,128,3584]{2,1,0:T(8,128)(2,1)S(1)}, bf16[1,128,3584]{2,1,0:T(8,128)(2,1)}, u32[]{:S(2)}) copy-start(bf16[1,128,3584]{2,1,0:T(8,128)(2,1)} %place.2.refs_5_.refs_1_) | copy-start | bytes 2752516
  72.4 3.7 %collective-permute-start.19 = (f32[8,128]{1,0:T(8,128)S(1)}, f32[8,128]{1,0:T(8,128)S(1)}, u32[]{:S(2)}, u32[]{:S(2)}) collective-permute-start(f32[8,128]{1,0:T(8,128)S(1)} %get-tuple-element.54.refs_0_), channel_id=1, source_target_pairs={{0,2},{2,0},{4,6},{6,4},{1,3},{3,1},{5,7},{7,5},{8,10},{10,8},{12,... | collective-permute-start | bytes 12296 | tf_op jit(solution)/shard_map/ppermute | solution.py:20
  73.9 5.2 %collective-permute-start.20 = (f32[8,128]{1,0:T(8,128)S(1)}, f32[8,128]{1,0:T(8,128)S(1)}, u32[]{:S(2)}, u32[]{:S(2)}) collective-permute-start(f32[8,128]{1,0:T(8,128)S(1)} %get-tuple-element.54.refs_0_), channel_id=1, source_target_pairs={{0,4},{2,6},{4,0},{6,2},{1,5},{3,7},{5,1},{7,3},{8,12},{10,14},{12... | collective-permute-start | bytes 12296 | tf_op jit(solution)/shard_map/ppermute | solution.py:20
  75.5 4.5 %collective-permute-start.21 = (f32[8,128]{1,0:T(8,128)S(1)}, f32[8,128]{1,0:T(8,128)S(1)}, u32[]{:S(2)}, u32[]{:S(2)}) collective-permute-start(f32[8,128]{1,0:T(8,128)S(1)} %get-tuple-element.54.refs_0_), channel_id=1, source_target_pairs={{0,6},{2,4},{4,2},{6,0},{1,7},{3,5},{5,3},{7,1},{8,14},{10,12},{12... | collective-permute-start | bytes 12296 | tf_op jit(solution)/shard_map/ppermute | solution.py:20
  77.3 1.2 %copy-start.4 = (bf16[2,1,64,3584]{3,2,1,0:T(8,128)(2,1)S(1)}, bf16[2,1,64,3584]{3,2,1,0:T(8,128)(2,1)}, u32[]{:S(2)}) copy-start(bf16[2,1,64,3584]{3,2,1,0:T(8,128)(2,1)} %codes.1.refs_2_.refs_4_) | copy-start | bytes 2752516
  80.0 1.2 %copy-start.5 = (bf16[2,1,64,3584]{3,2,1,0:T(8,128)(2,1)S(1)}, bf16[2,1,64,3584]{3,2,1,0:T(8,128)(2,1)}, u32[]{:S(2)}) copy-start(bf16[2,1,64,3584]{3,2,1,0:T(8,128)(2,1)} %codes.1.refs_2_.refs_4_) | copy-start | bytes 2752516

commit v8 on v7

--- a/solution.py
+++ b/solution.py
@@ -208,7 +208,8 @@
 
 
 def code_kernel(group, *refs):
-    peak_refs, fresh_refs, code_ref = refs[:group], refs[group:-1], refs[-1]
+    peak_refs, fresh_refs, (code_ref, token_ref) = refs[:group], refs[group:-2], refs[-2:]
+    token_ref[...] = jnp.zeros_like(token_ref)
     column = (1.0 / merged(peak_refs)).T
     for side in range(2):
         inverse = jnp.broadcast_to(column[:, side : side + 1], (LANES, LANES))
@@ -232,9 +233,10 @@
 
 
 def place_kernel(start, in_ref, *rest):
-    out_ref, sem = rest[-2:]
+    out_ref, token_ref, sem = rest[-3:]
     copy = pltpu.make_async_copy(in_ref, out_ref.at[0, pl.ds(start, in_ref.shape[0])], sem)
     copy.start()
+    token_ref[...] = jnp.zeros_like(token_ref)
     copy.wait()
 
 
@@ -334,14 +336,13 @@
             )
         )
         arrived.append(mirrored(shares[-1], "pipe"))
-    left_tail = turned(leaving(head, tokens - head, arrived[-2]), "pipe")
 
     def place(start, rows, kept=(), after=()):
         return pl.pallas_call(
             lambda *refs: place_kernel(start, *refs),
             in_specs=[ANY] * (1 + len(kept) + len(after)),
-            out_specs=ANY,
-            out_shape=shape((1, tokens, width), BF16),
+            out_specs=[ANY, VMEM],
+            out_shape=[shape((1, tokens, width), BF16), shape((8, LANES), F32)],
             scratch_shapes=[pltpu.SemaphoreType.DMA],
             input_output_aliases={1 + k: k for k in range(len(kept))},
             compiler_params=ROOM,
@@ -349,12 +350,12 @@
             name="place",
         )(rows, *kept, *after)
 
-    placed = place(0, left_head)
-
-    fresh, peaks = [], None
+    placed, token = place(0, left_head)
+
+    fresh, peaks, steps = [], None, []
     for chunk, (start, stop) in enumerate(chunks):
         kept = () if peaks is None else (peaks,)
-        after = (placed,) if chunk == len(chunks) - 1 else ()
+        after = (token,) if chunk == 1 else ()
         some, peaks = call(
             lambda *refs: update_kernel(start, *refs),
             "update",
@@ -370,13 +371,16 @@
             flops=40 * depth * (stop - start),
         )
         fresh.append(some)
+        steps.append(peaks)
+
+    left_tail = turned(leaving(head, tokens - head, steps[-2]), "pipe")
 
     group = LANES // depth
     peak_rows = [peaks] + [exchange(peaks, "expert", k) for k in range(1, experts)]
-    coded = call(
+    coded, token = call(
         lambda *refs: code_kernel(group, *refs),
         "codes",
-        shape((2, 1, depth, width), BF16),
+        [shape((2, 1, depth, width), BF16), shape((8, LANES), F32)],
         *peak_rows[:group],
         *fresh,
         read=group + len(fresh),
@@ -387,10 +391,11 @@
         "scales",
         shape((2, 1, experts // group, blocks), F32),
         *peak_rows,
-        coded,
+        token,
         read=experts,
     )
-    return (place(head, left_tail, (placed,), (coded,)), coded, scales)
+    left, _ = place(head, left_tail, (placed,), (token,))
+    return (left, coded, scales)
 
 
 def solution(mesh):

time: 82 us -> 78.8 us (0.961)
  the two profiles are of different devices: /device:TPU:0 before, /device:TPU:8 now
where the time goes in v8:
time: 78.8 us; the launch traced here: 78.6 us
  waiting for transfers between devices  36.4 us (46%)
  starting transfers between devices  26.3 us (33%)
  Pallas kernels  15.1 us (19%)
  between operations  0.8 us (1%)
    ppermute x16, waiting for transfers between devices, exchange(): return lax.ppermute(block, axis, [(i, i ^ offset) for i in range(count)])  22.1 us
    ppermute x16, starting transfers between devices, exchange(): return lax.ppermute(block, axis, [(i, i ^ offset) for i in range(count)])  19.5 us
    ppermute x4, waiting for transfers between devices, mirrored(): return lax.ppermute(block, axis, [(i, count - 1 - i) for i in range(count)])  14.2 us
    pallas_call x16, Pallas kernels, call(): pl.pallas_call(kernel, in_specs=[VMEM] * read + [ANY] * (len(operands) -...  7.27 us
    ppermute x4, starting transfers between devices, mirrored(): return lax.ppermute(block, axis, [(i, count - 1 - i) for i in range(count)])  5.17 us
    pallas_call x1, Pallas kernels, shards(): pl.pallas_call(lambda *refs: latent_kernel(tiles, *refs), in_specs=[ANY]...  4.15 us
    pallas_call x2, Pallas kernels, place(): pl.pallas_call(lambda *refs: place_kernel(start, *refs), in_specs=[ANY] *...  2.14 us
    ppermute x2, starting transfers between devices, turned(): lax.ppermute(block, axis, [(i, (i + 1) % count) for i in range(count)])  1.69 us
  transfers between devices with their start and end apart: 22, of which 13 were waited for; matrix products, arithmetic and copies ran while one was open for 0% of the time, Pallas kernels for 12%

profile of v8, /device:TPU:8, one launch (start us, length us, event | category | flops | bytes accessed | tf_op | source)
XLA Modules:
  0.0 78.6 jit_solution(16761131904778748798)
XLA Ops:
  0.6 4.2 %latents.1 = (f32[1024,128]{1,0:T(8,128)S(1)}, bf16[128,3584]{1,0:T(8,128)(2,1)S(1)}, bf16[128,3584]{1,0:T(8,128)(2,1)S(1)}, bf16[128,3584]{1,0:T(8,128)(2,1)S(1)}) custom-call(bf16[1,128,3584]{2,1,0:T(8,128)(2,1)} %refs_0_.1, bf16[1,128,3584]{2,1,0:T(8,128)(2,1)} %refs_1_.5, bf16[1,128,3584]{2,1,0:T(8,128)(2,1)} %refs_2_.5, ...), custom_call_target="tpu_custom_call" | custom-call | flops 704643072 | bytes 8257536 | tf_op jit(solution)/shard_map/latents/pallas_call | solution.py:259
  4.9 1.5 %fetch.1.refs_3_ = bf16[256,3584]{1,0:T(8,128)(2,1)S(1)} custom-call(bf16[2,1,256,3584]{3,2,1,0:T(8,128)(2,1)} %in_ref.1, f32[1024,128]{1,0:T(8,128)S(1)} %get-tuple-element.36.rest_0_.refs_0_), custom_call_target="tpu_custom_call" | custom-call | bytes 1835008 | tf_op jit(solution)/shard_map/fetch/pallas_call | solution.py:278
  7.3 1.6 %collective-permute-start.12 = (bf16[112,3584]{1,0:T(8,128)(2,1)S(1)}, bf16[112,3584]{1,0:T(8,128)(2,1)S(1)}, u32[]{:S(2)}, u32[]{:S(2)}) collective-permute-start(bf16[112,3584]{1,0:T(8,128)(2,1)S(1)} %leaving.2.refs_4_), channel_id=1, source_target_pairs={{0,8},{8,16},{16,24},{24,0},{1,9},{9,17},{17,25},{25,1},{2,10},{10... | collective-permute-start | bytes 2408456 | tf_op jit(solution)/shard_map/ppermute | solution.py:30
  9.5 1.6 %collective-permute-start.1 = (bf16[2,64,1024]{2,1,0:T(8,128)(2,1)S(1)}, bf16[2,64,1024]{2,1,0:T(8,128)(2,1)S(1)}, u32[]{:S(2)}, u32[]{:S(2)}) collective-permute-start(bf16[2,64,1024]{2,1,0:T(8,128)(2,1)S(1)} %get-tuple-element.41), channel_id=1, source_target_pairs={{0,2},{2,0},{4,6},{6,4},{1,3},{3,1},{5,7},{7,5},{8,10},{10,8},{12,... | collective-permute-start | bytes 786440 | tf_op jit(solution)/shard_map/ppermute | solution.py:20
  11.0 1.5 %collective-permute-start.2 = (bf16[2,64,1024]{2,1,0:T(8,128)(2,1)S(1)}, bf16[2,64,1024]{2,1,0:T(8,128)(2,1)S(1)}, u32[]{:S(2)}, u32[]{:S(2)}) collective-permute-start(bf16[2,64,1024]{2,1,0:T(8,128)(2,1)S(1)} %get-tuple-element.42), channel_id=1, source_target_pairs={{0,4},{2,6},{4,0},{6,2},{1,5},{3,7},{5,1},{7,3},{8,12},{10,14},{12... | collective-permute-start | bytes 786440 | tf_op jit(solution)/shard_map/ppermute | solution.py:20
  13.0 5.7 %collective-permute-done.1.refs_1_.refs_4_ = bf16[2,64,1024]{2,1,0:T(8,128)(2,1)S(1)} collective-permute-done((bf16[2,64,1024]{2,1,0:T(8,128)(2,1)S(1)}, bf16[2,64,1024]{2,1,0:T(8,128)(2,1)S(1)}, u32[]{:S(2)}, u32[]{:S(2)}) %collective-permute-start.1) | collective-permute-done | bytes 262176 | tf_op jit(solution)/shard_map/ppermute | solution.py:20
  19.2 1.6 %collective-permute-start.4 = (bf16[2,64,896]{2,1,0:T(8,128)(2,1)S(1)}, bf16[2,64,896]{2,1,0:T(8,128)(2,1)S(1)}, u32[]{:S(2)}, u32[]{:S(2)}) collective-permute-start(bf16[2,64,896]{2,1,0:T(8,128)(2,1)S(1)} %get-tuple-element.44), channel_id=1, source_target_pairs={{0,2},{2,0},{4,6},{6,4},{1,3},{3,1},{5,7},{7,5},{8,10},{10,8},{12,... | collective-permute-start | bytes 688136 | tf_op jit(solution)/shard_map/ppermute | solution.py:20
  20.8 1.5 %collective-permute-start.10 = (bf16[2,64,896]{2,1,0:T(8,128)(2,1)S(1)}, bf16[2,64,896]{2,1,0:T(8,128)(2,1)S(1)}, u32[]{:S(2)}, u32[]{:S(2)}) collective-permute-start(bf16[2,64,896]{2,1,0:T(8,128)(2,1)S(1)} %get-tuple-element.50), channel_id=1, source_target_pairs={{0,4},{2,6},{4,0},{6,2},{1,5},{3,7},{5,1},{7,3},{8,12},{10,14},{12... | collective-permute-start | bytes 688136 | tf_op jit(solution)/shard_map/ppermute | solution.py:20
  22.3 2.3 %collective-permute-done.2.refs_2_ = bf16[2,64,1024]{2,1,0:T(8,128)(2,1)S(1)} collective-permute-done((bf16[2,64,1024]{2,1,0:T(8,128)(2,1)S(1)}, bf16[2,64,1024]{2,1,0:T(8,128)(2,1)S(1)}, u32[]{:S(2)}, u32[]{:S(2)}) %collective-permute-start.2) | collective-permute-done | bytes 262176 | tf_op jit(solution)/shard_map/ppermute | solution.py:20
  24.6 0.8 %collective-permute-start.11 = (bf16[2,64,896]{2,1,0:T(8,128)(2,1)S(1)}, bf16[2,64,896]{2,1,0:T(8,128)(2,1)S(1)}, u32[]{:S(2)}, u32[]{:S(2)}) collective-permute-start(bf16[2,64,896]{2,1,0:T(8,128)(2,1)S(1)} %get-tuple-element.51), channel_id=1, source_target_pairs={{0,6},{2,4},{4,2},{6,0},{1,7},{3,5},{5,3},{7,1},{8,14},{10,12},{12... | collective-permute-start | bytes 688136 | tf_op jit(solution)/shard_map/ppermute | solution.py:20
  25.5 1.6 %collective-permute-start.8 = (bf16[2,64,1024]{2,1,0:T(8,128)(2,1)S(1)}, bf16[2,64,1024]{2,1,0:T(8,128)(2,1)S(1)}, u32[]{:S(2)}, u32[]{:S(2)}) collective-permute-start(bf16[2,64,1024]{2,1,0:T(8,128)(2,1)S(1)} %share.4.refs_4_), channel_id=1, source_target_pairs={{0,24},{8,16},{16,8},{24,0},{1,25},{9,17},{17,9},{25,1},{2,26},{10... | collective-permute-start | bytes 786440 | tf_op jit(solution)/shard_map/ppermute | solution.py:25
  27.1 2.1 %collective-permute-done.4.refs_5_.refs_1_ = bf16[2,64,896]{2,1,0:T(8,128)(2,1)S(1)} collective-permute-done((bf16[2,64,896]{2,1,0:T(8,128)(2,1)S(1)}, bf16[2,64,896]{2,1,0:T(8,128)(2,1)S(1)}, u32[]{:S(2)}, u32[]{:S(2)}) %collective-permute-start.4) | collective-permute-done | bytes 229408 | tf_op jit(solution)/shard_map/ppermute | solution.py:20
  29.8 1.6 %collective-permute-start.5 = (bf16[2,64,896]{2,1,0:T(8,128)(2,1)S(1)}, bf16[2,64,896]{2,1,0:T(8,128)(2,1)S(1)}, u32[]{:S(2)}, u32[]{:S(2)}) collective-permute-start(bf16[2,64,896]{2,1,0:T(8,128)(2,1)S(1)} %get-tuple-element.46), channel_id=1, source_target_pairs={{0,2},{2,0},{4,6},{6,4},{1,3},{3,1},{5,7},{7,5},{8,10},{10,8},{12,... | collective-permute-start | bytes 688136 | tf_op jit(solution)/shard_map/ppermute | solution.py:20
  31.4 1.9 %collective-permute-done.10.refs_2_ = bf16[2,64,896]{2,1,0:T(8,128)(2,1)S(1)} collective-permute-done((bf16[2,64,896]{2,1,0:T(8,128)(2,1)S(1)}, bf16[2,64,896]{2,1,0:T(8,128)(2,1)S(1)}, u32[]{:S(2)}, u32[]{:S(2)}) %collective-permute-start.10) | collective-permute-done | bytes 229408 | tf_op jit(solution)/shard_map/ppermute | solution.py:20
  33.3 1.7 %collective-permute-start.6 = (bf16[2,64,896]{2,1,0:T(8,128)(2,1)S(1)}, bf16[2,64,896]{2,1,0:T(8,128)(2,1)S(1)}, u32[]{:S(2)}, u32[]{:S(2)}) collective-permute-start(bf16[2,64,896]{2,1,0:T(8,128)(2,1)S(1)} %get-tuple-element.47), channel_id=1, source_target_pairs={{0,4},{2,6},{4,0},{6,2},{1,5},{3,7},{5,1},{7,3},{8,12},{10,14},{12... | collective-permute-start | bytes 688136 | tf_op jit(solution)/shard_map/ppermute | solution.py:20
  35.2 1.4 %collective-permute-start.7 = (bf16[2,64,896]{2,1,0:T(8,128)(2,1)S(1)}, bf16[2,64,896]{2,1,0:T(8,128)(2,1)S(1)}, u32[]{:S(2)}, u32[]{:S(2)}) collective-permute-start(bf16[2,64,896]{2,1,0:T(8,128)(2,1)S(1)} %get-tuple-element.48), channel_id=1, source_target_pairs={{0,6},{2,4},{4,2},{6,0},{1,7},{3,5},{5,3},{7,1},{8,14},{10,12},{12... | collective-permute-start | bytes 688136 | tf_op jit(solution)/shard_map/ppermute | solution.py:20
  36.8 1.6 %collective-permute-start.13 = (bf16[2,64,896]{2,1,0:T(8,128)(2,1)S(1)}, bf16[2,64,896]{2,1,0:T(8,128)(2,1)S(1)}, u32[]{:S(2)}, u32[]{:S(2)}) collective-permute-start(bf16[2,64,896]{2,1,0:T(8,128)(2,1)S(1)} %share.6.refs_4_), channel_id=1, source_target_pairs={{0,24},{8,16},{16,8},{24,0},{1,25},{9,17},{17,9},{25,1},{2,26},{10... | collective-permute-start | bytes 688136 | tf_op jit(solution)/shard_map/ppermute | solution.py:25
  38.4 1.6 %collective-permute-done.5.refs_1_.refs_5_ = bf16[2,64,896]{2,1,0:T(8,128)(2,1)S(1)} collective-permute-done((bf16[2,64,896]{2,1,0:T(8,128)(2,1)S(1)}, bf16[2,64,896]{2,1,0:T(8,128)(2,1)S(1)}, u32[]{:S(2)}, u32[]{:S(2)}) %collective-permute-start.5) | collective-permute-done | bytes 229408 | tf_op jit(solution)/shard_map/ppermute | solution.py:20
  40.4 0.7 collective-permute-start.15
  41.2 3.2 %collective-permute-done.8.refs_4_.refs_0_ = bf16[2,64,1024]{2,1,0:T(8,128)(2,1)S(1)} collective-permute-done((bf16[2,64,1024]{2,1,0:T(8,128)(2,1)S(1)}, bf16[2,64,1024]{2,1,0:T(8,128)(2,1)S(1)}, u32[]{:S(2)}, u32[]{:S(2)}) %collective-permute-start.8) | collective-permute-done | bytes 262176 | tf_op jit(solution)/shard_map/ppermute | solution.py:25
  44.4 1.5 %collective-permute-start.16 = (bf16[2,64,768]{2,1,0:T(8,128)(2,1)S(1)}, bf16[2,64,768]{2,1,0:T(8,128)(2,1)S(1)}, u32[]{:S(2)}, u32[]{:S(2)}) collective-permute-start(bf16[2,64,768]{2,1,0:T(8,128)(2,1)S(1)} %get-tuple-element.59), channel_id=1, source_target_pairs={{0,4},{2,6},{4,0},{6,2},{1,5},{3,7},{5,1},{7,3},{8,12},{10,14},{12... | collective-permute-start | bytes 589832 | tf_op jit(solution)/shard_map/ppermute | solution.py:20
  45.9 1.4 %collective-permute-start.17 = (bf16[2,64,768]{2,1,0:T(8,128)(2,1)S(1)}, bf16[2,64,768]{2,1,0:T(8,128)(2,1)S(1)}, u32[]{:S(2)}, u32[]{:S(2)}) collective-permute-start(bf16[2,64,768]{2,1,0:T(8,128)(2,1)S(1)} %get-tuple-element.60), channel_id=1, source_target_pairs={{0,6},{2,4},{4,2},{6,0},{1,7},{3,5},{5,3},{7,1},{8,14},{10,12},{12... | collective-permute-start | bytes 589832 | tf_op jit(solution)/shard_map/ppermute | solution.py:20
  47.5 1.5 %collective-permute-start.9 = (bf16[2,64,896]{2,1,0:T(8,128)(2,1)S(1)}, bf16[2,64,896]{2,1,0:T(8,128)(2,1)S(1)}, u32[]{:S(2)}, u32[]{:S(2)}) collective-permute-start(bf16[2,64,896]{2,1,0:T(8,128)(2,1)S(1)} %share.5), channel_id=1, source_target_pairs={{0,24},{8,16},{16,8},{24,0},{1,25},{9,17},{17,9},{25,1},{2,26},{10... | collective-permute-start | bytes 688136 | tf_op jit(solution)/shard_map/ppermute | solution.py:25
  49.0 6.4 %collective-permute-done.16.refs_2_ = bf16[2,64,768]{2,1,0:T(8,128)(2,1)S(1)} collective-permute-done((bf16[2,64,768]{2,1,0:T(8,128)(2,1)S(1)}, bf16[2,64,768]{2,1,0:T(8,128)(2,1)S(1)}, u32[]{:S(2)}, u32[]{:S(2)}) %collective-permute-start.16) | collective-permute-done | bytes 196640 | tf_op jit(solution)/shard_map/ppermute | solution.py:20
  56.4 0.9 %place.2 = (bf16[1,128,3584]{2,1,0:T(8,128)(2,1)}, f32[8,128]{1,0:T(8,128)S(1)}) custom-call(bf16[112,3584]{1,0:T(8,128)(2,1)S(1)} %collective-permute-done.12.refs_4_.refs_0_), custom_call_target="tpu_custom_call" | custom-call | bytes 1605632 | tf_op jit(solution)/shard_map/place/pallas_call | solution.py:341
  57.9 7.9 %collective-permute-done.9.refs_0_ = bf16[2,64,896]{2,1,0:T(8,128)(2,1)S(1)} collective-permute-done((bf16[2,64,896]{2,1,0:T(8,128)(2,1)S(1)}, bf16[2,64,896]{2,1,0:T(8,128)(2,1)S(1)}, u32[]{:S(2)}, u32[]{:S(2)}) %collective-permute-start.9) | collective-permute-done | bytes 229408 | tf_op jit(solution)/shard_map/ppermute | solution.py:25
  66.8 3.1 %collective-permute-done.18.refs_0_ = bf16[2,64,768]{2,1,0:T(8,128)(2,1)S(1)} collective-permute-done((bf16[2,64,768]{2,1,0:T(8,128)(2,1)S(1)}, bf16[2,64,768]{2,1,0:T(8,128)(2,1)S(1)}, u32[]{:S(2)}, u32[]{:S(2)}) %collective-permute-start.18) | collective-permute-done | bytes 196640 | tf_op jit(solution)/shard_map/ppermute | solution.py:25
  70.4 1.6 %collective-permute-start.19 = (f32[8,128]{1,0:T(8,128)S(1)}, f32[8,128]{1,0:T(8,128)S(1)}, u32[]{:S(2)}, u32[]{:S(2)}) collective-permute-start(f32[8,128]{1,0:T(8,128)S(1)} %get-tuple-element.61.refs_0_), channel_id=1, source_target_pairs={{0,2},{2,0},{4,6},{6,4},{1,3},{3,1},{5,7},{7,5},{8,10},{10,8},{12,... | collective-permute-start | bytes 12296 | tf_op jit(solution)/shard_map/ppermute | solution.py:20
  71.9 1.5 %collective-permute-start.20 = (f32[8,128]{1,0:T(8,128)S(1)}, f32[8,128]{1,0:T(8,128)S(1)}, u32[]{:S(2)}, u32[]{:S(2)}) collective-permute-start(f32[8,128]{1,0:T(8,128)S(1)} %get-tuple-element.61.refs_0_), channel_id=1, source_target_pairs={{0,4},{2,6},{4,0},{6,2},{1,5},{3,7},{5,1},{7,3},{8,12},{10,14},{12... | collective-permute-start | bytes 12296 | tf_op jit(solution)/shard_map/ppermute | solution.py:20
  74.1 1.2 %codes.1 = (bf16[2,1,64,3584]{3,2,1,0:T(8,128)(2,1)}, f32[8,128]{1,0:T(8,128)S(1)}) custom-call(f32[8,128]{1,0:T(8,128)S(1)} %get-tuple-element.61.refs_0_, f32[8,128]{1,0:T(8,128)S(1)} %collective-permute-done.19.refs_1_, f32[2,64,1024]{2,1,0:T(8,128)S(1)} %get-tuple-element.62.refs_2_, f32[2,64,896]{2,1,0:T(8,128)S(1)} %get-tuple-element.63.refs_3_, ...), custom_call_target="tpu_custom_call" | custom-call | flops 917504 | bytes 1843200 | tf_op jit(solution)/shard_map/codes/pallas_call | solution.py:51
  75.2 1.2 %place.3 = (bf16[1,128,3584]{2,1,0:T(8,128)(2,1)}, f32[8,128]{1,0:T(8,128)}) custom-call(bf16[16,3584]{1,0:T(8,128)(2,1)S(1)} %collective-permute-done.14.refs_0_, bf16[1,128,3584]{2,1,0:T(8,128)(2,1)} %get-tuple-element.56.refs_1_, f32[8,128]{1,0:T(8,128)S(1)} %get-tuple-element.66.refs_2_.refs_4_), custom_call_target="tpu_custom_call", output_to_operand_aliasing={{0}: (1, {})} | custom-call | bytes 229376 | tf_op jit(solution)/shard_map/place/pallas_call | solution.py:341
  76.5 1.5 %collective-permute-done.21.refs_3_ = f32[8,128]{1,0:T(8,128)S(1)} collective-permute-done((f32[8,128]{1,0:T(8,128)S(1)}, f32[8,128]{1,0:T(8,128)S(1)}, u32[]{:S(2)}, u32[]{:S(2)}) %collective-permute-start.21) | collective-permute-done | bytes 4128 | tf_op jit(solution)/shard_map/ppermute | solution.py:20
  (38 shorter events, 8.3 us)
Async XLA Ops:
  4.8 2.0 %collective-permute-start = (f32[1024,128]{1,0:T(8,128)S(1)}, f32[1024,128]{1,0:T(8,128)S(1)}, u32[]{:S(2)}, u32[]{:S(2)}) collective-permute-start(f32[1024,128]{1,0:T(8,128)S(1)} %get-tuple-element.36.rest_0_.refs_0_), channel_id=1, source_target_pairs={{0,1},{1,0},{2,3},{3,2},{4,5},{5,4},{6,7},{7,6},{8,9},{9,8},{10,11... | collective-permute-start | bytes 1572872 | tf_op jit(solution)/shard_map/ppermute | solution.py:20
  7.3 29.3 %collective-permute-start.12 = (bf16[112,3584]{1,0:T(8,128)(2,1)S(1)}, bf16[112,3584]{1,0:T(8,128)(2,1)S(1)}, u32[]{:S(2)}, u32[]{:S(2)}) collective-permute-start(bf16[112,3584]{1,0:T(8,128)(2,1)S(1)} %leaving.2.refs_4_), channel_id=1, source_target_pairs={{0,8},{8,16},{16,24},{24,0},{1,9},{9,17},{17,25},{25,1},{2,10},{10... | collective-permute-start | bytes 2408456 | tf_op jit(solution)/shard_map/ppermute | solution.py:30
  9.5 9.3 %collective-permute-start.1 = (bf16[2,64,1024]{2,1,0:T(8,128)(2,1)S(1)}, bf16[2,64,1024]{2,1,0:T(8,128)(2,1)S(1)}, u32[]{:S(2)}, u32[]{:S(2)}) collective-permute-start(bf16[2,64,1024]{2,1,0:T(8,128)(2,1)S(1)} %get-tuple-element.41), channel_id=1, source_target_pairs={{0,2},{2,0},{4,6},{6,4},{1,3},{3,1},{5,7},{7,5},{8,10},{10,8},{12,... | collective-permute-start | bytes 786440 | tf_op jit(solution)/shard_map/ppermute | solution.py:20
  11.0 13.5 %collective-permute-start.2 = (bf16[2,64,1024]{2,1,0:T(8,128)(2,1)S(1)}, bf16[2,64,1024]{2,1,0:T(8,128)(2,1)S(1)}, u32[]{:S(2)}, u32[]{:S(2)}) collective-permute-start(bf16[2,64,1024]{2,1,0:T(8,128)(2,1)S(1)} %get-tuple-element.42), channel_id=1, source_target_pairs={{0,4},{2,6},{4,0},{6,2},{1,5},{3,7},{5,1},{7,3},{8,12},{10,14},{12... | collective-permute-start | bytes 786440 | tf_op jit(solution)/shard_map/ppermute | solution.py:20
  12.5 12.8 %collective-permute-start.3 = (bf16[2,64,1024]{2,1,0:T(8,128)(2,1)S(1)}, bf16[2,64,1024]{2,1,0:T(8,128)(2,1)S(1)}, u32[]{:S(2)}, u32[]{:S(2)}) collective-permute-start(bf16[2,64,1024]{2,1,0:T(8,128)(2,1)S(1)} %get-tuple-element.43), channel_id=1, source_target_pairs={{0,6},{2,4},{4,2},{6,0},{1,7},{3,5},{5,3},{7,1},{8,14},{10,12},{12... | collective-permute-start | bytes 786440 | tf_op jit(solution)/shard_map/ppermute | solution.py:20
  19.2 10.1 %collective-permute-start.4 = (bf16[2,64,896]{2,1,0:T(8,128)(2,1)S(1)}, bf16[2,64,896]{2,1,0:T(8,128)(2,1)S(1)}, u32[]{:S(2)}, u32[]{:S(2)}) collective-permute-start(bf16[2,64,896]{2,1,0:T(8,128)(2,1)S(1)} %get-tuple-element.44), channel_id=1, source_target_pairs={{0,2},{2,0},{4,6},{6,4},{1,3},{3,1},{5,7},{7,5},{8,10},{10,8},{12,... | collective-permute-start | bytes 688136 | tf_op jit(solution)/shard_map/ppermute | solution.py:20
  20.8 12.5 %collective-permute-start.10 = (bf16[2,64,896]{2,1,0:T(8,128)(2,1)S(1)}, bf16[2,64,896]{2,1,0:T(8,128)(2,1)S(1)}, u32[]{:S(2)}, u32[]{:S(2)}) collective-permute-start(bf16[2,64,896]{2,1,0:T(8,128)(2,1)S(1)} %get-tuple-element.50), channel_id=1, source_target_pairs={{0,4},{2,6},{4,0},{6,2},{1,5},{3,7},{5,1},{7,3},{8,12},{10,14},{12... | collective-permute-start | bytes 688136 | tf_op jit(solution)/shard_map/ppermute | solution.py:20
  24.6 10.6 %collective-permute-start.11 = (bf16[2,64,896]{2,1,0:T(8,128)(2,1)S(1)}, bf16[2,64,896]{2,1,0:T(8,128)(2,1)S(1)}, u32[]{:S(2)}, u32[]{:S(2)}) collective-permute-start(bf16[2,64,896]{2,1,0:T(8,128)(2,1)S(1)} %get-tuple-element.51), channel_id=1, source_target_pairs={{0,6},{2,4},{4,2},{6,0},{1,7},{3,5},{5,3},{7,1},{8,14},{10,12},{12... | collective-permute-start | bytes 688136 | tf_op jit(solution)/shard_map/ppermute | solution.py:20
  25.5 18.9 %collective-permute-start.8 = (bf16[2,64,1024]{2,1,0:T(8,128)(2,1)S(1)}, bf16[2,64,1024]{2,1,0:T(8,128)(2,1)S(1)}, u32[]{:S(2)}, u32[]{:S(2)}) collective-permute-start(bf16[2,64,1024]{2,1,0:T(8,128)(2,1)S(1)} %share.4.refs_4_), channel_id=1, source_target_pairs={{0,24},{8,16},{16,8},{24,0},{1,25},{9,17},{17,9},{25,1},{2,26},{10... | collective-permute-start | bytes 786440 | tf_op jit(solution)/shard_map/ppermute | solution.py:25
  29.8 10.2 %collective-permute-start.5 = (bf16[2,64,896]{2,1,0:T(8,128)(2,1)S(1)}, bf16[2,64,896]{2,1,0:T(8,128)(2,1)S(1)}, u32[]{:S(2)}, u32[]{:S(2)}) collective-permute-start(bf16[2,64,896]{2,1,0:T(8,128)(2,1)S(1)} %get-tuple-element.46), channel_id=1, source_target_pairs={{0,2},{2,0},{4,6},{6,4},{1,3},{3,1},{5,7},{7,5},{8,10},{10,8},{12,... | collective-permute-start | bytes 688136 | tf_op jit(solution)/shard_map/ppermute | solution.py:20
  33.3 12.6 %collective-permute-start.6 = (bf16[2,64,896]{2,1,0:T(8,128)(2,1)S(1)}, bf16[2,64,896]{2,1,0:T(8,128)(2,1)S(1)}, u32[]{:S(2)}, u32[]{:S(2)}) collective-permute-start(bf16[2,64,896]{2,1,0:T(8,128)(2,1)S(1)} %get-tuple-element.47), channel_id=1, source_target_pairs={{0,4},{2,6},{4,0},{6,2},{1,5},{3,7},{5,1},{7,3},{8,12},{10,14},{12... | collective-permute-start | bytes 688136 | tf_op jit(solution)/shard_map/ppermute | solution.py:20
  35.2 12.1 %collective-permute-start.7 = (bf16[2,64,896]{2,1,0:T(8,128)(2,1)S(1)}, bf16[2,64,896]{2,1,0:T(8,128)(2,1)S(1)}, u32[]{:S(2)}, u32[]{:S(2)}) collective-permute-start(bf16[2,64,896]{2,1,0:T(8,128)(2,1)S(1)} %get-tuple-element.48), channel_id=1, source_target_pairs={{0,6},{2,4},{4,2},{6,0},{1,7},{3,5},{5,3},{7,1},{8,14},{10,12},{12... | collective-permute-start | bytes 688136 | tf_op jit(solution)/shard_map/ppermute | solution.py:20
  36.6 19.2 %copy-start = (f32[2,1,64,3584]{3,2,1,0:T(8,128)S(1)}, f32[2,1,64,3584]{3,2,1,0:T(8,128)}, u32[]{:S(2)}) copy-start(f32[2,1,64,3584]{3,2,1,0:T(8,128)} %refs_1_.9) | copy-start | bytes 5505028
  36.6 19.2 %copy-start.1 = (bf16[2,1,64,3584]{3,2,1,0:T(8,128)(2,1)S(1)}, bf16[2,1,64,3584]{3,2,1,0:T(8,128)(2,1)}, u32[]{:S(2)}) copy-start(bf16[2,1,64,3584]{3,2,1,0:T(8,128)(2,1)} %refs_2_.9) | copy-start | bytes 2752516
  36.6 19.2 %copy-start.2 = (bf16[2,1,64,3584]{3,2,1,0:T(8,128)(2,1)S(1)}, bf16[2,1,64,3584]{3,2,1,0:T(8,128)(2,1)}, u32[]{:S(2)}) copy-start(bf16[2,1,64,3584]{3,2,1,0:T(8,128)(2,1)} %refs_3_.9) | copy-start | bytes 2752516
  36.8 18.5 %collective-permute-start.13 = (bf16[2,64,896]{2,1,0:T(8,128)(2,1)S(1)}, bf16[2,64,896]{2,1,0:T(8,128)(2,1)S(1)}, u32[]{:S(2)}, u32[]{:S(2)}) collective-permute-start(bf16[2,64,896]{2,1,0:T(8,128)(2,1)S(1)} %share.6.refs_4_), channel_id=1, source_target_pairs={{0,24},{8,16},{16,8},{24,0},{1,25},{9,17},{17,9},{25,1},{2,26},{10... | collective-permute-start | bytes 688136 | tf_op jit(solution)/shard_map/ppermute | solution.py:25
  40.4 8.5 %collective-permute-start.15 = (bf16[2,64,768]{2,1,0:T(8,128)(2,1)S(1)}, bf16[2,64,768]{2,1,0:T(8,128)(2,1)S(1)}, u32[]{:S(2)}, u32[]{:S(2)}) collective-permute-start(bf16[2,64,768]{2,1,0:T(8,128)(2,1)S(1)} %get-tuple-element.58), channel_id=1, source_target_pairs={{0,2},{2,0},{4,6},{6,4},{1,3},{3,1},{5,7},{7,5},{8,10},{10,8},{12,... | collective-permute-start | bytes 589832 | tf_op jit(solution)/shard_map/ppermute | solution.py:20
  44.4 10.9 %collective-permute-start.16 = (bf16[2,64,768]{2,1,0:T(8,128)(2,1)S(1)}, bf16[2,64,768]{2,1,0:T(8,128)(2,1)S(1)}, u32[]{:S(2)}, u32[]{:S(2)}) collective-permute-start(bf16[2,64,768]{2,1,0:T(8,128)(2,1)S(1)} %get-tuple-element.59), channel_id=1, source_target_pairs={{0,4},{2,6},{4,0},{6,2},{1,5},{3,7},{5,1},{7,3},{8,12},{10,14},{12... | collective-permute-start | bytes 589832 | tf_op jit(solution)/shard_map/ppermute | solution.py:20
  45.9 9.4 %collective-permute-start.17 = (bf16[2,64,768]{2,1,0:T(8,128)(2,1)S(1)}, bf16[2,64,768]{2,1,0:T(8,128)(2,1)S(1)}, u32[]{:S(2)}, u32[]{:S(2)}) collective-permute-start(bf16[2,64,768]{2,1,0:T(8,128)(2,1)S(1)} %get-tuple-element.60), channel_id=1, source_target_pairs={{0,6},{2,4},{4,2},{6,0},{1,7},{3,5},{5,3},{7,1},{8,14},{10,12},{12... | collective-permute-start | bytes 589832 | tf_op jit(solution)/shard_map/ppermute | solution.py:20
  47.5 18.3 %collective-permute-start.9 = (bf16[2,64,896]{2,1,0:T(8,128)(2,1)S(1)}, bf16[2,64,896]{2,1,0:T(8,128)(2,1)S(1)}, u32[]{:S(2)}, u32[]{:S(2)}) collective-permute-start(bf16[2,64,896]{2,1,0:T(8,128)(2,1)S(1)} %share.5), channel_id=1, source_target_pairs={{0,24},{8,16},{16,8},{24,0},{1,25},{9,17},{17,9},{25,1},{2,26},{10... | collective-permute-start | bytes 688136 | tf_op jit(solution)/shard_map/ppermute | solution.py:25
  55.4 14.5 %collective-permute-start.18 = (bf16[2,64,768]{2,1,0:T(8,128)(2,1)S(1)}, bf16[2,64,768]{2,1,0:T(8,128)(2,1)S(1)}, u32[]{:S(2)}, u32[]{:S(2)}) collective-permute-start(bf16[2,64,768]{2,1,0:T(8,128)(2,1)S(1)} %share.7), channel_id=1, source_target_pairs={{0,24},{8,16},{16,8},{24,0},{1,25},{9,17},{17,9},{25,1},{2,26},{10... | collective-permute-start | bytes 589832 | tf_op jit(solution)/shard_map/ppermute | solution.py:25
  66.7 8.5 %collective-permute-start.14 = (bf16[16,3584]{1,0:T(8,128)(2,1)S(1)}, bf16[16,3584]{1,0:T(8,128)(2,1)S(1)}, u32[]{:S(2)}, u32[]{:S(2)}) collective-permute-start(bf16[16,3584]{1,0:T(8,128)(2,1)S(1)} %leaving.3), channel_id=1, source_target_pairs={{0,8},{8,16},{16,24},{24,0},{1,9},{9,17},{17,25},{25,1},{2,10},{10... | collective-permute-start | bytes 344072 | tf_op jit(solution)/shard_map/ppermute | solution.py:30
  70.4 3.7 %collective-permute-start.19 = (f32[8,128]{1,0:T(8,128)S(1)}, f32[8,128]{1,0:T(8,128)S(1)}, u32[]{:S(2)}, u32[]{:S(2)}) collective-permute-start(f32[8,128]{1,0:T(8,128)S(1)} %get-tuple-element.61.refs_0_), channel_id=1, source_target_pairs={{0,2},{2,0},{4,6},{6,4},{1,3},{3,1},{5,7},{7,5},{8,10},{10,8},{12,... | collective-permute-start | bytes 12296 | tf_op jit(solution)/shard_map/ppermute | solution.py:20
  71.9 4.6 %collective-permute-start.20 = (f32[8,128]{1,0:T(8,128)S(1)}, f32[8,128]{1,0:T(8,128)S(1)}, u32[]{:S(2)}, u32[]{:S(2)}) collective-permute-start(f32[8,128]{1,0:T(8,128)S(1)} %get-tuple-element.61.refs_0_), channel_id=1, source_target_pairs={{0,4},{2,6},{4,0},{6,2},{1,5},{3,7},{5,1},{7,3},{8,12},{10,14},{12... | collective-permute-start | bytes 12296 | tf_op jit(solution)/shard_map/ppermute | solution.py:20
  73.5 4.5 %collective-permute-start.21 = (f32[8,128]{1,0:T(8,128)S(1)}, f32[8,128]{1,0:T(8,128)S(1)}, u32[]{:S(2)}, u32[]{:S(2)}) collective-permute-start(f32[8,128]{1,0:T(8,128)S(1)} %get-tuple-element.61.refs_0_), channel_id=1, source_target_pairs={{0,6},{2,4},{4,2},{6,0},{1,7},{3,5},{5,3},{7,1},{8,14},{10,12},{12... | collective-permute-start | bytes 12296 | tf_op jit(solution)/shard_map/ppermute | solution.py:20

commit v9 on v8

--- a/solution.py
+++ b/solution.py
@@ -123,10 +123,16 @@
 
 
 def fetch_kernel(in_ref, *rest):
-    out_ref, sem = rest[-2:]
-    copy = pltpu.make_async_copy(in_ref.at[0, 0], out_ref, sem)
-    copy.start()
-    copy.wait()
+    out_ref, sems = rest[-2:]
+    step = out_ref.shape[0] // sems.shape[0]
+    copies = []
+    for k in range(sems.shape[0]):
+        rows = pl.ds(k * step, step)
+        copies.append(pltpu.make_async_copy(in_ref.at[0, 0, rows], out_ref.at[rows], sems.at[k]))
+    for copy in copies:
+        copy.start()
+    for copy in copies:
+        copy.wait()
 
 
 def leaving_kernel(start, own_ref, other_ref, x_ref, b_ref, *rest):
@@ -200,17 +206,10 @@
         )
 
 
-def merged(refs):
-    top = refs[0][...]
-    for ref in refs[1:]:
-        top = jnp.maximum(top, ref[...])
-    return top + 1e-06
-
-
-def code_kernel(group, *refs):
-    peak_refs, fresh_refs, (code_ref, token_ref) = refs[:group], refs[group:-2], refs[-2:]
+def code_kernel(peak_ref, *refs):
+    fresh_refs, (code_ref, token_ref) = refs[:-2], refs[-2:]
     token_ref[...] = jnp.zeros_like(token_ref)
-    column = (1.0 / merged(peak_refs)).T
+    column = (1.0 / (peak_ref[...] + 1e-06)).T
     for side in range(2):
         inverse = jnp.broadcast_to(column[:, side : side + 1], (LANES, LANES))
         block = 0
@@ -222,19 +221,20 @@
                 block += 1
 
 
-def scale_kernel(group, experts, *refs):
-    peak_refs, scale_ref = refs[:experts], refs[-1]
+def finish_kernel(start, group, tail_ref, placed_ref, token_ref, *refs):
+    peak_refs, (left_ref, scale_ref, sem) = refs[:-3], refs[-3:]
+    copy = pltpu.make_async_copy(tail_ref, left_ref.at[0, pl.ds(start, tail_ref.shape[0])], sem)
+    copy.start()
     blocks = scale_ref.shape[3]
     mine = lax.axis_index("expert") // group
-    for far in range(len(peak_refs) // group):
-        top = merged(peak_refs[far * group : (far + 1) * group])
+    for far, ref in enumerate(peak_refs):
         for side in range(2):
-            scale_ref[side, 0, pl.ds(mine ^ far, 1), :] = top[side : side + 1, :blocks]
-
-
-def place_kernel(start, in_ref, *rest):
-    out_ref, token_ref, sem = rest[-3:]
-    copy = pltpu.make_async_copy(in_ref, out_ref.at[0, pl.ds(start, in_ref.shape[0])], sem)
+            scale_ref[side, 0, pl.ds(mine ^ far, 1), :] = ref[side : side + 1, :blocks] + 1e-06
+    copy.wait()
+
+
+def place_kernel(in_ref, out_ref, token_ref, sem):
+    copy = pltpu.make_async_copy(in_ref, out_ref.at[0, pl.ds(0, in_ref.shape[0])], sem)
     copy.start()
     token_ref[...] = jnp.zeros_like(token_ref)
     copy.wait()
@@ -280,7 +280,7 @@
         in_specs=[ANY] * 2,
         out_specs=VMEM,
         out_shape=pltpu.VMEM((latent, width), BF16),
-        scratch_shapes=[pltpu.SemaphoreType.DMA],
+        scratch_shapes=[pltpu.SemaphoreType.DMA((4,))],
         compiler_params=ROOM,
         cost_estimate=pl.CostEstimate(flops=0, bytes_accessed=2 * latent * width, transcendentals=0),
         name="fetch",
@@ -337,20 +337,16 @@
         )
         arrived.append(mirrored(shares[-1], "pipe"))
 
-    def place(start, rows, kept=(), after=()):
-        return pl.pallas_call(
-            lambda *refs: place_kernel(start, *refs),
-            in_specs=[ANY] * (1 + len(kept) + len(after)),
-            out_specs=[ANY, VMEM],
-            out_shape=[shape((1, tokens, width), BF16), shape((8, LANES), F32)],
-            scratch_shapes=[pltpu.SemaphoreType.DMA],
-            input_output_aliases={1 + k: k for k in range(len(kept))},
-            compiler_params=ROOM,
-            cost_estimate=pl.CostEstimate(flops=0, bytes_accessed=4 * rows.shape[0] * width, transcendentals=0),
-            name="place",
-        )(rows, *kept, *after)
-
-    placed, token = place(0, left_head)
+    placed, token = pl.pallas_call(
+        place_kernel,
+        in_specs=[ANY],
+        out_specs=[ANY, VMEM],
+        out_shape=[shape((1, tokens, width), BF16), shape((8, LANES), F32)],
+        scratch_shapes=[pltpu.SemaphoreType.DMA],
+        compiler_params=ROOM,
+        cost_estimate=pl.CostEstimate(flops=0, bytes_accessed=4 * head * width, transcendentals=0),
+        name="place",
+    )(left_head)
 
     fresh, peaks, steps = [], None, []
     for chunk, (start, stop) in enumerate(chunks):
@@ -376,25 +372,29 @@
     left_tail = turned(leaving(head, tokens - head, steps[-2]), "pipe")
 
     group = LANES // depth
-    peak_rows = [peaks] + [exchange(peaks, "expert", k) for k in range(1, experts)]
+    for level in range(group.bit_length() - 1):
+        peaks = jnp.maximum(peaks, exchange(peaks, "expert", 1 << level))
+    peak_rows = [peaks] + [exchange(peaks, "expert", k * group) for k in range(1, experts // group)]
     coded, token = call(
-        lambda *refs: code_kernel(group, *refs),
+        code_kernel,
         "codes",
         [shape((2, 1, depth, width), BF16), shape((8, LANES), F32)],
-        *peak_rows[:group],
+        peaks,
         *fresh,
-        read=group + len(fresh),
+        read=1 + len(fresh),
         flops=4 * depth * width,
     )
-    scales = call(
-        lambda *refs: scale_kernel(group, experts, *refs),
-        "scales",
-        shape((2, 1, experts // group, blocks), F32),
-        *peak_rows,
-        token,
-        read=experts,
-    )
-    left, _ = place(head, left_tail, (placed,), (token,))
+    left, scales = pl.pallas_call(
+        lambda *refs: finish_kernel(head, group, *refs),
+        in_specs=[ANY] * 3 + [VMEM] * len(peak_rows),
+        out_specs=[ANY, VMEM],
+        out_shape=[shape((1, tokens, width), BF16), shape((2, 1, experts // group, blocks), F32)],
+        scratch_shapes=[pltpu.SemaphoreType.DMA],
+        input_output_aliases={1: 0},
+        compiler_params=ROOM,
+        cost_estimate=pl.CostEstimate(flops=0, bytes_accessed=4 * (tokens - head) * width, transcendentals=0),
+        name="finish",
+    )(left_tail, placed, token, *peak_rows)
     return (left, coded, scales)
 
 

time: 78.8 us -> 79.1 us (level)
  waiting for transfers between devices: 36.4 us -> 37.8 us
    ppermute x16 -> x15, waiting for transfers between devices: 22.1 us -> 23.6 us  [exchange(): return lax.ppermute(block, axis, [(i, i ^ offset) for i in range(count)])]
    pallas_call x16 -> x15, Pallas kernels: 7.27 us -> 6.69 us  [call(): pl.pallas_call(kernel, in_specs=[VMEM] * read + [ANY] * (len(operands) -...]
    ppermute x16 -> x15, starting transfers between devices: 19.5 us -> 19 us  [exchange(): return lax.ppermute(block, axis, [(i, i ^ offset) for i in range(count)])]
  transfers between devices with their start and end apart: 22 -> 21, of which waited for: 13 -> 13; matrix products, arithmetic and copies ran while one was open for 0% -> 0% of each run, Pallas kernels for 12% -> 11%
where the time goes in v9:
time: 79.1 us; the launch traced here: 78.9 us
  waiting for transfers between devices  37.8 us (48%)
  starting transfers between devices  25.9 us (33%)
  Pallas kernels  14.4 us (18%)
    ppermute x15, waiting for transfers between devices, exchange(): return lax.ppermute(block, axis, [(i, i ^ offset) for i in range(count)])  23.6 us
    ppermute x15, starting transfers between devices, exchange(): return lax.ppermute(block, axis, [(i, i ^ offset) for i in range(count)])  19 us
    ppermute x4, waiting for transfers between devices, mirrored(): return lax.ppermute(block, axis, [(i, count - 1 - i) for i in range(count)])  14.2 us
    pallas_call x15, Pallas kernels, call(): pl.pallas_call(kernel, in_specs=[VMEM] * read + [ANY] * (len(operands) -...  6.69 us
    ppermute x4, starting transfers between devices, mirrored(): return lax.ppermute(block, axis, [(i, count - 1 - i) for i in range(count)])  5.17 us
    pallas_call x1, Pallas kernels, shards(): pl.pallas_call(lambda *refs: latent_kernel(tiles, *refs), in_specs=[ANY]...  4.15 us
    ppermute x2, starting transfers between devices, turned(): lax.ppermute(block, axis, [(i, (i + 1) % count) for i in range(count)])  1.69 us
  transfers between devices with their start and end apart: 21, of which 13 were waited for; matrix products, arithmetic and copies ran while one was open for 0% of the time, Pallas kernels for 11%

profile of v9, /device:TPU:8, one launch (start us, length us, event | category | flops | bytes accessed | tf_op | source)
XLA Modules:
  0.0 78.9 jit_solution(2614936278449749053)
XLA Ops:
  0.6 4.2 %latents.1 = (f32[1024,128]{1,0:T(8,128)S(1)}, bf16[128,3584]{1,0:T(8,128)(2,1)S(1)}, bf16[128,3584]{1,0:T(8,128)(2,1)S(1)}, bf16[128,3584]{1,0:T(8,128)(2,1)S(1)}) custom-call(bf16[1,128,3584]{2,1,0:T(8,128)(2,1)} %refs_0_.1, bf16[1,128,3584]{2,1,0:T(8,128)(2,1)} %refs_1_.5, bf16[1,128,3584]{2,1,0:T(8,128)(2,1)} %refs_2_.5, ...), custom_call_target="tpu_custom_call" | custom-call | flops 704643072 | bytes 8257536 | tf_op jit(solution)/shard_map/latents/pallas_call | solution.py:259
  4.9 1.5 %fetch.1.refs_3_ = bf16[256,3584]{1,0:T(8,128)(2,1)S(1)} custom-call(bf16[2,1,256,3584]{3,2,1,0:T(8,128)(2,1)} %in_ref.1, f32[1024,128]{1,0:T(8,128)S(1)} %get-tuple-element.37.rest_0_.refs_0_), custom_call_target="tpu_custom_call" | custom-call | bytes 1835008 | tf_op jit(solution)/shard_map/fetch/pallas_call | solution.py:278
  7.3 1.6 %collective-permute-start.12 = (bf16[112,3584]{1,0:T(8,128)(2,1)S(1)}, bf16[112,3584]{1,0:T(8,128)(2,1)S(1)}, u32[]{:S(2)}, u32[]{:S(2)}) collective-permute-start(bf16[112,3584]{1,0:T(8,128)(2,1)S(1)} %leaving.2.refs_4_), channel_id=1, source_target_pairs={{0,8},{8,16},{16,24},{24,0},{1,9},{9,17},{17,25},{25,1},{2,10},{10... | collective-permute-start | bytes 2408456 | tf_op jit(solution)/shard_map/ppermute | solution.py:30
  9.5 1.6 %collective-permute-start.1 = (bf16[2,64,1024]{2,1,0:T(8,128)(2,1)S(1)}, bf16[2,64,1024]{2,1,0:T(8,128)(2,1)S(1)}, u32[]{:S(2)}, u32[]{:S(2)}) collective-permute-start(bf16[2,64,1024]{2,1,0:T(8,128)(2,1)S(1)} %get-tuple-element.42), channel_id=1, source_target_pairs={{0,2},{2,0},{4,6},{6,4},{1,3},{3,1},{5,7},{7,5},{8,10},{10,8},{12,... | collective-permute-start | bytes 786440 | tf_op jit(solution)/shard_map/ppermute | solution.py:20
  11.0 1.5 %collective-permute-start.2 = (bf16[2,64,1024]{2,1,0:T(8,128)(2,1)S(1)}, bf16[2,64,1024]{2,1,0:T(8,128)(2,1)S(1)}, u32[]{:S(2)}, u32[]{:S(2)}) collective-permute-start(bf16[2,64,1024]{2,1,0:T(8,128)(2,1)S(1)} %get-tuple-element.43), channel_id=1, source_target_pairs={{0,4},{2,6},{4,0},{6,2},{1,5},{3,7},{5,1},{7,3},{8,12},{10,14},{12... | collective-permute-start | bytes 786440 | tf_op jit(solution)/shard_map/ppermute | solution.py:20
  13.0 5.7 %collective-permute-done.1.refs_1_.refs_4_ = bf16[2,64,1024]{2,1,0:T(8,128)(2,1)S(1)} collective-permute-done((bf16[2,64,1024]{2,1,0:T(8,128)(2,1)S(1)}, bf16[2,64,1024]{2,1,0:T(8,128)(2,1)S(1)}, u32[]{:S(2)}, u32[]{:S(2)}) %collective-permute-start.1) | collective-permute-done | bytes 262176 | tf_op jit(solution)/shard_map/ppermute | solution.py:20
  19.2 1.6 %collective-permute-start.4 = (bf16[2,64,896]{2,1,0:T(8,128)(2,1)S(1)}, bf16[2,64,896]{2,1,0:T(8,128)(2,1)S(1)}, u32[]{:S(2)}, u32[]{:S(2)}) collective-permute-start(bf16[2,64,896]{2,1,0:T(8,128)(2,1)S(1)} %get-tuple-element.45), channel_id=1, source_target_pairs={{0,2},{2,0},{4,6},{6,4},{1,3},{3,1},{5,7},{7,5},{8,10},{10,8},{12,... | collective-permute-start | bytes 688136 | tf_op jit(solution)/shard_map/ppermute | solution.py:20
  20.8 1.5 %collective-permute-start.10 = (bf16[2,64,896]{2,1,0:T(8,128)(2,1)S(1)}, bf16[2,64,896]{2,1,0:T(8,128)(2,1)S(1)}, u32[]{:S(2)}, u32[]{:S(2)}) collective-permute-start(bf16[2,64,896]{2,1,0:T(8,128)(2,1)S(1)} %get-tuple-element.51), channel_id=1, source_target_pairs={{0,4},{2,6},{4,0},{6,2},{1,5},{3,7},{5,1},{7,3},{8,12},{10,14},{12... | collective-permute-start | bytes 688136 | tf_op jit(solution)/shard_map/ppermute | solution.py:20
  22.3 2.3 %collective-permute-done.2.refs_2_ = bf16[2,64,1024]{2,1,0:T(8,128)(2,1)S(1)} collective-permute-done((bf16[2,64,1024]{2,1,0:T(8,128)(2,1)S(1)}, bf16[2,64,1024]{2,1,0:T(8,128)(2,1)S(1)}, u32[]{:S(2)}, u32[]{:S(2)}) %collective-permute-start.2) | collective-permute-done | bytes 262176 | tf_op jit(solution)/shard_map/ppermute | solution.py:20
  24.6 0.8 %collective-permute-start.11 = (bf16[2,64,896]{2,1,0:T(8,128)(2,1)S(1)}, bf16[2,64,896]{2,1,0:T(8,128)(2,1)S(1)}, u32[]{:S(2)}, u32[]{:S(2)}) collective-permute-start(bf16[2,64,896]{2,1,0:T(8,128)(2,1)S(1)} %get-tuple-element.52), channel_id=1, source_target_pairs={{0,6},{2,4},{4,2},{6,0},{1,7},{3,5},{5,3},{7,1},{8,14},{10,12},{12... | collective-permute-start | bytes 688136 | tf_op jit(solution)/shard_map/ppermute | solution.py:20
  25.5 1.6 %collective-permute-start.8 = (bf16[2,64,1024]{2,1,0:T(8,128)(2,1)S(1)}, bf16[2,64,1024]{2,1,0:T(8,128)(2,1)S(1)}, u32[]{:S(2)}, u32[]{:S(2)}) collective-permute-start(bf16[2,64,1024]{2,1,0:T(8,128)(2,1)S(1)} %share.4.refs_4_), channel_id=1, source_target_pairs={{0,24},{8,16},{16,8},{24,0},{1,25},{9,17},{17,9},{25,1},{2,26},{10... | collective-permute-start | bytes 786440 | tf_op jit(solution)/shard_map/ppermute | solution.py:25
  27.1 2.1 %collective-permute-done.4.refs_5_.refs_1_ = bf16[2,64,896]{2,1,0:T(8,128)(2,1)S(1)} collective-permute-done((bf16[2,64,896]{2,1,0:T(8,128)(2,1)S(1)}, bf16[2,64,896]{2,1,0:T(8,128)(2,1)S(1)}, u32[]{:S(2)}, u32[]{:S(2)}) %collective-permute-start.4) | collective-permute-done | bytes 229408 | tf_op jit(solution)/shard_map/ppermute | solution.py:20
  29.8 1.6 %collective-permute-start.5 = (bf16[2,64,896]{2,1,0:T(8,128)(2,1)S(1)}, bf16[2,64,896]{2,1,0:T(8,128)(2,1)S(1)}, u32[]{:S(2)}, u32[]{:S(2)}) collective-permute-start(bf16[2,64,896]{2,1,0:T(8,128)(2,1)S(1)} %get-tuple-element.47), channel_id=1, source_target_pairs={{0,2},{2,0},{4,6},{6,4},{1,3},{3,1},{5,7},{7,5},{8,10},{10,8},{12,... | collective-permute-start | bytes 688136 | tf_op jit(solution)/shard_map/ppermute | solution.py:20
  31.4 1.9 %collective-permute-done.10.refs_2_ = bf16[2,64,896]{2,1,0:T(8,128)(2,1)S(1)} collective-permute-done((bf16[2,64,896]{2,1,0:T(8,128)(2,1)S(1)}, bf16[2,64,896]{2,1,0:T(8,128)(2,1)S(1)}, u32[]{:S(2)}, u32[]{:S(2)}) %collective-permute-start.10) | collective-permute-done | bytes 229408 | tf_op jit(solution)/shard_map/ppermute | solution.py:20
  33.3 1.7 %collective-permute-start.6 = (bf16[2,64,896]{2,1,0:T(8,128)(2,1)S(1)}, bf16[2,64,896]{2,1,0:T(8,128)(2,1)S(1)}, u32[]{:S(2)}, u32[]{:S(2)}) collective-permute-start(bf16[2,64,896]{2,1,0:T(8,128)(2,1)S(1)} %get-tuple-element.48), channel_id=1, source_target_pairs={{0,4},{2,6},{4,0},{6,2},{1,5},{3,7},{5,1},{7,3},{8,12},{10,14},{12... | collective-permute-start | bytes 688136 | tf_op jit(solution)/shard_map/ppermute | solution.py:20
  35.2 1.4 %collective-permute-start.7 = (bf16[2,64,896]{2,1,0:T(8,128)(2,1)S(1)}, bf16[2,64,896]{2,1,0:T(8,128)(2,1)S(1)}, u32[]{:S(2)}, u32[]{:S(2)}) collective-permute-start(bf16[2,64,896]{2,1,0:T(8,128)(2,1)S(1)} %get-tuple-element.49), channel_id=1, source_target_pairs={{0,6},{2,4},{4,2},{6,0},{1,7},{3,5},{5,3},{7,1},{8,14},{10,12},{12... | collective-permute-start | bytes 688136 | tf_op jit(solution)/shard_map/ppermute | solution.py:20
  36.8 1.6 %collective-permute-start.13 = (bf16[2,64,896]{2,1,0:T(8,128)(2,1)S(1)}, bf16[2,64,896]{2,1,0:T(8,128)(2,1)S(1)}, u32[]{:S(2)}, u32[]{:S(2)}) collective-permute-start(bf16[2,64,896]{2,1,0:T(8,128)(2,1)S(1)} %share.6.refs_4_), channel_id=1, source_target_pairs={{0,24},{8,16},{16,8},{24,0},{1,25},{9,17},{17,9},{25,1},{2,26},{10... | collective-permute-start | bytes 688136 | tf_op jit(solution)/shard_map/ppermute | solution.py:25
  38.4 1.6 %collective-permute-done.5.refs_1_.refs_5_ = bf16[2,64,896]{2,1,0:T(8,128)(2,1)S(1)} collective-permute-done((bf16[2,64,896]{2,1,0:T(8,128)(2,1)S(1)}, bf16[2,64,896]{2,1,0:T(8,128)(2,1)S(1)}, u32[]{:S(2)}, u32[]{:S(2)}) %collective-permute-start.5) | collective-permute-done | bytes 229408 | tf_op jit(solution)/shard_map/ppermute | solution.py:20
  41.2 3.2 %collective-permute-done.8.refs_4_.refs_0_ = bf16[2,64,1024]{2,1,0:T(8,128)(2,1)S(1)} collective-permute-done((bf16[2,64,1024]{2,1,0:T(8,128)(2,1)S(1)}, bf16[2,64,1024]{2,1,0:T(8,128)(2,1)S(1)}, u32[]{:S(2)}, u32[]{:S(2)}) %collective-permute-start.8) | collective-permute-done | bytes 262176 | tf_op jit(solution)/shard_map/ppermute | solution.py:25
  44.4 1.5 %collective-permute-start.16 = (bf16[2,64,768]{2,1,0:T(8,128)(2,1)S(1)}, bf16[2,64,768]{2,1,0:T(8,128)(2,1)S(1)}, u32[]{:S(2)}, u32[]{:S(2)}) collective-permute-start(bf16[2,64,768]{2,1,0:T(8,128)(2,1)S(1)} %get-tuple-element.60), channel_id=1, source_target_pairs={{0,4},{2,6},{4,0},{6,2},{1,5},{3,7},{5,1},{7,3},{8,12},{10,14},{12... | collective-permute-start | bytes 589832 | tf_op jit(solution)/shard_map/ppermute | solution.py:20
  45.9 1.4 %collective-permute-start.17 = (bf16[2,64,768]{2,1,0:T(8,128)(2,1)S(1)}, bf16[2,64,768]{2,1,0:T(8,128)(2,1)S(1)}, u32[]{:S(2)}, u32[]{:S(2)}) collective-permute-start(bf16[2,64,768]{2,1,0:T(8,128)(2,1)S(1)} %get-tuple-element.61), channel_id=1, source_target_pairs={{0,6},{2,4},{4,2},{6,0},{1,7},{3,5},{5,3},{7,1},{8,14},{10,12},{12... | collective-permute-start | bytes 589832 | tf_op jit(solution)/shard_map/ppermute | solution.py:20
  47.5 1.5 %collective-permute-start.9 = (bf16[2,64,896]{2,1,0:T(8,128)(2,1)S(1)}, bf16[2,64,896]{2,1,0:T(8,128)(2,1)S(1)}, u32[]{:S(2)}, u32[]{:S(2)}) collective-permute-start(bf16[2,64,896]{2,1,0:T(8,128)(2,1)S(1)} %share.5), channel_id=1, source_target_pairs={{0,24},{8,16},{16,8},{24,0},{1,25},{9,17},{17,9},{25,1},{2,26},{10... | collective-permute-start | bytes 688136 | tf_op jit(solution)/shard_map/ppermute | solution.py:25
  49.0 6.4 %collective-permute-done.16.refs_2_ = bf16[2,64,768]{2,1,0:T(8,128)(2,1)S(1)} collective-permute-done((bf16[2,64,768]{2,1,0:T(8,128)(2,1)S(1)}, bf16[2,64,768]{2,1,0:T(8,128)(2,1)S(1)}, u32[]{:S(2)}, u32[]{:S(2)}) %collective-permute-start.16) | collective-permute-done | bytes 196640 | tf_op jit(solution)/shard_map/ppermute | solution.py:20
  56.4 0.9 %place.1 = (bf16[1,128,3584]{2,1,0:T(8,128)(2,1)}, f32[8,128]{1,0:T(8,128)S(1)}) custom-call(bf16[112,3584]{1,0:T(8,128)(2,1)S(1)} %collective-permute-done.12.refs_4_.in_ref), custom_call_target="tpu_custom_call" | custom-call | bytes 1605632 | tf_op jit(solution)/shard_map/place/pallas_call | solution.py:340
  57.9 7.9 %collective-permute-done.9.refs_0_ = bf16[2,64,896]{2,1,0:T(8,128)(2,1)S(1)} collective-permute-done((bf16[2,64,896]{2,1,0:T(8,128)(2,1)S(1)}, bf16[2,64,896]{2,1,0:T(8,128)(2,1)S(1)}, u32[]{:S(2)}, u32[]{:S(2)}) %collective-permute-start.9) | collective-permute-done | bytes 229408 | tf_op jit(solution)/shard_map/ppermute | solution.py:25
  66.8 3.1 %collective-permute-done.18.refs_0_ = bf16[2,64,768]{2,1,0:T(8,128)(2,1)S(1)} collective-permute-done((bf16[2,64,768]{2,1,0:T(8,128)(2,1)S(1)}, bf16[2,64,768]{2,1,0:T(8,128)(2,1)S(1)}, u32[]{:S(2)}, u32[]{:S(2)}) %collective-permute-start.18) | collective-permute-done | bytes 196640 | tf_op jit(solution)/shard_map/ppermute | solution.py:25
  70.4 1.6 %collective-permute-start.19 = (f32[8,128]{1,0:T(8,128)S(1)}, f32[8,128]{1,0:T(8,128)S(1)}, u32[]{:S(2)}, u32[]{:S(2)}) collective-permute-start(f32[8,128]{1,0:T(8,128)S(1)} %get-tuple-element.62), channel_id=1, source_target_pairs={{0,2},{2,0},{4,6},{6,4},{1,3},{3,1},{5,7},{7,5},{8,10},{10,8},{12,... | collective-permute-start | bytes 12296 | tf_op jit(solution)/shard_map/ppermute | solution.py:20
  71.9 2.1 %collective-permute-done.19 = f32[8,128]{1,0:T(8,128)S(1)} collective-permute-done((f32[8,128]{1,0:T(8,128)S(1)}, f32[8,128]{1,0:T(8,128)S(1)}, u32[]{:S(2)}, u32[]{:S(2)}) %collective-permute-start.19) | collective-permute-done | bytes 4128 | tf_op jit(solution)/shard_map/ppermute | solution.py:20
  74.1 1.5 %collective-permute-start.20 = (f32[8,128]{1,0:T(8,128)S(1)}, f32[8,128]{1,0:T(8,128)S(1)}, u32[]{:S(2)}, u32[]{:S(2)}) collective-permute-start(f32[8,128]{1,0:T(8,128)S(1)} %max.3.peak_ref.refs_3_), channel_id=1, source_target_pairs={{0,4},{2,6},{4,0},{6,2},{1,5},{3,7},{5,1},{7,3},{8,12},{10,14},{12... | collective-permute-start | bytes 12296 | tf_op jit(solution)/shard_map/ppermute | solution.py:20
  75.6 1.2 %codes.1 = (bf16[2,1,64,3584]{3,2,1,0:T(8,128)(2,1)}, f32[8,128]{1,0:T(8,128)S(1)}) custom-call(f32[8,128]{1,0:T(8,128)S(1)} %max.3.peak_ref.refs_3_, f32[2,64,1024]{2,1,0:T(8,128)S(1)} %get-tuple-element.63.refs_0_, f32[2,64,896]{2,1,0:T(8,128)S(1)} %get-tuple-element.64.refs_1_, f32[2,64,896]{2,1,0:T(8,128)S(1)} %get-tuple-element.65.refs_2_, ...), custom_call_target="tpu_custom_call" | custom-call | flops 917504 | bytes 1839104 | tf_op jit(solution)/shard_map/codes/pallas_call | solution.py:51
  76.8 0.9 %collective-permute-done.20.refs_4_ = f32[8,128]{1,0:T(8,128)S(1)} collective-permute-done((f32[8,128]{1,0:T(8,128)S(1)}, f32[8,128]{1,0:T(8,128)S(1)}, u32[]{:S(2)}, u32[]{:S(2)}) %collective-permute-start.20) | collective-permute-done | bytes 4128 | tf_op jit(solution)/shard_map/ppermute | solution.py:20
  77.7 1.2 %finish.1 = (bf16[1,128,3584]{2,1,0:T(8,128)(2,1)}, f32[2,1,2,28]{3,2,1,0:T(2,128)}) custom-call(bf16[16,3584]{1,0:T(8,128)(2,1)S(1)} %collective-permute-done.14.refs_0_, bf16[1,128,3584]{2,1,0:T(8,128)(2,1)} %get-tuple-element.57.refs_1_, f32[8,128]{1,0:T(8,128)S(1)} %get-tuple-element.67.refs_2_, ...), custom_call_target="tpu_custom_call", output_to_operand_aliasing={{0}: (1, {})} | custom-call | bytes 229376 | tf_op jit(solution)/shard_map/finish/pallas_call | solution.py:387
  (36 shorter events, 7.9 us)
Async XLA Ops:
  4.8 2.0 %collective-permute-start = (f32[1024,128]{1,0:T(8,128)S(1)}, f32[1024,128]{1,0:T(8,128)S(1)}, u32[]{:S(2)}, u32[]{:S(2)}) collective-permute-start(f32[1024,128]{1,0:T(8,128)S(1)} %get-tuple-element.37.rest_0_.refs_0_), channel_id=1, source_target_pairs={{0,1},{1,0},{2,3},{3,2},{4,5},{5,4},{6,7},{7,6},{8,9},{9,8},{10,11... | collective-permute-start | bytes 1572872 | tf_op jit(solution)/shard_map/ppermute | solution.py:20
  7.3 29.3 %collective-permute-start.12 = (bf16[112,3584]{1,0:T(8,128)(2,1)S(1)}, bf16[112,3584]{1,0:T(8,128)(2,1)S(1)}, u32[]{:S(2)}, u32[]{:S(2)}) collective-permute-start(bf16[112,3584]{1,0:T(8,128)(2,1)S(1)} %leaving.2.refs_4_), channel_id=1, source_target_pairs={{0,8},{8,16},{16,24},{24,0},{1,9},{9,17},{17,25},{25,1},{2,10},{10... | collective-permute-start | bytes 2408456 | tf_op jit(solution)/shard_map/ppermute | solution.py:30
  9.5 9.3 %collective-permute-start.1 = (bf16[2,64,1024]{2,1,0:T(8,128)(2,1)S(1)}, bf16[2,64,1024]{2,1,0:T(8,128)(2,1)S(1)}, u32[]{:S(2)}, u32[]{:S(2)}) collective-permute-start(bf16[2,64,1024]{2,1,0:T(8,128)(2,1)S(1)} %get-tuple-element.42), channel_id=1, source_target_pairs={{0,2},{2,0},{4,6},{6,4},{1,3},{3,1},{5,7},{7,5},{8,10},{10,8},{12,... | collective-permute-start | bytes 786440 | tf_op jit(solution)/shard_map/ppermute | solution.py:20
  11.0 13.5 %collective-permute-start.2 = (bf16[2,64,1024]{2,1,0:T(8,128)(2,1)S(1)}, bf16[2,64,1024]{2,1,0:T(8,128)(2,1)S(1)}, u32[]{:S(2)}, u32[]{:S(2)}) collective-permute-start(bf16[2,64,1024]{2,1,0:T(8,128)(2,1)S(1)} %get-tuple-element.43), channel_id=1, source_target_pairs={{0,4},{2,6},{4,0},{6,2},{1,5},{3,7},{5,1},{7,3},{8,12},{10,14},{12... | collective-permute-start | bytes 786440 | tf_op jit(solution)/shard_map/ppermute | solution.py:20
  12.5 12.8 %collective-permute-start.3 = (bf16[2,64,1024]{2,1,0:T(8,128)(2,1)S(1)}, bf16[2,64,1024]{2,1,0:T(8,128)(2,1)S(1)}, u32[]{:S(2)}, u32[]{:S(2)}) collective-permute-start(bf16[2,64,1024]{2,1,0:T(8,128)(2,1)S(1)} %get-tuple-element.44), channel_id=1, source_target_pairs={{0,6},{2,4},{4,2},{6,0},{1,7},{3,5},{5,3},{7,1},{8,14},{10,12},{12... | collective-permute-start | bytes 786440 | tf_op jit(solution)/shard_map/ppermute | solution.py:20
  19.2 10.1 %collective-permute-start.4 = (bf16[2,64,896]{2,1,0:T(8,128)(2,1)S(1)}, bf16[2,64,896]{2,1,0:T(8,128)(2,1)S(1)}, u32[]{:S(2)}, u32[]{:S(2)}) collective-permute-start(bf16[2,64,896]{2,1,0:T(8,128)(2,1)S(1)} %get-tuple-element.45), channel_id=1, source_target_pairs={{0,2},{2,0},{4,6},{6,4},{1,3},{3,1},{5,7},{7,5},{8,10},{10,8},{12,... | collective-permute-start | bytes 688136 | tf_op jit(solution)/shard_map/ppermute | solution.py:20
  20.8 12.5 %collective-permute-start.10 = (bf16[2,64,896]{2,1,0:T(8,128)(2,1)S(1)}, bf16[2,64,896]{2,1,0:T(8,128)(2,1)S(1)}, u32[]{:S(2)}, u32[]{:S(2)}) collective-permute-start(bf16[2,64,896]{2,1,0:T(8,128)(2,1)S(1)} %get-tuple-element.51), channel_id=1, source_target_pairs={{0,4},{2,6},{4,0},{6,2},{1,5},{3,7},{5,1},{7,3},{8,12},{10,14},{12... | collective-permute-start | bytes 688136 | tf_op jit(solution)/shard_map/ppermute | solution.py:20
  24.6 10.6 %collective-permute-start.11 = (bf16[2,64,896]{2,1,0:T(8,128)(2,1)S(1)}, bf16[2,64,896]{2,1,0:T(8,128)(2,1)S(1)}, u32[]{:S(2)}, u32[]{:S(2)}) collective-permute-start(bf16[2,64,896]{2,1,0:T(8,128)(2,1)S(1)} %get-tuple-element.52), channel_id=1, source_target_pairs={{0,6},{2,4},{4,2},{6,0},{1,7},{3,5},{5,3},{7,1},{8,14},{10,12},{12... | collective-permute-start | bytes 688136 | tf_op jit(solution)/shard_map/ppermute | solution.py:20
  25.5 18.9 %collective-permute-start.8 = (bf16[2,64,1024]{2,1,0:T(8,128)(2,1)S(1)}, bf16[2,64,1024]{2,1,0:T(8,128)(2,1)S(1)}, u32[]{:S(2)}, u32[]{:S(2)}) collective-permute-start(bf16[2,64,1024]{2,1,0:T(8,128)(2,1)S(1)} %share.4.refs_4_), channel_id=1, source_target_pairs={{0,24},{8,16},{16,8},{24,0},{1,25},{9,17},{17,9},{25,1},{2,26},{10... | collective-permute-start | bytes 786440 | tf_op jit(solution)/shard_map/ppermute | solution.py:25
  29.8 10.2 %collective-permute-start.5 = (bf16[2,64,896]{2,1,0:T(8,128)(2,1)S(1)}, bf16[2,64,896]{2,1,0:T(8,128)(2,1)S(1)}, u32[]{:S(2)}, u32[]{:S(2)}) collective-permute-start(bf16[2,64,896]{2,1,0:T(8,128)(2,1)S(1)} %get-tuple-element.47), channel_id=1, source_target_pairs={{0,2},{2,0},{4,6},{6,4},{1,3},{3,1},{5,7},{7,5},{8,10},{10,8},{12,... | collective-permute-start | bytes 688136 | tf_op jit(solution)/shard_map/ppermute | solution.py:20
  33.3 12.6 %collective-permute-start.6 = (bf16[2,64,896]{2,1,0:T(8,128)(2,1)S(1)}, bf16[2,64,896]{2,1,0:T(8,128)(2,1)S(1)}, u32[]{:S(2)}, u32[]{:S(2)}) collective-permute-start(bf16[2,64,896]{2,1,0:T(8,128)(2,1)S(1)} %get-tuple-element.48), channel_id=1, source_target_pairs={{0,4},{2,6},{4,0},{6,2},{1,5},{3,7},{5,1},{7,3},{8,12},{10,14},{12... | collective-permute-start | bytes 688136 | tf_op jit(solution)/shard_map/ppermute | solution.py:20
  35.2 12.1 %collective-permute-start.7 = (bf16[2,64,896]{2,1,0:T(8,128)(2,1)S(1)}, bf16[2,64,896]{2,1,0:T(8,128)(2,1)S(1)}, u32[]{:S(2)}, u32[]{:S(2)}) collective-permute-start(bf16[2,64,896]{2,1,0:T(8,128)(2,1)S(1)} %get-tuple-element.49), channel_id=1, source_target_pairs={{0,6},{2,4},{4,2},{6,0},{1,7},{3,5},{5,3},{7,1},{8,14},{10,12},{12... | collective-permute-start | bytes 688136 | tf_op jit(solution)/shard_map/ppermute | solution.py:20
  36.6 19.2 %copy-start = (f32[2,1,64,3584]{3,2,1,0:T(8,128)S(1)}, f32[2,1,64,3584]{3,2,1,0:T(8,128)}, u32[]{:S(2)}) copy-start(f32[2,1,64,3584]{3,2,1,0:T(8,128)} %refs_1_.9) | copy-start | bytes 5505028
  36.6 19.2 %copy-start.1 = (bf16[2,1,64,3584]{3,2,1,0:T(8,128)(2,1)S(1)}, bf16[2,1,64,3584]{3,2,1,0:T(8,128)(2,1)}, u32[]{:S(2)}) copy-start(bf16[2,1,64,3584]{3,2,1,0:T(8,128)(2,1)} %refs_2_.9) | copy-start | bytes 2752516
  36.6 19.2 %copy-start.2 = (bf16[2,1,64,3584]{3,2,1,0:T(8,128)(2,1)S(1)}, bf16[2,1,64,3584]{3,2,1,0:T(8,128)(2,1)}, u32[]{:S(2)}) copy-start(bf16[2,1,64,3584]{3,2,1,0:T(8,128)(2,1)} %refs_3_.9) | copy-start | bytes 2752516
  36.8 18.5 %collective-permute-start.13 = (bf16[2,64,896]{2,1,0:T(8,128)(2,1)S(1)}, bf16[2,64,896]{2,1,0:T(8,128)(2,1)S(1)}, u32[]{:S(2)}, u32[]{:S(2)}) collective-permute-start(bf16[2,64,896]{2,1,0:T(8,128)(2,1)S(1)} %share.6.refs_4_), channel_id=1, source_target_pairs={{0,24},{8,16},{16,8},{24,0},{1,25},{9,17},{17,9},{25,1},{2,26},{10... | collective-permute-start | bytes 688136 | tf_op jit(solution)/shard_map/ppermute | solution.py:25
  40.4 8.5 %collective-permute-start.15 = (bf16[2,64,768]{2,1,0:T(8,128)(2,1)S(1)}, bf16[2,64,768]{2,1,0:T(8,128)(2,1)S(1)}, u32[]{:S(2)}, u32[]{:S(2)}) collective-permute-start(bf16[2,64,768]{2,1,0:T(8,128)(2,1)S(1)} %get-tuple-element.59), channel_id=1, source_target_pairs={{0,2},{2,0},{4,6},{6,4},{1,3},{3,1},{5,7},{7,5},{8,10},{10,8},{12,... | collective-permute-start | bytes 589832 | tf_op jit(solution)/shard_map/ppermute | solution.py:20
  44.4 10.9 %collective-permute-start.16 = (bf16[2,64,768]{2,1,0:T(8,128)(2,1)S(1)}, bf16[2,64,768]{2,1,0:T(8,128)(2,1)S(1)}, u32[]{:S(2)}, u32[]{:S(2)}) collective-permute-start(bf16[2,64,768]{2,1,0:T(8,128)(2,1)S(1)} %get-tuple-element.60), channel_id=1, source_target_pairs={{0,4},{2,6},{4,0},{6,2},{1,5},{3,7},{5,1},{7,3},{8,12},{10,14},{12... | collective-permute-start | bytes 589832 | tf_op jit(solution)/shard_map/ppermute | solution.py:20
  45.9 9.4 %collective-permute-start.17 = (bf16[2,64,768]{2,1,0:T(8,128)(2,1)S(1)}, bf16[2,64,768]{2,1,0:T(8,128)(2,1)S(1)}, u32[]{:S(2)}, u32[]{:S(2)}) collective-permute-start(bf16[2,64,768]{2,1,0:T(8,128)(2,1)S(1)} %get-tuple-element.61), channel_id=1, source_target_pairs={{0,6},{2,4},{4,2},{6,0},{1,7},{3,5},{5,3},{7,1},{8,14},{10,12},{12... | collective-permute-start | bytes 589832 | tf_op jit(solution)/shard_map/ppermute | solution.py:20
  47.5 18.3 %collective-permute-start.9 = (bf16[2,64,896]{2,1,0:T(8,128)(2,1)S(1)}, bf16[2,64,896]{2,1,0:T(8,128)(2,1)S(1)}, u32[]{:S(2)}, u32[]{:S(2)}) collective-permute-start(bf16[2,64,896]{2,1,0:T(8,128)(2,1)S(1)} %share.5), channel_id=1, source_target_pairs={{0,24},{8,16},{16,8},{24,0},{1,25},{9,17},{17,9},{25,1},{2,26},{10... | collective-permute-start | bytes 688136 | tf_op jit(solution)/shard_map/ppermute | solution.py:25
  55.4 14.5 %collective-permute-start.18 = (bf16[2,64,768]{2,1,0:T(8,128)(2,1)S(1)}, bf16[2,64,768]{2,1,0:T(8,128)(2,1)S(1)}, u32[]{:S(2)}, u32[]{:S(2)}) collective-permute-start(bf16[2,64,768]{2,1,0:T(8,128)(2,1)S(1)} %share.7), channel_id=1, source_target_pairs={{0,24},{8,16},{16,8},{24,0},{1,25},{9,17},{17,9},{25,1},{2,26},{10... | collective-permute-start | bytes 589832 | tf_op jit(solution)/shard_map/ppermute | solution.py:25
  66.7 10.0 %collective-permute-start.14 = (bf16[16,3584]{1,0:T(8,128)(2,1)S(1)}, bf16[16,3584]{1,0:T(8,128)(2,1)S(1)}, u32[]{:S(2)}, u32[]{:S(2)}) collective-permute-start(bf16[16,3584]{1,0:T(8,128)(2,1)S(1)} %leaving.3), channel_id=1, source_target_pairs={{0,8},{8,16},{16,24},{24,0},{1,9},{9,17},{17,25},{25,1},{2,10},{10... | collective-permute-start | bytes 344072 | tf_op jit(solution)/shard_map/ppermute | solution.py:30
  70.4 3.7 %collective-permute-start.19 = (f32[8,128]{1,0:T(8,128)S(1)}, f32[8,128]{1,0:T(8,128)S(1)}, u32[]{:S(2)}, u32[]{:S(2)}) collective-permute-start(f32[8,128]{1,0:T(8,128)S(1)} %get-tuple-element.62), channel_id=1, source_target_pairs={{0,2},{2,0},{4,6},{6,4},{1,3},{3,1},{5,7},{7,5},{8,10},{10,8},{12,... | collective-permute-start | bytes 12296 | tf_op jit(solution)/shard_map/ppermute | solution.py:20
  74.1 3.6 %collective-permute-start.20 = (f32[8,128]{1,0:T(8,128)S(1)}, f32[8,128]{1,0:T(8,128)S(1)}, u32[]{:S(2)}, u32[]{:S(2)}) collective-permute-start(f32[8,128]{1,0:T(8,128)S(1)} %max.3.peak_ref.refs_3_), channel_id=1, source_target_pairs={{0,4},{2,6},{4,0},{6,2},{1,5},{3,7},{5,1},{7,3},{8,12},{10,14},{12... | collective-permute-start | bytes 12296 | tf_op jit(solution)/shard_map/ppermute | solution.py:20

commit v10 on v9

--- a/solution.py
+++ b/solution.py
@@ -28,6 +28,11 @@
 def turned(block, axis):
     count = lax.axis_size(axis)
     return lax.ppermute(block, axis, [(i, (i + 1) % count) for i in range(count)])
+
+
+def shifted(block, axis):
+    count = lax.axis_size(axis)
+    return lax.ppermute(block, axis, [(i, i + 1) for i in range(count - 1)])
 
 
 def halves_of_sum(block, axis):
@@ -233,11 +238,17 @@
     copy.wait()
 
 
-def place_kernel(in_ref, out_ref, token_ref, sem):
-    copy = pltpu.make_async_copy(in_ref, out_ref.at[0, pl.ds(0, in_ref.shape[0])], sem)
-    copy.start()
+def place_kernel(*refs):
+    in_refs, (out_ref, token_ref, sems) = refs[:-3], refs[-3:]
+    copies, start = [], 0
+    for k, ref in enumerate(in_refs):
+        copies.append(pltpu.make_async_copy(ref, out_ref.at[0, pl.ds(start, ref.shape[0])], sems.at[k]))
+        start += ref.shape[0]
+    for copy in copies:
+        copy.start()
     token_ref[...] = jnp.zeros_like(token_ref)
-    copy.wait()
+    for copy in copies:
+        copy.wait()
 
 
 def shards(enter_fwd, enter_rev, cot_rev, gain, proj_down, proj_up, master, moment, second):
@@ -315,15 +326,17 @@
             flops=4 * tokens * latent * (stop - start),
         )
 
-    head = 112
-    first_rows = leaving(0, head)
-    left_head = turned(first_rows, "pipe")
+    pieces_of = (48, 64, 16)
+    head = pieces_of[0] + pieces_of[1]
+    first_rows = leaving(0, pieces_of[0])
+    left_first = turned(first_rows, "pipe")
     first = grads(0, first_rows)
+    left_second = shifted(leaving(pieces_of[0], pieces_of[1], first[0]), "pipe")
     shares, arrived, others = [], [], []
     for chunk in range(len(chunks)):
-        own, *pieces = grads(chunk, *shares[-2:-1], *others[-1][:1]) if chunk else first
+        own, *pieces = grads(chunk, *shares[-2:-1], *others[-1][:2], *([left_first] if chunk == 1 else [])) if chunk else first
         others.append([exchange(piece, "expert", 1 + k) for k, piece in enumerate(pieces)])
-        after = [left_head] if chunk == 1 else arrived[chunk - 2 : chunk - 1] if chunk > 1 else []
+        after = [left_second] if chunk == 1 else arrived[chunk - 2 : chunk - 1] if chunk > 1 else []
         shares.append(
             call(
                 lambda *refs: share_kernel(experts, *refs),
@@ -339,14 +352,14 @@
 
     placed, token = pl.pallas_call(
         place_kernel,
-        in_specs=[ANY],
+        in_specs=[ANY] * 2,
         out_specs=[ANY, VMEM],
         out_shape=[shape((1, tokens, width), BF16), shape((8, LANES), F32)],
-        scratch_shapes=[pltpu.SemaphoreType.DMA],
+        scratch_shapes=[pltpu.SemaphoreType.DMA((2,))],
         compiler_params=ROOM,
         cost_estimate=pl.CostEstimate(flops=0, bytes_accessed=4 * head * width, transcendentals=0),
         name="place",
-    )(left_head)
+    )(left_first, left_second)
 
     fresh, peaks, steps = [], None, []
     for chunk, (start, stop) in enumerate(chunks):

time: 79.1 us -> 80.9 us (1.023)
  starting transfers between devices: 25.9 us -> 32.9 us
  waiting for transfers between devices: 37.8 us -> 31.9 us
    ppermute x4, waiting for transfers between devices: 14.2 us -> 3.51 us  [mirrored(): return lax.ppermute(block, axis, [(i, count - 1 - i) for i in range(count)])]
    ppermute x15, waiting for transfers between devices: 23.6 us -> 28.4 us  [exchange(): return lax.ppermute(block, axis, [(i, i ^ offset) for i in range(count)])]
    ppermute x0 -> x1, starting transfers between devices: none -> 3.49 us  [shifted(): return lax.ppermute(block, axis, [(i, i + 1) for i in range(count - 1)])]
    ppermute x15, starting transfers between devices: 19 us -> 22.3 us  [exchange(): return lax.ppermute(block, axis, [(i, i ^ offset) for i in range(count)])]
    ppermute x2, starting transfers between devices: 1.69 us -> 4.1 us  [turned(): lax.ppermute(block, axis, [(i, (i + 1) % count) for i in range(count)])]
    ppermute x4, starting transfers between devices: 5.17 us -> 3.06 us  [mirrored(): return lax.ppermute(block, axis, [(i, count - 1 - i) for i in range(count)])]
    pallas_call x15 -> x16, Pallas kernels: 6.69 us -> 7.03 us  [call(): pl.pallas_call(kernel, in_specs=[VMEM] * read + [ANY] * (len(operands) -...]
  transfers between devices with their start and end apart: 21 -> 22, of which waited for: 13 -> 14; matrix products, arithmetic and copies ran while one was open for 0% -> 0% of each run, Pallas kernels for 11% -> 11%
where the time goes in v10:
time: 80.9 us; the launch traced here: 80.5 us
  starting transfers between devices  32.9 us (41%)
  waiting for transfers between devices  31.9 us (39%)
  Pallas kernels  14.8 us (18%)
  between operations  0.88 us (1%)
    ppermute x15, waiting for transfers between devices, exchange(): return lax.ppermute(block, axis, [(i, i ^ offset) for i in range(count)])  28.4 us
    ppermute x15, starting transfers between devices, exchange(): return lax.ppermute(block, axis, [(i, i ^ offset) for i in range(count)])  22.3 us
    pallas_call x16, Pallas kernels, call(): pl.pallas_call(kernel, in_specs=[VMEM] * read + [ANY] * (len(operands) -...  7.03 us
    pallas_call x1, Pallas kernels, shards(): pl.pallas_call(lambda *refs: latent_kernel(tiles, *refs), in_specs=[ANY]...  4.12 us
    ppermute x2, starting transfers between devices, turned(): lax.ppermute(block, axis, [(i, (i + 1) % count) for i in range(count)])  4.1 us
    ppermute x4, waiting for transfers between devices, mirrored(): return lax.ppermute(block, axis, [(i, count - 1 - i) for i in range(count)])  3.51 us
    ppermute x1, starting transfers between devices, shifted(): return lax.ppermute(block, axis, [(i, i + 1) for i in range(count - 1)])  3.49 us
    ppermute x4, starting transfers between devices, mirrored(): return lax.ppermute(block, axis, [(i, count - 1 - i) for i in range(count)])  3.06 us
  transfers between devices with their start and end apart: 22, of which 14 were waited for; matrix products, arithmetic and copies ran while one was open for 0% of the time, Pallas kernels for 11%

profile of v10, /device:TPU:8, one launch (start us, length us, event | category | flops | bytes accessed | tf_op | source)
XLA Modules:
  0.0 80.5 jit_solution(17032112726599213194)
XLA Ops:
  0.6 4.1 %latents.1 = (f32[1024,128]{1,0:T(8,128)S(1)}, bf16[128,3584]{1,0:T(8,128)(2,1)S(1)}, bf16[128,3584]{1,0:T(8,128)(2,1)S(1)}, bf16[128,3584]{1,0:T(8,128)(2,1)S(1)}) custom-call(bf16[1,128,3584]{2,1,0:T(8,128)(2,1)} %refs_0_.1, bf16[1,128,3584]{2,1,0:T(8,128)(2,1)} %refs_1_.5, bf16[1,128,3584]{2,1,0:T(8,128)(2,1)} %refs_2_.5, ...), custom_call_target="tpu_custom_call" | custom-call | flops 704643072 | bytes 8257536 | tf_op jit(solution)/shard_map/latents/pallas_call | solution.py:270
  4.8 1.5 %fetch.1.refs_3_ = bf16[256,3584]{1,0:T(8,128)(2,1)S(1)} custom-call(bf16[2,1,256,3584]{3,2,1,0:T(8,128)(2,1)} %in_ref.1, f32[1024,128]{1,0:T(8,128)S(1)} %get-tuple-element.37.rest_0_.refs_0_), custom_call_target="tpu_custom_call" | custom-call | bytes 1835008 | tf_op jit(solution)/shard_map/fetch/pallas_call | solution.py:289
  7.2 1.6 %collective-permute-start.4 = (bf16[48,3584]{1,0:T(8,128)(2,1)S(1)}, bf16[48,3584]{1,0:T(8,128)(2,1)S(1)}, u32[]{:S(2)}, u32[]{:S(2)}) collective-permute-start(bf16[48,3584]{1,0:T(8,128)(2,1)S(1)} %leaving.3.refs_4_), channel_id=1, source_target_pairs={{0,8},{8,16},{16,24},{24,0},{1,9},{9,17},{17,25},{25,1},{2,10},{10... | collective-permute-start | bytes 1032200 | tf_op jit(solution)/shard_map/ppermute | solution.py:30
  9.3 1.6 %collective-permute-start.1 = (bf16[2,64,1024]{2,1,0:T(8,128)(2,1)S(1)}, bf16[2,64,1024]{2,1,0:T(8,128)(2,1)S(1)}, u32[]{:S(2)}, u32[]{:S(2)}) collective-permute-start(bf16[2,64,1024]{2,1,0:T(8,128)(2,1)S(1)} %get-tuple-element.42), channel_id=1, source_target_pairs={{0,2},{2,0},{4,6},{6,4},{1,3},{3,1},{5,7},{7,5},{8,10},{10,8},{12,... | collective-permute-start | bytes 786440 | tf_op jit(solution)/shard_map/ppermute | solution.py:20
  10.9 1.5 %collective-permute-start.2 = (bf16[2,64,1024]{2,1,0:T(8,128)(2,1)S(1)}, bf16[2,64,1024]{2,1,0:T(8,128)(2,1)S(1)}, u32[]{:S(2)}, u32[]{:S(2)}) collective-permute-start(bf16[2,64,1024]{2,1,0:T(8,128)(2,1)S(1)} %get-tuple-element.43), channel_id=1, source_target_pairs={{0,4},{2,6},{4,0},{6,2},{1,5},{3,7},{5,1},{7,3},{8,12},{10,14},{12... | collective-permute-start | bytes 786440 | tf_op jit(solution)/shard_map/ppermute | solution.py:20
  12.9 3.5 %collective-permute-start.13 = (bf16[64,3584]{1,0:T(8,128)(2,1)S(1)}, bf16[64,3584]{1,0:T(8,128)(2,1)S(1)}, u32[]{:S(2)}, u32[]{:S(2)}) collective-permute-start(bf16[64,3584]{1,0:T(8,128)(2,1)S(1)} %leaving.4), channel_id=1, source_target_pairs={{0,8},{8,16},{16,24},{1,9},{9,17},{17,25},{2,10},{10,18},{18,26},{... | collective-permute-start | bytes 1376264 | tf_op jit(solution)/shard_map/ppermute | solution.py:35
  17.5 5.3 %collective-permute-done.2.refs_2_.refs_5_ = bf16[2,64,1024]{2,1,0:T(8,128)(2,1)S(1)} collective-permute-done((bf16[2,64,1024]{2,1,0:T(8,128)(2,1)S(1)}, bf16[2,64,1024]{2,1,0:T(8,128)(2,1)S(1)}, u32[]{:S(2)}, u32[]{:S(2)}) %collective-permute-start.2) | collective-permute-done | bytes 262176 | tf_op jit(solution)/shard_map/ppermute | solution.py:20
  23.3 3.0 %collective-permute-start.6 = (bf16[2,64,896]{2,1,0:T(8,128)(2,1)S(1)}, bf16[2,64,896]{2,1,0:T(8,128)(2,1)S(1)}, u32[]{:S(2)}, u32[]{:S(2)}) collective-permute-start(bf16[2,64,896]{2,1,0:T(8,128)(2,1)S(1)} %get-tuple-element.46), channel_id=1, source_target_pairs={{0,4},{2,6},{4,0},{6,2},{1,5},{3,7},{5,1},{7,3},{8,12},{10,14},{12... | collective-permute-start | bytes 688136 | tf_op jit(solution)/shard_map/ppermute | solution.py:20
  26.4 1.4 %collective-permute-start.12 = (bf16[2,64,896]{2,1,0:T(8,128)(2,1)S(1)}, bf16[2,64,896]{2,1,0:T(8,128)(2,1)S(1)}, u32[]{:S(2)}, u32[]{:S(2)}) collective-permute-start(bf16[2,64,896]{2,1,0:T(8,128)(2,1)S(1)} %get-tuple-element.52), channel_id=1, source_target_pairs={{0,6},{2,4},{4,2},{6,0},{1,7},{3,5},{5,3},{7,1},{8,14},{10,12},{12... | collective-permute-start | bytes 688136 | tf_op jit(solution)/shard_map/ppermute | solution.py:20
  27.9 2.9 %collective-permute-start.10 = (bf16[2,64,1024]{2,1,0:T(8,128)(2,1)S(1)}, bf16[2,64,1024]{2,1,0:T(8,128)(2,1)S(1)}, u32[]{:S(2)}, u32[]{:S(2)}) collective-permute-start(bf16[2,64,1024]{2,1,0:T(8,128)(2,1)S(1)} %share.4.refs_4_), channel_id=1, source_target_pairs={{0,24},{8,16},{16,8},{24,0},{1,25},{9,17},{17,9},{25,1},{2,26},{10... | collective-permute-start | bytes 786440 | tf_op jit(solution)/shard_map/ppermute | solution.py:25
  30.8 0.7 collective-permute-done.5.refs_5_.refs_1_
  31.5 2.2 %collective-permute-done.6.refs_6_.refs_2_ = bf16[2,64,896]{2,1,0:T(8,128)(2,1)S(1)} collective-permute-done((bf16[2,64,896]{2,1,0:T(8,128)(2,1)S(1)}, bf16[2,64,896]{2,1,0:T(8,128)(2,1)S(1)}, u32[]{:S(2)}, u32[]{:S(2)}) %collective-permute-start.6) | collective-permute-done | bytes 229408 | tf_op jit(solution)/shard_map/ppermute | solution.py:20
  34.3 5.0 %collective-permute-start.7 = (bf16[2,64,896]{2,1,0:T(8,128)(2,1)S(1)}, bf16[2,64,896]{2,1,0:T(8,128)(2,1)S(1)}, u32[]{:S(2)}, u32[]{:S(2)}) collective-permute-start(bf16[2,64,896]{2,1,0:T(8,128)(2,1)S(1)} %get-tuple-element.48), channel_id=1, source_target_pairs={{0,2},{2,0},{4,6},{6,4},{1,3},{3,1},{5,7},{7,5},{8,10},{10,8},{12,... | collective-permute-start | bytes 688136 | tf_op jit(solution)/shard_map/ppermute | solution.py:20
  39.2 2.6 %collective-permute-start.8 = (bf16[2,64,896]{2,1,0:T(8,128)(2,1)S(1)}, bf16[2,64,896]{2,1,0:T(8,128)(2,1)S(1)}, u32[]{:S(2)}, u32[]{:S(2)}) collective-permute-start(bf16[2,64,896]{2,1,0:T(8,128)(2,1)S(1)} %get-tuple-element.49), channel_id=1, source_target_pairs={{0,4},{2,6},{4,0},{6,2},{1,5},{3,7},{5,1},{7,3},{8,12},{10,14},{12... | collective-permute-start | bytes 688136 | tf_op jit(solution)/shard_map/ppermute | solution.py:20
  42.1 2.3 %collective-permute-done.7.refs_1_.refs_5_ = bf16[2,64,896]{2,1,0:T(8,128)(2,1)S(1)} collective-permute-done((bf16[2,64,896]{2,1,0:T(8,128)(2,1)S(1)}, bf16[2,64,896]{2,1,0:T(8,128)(2,1)S(1)}, u32[]{:S(2)}, u32[]{:S(2)}) %collective-permute-start.7) | collective-permute-done | bytes 229408 | tf_op jit(solution)/shard_map/ppermute | solution.py:20
  44.4 8.2 %collective-permute-done.8.refs_2_.refs_6_ = bf16[2,64,896]{2,1,0:T(8,128)(2,1)S(1)} collective-permute-done((bf16[2,64,896]{2,1,0:T(8,128)(2,1)S(1)}, bf16[2,64,896]{2,1,0:T(8,128)(2,1)S(1)}, u32[]{:S(2)}, u32[]{:S(2)}) %collective-permute-start.8) | collective-permute-done | bytes 229408 | tf_op jit(solution)/shard_map/ppermute | solution.py:20
  53.1 2.1 %collective-permute-start.17 = (bf16[2,64,768]{2,1,0:T(8,128)(2,1)S(1)}, bf16[2,64,768]{2,1,0:T(8,128)(2,1)S(1)}, u32[]{:S(2)}, u32[]{:S(2)}) collective-permute-start(bf16[2,64,768]{2,1,0:T(8,128)(2,1)S(1)} %get-tuple-element.60), channel_id=1, source_target_pairs={{0,4},{2,6},{4,0},{6,2},{1,5},{3,7},{5,1},{7,3},{8,12},{10,14},{12... | collective-permute-start | bytes 589832 | tf_op jit(solution)/shard_map/ppermute | solution.py:20
  55.2 1.4 %collective-permute-start.18 = (bf16[2,64,768]{2,1,0:T(8,128)(2,1)S(1)}, bf16[2,64,768]{2,1,0:T(8,128)(2,1)S(1)}, u32[]{:S(2)}, u32[]{:S(2)}) collective-permute-start(bf16[2,64,768]{2,1,0:T(8,128)(2,1)S(1)} %get-tuple-element.61), channel_id=1, source_target_pairs={{0,6},{2,4},{4,2},{6,0},{1,7},{3,5},{5,3},{7,1},{8,14},{10,12},{12... | collective-permute-start | bytes 589832 | tf_op jit(solution)/shard_map/ppermute | solution.py:20
  56.8 2.0 %collective-permute-done.16.refs_1_ = bf16[2,64,768]{2,1,0:T(8,128)(2,1)S(1)} collective-permute-done((bf16[2,64,768]{2,1,0:T(8,128)(2,1)S(1)}, bf16[2,64,768]{2,1,0:T(8,128)(2,1)S(1)}, u32[]{:S(2)}, u32[]{:S(2)}) %collective-permute-start.16) | collective-permute-done | bytes 196640 | tf_op jit(solution)/shard_map/ppermute | solution.py:20
  58.7 1.8 %collective-permute-done.17.refs_2_ = bf16[2,64,768]{2,1,0:T(8,128)(2,1)S(1)} collective-permute-done((bf16[2,64,768]{2,1,0:T(8,128)(2,1)S(1)}, bf16[2,64,768]{2,1,0:T(8,128)(2,1)S(1)}, u32[]{:S(2)}, u32[]{:S(2)}) %collective-permute-start.17) | collective-permute-done | bytes 196640 | tf_op jit(solution)/shard_map/ppermute | solution.py:20
  60.5 1.8 %collective-permute-done.18.refs_3_ = bf16[2,64,768]{2,1,0:T(8,128)(2,1)S(1)} collective-permute-done((bf16[2,64,768]{2,1,0:T(8,128)(2,1)S(1)}, bf16[2,64,768]{2,1,0:T(8,128)(2,1)S(1)}, u32[]{:S(2)}, u32[]{:S(2)}) %collective-permute-start.18) | collective-permute-done | bytes 196640 | tf_op jit(solution)/shard_map/ppermute | solution.py:20
  62.5 0.9 %place.1 = (bf16[1,128,3584]{2,1,0:T(8,128)(2,1)}, f32[8,128]{1,0:T(8,128)S(1)}) custom-call(bf16[48,3584]{1,0:T(8,128)(2,1)S(1)} %collective-permute-done.4.refs_6_.refs_0_, bf16[64,3584]{1,0:T(8,128)(2,1)S(1)} %collective-permute-done.13.refs_4_.refs_1_), custom_call_target="tpu_custom_call" | custom-call | bytes 1605632 | tf_op jit(solution)/shard_map/place/pallas_call | solution.py:353
  63.4 0.6 update.4
  64.6 1.3 %collective-permute-done.11.refs_0_ = bf16[2,64,896]{2,1,0:T(8,128)(2,1)S(1)} collective-permute-done((bf16[2,64,896]{2,1,0:T(8,128)(2,1)S(1)}, bf16[2,64,896]{2,1,0:T(8,128)(2,1)S(1)}, u32[]{:S(2)}, u32[]{:S(2)}) %collective-permute-start.11) | collective-permute-done | bytes 229408 | tf_op jit(solution)/shard_map/ppermute | solution.py:25
  66.8 2.5 %collective-permute-start.15 = (bf16[16,3584]{1,0:T(8,128)(2,1)S(1)}, bf16[16,3584]{1,0:T(8,128)(2,1)S(1)}, u32[]{:S(2)}, u32[]{:S(2)}) collective-permute-start(bf16[16,3584]{1,0:T(8,128)(2,1)S(1)} %leaving.5), channel_id=1, source_target_pairs={{0,8},{8,16},{16,24},{24,0},{1,9},{9,17},{17,25},{25,1},{2,10},{10... | collective-permute-start | bytes 344072 | tf_op jit(solution)/shard_map/ppermute | solution.py:30
  69.3 2.2 %collective-permute-done.19.refs_0_ = bf16[2,64,768]{2,1,0:T(8,128)(2,1)S(1)} collective-permute-done((bf16[2,64,768]{2,1,0:T(8,128)(2,1)S(1)}, bf16[2,64,768]{2,1,0:T(8,128)(2,1)S(1)}, u32[]{:S(2)}, u32[]{:S(2)}) %collective-permute-start.19) | collective-permute-done | bytes 196640 | tf_op jit(solution)/shard_map/ppermute | solution.py:25
  71.9 1.5 %collective-permute-start.20 = (f32[8,128]{1,0:T(8,128)S(1)}, f32[8,128]{1,0:T(8,128)S(1)}, u32[]{:S(2)}, u32[]{:S(2)}) collective-permute-start(f32[8,128]{1,0:T(8,128)S(1)} %get-tuple-element.62), channel_id=1, source_target_pairs={{0,2},{2,0},{4,6},{6,4},{1,3},{3,1},{5,7},{7,5},{8,10},{10,8},{12,... | collective-permute-start | bytes 12296 | tf_op jit(solution)/shard_map/ppermute | solution.py:20
  73.4 2.2 %collective-permute-done.20 = f32[8,128]{1,0:T(8,128)S(1)} collective-permute-done((f32[8,128]{1,0:T(8,128)S(1)}, f32[8,128]{1,0:T(8,128)S(1)}, u32[]{:S(2)}, u32[]{:S(2)}) %collective-permute-start.20) | collective-permute-done | bytes 4128 | tf_op jit(solution)/shard_map/ppermute | solution.py:20
  75.6 1.5 %collective-permute-start.21 = (f32[8,128]{1,0:T(8,128)S(1)}, f32[8,128]{1,0:T(8,128)S(1)}, u32[]{:S(2)}, u32[]{:S(2)}) collective-permute-start(f32[8,128]{1,0:T(8,128)S(1)} %max.3.peak_ref.refs_3_), channel_id=1, source_target_pairs={{0,4},{2,6},{4,0},{6,2},{1,5},{3,7},{5,1},{7,3},{8,12},{10,14},{12... | collective-permute-start | bytes 12296 | tf_op jit(solution)/shard_map/ppermute | solution.py:20
  77.1 1.2 %codes.1 = (bf16[2,1,64,3584]{3,2,1,0:T(8,128)(2,1)}, f32[8,128]{1,0:T(8,128)S(1)}) custom-call(f32[8,128]{1,0:T(8,128)S(1)} %max.3.peak_ref.refs_3_, f32[2,64,1024]{2,1,0:T(8,128)S(1)} %get-tuple-element.63.refs_0_, f32[2,64,896]{2,1,0:T(8,128)S(1)} %get-tuple-element.64.refs_1_, f32[2,64,896]{2,1,0:T(8,128)S(1)} %get-tuple-element.65.refs_2_, ...), custom_call_target="tpu_custom_call" | custom-call | flops 917504 | bytes 1839104 | tf_op jit(solution)/shard_map/codes/pallas_call | solution.py:56
  78.3 0.9 %collective-permute-done.21.refs_4_ = f32[8,128]{1,0:T(8,128)S(1)} collective-permute-done((f32[8,128]{1,0:T(8,128)S(1)}, f32[8,128]{1,0:T(8,128)S(1)}, u32[]{:S(2)}, u32[]{:S(2)}) %collective-permute-start.21) | collective-permute-done | bytes 4128 | tf_op jit(solution)/shard_map/ppermute | solution.py:20
  79.2 1.2 %finish.1 = (bf16[1,128,3584]{2,1,0:T(8,128)(2,1)}, f32[2,1,2,28]{3,2,1,0:T(2,128)}) custom-call(bf16[16,3584]{1,0:T(8,128)(2,1)S(1)} %collective-permute-done.15.refs_0_, bf16[1,128,3584]{2,1,0:T(8,128)(2,1)} %get-tuple-element.57.refs_1_, f32[8,128]{1,0:T(8,128)S(1)} %get-tuple-element.67.refs_2_, ...), custom_call_target="tpu_custom_call", output_to_operand_aliasing={{0}: (1, {})} | custom-call | bytes 229376 | tf_op jit(solution)/shard_map/finish/pallas_call | solution.py:400
  (39 shorter events, 7.2 us)
Async XLA Ops:
  4.8 2.0 %collective-permute-start = (f32[1024,128]{1,0:T(8,128)S(1)}, f32[1024,128]{1,0:T(8,128)S(1)}, u32[]{:S(2)}, u32[]{:S(2)}) collective-permute-start(f32[1024,128]{1,0:T(8,128)S(1)} %get-tuple-element.37.rest_0_.refs_0_), channel_id=1, source_target_pairs={{0,1},{1,0},{2,3},{3,2},{4,5},{5,4},{6,7},{7,6},{8,9},{9,8},{10,11... | collective-permute-start | bytes 1572872 | tf_op jit(solution)/shard_map/ppermute | solution.py:20
  7.2 15.6 %collective-permute-start.4 = (bf16[48,3584]{1,0:T(8,128)(2,1)S(1)}, bf16[48,3584]{1,0:T(8,128)(2,1)S(1)}, u32[]{:S(2)}, u32[]{:S(2)}) collective-permute-start(bf16[48,3584]{1,0:T(8,128)(2,1)S(1)} %leaving.3.refs_4_), channel_id=1, source_target_pairs={{0,8},{8,16},{16,24},{24,0},{1,9},{9,17},{17,25},{25,1},{2,10},{10... | collective-permute-start | bytes 1032200 | tf_op jit(solution)/shard_map/ppermute | solution.py:30
  9.3 8.1 %collective-permute-start.1 = (bf16[2,64,1024]{2,1,0:T(8,128)(2,1)S(1)}, bf16[2,64,1024]{2,1,0:T(8,128)(2,1)S(1)}, u32[]{:S(2)}, u32[]{:S(2)}) collective-permute-start(bf16[2,64,1024]{2,1,0:T(8,128)(2,1)S(1)} %get-tuple-element.42), channel_id=1, source_target_pairs={{0,2},{2,0},{4,6},{6,4},{1,3},{3,1},{5,7},{7,5},{8,10},{10,8},{12,... | collective-permute-start | bytes 786440 | tf_op jit(solution)/shard_map/ppermute | solution.py:20
  10.9 11.9 %collective-permute-start.2 = (bf16[2,64,1024]{2,1,0:T(8,128)(2,1)S(1)}, bf16[2,64,1024]{2,1,0:T(8,128)(2,1)S(1)}, u32[]{:S(2)}, u32[]{:S(2)}) collective-permute-start(bf16[2,64,1024]{2,1,0:T(8,128)(2,1)S(1)} %get-tuple-element.43), channel_id=1, source_target_pairs={{0,4},{2,6},{4,0},{6,2},{1,5},{3,7},{5,1},{7,3},{8,12},{10,14},{12... | collective-permute-start | bytes 786440 | tf_op jit(solution)/shard_map/ppermute | solution.py:20
  12.9 29.0 %collective-permute-start.13 = (bf16[64,3584]{1,0:T(8,128)(2,1)S(1)}, bf16[64,3584]{1,0:T(8,128)(2,1)S(1)}, u32[]{:S(2)}, u32[]{:S(2)}) collective-permute-start(bf16[64,3584]{1,0:T(8,128)(2,1)S(1)} %leaving.4), channel_id=1, source_target_pairs={{0,8},{8,16},{16,24},{1,9},{9,17},{17,25},{2,10},{10,18},{18,26},{... | collective-permute-start | bytes 1376264 | tf_op jit(solution)/shard_map/ppermute | solution.py:35
  16.4 11.4 %collective-permute-start.3 = (bf16[2,64,1024]{2,1,0:T(8,128)(2,1)S(1)}, bf16[2,64,1024]{2,1,0:T(8,128)(2,1)S(1)}, u32[]{:S(2)}, u32[]{:S(2)}) collective-permute-start(bf16[2,64,1024]{2,1,0:T(8,128)(2,1)S(1)} %get-tuple-element.44), channel_id=1, source_target_pairs={{0,6},{2,4},{4,2},{6,0},{1,7},{3,5},{5,3},{7,1},{8,14},{10,12},{12... | collective-permute-start | bytes 786440 | tf_op jit(solution)/shard_map/ppermute | solution.py:20
  23.3 8.2 %collective-permute-start.5 = (bf16[2,64,896]{2,1,0:T(8,128)(2,1)S(1)}, bf16[2,64,896]{2,1,0:T(8,128)(2,1)S(1)}, u32[]{:S(2)}, u32[]{:S(2)}) collective-permute-start(bf16[2,64,896]{2,1,0:T(8,128)(2,1)S(1)} %get-tuple-element.45), channel_id=1, source_target_pairs={{0,2},{2,0},{4,6},{6,4},{1,3},{3,1},{5,7},{7,5},{8,10},{10,8},{12,... | collective-permute-start | bytes 688136 | tf_op jit(solution)/shard_map/ppermute | solution.py:20
  23.3 10.4 %collective-permute-start.6 = (bf16[2,64,896]{2,1,0:T(8,128)(2,1)S(1)}, bf16[2,64,896]{2,1,0:T(8,128)(2,1)S(1)}, u32[]{:S(2)}, u32[]{:S(2)}) collective-permute-start(bf16[2,64,896]{2,1,0:T(8,128)(2,1)S(1)} %get-tuple-element.46), channel_id=1, source_target_pairs={{0,4},{2,6},{4,0},{6,2},{1,5},{3,7},{5,1},{7,3},{8,12},{10,14},{12... | collective-permute-start | bytes 688136 | tf_op jit(solution)/shard_map/ppermute | solution.py:20
  26.4 15.5 %collective-permute-start.12 = (bf16[2,64,896]{2,1,0:T(8,128)(2,1)S(1)}, bf16[2,64,896]{2,1,0:T(8,128)(2,1)S(1)}, u32[]{:S(2)}, u32[]{:S(2)}) collective-permute-start(bf16[2,64,896]{2,1,0:T(8,128)(2,1)S(1)} %get-tuple-element.52), channel_id=1, source_target_pairs={{0,6},{2,4},{4,2},{6,0},{1,7},{3,5},{5,3},{7,1},{8,14},{10,12},{12... | collective-permute-start | bytes 688136 | tf_op jit(solution)/shard_map/ppermute | solution.py:20
  27.9 27.3 %collective-permute-start.10 = (bf16[2,64,1024]{2,1,0:T(8,128)(2,1)S(1)}, bf16[2,64,1024]{2,1,0:T(8,128)(2,1)S(1)}, u32[]{:S(2)}, u32[]{:S(2)}) collective-permute-start(bf16[2,64,1024]{2,1,0:T(8,128)(2,1)S(1)} %share.4.refs_4_), channel_id=1, source_target_pairs={{0,24},{8,16},{16,8},{24,0},{1,25},{9,17},{17,9},{25,1},{2,26},{10... | collective-permute-start | bytes 786440 | tf_op jit(solution)/shard_map/ppermute | solution.py:25
  34.3 10.1 %collective-permute-start.7 = (bf16[2,64,896]{2,1,0:T(8,128)(2,1)S(1)}, bf16[2,64,896]{2,1,0:T(8,128)(2,1)S(1)}, u32[]{:S(2)}, u32[]{:S(2)}) collective-permute-start(bf16[2,64,896]{2,1,0:T(8,128)(2,1)S(1)} %get-tuple-element.48), channel_id=1, source_target_pairs={{0,2},{2,0},{4,6},{6,4},{1,3},{3,1},{5,7},{7,5},{8,10},{10,8},{12,... | collective-permute-start | bytes 688136 | tf_op jit(solution)/shard_map/ppermute | solution.py:20
  39.2 13.3 %collective-permute-start.8 = (bf16[2,64,896]{2,1,0:T(8,128)(2,1)S(1)}, bf16[2,64,896]{2,1,0:T(8,128)(2,1)S(1)}, u32[]{:S(2)}, u32[]{:S(2)}) collective-permute-start(bf16[2,64,896]{2,1,0:T(8,128)(2,1)S(1)} %get-tuple-element.49), channel_id=1, source_target_pairs={{0,4},{2,6},{4,0},{6,2},{1,5},{3,7},{5,1},{7,3},{8,12},{10,14},{12... | collective-permute-start | bytes 688136 | tf_op jit(solution)/shard_map/ppermute | solution.py:20
  41.9 14.7 %collective-permute-start.9 = (bf16[2,64,896]{2,1,0:T(8,128)(2,1)S(1)}, bf16[2,64,896]{2,1,0:T(8,128)(2,1)S(1)}, u32[]{:S(2)}, u32[]{:S(2)}) collective-permute-start(bf16[2,64,896]{2,1,0:T(8,128)(2,1)S(1)} %get-tuple-element.50), channel_id=1, source_target_pairs={{0,6},{2,4},{4,2},{6,0},{1,7},{3,5},{5,3},{7,1},{8,14},{10,12},{12... | collective-permute-start | bytes 688136 | tf_op jit(solution)/shard_map/ppermute | solution.py:20
  42.0 21.4 %copy-start = (f32[2,1,64,3584]{3,2,1,0:T(8,128)S(1)}, f32[2,1,64,3584]{3,2,1,0:T(8,128)}, u32[]{:S(2)}) copy-start(f32[2,1,64,3584]{3,2,1,0:T(8,128)} %refs_1_.9) | copy-start | bytes 5505028
  42.0 21.4 %copy-start.1 = (bf16[2,1,64,3584]{3,2,1,0:T(8,128)(2,1)S(1)}, bf16[2,1,64,3584]{3,2,1,0:T(8,128)(2,1)}, u32[]{:S(2)}) copy-start(bf16[2,1,64,3584]{3,2,1,0:T(8,128)(2,1)} %refs_2_.9) | copy-start | bytes 2752516
  42.0 21.4 %copy-start.2 = (bf16[2,1,64,3584]{3,2,1,0:T(8,128)(2,1)S(1)}, bf16[2,1,64,3584]{3,2,1,0:T(8,128)(2,1)}, u32[]{:S(2)}) copy-start(bf16[2,1,64,3584]{3,2,1,0:T(8,128)(2,1)} %refs_3_.9) | copy-start | bytes 2752516
  42.0 14.7 %collective-permute-start.14 = (bf16[2,64,896]{2,1,0:T(8,128)(2,1)S(1)}, bf16[2,64,896]{2,1,0:T(8,128)(2,1)S(1)}, u32[]{:S(2)}, u32[]{:S(2)}) collective-permute-start(bf16[2,64,896]{2,1,0:T(8,128)(2,1)S(1)} %share.6.refs_4_), channel_id=1, source_target_pairs={{0,24},{8,16},{16,8},{24,0},{1,25},{9,17},{17,9},{25,1},{2,26},{10... | collective-permute-start | bytes 688136 | tf_op jit(solution)/shard_map/ppermute | solution.py:25
  53.0 5.7 %collective-permute-start.16 = (bf16[2,64,768]{2,1,0:T(8,128)(2,1)S(1)}, bf16[2,64,768]{2,1,0:T(8,128)(2,1)S(1)}, u32[]{:S(2)}, u32[]{:S(2)}) collective-permute-start(bf16[2,64,768]{2,1,0:T(8,128)(2,1)S(1)} %get-tuple-element.59), channel_id=1, source_target_pairs={{0,2},{2,0},{4,6},{6,4},{1,3},{3,1},{5,7},{7,5},{8,10},{10,8},{12,... | collective-permute-start | bytes 589832 | tf_op jit(solution)/shard_map/ppermute | solution.py:20
  53.1 7.4 %collective-permute-start.17 = (bf16[2,64,768]{2,1,0:T(8,128)(2,1)S(1)}, bf16[2,64,768]{2,1,0:T(8,128)(2,1)S(1)}, u32[]{:S(2)}, u32[]{:S(2)}) collective-permute-start(bf16[2,64,768]{2,1,0:T(8,128)(2,1)S(1)} %get-tuple-element.60), channel_id=1, source_target_pairs={{0,4},{2,6},{4,0},{6,2},{1,5},{3,7},{5,1},{7,3},{8,12},{10,14},{12... | collective-permute-start | bytes 589832 | tf_op jit(solution)/shard_map/ppermute | solution.py:20
  55.2 7.1 %collective-permute-start.18 = (bf16[2,64,768]{2,1,0:T(8,128)(2,1)S(1)}, bf16[2,64,768]{2,1,0:T(8,128)(2,1)S(1)}, u32[]{:S(2)}, u32[]{:S(2)}) collective-permute-start(bf16[2,64,768]{2,1,0:T(8,128)(2,1)S(1)} %get-tuple-element.61), channel_id=1, source_target_pairs={{0,6},{2,4},{4,2},{6,0},{1,7},{3,5},{5,3},{7,1},{8,14},{10,12},{12... | collective-permute-start | bytes 589832 | tf_op jit(solution)/shard_map/ppermute | solution.py:20
  56.7 9.2 %collective-permute-start.11 = (bf16[2,64,896]{2,1,0:T(8,128)(2,1)S(1)}, bf16[2,64,896]{2,1,0:T(8,128)(2,1)S(1)}, u32[]{:S(2)}, u32[]{:S(2)}) collective-permute-start(bf16[2,64,896]{2,1,0:T(8,128)(2,1)S(1)} %share.5), channel_id=1, source_target_pairs={{0,24},{8,16},{16,8},{24,0},{1,25},{9,17},{17,9},{25,1},{2,26},{10... | collective-permute-start | bytes 688136 | tf_op jit(solution)/shard_map/ppermute | solution.py:25
  62.4 9.1 %collective-permute-start.19 = (bf16[2,64,768]{2,1,0:T(8,128)(2,1)S(1)}, bf16[2,64,768]{2,1,0:T(8,128)(2,1)S(1)}, u32[]{:S(2)}, u32[]{:S(2)}) collective-permute-start(bf16[2,64,768]{2,1,0:T(8,128)(2,1)S(1)} %share.7), channel_id=1, source_target_pairs={{0,24},{8,16},{16,8},{24,0},{1,25},{9,17},{17,9},{25,1},{2,26},{10... | collective-permute-start | bytes 589832 | tf_op jit(solution)/shard_map/ppermute | solution.py:25
  66.8 11.5 %collective-permute-start.15 = (bf16[16,3584]{1,0:T(8,128)(2,1)S(1)}, bf16[16,3584]{1,0:T(8,128)(2,1)S(1)}, u32[]{:S(2)}, u32[]{:S(2)}) collective-permute-start(bf16[16,3584]{1,0:T(8,128)(2,1)S(1)} %leaving.5), channel_id=1, source_target_pairs={{0,8},{8,16},{16,24},{24,0},{1,9},{9,17},{17,25},{25,1},{2,10},{10... | collective-permute-start | bytes 344072 | tf_op jit(solution)/shard_map/ppermute | solution.py:30
  71.9 3.7 %collective-permute-start.20 = (f32[8,128]{1,0:T(8,128)S(1)}, f32[8,128]{1,0:T(8,128)S(1)}, u32[]{:S(2)}, u32[]{:S(2)}) collective-permute-start(f32[8,128]{1,0:T(8,128)S(1)} %get-tuple-element.62), channel_id=1, source_target_pairs={{0,2},{2,0},{4,6},{6,4},{1,3},{3,1},{5,7},{7,5},{8,10},{10,8},{12,... | collective-permute-start | bytes 12296 | tf_op jit(solution)/shard_map/ppermute | solution.py:20
  75.6 3.6 %collective-permute-start.21 = (f32[8,128]{1,0:T(8,128)S(1)}, f32[8,128]{1,0:T(8,128)S(1)}, u32[]{:S(2)}, u32[]{:S(2)}) collective-permute-start(f32[8,128]{1,0:T(8,128)S(1)} %max.3.peak_ref.refs_3_), channel_id=1, source_target_pairs={{0,4},{2,6},{4,0},{6,2},{1,5},{3,7},{5,1},{7,3},{8,12},{10,14},{12... | collective-permute-start | bytes 12296 | tf_op jit(solution)/shard_map/ppermute | solution.py:20

commit v11 on v8

--- a/solution.py
+++ b/solution.py
@@ -28,6 +28,11 @@
 def turned(block, axis):
     count = lax.axis_size(axis)
     return lax.ppermute(block, axis, [(i, (i + 1) % count) for i in range(count)])
+
+
+def shifted(block, axis):
+    count = lax.axis_size(axis)
+    return lax.ppermute(block, axis, [(i, i + 1) for i in range(count - 1)])
 
 
 def halves_of_sum(block, axis):
@@ -373,7 +378,7 @@
         fresh.append(some)
         steps.append(peaks)
 
-    left_tail = turned(leaving(head, tokens - head, steps[-2]), "pipe")
+    left_tail = shifted(leaving(head, tokens - head, steps[-2]), "pipe")
 
     group = LANES // depth
     peak_rows = [peaks] + [exchange(peaks, "expert", k) for k in range(1, experts)]

time: 78.8 us -> 78.1 us (level)
  the two profiles are of different devices: /device:TPU:8 before, /device:TPU:0 now
where the time goes in v11:
time: 78.1 us; the launch traced here: 77.9 us
  starting transfers between devices  43 us (55%)
  waiting for transfers between devices  19 us (24%)
  Pallas kernels  15.1 us (19%)
  between operations  0.81 us (1%)
    ppermute x16, starting transfers between devices, exchange(): return lax.ppermute(block, axis, [(i, i ^ offset) for i in range(count)])  20.7 us
    ppermute x16, waiting for transfers between devices, exchange(): return lax.ppermute(block, axis, [(i, i ^ offset) for i in range(count)])  19 us
    ppermute x4, starting transfers between devices, mirrored(): return lax.ppermute(block, axis, [(i, count - 1 - i) for i in range(count)])  9.77 us
    ppermute x1, starting transfers between devices, shifted(): return lax.ppermute(block, axis, [(i, i + 1) for i in range(count - 1)])  9.5 us
    pallas_call x16, Pallas kernels, call(): pl.pallas_call(kernel, in_specs=[VMEM] * read + [ANY] * (len(operands) -...  7.28 us
    pallas_call x1, Pallas kernels, shards(): pl.pallas_call(lambda *refs: latent_kernel(tiles, *refs), in_specs=[ANY]...  4.15 us
    ppermute x1, starting transfers between devices, turned(): lax.ppermute(block, axis, [(i, (i + 1) % count) for i in range(count)])  3 us
    pallas_call x2, Pallas kernels, place(): pl.pallas_call(lambda *refs: place_kernel(start, *refs), in_specs=[ANY] *...  2.14 us
  transfers between devices with their start and end apart: 22, of which 10 were waited for; matrix products, arithmetic and copies ran while one was open for 0% of the time, Pallas kernels for 13%

profile of v11, /device:TPU:0, one launch (start us, length us, event | category | flops | bytes accessed | tf_op | source)
XLA Modules:
  0.0 77.9 jit_solution(18160699774675060182)
XLA Ops:
  0.6 4.1 %latents.1 = (f32[1024,128]{1,0:T(8,128)S(1)}, bf16[128,3584]{1,0:T(8,128)(2,1)S(1)}, bf16[128,3584]{1,0:T(8,128)(2,1)S(1)}, bf16[128,3584]{1,0:T(8,128)(2,1)S(1)}) custom-call(bf16[1,128,3584]{2,1,0:T(8,128)(2,1)} %refs_0_.1, bf16[1,128,3584]{2,1,0:T(8,128)(2,1)} %refs_1_.5, bf16[1,128,3584]{2,1,0:T(8,128)(2,1)} %refs_2_.5, ...), custom_call_target="tpu_custom_call" | custom-call | flops 704643072 | bytes 8257536 | tf_op jit(solution)/shard_map/latents/pallas_call | solution.py:264
  5.3 1.5 %fetch.1.refs_3_ = bf16[256,3584]{1,0:T(8,128)(2,1)S(1)} custom-call(bf16[2,1,256,3584]{3,2,1,0:T(8,128)(2,1)} %in_ref.1, f32[1024,128]{1,0:T(8,128)S(1)} %get-tuple-element.36.rest_0_.refs_0_), custom_call_target="tpu_custom_call" | custom-call | bytes 1835008 | tf_op jit(solution)/shard_map/fetch/pallas_call | solution.py:283
  7.4 3.0 %collective-permute-start.12 = (bf16[112,3584]{1,0:T(8,128)(2,1)S(1)}, bf16[112,3584]{1,0:T(8,128)(2,1)S(1)}, u32[]{:S(2)}, u32[]{:S(2)}) collective-permute-start(bf16[112,3584]{1,0:T(8,128)(2,1)S(1)} %leaving.2.refs_4_), channel_id=1, source_target_pairs={{0,8},{8,16},{16,24},{24,0},{1,9},{9,17},{17,25},{25,1},{2,10},{10... | collective-permute-start | bytes 2408456 | tf_op jit(solution)/shard_map/ppermute | solution.py:30
  10.9 1.6 %collective-permute-start.1 = (bf16[2,64,1024]{2,1,0:T(8,128)(2,1)S(1)}, bf16[2,64,1024]{2,1,0:T(8,128)(2,1)S(1)}, u32[]{:S(2)}, u32[]{:S(2)}) collective-permute-start(bf16[2,64,1024]{2,1,0:T(8,128)(2,1)S(1)} %get-tuple-element.41), channel_id=1, source_target_pairs={{0,2},{2,0},{4,6},{6,4},{1,3},{3,1},{5,7},{7,5},{8,10},{10,8},{12,... | collective-permute-start | bytes 786440 | tf_op jit(solution)/shard_map/ppermute | solution.py:20
  12.5 1.5 %collective-permute-start.2 = (bf16[2,64,1024]{2,1,0:T(8,128)(2,1)S(1)}, bf16[2,64,1024]{2,1,0:T(8,128)(2,1)S(1)}, u32[]{:S(2)}, u32[]{:S(2)}) collective-permute-start(bf16[2,64,1024]{2,1,0:T(8,128)(2,1)S(1)} %get-tuple-element.42), channel_id=1, source_target_pairs={{0,4},{2,6},{4,0},{6,2},{1,5},{3,7},{5,1},{7,3},{8,12},{10,14},{12... | collective-permute-start | bytes 786440 | tf_op jit(solution)/shard_map/ppermute | solution.py:20
  14.5 5.7 %collective-permute-done.1.refs_1_.refs_4_ = bf16[2,64,1024]{2,1,0:T(8,128)(2,1)S(1)} collective-permute-done((bf16[2,64,1024]{2,1,0:T(8,128)(2,1)S(1)}, bf16[2,64,1024]{2,1,0:T(8,128)(2,1)S(1)}, u32[]{:S(2)}, u32[]{:S(2)}) %collective-permute-start.1) | collective-permute-done | bytes 262176 | tf_op jit(solution)/shard_map/ppermute | solution.py:20
  20.7 1.6 %collective-permute-start.4 = (bf16[2,64,896]{2,1,0:T(8,128)(2,1)S(1)}, bf16[2,64,896]{2,1,0:T(8,128)(2,1)S(1)}, u32[]{:S(2)}, u32[]{:S(2)}) collective-permute-start(bf16[2,64,896]{2,1,0:T(8,128)(2,1)S(1)} %get-tuple-element.44), channel_id=1, source_target_pairs={{0,2},{2,0},{4,6},{6,4},{1,3},{3,1},{5,7},{7,5},{8,10},{10,8},{12,... | collective-permute-start | bytes 688136 | tf_op jit(solution)/shard_map/ppermute | solution.py:20
  22.2 1.5 %collective-permute-start.10 = (bf16[2,64,896]{2,1,0:T(8,128)(2,1)S(1)}, bf16[2,64,896]{2,1,0:T(8,128)(2,1)S(1)}, u32[]{:S(2)}, u32[]{:S(2)}) collective-permute-start(bf16[2,64,896]{2,1,0:T(8,128)(2,1)S(1)} %get-tuple-element.50), channel_id=1, source_target_pairs={{0,4},{2,6},{4,0},{6,2},{1,5},{3,7},{5,1},{7,3},{8,12},{10,14},{12... | collective-permute-start | bytes 688136 | tf_op jit(solution)/shard_map/ppermute | solution.py:20
  23.7 2.3 %collective-permute-done.2.refs_2_ = bf16[2,64,1024]{2,1,0:T(8,128)(2,1)S(1)} collective-permute-done((bf16[2,64,1024]{2,1,0:T(8,128)(2,1)S(1)}, bf16[2,64,1024]{2,1,0:T(8,128)(2,1)S(1)}, u32[]{:S(2)}, u32[]{:S(2)}) %collective-permute-start.2) | collective-permute-done | bytes 262176 | tf_op jit(solution)/shard_map/ppermute | solution.py:20
  26.0 0.8 %collective-permute-start.11 = (bf16[2,64,896]{2,1,0:T(8,128)(2,1)S(1)}, bf16[2,64,896]{2,1,0:T(8,128)(2,1)S(1)}, u32[]{:S(2)}, u32[]{:S(2)}) collective-permute-start(bf16[2,64,896]{2,1,0:T(8,128)(2,1)S(1)} %get-tuple-element.51), channel_id=1, source_target_pairs={{0,6},{2,4},{4,2},{6,0},{1,7},{3,5},{5,3},{7,1},{8,14},{10,12},{12... | collective-permute-start | bytes 688136 | tf_op jit(solution)/shard_map/ppermute | solution.py:20
  26.9 2.5 %collective-permute-start.8 = (bf16[2,64,1024]{2,1,0:T(8,128)(2,1)S(1)}, bf16[2,64,1024]{2,1,0:T(8,128)(2,1)S(1)}, u32[]{:S(2)}, u32[]{:S(2)}) collective-permute-start(bf16[2,64,1024]{2,1,0:T(8,128)(2,1)S(1)} %share.4.refs_4_), channel_id=1, source_target_pairs={{0,24},{8,16},{16,8},{24,0},{1,25},{9,17},{17,9},{25,1},{2,26},{10... | collective-permute-start | bytes 786440 | tf_op jit(solution)/shard_map/ppermute | solution.py:25
  29.4 1.3 %collective-permute-done.4.refs_5_.refs_1_ = bf16[2,64,896]{2,1,0:T(8,128)(2,1)S(1)} collective-permute-done((bf16[2,64,896]{2,1,0:T(8,128)(2,1)S(1)}, bf16[2,64,896]{2,1,0:T(8,128)(2,1)S(1)}, u32[]{:S(2)}, u32[]{:S(2)}) %collective-permute-start.4) | collective-permute-done | bytes 229408 | tf_op jit(solution)/shard_map/ppermute | solution.py:20
  31.2 1.8 %collective-permute-start.5 = (bf16[2,64,896]{2,1,0:T(8,128)(2,1)S(1)}, bf16[2,64,896]{2,1,0:T(8,128)(2,1)S(1)}, u32[]{:S(2)}, u32[]{:S(2)}) collective-permute-start(bf16[2,64,896]{2,1,0:T(8,128)(2,1)S(1)} %get-tuple-element.46), channel_id=1, source_target_pairs={{0,2},{2,0},{4,6},{6,4},{1,3},{3,1},{5,7},{7,5},{8,10},{10,8},{12,... | collective-permute-start | bytes 688136 | tf_op jit(solution)/shard_map/ppermute | solution.py:20
  33.1 1.7 %collective-permute-done.10.refs_2_ = bf16[2,64,896]{2,1,0:T(8,128)(2,1)S(1)} collective-permute-done((bf16[2,64,896]{2,1,0:T(8,128)(2,1)S(1)}, bf16[2,64,896]{2,1,0:T(8,128)(2,1)S(1)}, u32[]{:S(2)}, u32[]{:S(2)}) %collective-permute-start.10) | collective-permute-done | bytes 229408 | tf_op jit(solution)/shard_map/ppermute | solution.py:20
  34.7 1.7 %collective-permute-start.6 = (bf16[2,64,896]{2,1,0:T(8,128)(2,1)S(1)}, bf16[2,64,896]{2,1,0:T(8,128)(2,1)S(1)}, u32[]{:S(2)}, u32[]{:S(2)}) collective-permute-start(bf16[2,64,896]{2,1,0:T(8,128)(2,1)S(1)} %get-tuple-element.47), channel_id=1, source_target_pairs={{0,4},{2,6},{4,0},{6,2},{1,5},{3,7},{5,1},{7,3},{8,12},{10,14},{12... | collective-permute-start | bytes 688136 | tf_op jit(solution)/shard_map/ppermute | solution.py:20
  36.7 1.4 %collective-permute-start.7 = (bf16[2,64,896]{2,1,0:T(8,128)(2,1)S(1)}, bf16[2,64,896]{2,1,0:T(8,128)(2,1)S(1)}, u32[]{:S(2)}, u32[]{:S(2)}) collective-permute-start(bf16[2,64,896]{2,1,0:T(8,128)(2,1)S(1)} %get-tuple-element.48), channel_id=1, source_target_pairs={{0,6},{2,4},{4,2},{6,0},{1,7},{3,5},{5,3},{7,1},{8,14},{10,12},{12... | collective-permute-start | bytes 688136 | tf_op jit(solution)/shard_map/ppermute | solution.py:20
  38.2 2.3 %collective-permute-start.13 = (bf16[2,64,896]{2,1,0:T(8,128)(2,1)S(1)}, bf16[2,64,896]{2,1,0:T(8,128)(2,1)S(1)}, u32[]{:S(2)}, u32[]{:S(2)}) collective-permute-start(bf16[2,64,896]{2,1,0:T(8,128)(2,1)S(1)} %share.6.refs_4_), channel_id=1, source_target_pairs={{0,24},{8,16},{16,8},{24,0},{1,25},{9,17},{17,9},{25,1},{2,26},{10... | collective-permute-start | bytes 688136 | tf_op jit(solution)/shard_map/ppermute | solution.py:25
  40.5 0.9 %collective-permute-done.5.refs_1_.refs_5_ = bf16[2,64,896]{2,1,0:T(8,128)(2,1)S(1)} collective-permute-done((bf16[2,64,896]{2,1,0:T(8,128)(2,1)S(1)}, bf16[2,64,896]{2,1,0:T(8,128)(2,1)S(1)}, u32[]{:S(2)}, u32[]{:S(2)}) %collective-permute-start.5) | collective-permute-done | bytes 229408 | tf_op jit(solution)/shard_map/ppermute | solution.py:20
  41.9 0.7 collective-permute-start.15
  42.6 1.5 %collective-permute-start.16 = (bf16[2,64,768]{2,1,0:T(8,128)(2,1)S(1)}, bf16[2,64,768]{2,1,0:T(8,128)(2,1)S(1)}, u32[]{:S(2)}, u32[]{:S(2)}) collective-permute-start(bf16[2,64,768]{2,1,0:T(8,128)(2,1)S(1)} %get-tuple-element.59), channel_id=1, source_target_pairs={{0,4},{2,6},{4,0},{6,2},{1,5},{3,7},{5,1},{7,3},{8,12},{10,14},{12... | collective-permute-start | bytes 589832 | tf_op jit(solution)/shard_map/ppermute | solution.py:20
  44.1 1.7 %collective-permute-done.6.refs_2_ = bf16[2,64,896]{2,1,0:T(8,128)(2,1)S(1)} collective-permute-done((bf16[2,64,896]{2,1,0:T(8,128)(2,1)S(1)}, bf16[2,64,896]{2,1,0:T(8,128)(2,1)S(1)}, u32[]{:S(2)}, u32[]{:S(2)}) %collective-permute-start.6) | collective-permute-done | bytes 229408 | tf_op jit(solution)/shard_map/ppermute | solution.py:20
  45.8 2.0 %collective-permute-start.17 = (bf16[2,64,768]{2,1,0:T(8,128)(2,1)S(1)}, bf16[2,64,768]{2,1,0:T(8,128)(2,1)S(1)}, u32[]{:S(2)}, u32[]{:S(2)}) collective-permute-start(bf16[2,64,768]{2,1,0:T(8,128)(2,1)S(1)} %get-tuple-element.60), channel_id=1, source_target_pairs={{0,6},{2,4},{4,2},{6,0},{1,7},{3,5},{5,3},{7,1},{8,14},{10,12},{12... | collective-permute-start | bytes 589832 | tf_op jit(solution)/shard_map/ppermute | solution.py:20
  48.0 2.6 %collective-permute-start.9 = (bf16[2,64,896]{2,1,0:T(8,128)(2,1)S(1)}, bf16[2,64,896]{2,1,0:T(8,128)(2,1)S(1)}, u32[]{:S(2)}, u32[]{:S(2)}) collective-permute-start(bf16[2,64,896]{2,1,0:T(8,128)(2,1)S(1)} %share.5), channel_id=1, source_target_pairs={{0,24},{8,16},{16,8},{24,0},{1,25},{9,17},{17,9},{25,1},{2,26},{10... | collective-permute-start | bytes 688136 | tf_op jit(solution)/shard_map/ppermute | solution.py:25
  50.6 3.6 %collective-permute-done.16.refs_2_ = bf16[2,64,768]{2,1,0:T(8,128)(2,1)S(1)} collective-permute-done((bf16[2,64,768]{2,1,0:T(8,128)(2,1)S(1)}, bf16[2,64,768]{2,1,0:T(8,128)(2,1)S(1)}, u32[]{:S(2)}, u32[]{:S(2)}) %collective-permute-start.16) | collective-permute-done | bytes 196640 | tf_op jit(solution)/shard_map/ppermute | solution.py:20
  54.3 2.4 %collective-permute-start.18 = (bf16[2,64,768]{2,1,0:T(8,128)(2,1)S(1)}, bf16[2,64,768]{2,1,0:T(8,128)(2,1)S(1)}, u32[]{:S(2)}, u32[]{:S(2)}) collective-permute-start(bf16[2,64,768]{2,1,0:T(8,128)(2,1)S(1)} %share.7), channel_id=1, source_target_pairs={{0,24},{8,16},{16,8},{24,0},{1,25},{9,17},{17,9},{25,1},{2,26},{10... | collective-permute-start | bytes 589832 | tf_op jit(solution)/shard_map/ppermute | solution.py:25
  57.3 0.9 %place.2 = (bf16[1,128,3584]{2,1,0:T(8,128)(2,1)}, f32[8,128]{1,0:T(8,128)S(1)}) custom-call(bf16[112,3584]{1,0:T(8,128)(2,1)S(1)} %collective-permute-done.12.refs_4_.refs_0_), custom_call_target="tpu_custom_call" | custom-call | bytes 1605632 | tf_op jit(solution)/shard_map/place/pallas_call | solution.py:346
  59.7 9.5 %collective-permute-start.14 = (bf16[16,3584]{1,0:T(8,128)(2,1)S(1)}, bf16[16,3584]{1,0:T(8,128)(2,1)S(1)}, u32[]{:S(2)}, u32[]{:S(2)}) collective-permute-start(bf16[16,3584]{1,0:T(8,128)(2,1)S(1)} %leaving.3), channel_id=1, source_target_pairs={{0,8},{8,16},{16,24},{1,9},{9,17},{17,25},{2,10},{10,18},{18,26},{... | collective-permute-start | bytes 344072 | tf_op jit(solution)/shard_map/ppermute | solution.py:35
  69.7 1.6 %collective-permute-start.19 = (f32[8,128]{1,0:T(8,128)S(1)}, f32[8,128]{1,0:T(8,128)S(1)}, u32[]{:S(2)}, u32[]{:S(2)}) collective-permute-start(f32[8,128]{1,0:T(8,128)S(1)} %get-tuple-element.61.refs_0_), channel_id=1, source_target_pairs={{0,2},{2,0},{4,6},{6,4},{1,3},{3,1},{5,7},{7,5},{8,10},{10,8},{12,... | collective-permute-start | bytes 12296 | tf_op jit(solution)/shard_map/ppermute | solution.py:20
  71.3 1.5 %collective-permute-start.20 = (f32[8,128]{1,0:T(8,128)S(1)}, f32[8,128]{1,0:T(8,128)S(1)}, u32[]{:S(2)}, u32[]{:S(2)}) collective-permute-start(f32[8,128]{1,0:T(8,128)S(1)} %get-tuple-element.61.refs_0_), channel_id=1, source_target_pairs={{0,4},{2,6},{4,0},{6,2},{1,5},{3,7},{5,1},{7,3},{8,12},{10,14},{12... | collective-permute-start | bytes 12296 | tf_op jit(solution)/shard_map/ppermute | solution.py:20
  73.4 1.2 %codes.1 = (bf16[2,1,64,3584]{3,2,1,0:T(8,128)(2,1)}, f32[8,128]{1,0:T(8,128)S(1)}) custom-call(f32[8,128]{1,0:T(8,128)S(1)} %get-tuple-element.61.refs_0_, f32[8,128]{1,0:T(8,128)S(1)} %collective-permute-done.19.refs_1_, f32[2,64,1024]{2,1,0:T(8,128)S(1)} %get-tuple-element.62.refs_2_, f32[2,64,896]{2,1,0:T(8,128)S(1)} %get-tuple-element.63.refs_3_, ...), custom_call_target="tpu_custom_call" | custom-call | flops 917504 | bytes 1843200 | tf_op jit(solution)/shard_map/codes/pallas_call | solution.py:56
  74.6 1.2 %place.3 = (bf16[1,128,3584]{2,1,0:T(8,128)(2,1)}, f32[8,128]{1,0:T(8,128)}) custom-call(bf16[16,3584]{1,0:T(8,128)(2,1)S(1)} %collective-permute-done.14.refs_0_, bf16[1,128,3584]{2,1,0:T(8,128)(2,1)} %get-tuple-element.56.refs_1_, f32[8,128]{1,0:T(8,128)S(1)} %get-tuple-element.66.refs_2_.refs_4_), custom_call_target="tpu_custom_call", output_to_operand_aliasing={{0}: (1, {})} | custom-call | bytes 229376 | tf_op jit(solution)/shard_map/place/pallas_call | solution.py:346
  75.8 1.5 %collective-permute-done.21.refs_3_ = f32[8,128]{1,0:T(8,128)S(1)} collective-permute-done((f32[8,128]{1,0:T(8,128)S(1)}, f32[8,128]{1,0:T(8,128)S(1)}, u32[]{:S(2)}, u32[]{:S(2)}) %collective-permute-start.21) | collective-permute-done | bytes 4128 | tf_op jit(solution)/shard_map/ppermute | solution.py:20
  (38 shorter events, 7.9 us)
Async XLA Ops:
  4.8 2.1 %collective-permute-start = (f32[1024,128]{1,0:T(8,128)S(1)}, f32[1024,128]{1,0:T(8,128)S(1)}, u32[]{:S(2)}, u32[]{:S(2)}) collective-permute-start(f32[1024,128]{1,0:T(8,128)S(1)} %get-tuple-element.36.rest_0_.refs_0_), channel_id=1, source_target_pairs={{0,1},{1,0},{2,3},{3,2},{4,5},{5,4},{6,7},{7,6},{8,9},{9,8},{10,11... | collective-permute-start | bytes 1572872 | tf_op jit(solution)/shard_map/ppermute | solution.py:20
  7.4 30.7 %collective-permute-start.12 = (bf16[112,3584]{1,0:T(8,128)(2,1)S(1)}, bf16[112,3584]{1,0:T(8,128)(2,1)S(1)}, u32[]{:S(2)}, u32[]{:S(2)}) collective-permute-start(bf16[112,3584]{1,0:T(8,128)(2,1)S(1)} %leaving.2.refs_4_), channel_id=1, source_target_pairs={{0,8},{8,16},{16,24},{24,0},{1,9},{9,17},{17,25},{25,1},{2,10},{10... | collective-permute-start | bytes 2408456 | tf_op jit(solution)/shard_map/ppermute | solution.py:30
  10.9 9.3 %collective-permute-start.1 = (bf16[2,64,1024]{2,1,0:T(8,128)(2,1)S(1)}, bf16[2,64,1024]{2,1,0:T(8,128)(2,1)S(1)}, u32[]{:S(2)}, u32[]{:S(2)}) collective-permute-start(bf16[2,64,1024]{2,1,0:T(8,128)(2,1)S(1)} %get-tuple-element.41), channel_id=1, source_target_pairs={{0,2},{2,0},{4,6},{6,4},{1,3},{3,1},{5,7},{7,5},{8,10},{10,8},{12,... | collective-permute-start | bytes 786440 | tf_op jit(solution)/shard_map/ppermute | solution.py:20
  12.5 13.5 %collective-permute-start.2 = (bf16[2,64,1024]{2,1,0:T(8,128)(2,1)S(1)}, bf16[2,64,1024]{2,1,0:T(8,128)(2,1)S(1)}, u32[]{:S(2)}, u32[]{:S(2)}) collective-permute-start(bf16[2,64,1024]{2,1,0:T(8,128)(2,1)S(1)} %get-tuple-element.42), channel_id=1, source_target_pairs={{0,4},{2,6},{4,0},{6,2},{1,5},{3,7},{5,1},{7,3},{8,12},{10,14},{12... | collective-permute-start | bytes 786440 | tf_op jit(solution)/shard_map/ppermute | solution.py:20
  14.0 12.8 %collective-permute-start.3 = (bf16[2,64,1024]{2,1,0:T(8,128)(2,1)S(1)}, bf16[2,64,1024]{2,1,0:T(8,128)(2,1)S(1)}, u32[]{:S(2)}, u32[]{:S(2)}) collective-permute-start(bf16[2,64,1024]{2,1,0:T(8,128)(2,1)S(1)} %get-tuple-element.43), channel_id=1, source_target_pairs={{0,6},{2,4},{4,2},{6,0},{1,7},{3,5},{5,3},{7,1},{8,14},{10,12},{12... | collective-permute-start | bytes 786440 | tf_op jit(solution)/shard_map/ppermute | solution.py:20
  20.7 10.1 %collective-permute-start.4 = (bf16[2,64,896]{2,1,0:T(8,128)(2,1)S(1)}, bf16[2,64,896]{2,1,0:T(8,128)(2,1)S(1)}, u32[]{:S(2)}, u32[]{:S(2)}) collective-permute-start(bf16[2,64,896]{2,1,0:T(8,128)(2,1)S(1)} %get-tuple-element.44), channel_id=1, source_target_pairs={{0,2},{2,0},{4,6},{6,4},{1,3},{3,1},{5,7},{7,5},{8,10},{10,8},{12,... | collective-permute-start | bytes 688136 | tf_op jit(solution)/shard_map/ppermute | solution.py:20
  22.2 12.5 %collective-permute-start.10 = (bf16[2,64,896]{2,1,0:T(8,128)(2,1)S(1)}, bf16[2,64,896]{2,1,0:T(8,128)(2,1)S(1)}, u32[]{:S(2)}, u32[]{:S(2)}) collective-permute-start(bf16[2,64,896]{2,1,0:T(8,128)(2,1)S(1)} %get-tuple-element.50), channel_id=1, source_target_pairs={{0,4},{2,6},{4,0},{6,2},{1,5},{3,7},{5,1},{7,3},{8,12},{10,14},{12... | collective-permute-start | bytes 688136 | tf_op jit(solution)/shard_map/ppermute | solution.py:20
  26.0 10.6 %collective-permute-start.11 = (bf16[2,64,896]{2,1,0:T(8,128)(2,1)S(1)}, bf16[2,64,896]{2,1,0:T(8,128)(2,1)S(1)}, u32[]{:S(2)}, u32[]{:S(2)}) collective-permute-start(bf16[2,64,896]{2,1,0:T(8,128)(2,1)S(1)} %get-tuple-element.51), channel_id=1, source_target_pairs={{0,6},{2,4},{4,2},{6,0},{1,7},{3,5},{5,3},{7,1},{8,14},{10,12},{12... | collective-permute-start | bytes 688136 | tf_op jit(solution)/shard_map/ppermute | solution.py:20
  26.9 15.7 %collective-permute-start.8 = (bf16[2,64,1024]{2,1,0:T(8,128)(2,1)S(1)}, bf16[2,64,1024]{2,1,0:T(8,128)(2,1)S(1)}, u32[]{:S(2)}, u32[]{:S(2)}) collective-permute-start(bf16[2,64,1024]{2,1,0:T(8,128)(2,1)S(1)} %share.4.refs_4_), channel_id=1, source_target_pairs={{0,24},{8,16},{16,8},{24,0},{1,25},{9,17},{17,9},{25,1},{2,26},{10... | collective-permute-start | bytes 786440 | tf_op jit(solution)/shard_map/ppermute | solution.py:25
  31.2 10.2 %collective-permute-start.5 = (bf16[2,64,896]{2,1,0:T(8,128)(2,1)S(1)}, bf16[2,64,896]{2,1,0:T(8,128)(2,1)S(1)}, u32[]{:S(2)}, u32[]{:S(2)}) collective-permute-start(bf16[2,64,896]{2,1,0:T(8,128)(2,1)S(1)} %get-tuple-element.46), channel_id=1, source_target_pairs={{0,2},{2,0},{4,6},{6,4},{1,3},{3,1},{5,7},{7,5},{8,10},{10,8},{12,... | collective-permute-start | bytes 688136 | tf_op jit(solution)/shard_map/ppermute | solution.py:20
  34.7 11.1 %collective-permute-start.6 = (bf16[2,64,896]{2,1,0:T(8,128)(2,1)S(1)}, bf16[2,64,896]{2,1,0:T(8,128)(2,1)S(1)}, u32[]{:S(2)}, u32[]{:S(2)}) collective-permute-start(bf16[2,64,896]{2,1,0:T(8,128)(2,1)S(1)} %get-tuple-element.47), channel_id=1, source_target_pairs={{0,4},{2,6},{4,0},{6,2},{1,5},{3,7},{5,1},{7,3},{8,12},{10,14},{12... | collective-permute-start | bytes 688136 | tf_op jit(solution)/shard_map/ppermute | solution.py:20
  36.7 11.2 %collective-permute-start.7 = (bf16[2,64,896]{2,1,0:T(8,128)(2,1)S(1)}, bf16[2,64,896]{2,1,0:T(8,128)(2,1)S(1)}, u32[]{:S(2)}, u32[]{:S(2)}) collective-permute-start(bf16[2,64,896]{2,1,0:T(8,128)(2,1)S(1)} %get-tuple-element.48), channel_id=1, source_target_pairs={{0,6},{2,4},{4,2},{6,0},{1,7},{3,5},{5,3},{7,1},{8,14},{10,12},{12... | collective-permute-start | bytes 688136 | tf_op jit(solution)/shard_map/ppermute | solution.py:20
  38.1 18.6 %copy-start = (f32[2,1,64,3584]{3,2,1,0:T(8,128)S(1)}, f32[2,1,64,3584]{3,2,1,0:T(8,128)}, u32[]{:S(2)}) copy-start(f32[2,1,64,3584]{3,2,1,0:T(8,128)} %refs_1_.9) | copy-start | bytes 5505028
  38.1 18.6 %copy-start.1 = (bf16[2,1,64,3584]{3,2,1,0:T(8,128)(2,1)S(1)}, bf16[2,1,64,3584]{3,2,1,0:T(8,128)(2,1)}, u32[]{:S(2)}) copy-start(bf16[2,1,64,3584]{3,2,1,0:T(8,128)(2,1)} %refs_2_.9) | copy-start | bytes 2752516
  38.1 18.6 %copy-start.2 = (bf16[2,1,64,3584]{3,2,1,0:T(8,128)(2,1)S(1)}, bf16[2,1,64,3584]{3,2,1,0:T(8,128)(2,1)}, u32[]{:S(2)}) copy-start(bf16[2,1,64,3584]{3,2,1,0:T(8,128)(2,1)} %refs_3_.9) | copy-start | bytes 2752516
  38.2 16.0 %collective-permute-start.13 = (bf16[2,64,896]{2,1,0:T(8,128)(2,1)S(1)}, bf16[2,64,896]{2,1,0:T(8,128)(2,1)S(1)}, u32[]{:S(2)}, u32[]{:S(2)}) collective-permute-start(bf16[2,64,896]{2,1,0:T(8,128)(2,1)S(1)} %share.6.refs_4_), channel_id=1, source_target_pairs={{0,24},{8,16},{16,8},{24,0},{1,25},{9,17},{17,9},{25,1},{2,26},{10... | collective-permute-start | bytes 688136 | tf_op jit(solution)/shard_map/ppermute | solution.py:25
  41.9 8.7 %collective-permute-start.15 = (bf16[2,64,768]{2,1,0:T(8,128)(2,1)S(1)}, bf16[2,64,768]{2,1,0:T(8,128)(2,1)S(1)}, u32[]{:S(2)}, u32[]{:S(2)}) collective-permute-start(bf16[2,64,768]{2,1,0:T(8,128)(2,1)S(1)} %get-tuple-element.58), channel_id=1, source_target_pairs={{0,2},{2,0},{4,6},{6,4},{1,3},{3,1},{5,7},{7,5},{8,10},{10,8},{12,... | collective-permute-start | bytes 589832 | tf_op jit(solution)/shard_map/ppermute | solution.py:20
  42.6 11.6 %collective-permute-start.16 = (bf16[2,64,768]{2,1,0:T(8,128)(2,1)S(1)}, bf16[2,64,768]{2,1,0:T(8,128)(2,1)S(1)}, u32[]{:S(2)}, u32[]{:S(2)}) collective-permute-start(bf16[2,64,768]{2,1,0:T(8,128)(2,1)S(1)} %get-tuple-element.59), channel_id=1, source_target_pairs={{0,4},{2,6},{4,0},{6,2},{1,5},{3,7},{5,1},{7,3},{8,12},{10,14},{12... | collective-permute-start | bytes 589832 | tf_op jit(solution)/shard_map/ppermute | solution.py:20
  45.8 8.4 %collective-permute-start.17 = (bf16[2,64,768]{2,1,0:T(8,128)(2,1)S(1)}, bf16[2,64,768]{2,1,0:T(8,128)(2,1)S(1)}, u32[]{:S(2)}, u32[]{:S(2)}) collective-permute-start(bf16[2,64,768]{2,1,0:T(8,128)(2,1)S(1)} %get-tuple-element.60), channel_id=1, source_target_pairs={{0,6},{2,4},{4,2},{6,0},{1,7},{3,5},{5,3},{7,1},{8,14},{10,12},{12... | collective-permute-start | bytes 589832 | tf_op jit(solution)/shard_map/ppermute | solution.py:20
  48.0 10.7 %collective-permute-start.9 = (bf16[2,64,896]{2,1,0:T(8,128)(2,1)S(1)}, bf16[2,64,896]{2,1,0:T(8,128)(2,1)S(1)}, u32[]{:S(2)}, u32[]{:S(2)}) collective-permute-start(bf16[2,64,896]{2,1,0:T(8,128)(2,1)S(1)} %share.5), channel_id=1, source_target_pairs={{0,24},{8,16},{16,8},{24,0},{1,25},{9,17},{17,9},{25,1},{2,26},{10... | collective-permute-start | bytes 688136 | tf_op jit(solution)/shard_map/ppermute | solution.py:25
  54.3 14.9 %collective-permute-start.18 = (bf16[2,64,768]{2,1,0:T(8,128)(2,1)S(1)}, bf16[2,64,768]{2,1,0:T(8,128)(2,1)S(1)}, u32[]{:S(2)}, u32[]{:S(2)}) collective-permute-start(bf16[2,64,768]{2,1,0:T(8,128)(2,1)S(1)} %share.7), channel_id=1, source_target_pairs={{0,24},{8,16},{16,8},{24,0},{1,25},{9,17},{17,9},{25,1},{2,26},{10... | collective-permute-start | bytes 589832 | tf_op jit(solution)/shard_map/ppermute | solution.py:25
  59.7 14.9 %collective-permute-start.14 = (bf16[16,3584]{1,0:T(8,128)(2,1)S(1)}, bf16[16,3584]{1,0:T(8,128)(2,1)S(1)}, u32[]{:S(2)}, u32[]{:S(2)}) collective-permute-start(bf16[16,3584]{1,0:T(8,128)(2,1)S(1)} %leaving.3), channel_id=1, source_target_pairs={{0,8},{8,16},{16,24},{1,9},{9,17},{17,25},{2,10},{10,18},{18,26},{... | collective-permute-start | bytes 344072 | tf_op jit(solution)/shard_map/ppermute | solution.py:35
  69.7 3.7 %collective-permute-start.19 = (f32[8,128]{1,0:T(8,128)S(1)}, f32[8,128]{1,0:T(8,128)S(1)}, u32[]{:S(2)}, u32[]{:S(2)}) collective-permute-start(f32[8,128]{1,0:T(8,128)S(1)} %get-tuple-element.61.refs_0_), channel_id=1, source_target_pairs={{0,2},{2,0},{4,6},{6,4},{1,3},{3,1},{5,7},{7,5},{8,10},{10,8},{12,... | collective-permute-start | bytes 12296 | tf_op jit(solution)/shard_map/ppermute | solution.py:20
  71.3 4.6 %collective-permute-start.20 = (f32[8,128]{1,0:T(8,128)S(1)}, f32[8,128]{1,0:T(8,128)S(1)}, u32[]{:S(2)}, u32[]{:S(2)}) collective-permute-start(f32[8,128]{1,0:T(8,128)S(1)} %get-tuple-element.61.refs_0_), channel_id=1, source_target_pairs={{0,4},{2,6},{4,0},{6,2},{1,5},{3,7},{5,1},{7,3},{8,12},{10,14},{12... | collective-permute-start | bytes 12296 | tf_op jit(solution)/shard_map/ppermute | solution.py:20
  72.8 4.5 %collective-permute-start.21 = (f32[8,128]{1,0:T(8,128)S(1)}, f32[8,128]{1,0:T(8,128)S(1)}, u32[]{:S(2)}, u32[]{:S(2)}) collective-permute-start(f32[8,128]{1,0:T(8,128)S(1)} %get-tuple-element.61.refs_0_), channel_id=1, source_target_pairs={{0,6},{2,4},{4,2},{6,0},{1,7},{3,5},{5,3},{7,1},{8,14},{10,12},{12... | collective-permute-start | bytes 12296 | tf_op jit(solution)/shard_map/ppermute | solution.py:20

commit v12 on v11

--- a/solution.py
+++ b/solution.py
@@ -378,7 +378,7 @@
         fresh.append(some)
         steps.append(peaks)
 
-    left_tail = shifted(leaving(head, tokens - head, steps[-2]), "pipe")
+    left_tail = shifted(leaving(head, tokens - head, steps[-3]), "pipe")
 
     group = LANES // depth
     peak_rows = [peaks] + [exchange(peaks, "expert", k) for k in range(1, experts)]

time: 78.1 us -> 76.3 us (0.977)
  the two profiles are of different devices: /device:TPU:0 before, /device:TPU:8 now
where the time goes in v12:
time: 76.3 us; the launch traced here: 76.1 us
  waiting for transfers between devices  30.3 us (40%)
  starting transfers between devices  29.9 us (39%)
  Pallas kernels  15.1 us (20%)
  between operations  0.8 us (1%)
    ppermute x16, waiting for transfers between devices, exchange(): return lax.ppermute(block, axis, [(i, i ^ offset) for i in range(count)])  22.1 us
    ppermute x16, starting transfers between devices, exchange(): return lax.ppermute(block, axis, [(i, i ^ offset) for i in range(count)])  19.5 us
    ppermute x4, waiting for transfers between devices, mirrored(): return lax.ppermute(block, axis, [(i, count - 1 - i) for i in range(count)])  8.21 us
    pallas_call x16, Pallas kernels, call(): pl.pallas_call(kernel, in_specs=[VMEM] * read + [ANY] * (len(operands) -...  7.27 us
    ppermute x4, starting transfers between devices, mirrored(): return lax.ppermute(block, axis, [(i, count - 1 - i) for i in range(count)])  5.17 us
    pallas_call x1, Pallas kernels, shards(): pl.pallas_call(lambda *refs: latent_kernel(tiles, *refs), in_specs=[ANY]...  4.15 us
    ppermute x1, starting transfers between devices, shifted(): return lax.ppermute(block, axis, [(i, i + 1) for i in range(count - 1)])  3.61 us
    pallas_call x2, Pallas kernels, place(): pl.pallas_call(lambda *refs: place_kernel(start, *refs), in_specs=[ANY] *...  2.14 us
  transfers between devices with their start and end apart: 22, of which 13 were waited for; matrix products, arithmetic and copies ran while one was open for 0% of the time, Pallas kernels for 13%

profile of v12, /device:TPU:8, one launch (start us, length us, event | category | flops | bytes accessed | tf_op | source)
XLA Modules:
  0.0 76.1 jit_solution(14305440428744981887)
XLA Ops:
  0.6 4.2 %latents.1 = (f32[1024,128]{1,0:T(8,128)S(1)}, bf16[128,3584]{1,0:T(8,128)(2,1)S(1)}, bf16[128,3584]{1,0:T(8,128)(2,1)S(1)}, bf16[128,3584]{1,0:T(8,128)(2,1)S(1)}) custom-call(bf16[1,128,3584]{2,1,0:T(8,128)(2,1)} %refs_0_.1, bf16[1,128,3584]{2,1,0:T(8,128)(2,1)} %refs_1_.5, bf16[1,128,3584]{2,1,0:T(8,128)(2,1)} %refs_2_.5, ...), custom_call_target="tpu_custom_call" | custom-call | flops 704643072 | bytes 8257536 | tf_op jit(solution)/shard_map/latents/pallas_call | solution.py:264
  4.9 1.5 %fetch.1.refs_3_ = bf16[256,3584]{1,0:T(8,128)(2,1)S(1)} custom-call(bf16[2,1,256,3584]{3,2,1,0:T(8,128)(2,1)} %in_ref.1, f32[1024,128]{1,0:T(8,128)S(1)} %get-tuple-element.36.rest_0_.refs_0_), custom_call_target="tpu_custom_call" | custom-call | bytes 1835008 | tf_op jit(solution)/shard_map/fetch/pallas_call | solution.py:283
  7.3 1.6 %collective-permute-start.5 = (bf16[112,3584]{1,0:T(8,128)(2,1)S(1)}, bf16[112,3584]{1,0:T(8,128)(2,1)S(1)}, u32[]{:S(2)}, u32[]{:S(2)}) collective-permute-start(bf16[112,3584]{1,0:T(8,128)(2,1)S(1)} %leaving.2.refs_4_), channel_id=1, source_target_pairs={{0,8},{8,16},{16,24},{24,0},{1,9},{9,17},{17,25},{25,1},{2,10},{10... | collective-permute-start | bytes 2408456 | tf_op jit(solution)/shard_map/ppermute | solution.py:30
  9.5 1.6 %collective-permute-start.1 = (bf16[2,64,1024]{2,1,0:T(8,128)(2,1)S(1)}, bf16[2,64,1024]{2,1,0:T(8,128)(2,1)S(1)}, u32[]{:S(2)}, u32[]{:S(2)}) collective-permute-start(bf16[2,64,1024]{2,1,0:T(8,128)(2,1)S(1)} %get-tuple-element.40), channel_id=1, source_target_pairs={{0,2},{2,0},{4,6},{6,4},{1,3},{3,1},{5,7},{7,5},{8,10},{10,8},{12,... | collective-permute-start | bytes 786440 | tf_op jit(solution)/shard_map/ppermute | solution.py:20
  11.0 1.5 %collective-permute-start.7 = (bf16[2,64,1024]{2,1,0:T(8,128)(2,1)S(1)}, bf16[2,64,1024]{2,1,0:T(8,128)(2,1)S(1)}, u32[]{:S(2)}, u32[]{:S(2)}) collective-permute-start(bf16[2,64,1024]{2,1,0:T(8,128)(2,1)S(1)} %get-tuple-element.46), channel_id=1, source_target_pairs={{0,4},{2,6},{4,0},{6,2},{1,5},{3,7},{5,1},{7,3},{8,12},{10,14},{12... | collective-permute-start | bytes 786440 | tf_op jit(solution)/shard_map/ppermute | solution.py:20
  13.0 5.7 %collective-permute-done.1.refs_4_.refs_1_ = bf16[2,64,1024]{2,1,0:T(8,128)(2,1)S(1)} collective-permute-done((bf16[2,64,1024]{2,1,0:T(8,128)(2,1)S(1)}, bf16[2,64,1024]{2,1,0:T(8,128)(2,1)S(1)}, u32[]{:S(2)}, u32[]{:S(2)}) %collective-permute-start.1) | collective-permute-done | bytes 262176 | tf_op jit(solution)/shard_map/ppermute | solution.py:20
  19.2 1.6 %collective-permute-start.2 = (bf16[2,64,896]{2,1,0:T(8,128)(2,1)S(1)}, bf16[2,64,896]{2,1,0:T(8,128)(2,1)S(1)}, u32[]{:S(2)}, u32[]{:S(2)}) collective-permute-start(bf16[2,64,896]{2,1,0:T(8,128)(2,1)S(1)} %get-tuple-element.42), channel_id=1, source_target_pairs={{0,2},{2,0},{4,6},{6,4},{1,3},{3,1},{5,7},{7,5},{8,10},{10,8},{12,... | collective-permute-start | bytes 688136 | tf_op jit(solution)/shard_map/ppermute | solution.py:20
  20.8 1.5 %collective-permute-start.3 = (bf16[2,64,896]{2,1,0:T(8,128)(2,1)S(1)}, bf16[2,64,896]{2,1,0:T(8,128)(2,1)S(1)}, u32[]{:S(2)}, u32[]{:S(2)}) collective-permute-start(bf16[2,64,896]{2,1,0:T(8,128)(2,1)S(1)} %get-tuple-element.43), channel_id=1, source_target_pairs={{0,4},{2,6},{4,0},{6,2},{1,5},{3,7},{5,1},{7,3},{8,12},{10,14},{12... | collective-permute-start | bytes 688136 | tf_op jit(solution)/shard_map/ppermute | solution.py:20
  22.3 2.3 %collective-permute-done.7.refs_2_ = bf16[2,64,1024]{2,1,0:T(8,128)(2,1)S(1)} collective-permute-done((bf16[2,64,1024]{2,1,0:T(8,128)(2,1)S(1)}, bf16[2,64,1024]{2,1,0:T(8,128)(2,1)S(1)}, u32[]{:S(2)}, u32[]{:S(2)}) %collective-permute-start.7) | collective-permute-done | bytes 262176 | tf_op jit(solution)/shard_map/ppermute | solution.py:20
  24.6 0.8 %collective-permute-start.4 = (bf16[2,64,896]{2,1,0:T(8,128)(2,1)S(1)}, bf16[2,64,896]{2,1,0:T(8,128)(2,1)S(1)}, u32[]{:S(2)}, u32[]{:S(2)}) collective-permute-start(bf16[2,64,896]{2,1,0:T(8,128)(2,1)S(1)} %get-tuple-element.44), channel_id=1, source_target_pairs={{0,6},{2,4},{4,2},{6,0},{1,7},{3,5},{5,3},{7,1},{8,14},{10,12},{12... | collective-permute-start | bytes 688136 | tf_op jit(solution)/shard_map/ppermute | solution.py:20
  25.5 1.6 %collective-permute-start.9 = (bf16[2,64,1024]{2,1,0:T(8,128)(2,1)S(1)}, bf16[2,64,1024]{2,1,0:T(8,128)(2,1)S(1)}, u32[]{:S(2)}, u32[]{:S(2)}) collective-permute-start(bf16[2,64,1024]{2,1,0:T(8,128)(2,1)S(1)} %share.5.refs_4_), channel_id=1, source_target_pairs={{0,24},{8,16},{16,8},{24,0},{1,25},{9,17},{17,9},{25,1},{2,26},{10... | collective-permute-start | bytes 786440 | tf_op jit(solution)/shard_map/ppermute | solution.py:25
  27.1 2.1 %collective-permute-done.2.refs_1_.refs_5_ = bf16[2,64,896]{2,1,0:T(8,128)(2,1)S(1)} collective-permute-done((bf16[2,64,896]{2,1,0:T(8,128)(2,1)S(1)}, bf16[2,64,896]{2,1,0:T(8,128)(2,1)S(1)}, u32[]{:S(2)}, u32[]{:S(2)}) %collective-permute-start.2) | collective-permute-done | bytes 229408 | tf_op jit(solution)/shard_map/ppermute | solution.py:20
  29.8 1.6 %collective-permute-start.11 = (bf16[2,64,896]{2,1,0:T(8,128)(2,1)S(1)}, bf16[2,64,896]{2,1,0:T(8,128)(2,1)S(1)}, u32[]{:S(2)}, u32[]{:S(2)}) collective-permute-start(bf16[2,64,896]{2,1,0:T(8,128)(2,1)S(1)} %get-tuple-element.52), channel_id=1, source_target_pairs={{0,2},{2,0},{4,6},{6,4},{1,3},{3,1},{5,7},{7,5},{8,10},{10,8},{12,... | collective-permute-start | bytes 688136 | tf_op jit(solution)/shard_map/ppermute | solution.py:20
  31.4 1.9 %collective-permute-done.3.refs_2_ = bf16[2,64,896]{2,1,0:T(8,128)(2,1)S(1)} collective-permute-done((bf16[2,64,896]{2,1,0:T(8,128)(2,1)S(1)}, bf16[2,64,896]{2,1,0:T(8,128)(2,1)S(1)}, u32[]{:S(2)}, u32[]{:S(2)}) %collective-permute-start.3) | collective-permute-done | bytes 229408 | tf_op jit(solution)/shard_map/ppermute | solution.py:20
  33.3 1.7 %collective-permute-start.16 = (bf16[2,64,896]{2,1,0:T(8,128)(2,1)S(1)}, bf16[2,64,896]{2,1,0:T(8,128)(2,1)S(1)}, u32[]{:S(2)}, u32[]{:S(2)}) collective-permute-start(bf16[2,64,896]{2,1,0:T(8,128)(2,1)S(1)} %get-tuple-element.58), channel_id=1, source_target_pairs={{0,4},{2,6},{4,0},{6,2},{1,5},{3,7},{5,1},{7,3},{8,12},{10,14},{12... | collective-permute-start | bytes 688136 | tf_op jit(solution)/shard_map/ppermute | solution.py:20
  35.2 1.4 %collective-permute-start.17 = (bf16[2,64,896]{2,1,0:T(8,128)(2,1)S(1)}, bf16[2,64,896]{2,1,0:T(8,128)(2,1)S(1)}, u32[]{:S(2)}, u32[]{:S(2)}) collective-permute-start(bf16[2,64,896]{2,1,0:T(8,128)(2,1)S(1)} %get-tuple-element.59), channel_id=1, source_target_pairs={{0,6},{2,4},{4,2},{6,0},{1,7},{3,5},{5,3},{7,1},{8,14},{10,12},{12... | collective-permute-start | bytes 688136 | tf_op jit(solution)/shard_map/ppermute | solution.py:20
  36.8 1.6 %collective-permute-start.6 = (bf16[2,64,896]{2,1,0:T(8,128)(2,1)S(1)}, bf16[2,64,896]{2,1,0:T(8,128)(2,1)S(1)}, u32[]{:S(2)}, u32[]{:S(2)}) collective-permute-start(bf16[2,64,896]{2,1,0:T(8,128)(2,1)S(1)} %share.4.refs_4_), channel_id=1, source_target_pairs={{0,24},{8,16},{16,8},{24,0},{1,25},{9,17},{17,9},{25,1},{2,26},{10... | collective-permute-start | bytes 688136 | tf_op jit(solution)/shard_map/ppermute | solution.py:25
  38.4 1.6 %collective-permute-done.11.refs_5_.refs_1_ = bf16[2,64,896]{2,1,0:T(8,128)(2,1)S(1)} collective-permute-done((bf16[2,64,896]{2,1,0:T(8,128)(2,1)S(1)}, bf16[2,64,896]{2,1,0:T(8,128)(2,1)S(1)}, u32[]{:S(2)}, u32[]{:S(2)}) %collective-permute-start.11) | collective-permute-done | bytes 229408 | tf_op jit(solution)/shard_map/ppermute | solution.py:20
  41.2 3.2 %collective-permute-done.9.refs_0_.refs_4_ = bf16[2,64,1024]{2,1,0:T(8,128)(2,1)S(1)} collective-permute-done((bf16[2,64,1024]{2,1,0:T(8,128)(2,1)S(1)}, bf16[2,64,1024]{2,1,0:T(8,128)(2,1)S(1)}, u32[]{:S(2)}, u32[]{:S(2)}) %collective-permute-start.9) | collective-permute-done | bytes 262176 | tf_op jit(solution)/shard_map/ppermute | solution.py:25
  44.4 1.5 %collective-permute-start.13 = (bf16[2,64,768]{2,1,0:T(8,128)(2,1)S(1)}, bf16[2,64,768]{2,1,0:T(8,128)(2,1)S(1)}, u32[]{:S(2)}, u32[]{:S(2)}) collective-permute-start(bf16[2,64,768]{2,1,0:T(8,128)(2,1)S(1)} %get-tuple-element.55), channel_id=1, source_target_pairs={{0,4},{2,6},{4,0},{6,2},{1,5},{3,7},{5,1},{7,3},{8,12},{10,14},{12... | collective-permute-start | bytes 589832 | tf_op jit(solution)/shard_map/ppermute | solution.py:20
  45.9 1.4 %collective-permute-start.14 = (bf16[2,64,768]{2,1,0:T(8,128)(2,1)S(1)}, bf16[2,64,768]{2,1,0:T(8,128)(2,1)S(1)}, u32[]{:S(2)}, u32[]{:S(2)}) collective-permute-start(bf16[2,64,768]{2,1,0:T(8,128)(2,1)S(1)} %get-tuple-element.56), channel_id=1, source_target_pairs={{0,6},{2,4},{4,2},{6,0},{1,7},{3,5},{5,3},{7,1},{8,14},{10,12},{12... | collective-permute-start | bytes 589832 | tf_op jit(solution)/shard_map/ppermute | solution.py:20
  47.5 1.5 %collective-permute-start.18 = (bf16[2,64,896]{2,1,0:T(8,128)(2,1)S(1)}, bf16[2,64,896]{2,1,0:T(8,128)(2,1)S(1)}, u32[]{:S(2)}, u32[]{:S(2)}) collective-permute-start(bf16[2,64,896]{2,1,0:T(8,128)(2,1)S(1)} %share.7), channel_id=1, source_target_pairs={{0,24},{8,16},{16,8},{24,0},{1,25},{9,17},{17,9},{25,1},{2,26},{10... | collective-permute-start | bytes 688136 | tf_op jit(solution)/shard_map/ppermute | solution.py:25
  49.0 6.4 %collective-permute-done.13.refs_2_ = bf16[2,64,768]{2,1,0:T(8,128)(2,1)S(1)} collective-permute-done((bf16[2,64,768]{2,1,0:T(8,128)(2,1)S(1)}, bf16[2,64,768]{2,1,0:T(8,128)(2,1)S(1)}, u32[]{:S(2)}, u32[]{:S(2)}) %collective-permute-start.13) | collective-permute-done | bytes 196640 | tf_op jit(solution)/shard_map/ppermute | solution.py:20
  56.4 0.9 %place.2 = (bf16[1,128,3584]{2,1,0:T(8,128)(2,1)}, f32[8,128]{1,0:T(8,128)S(1)}) custom-call(bf16[112,3584]{1,0:T(8,128)(2,1)S(1)} %collective-permute-done.5.refs_4_.refs_0_), custom_call_target="tpu_custom_call" | custom-call | bytes 1605632 | tf_op jit(solution)/shard_map/place/pallas_call | solution.py:346
  58.3 3.6 %collective-permute-start.10 = (bf16[16,3584]{1,0:T(8,128)(2,1)S(1)}, bf16[16,3584]{1,0:T(8,128)(2,1)S(1)}, u32[]{:S(2)}, u32[]{:S(2)}) collective-permute-start(bf16[16,3584]{1,0:T(8,128)(2,1)S(1)} %leaving.3), channel_id=1, source_target_pairs={{0,8},{8,16},{16,24},{1,9},{9,17},{17,25},{2,10},{10,18},{18,26},{... | collective-permute-start | bytes 344072 | tf_op jit(solution)/shard_map/ppermute | solution.py:35
  61.9 1.4 %collective-permute-done.18.refs_0_ = bf16[2,64,896]{2,1,0:T(8,128)(2,1)S(1)} collective-permute-done((bf16[2,64,896]{2,1,0:T(8,128)(2,1)S(1)}, bf16[2,64,896]{2,1,0:T(8,128)(2,1)S(1)}, u32[]{:S(2)}, u32[]{:S(2)}) %collective-permute-start.18) | collective-permute-done | bytes 229408 | tf_op jit(solution)/shard_map/ppermute | solution.py:25
  63.9 3.6 %collective-permute-done.15.refs_0_ = bf16[2,64,768]{2,1,0:T(8,128)(2,1)S(1)} collective-permute-done((bf16[2,64,768]{2,1,0:T(8,128)(2,1)S(1)}, bf16[2,64,768]{2,1,0:T(8,128)(2,1)S(1)}, u32[]{:S(2)}, u32[]{:S(2)}) %collective-permute-start.15) | collective-permute-done | bytes 196640 | tf_op jit(solution)/shard_map/ppermute | solution.py:25
  67.9 1.6 %collective-permute-start.19 = (f32[8,128]{1,0:T(8,128)S(1)}, f32[8,128]{1,0:T(8,128)S(1)}, u32[]{:S(2)}, u32[]{:S(2)}) collective-permute-start(f32[8,128]{1,0:T(8,128)S(1)} %get-tuple-element.61.refs_0_), channel_id=1, source_target_pairs={{0,2},{2,0},{4,6},{6,4},{1,3},{3,1},{5,7},{7,5},{8,10},{10,8},{12,... | collective-permute-start | bytes 12296 | tf_op jit(solution)/shard_map/ppermute | solution.py:20
  69.5 1.5 %collective-permute-start.20 = (f32[8,128]{1,0:T(8,128)S(1)}, f32[8,128]{1,0:T(8,128)S(1)}, u32[]{:S(2)}, u32[]{:S(2)}) collective-permute-start(f32[8,128]{1,0:T(8,128)S(1)} %get-tuple-element.61.refs_0_), channel_id=1, source_target_pairs={{0,4},{2,6},{4,0},{6,2},{1,5},{3,7},{5,1},{7,3},{8,12},{10,14},{12... | collective-permute-start | bytes 12296 | tf_op jit(solution)/shard_map/ppermute | solution.py:20
  71.6 1.2 %codes.1 = (bf16[2,1,64,3584]{3,2,1,0:T(8,128)(2,1)}, f32[8,128]{1,0:T(8,128)S(1)}) custom-call(f32[8,128]{1,0:T(8,128)S(1)} %get-tuple-element.61.refs_0_, f32[8,128]{1,0:T(8,128)S(1)} %collective-permute-done.19.refs_1_, f32[2,64,1024]{2,1,0:T(8,128)S(1)} %get-tuple-element.62.refs_2_, f32[2,64,896]{2,1,0:T(8,128)S(1)} %get-tuple-element.63.refs_3_, ...), custom_call_target="tpu_custom_call" | custom-call | flops 917504 | bytes 1843200 | tf_op jit(solution)/shard_map/codes/pallas_call | solution.py:56
  72.8 1.2 %place.3 = (bf16[1,128,3584]{2,1,0:T(8,128)(2,1)}, f32[8,128]{1,0:T(8,128)}) custom-call(bf16[16,3584]{1,0:T(8,128)(2,1)S(1)} %collective-permute-done.10.refs_0_, bf16[1,128,3584]{2,1,0:T(8,128)(2,1)} %get-tuple-element.51.refs_1_, f32[8,128]{1,0:T(8,128)S(1)} %get-tuple-element.66.refs_2_.refs_4_), custom_call_target="tpu_custom_call", output_to_operand_aliasing={{0}: (1, {})} | custom-call | bytes 229376 | tf_op jit(solution)/shard_map/place/pallas_call | solution.py:346
  74.1 1.5 %collective-permute-done.21.refs_3_ = f32[8,128]{1,0:T(8,128)S(1)} collective-permute-done((f32[8,128]{1,0:T(8,128)S(1)}, f32[8,128]{1,0:T(8,128)S(1)}, u32[]{:S(2)}, u32[]{:S(2)}) %collective-permute-start.21) | collective-permute-done | bytes 4128 | tf_op jit(solution)/shard_map/ppermute | solution.py:20
  (38 shorter events, 8.9 us)
Async XLA Ops:
  4.8 2.0 %collective-permute-start = (f32[1024,128]{1,0:T(8,128)S(1)}, f32[1024,128]{1,0:T(8,128)S(1)}, u32[]{:S(2)}, u32[]{:S(2)}) collective-permute-start(f32[1024,128]{1,0:T(8,128)S(1)} %get-tuple-element.36.rest_0_.refs_0_), channel_id=1, source_target_pairs={{0,1},{1,0},{2,3},{3,2},{4,5},{5,4},{6,7},{7,6},{8,9},{9,8},{10,11... | collective-permute-start | bytes 1572872 | tf_op jit(solution)/shard_map/ppermute | solution.py:20
  7.3 29.3 %collective-permute-start.5 = (bf16[112,3584]{1,0:T(8,128)(2,1)S(1)}, bf16[112,3584]{1,0:T(8,128)(2,1)S(1)}, u32[]{:S(2)}, u32[]{:S(2)}) collective-permute-start(bf16[112,3584]{1,0:T(8,128)(2,1)S(1)} %leaving.2.refs_4_), channel_id=1, source_target_pairs={{0,8},{8,16},{16,24},{24,0},{1,9},{9,17},{17,25},{25,1},{2,10},{10... | collective-permute-start | bytes 2408456 | tf_op jit(solution)/shard_map/ppermute | solution.py:30
  9.5 9.3 %collective-permute-start.1 = (bf16[2,64,1024]{2,1,0:T(8,128)(2,1)S(1)}, bf16[2,64,1024]{2,1,0:T(8,128)(2,1)S(1)}, u32[]{:S(2)}, u32[]{:S(2)}) collective-permute-start(bf16[2,64,1024]{2,1,0:T(8,128)(2,1)S(1)} %get-tuple-element.40), channel_id=1, source_target_pairs={{0,2},{2,0},{4,6},{6,4},{1,3},{3,1},{5,7},{7,5},{8,10},{10,8},{12,... | collective-permute-start | bytes 786440 | tf_op jit(solution)/shard_map/ppermute | solution.py:20
  11.0 13.5 %collective-permute-start.7 = (bf16[2,64,1024]{2,1,0:T(8,128)(2,1)S(1)}, bf16[2,64,1024]{2,1,0:T(8,128)(2,1)S(1)}, u32[]{:S(2)}, u32[]{:S(2)}) collective-permute-start(bf16[2,64,1024]{2,1,0:T(8,128)(2,1)S(1)} %get-tuple-element.46), channel_id=1, source_target_pairs={{0,4},{2,6},{4,0},{6,2},{1,5},{3,7},{5,1},{7,3},{8,12},{10,14},{12... | collective-permute-start | bytes 786440 | tf_op jit(solution)/shard_map/ppermute | solution.py:20
  12.5 12.8 %collective-permute-start.8 = (bf16[2,64,1024]{2,1,0:T(8,128)(2,1)S(1)}, bf16[2,64,1024]{2,1,0:T(8,128)(2,1)S(1)}, u32[]{:S(2)}, u32[]{:S(2)}) collective-permute-start(bf16[2,64,1024]{2,1,0:T(8,128)(2,1)S(1)} %get-tuple-element.47), channel_id=1, source_target_pairs={{0,6},{2,4},{4,2},{6,0},{1,7},{3,5},{5,3},{7,1},{8,14},{10,12},{12... | collective-permute-start | bytes 786440 | tf_op jit(solution)/shard_map/ppermute | solution.py:20
  19.2 10.1 %collective-permute-start.2 = (bf16[2,64,896]{2,1,0:T(8,128)(2,1)S(1)}, bf16[2,64,896]{2,1,0:T(8,128)(2,1)S(1)}, u32[]{:S(2)}, u32[]{:S(2)}) collective-permute-start(bf16[2,64,896]{2,1,0:T(8,128)(2,1)S(1)} %get-tuple-element.42), channel_id=1, source_target_pairs={{0,2},{2,0},{4,6},{6,4},{1,3},{3,1},{5,7},{7,5},{8,10},{10,8},{12,... | collective-permute-start | bytes 688136 | tf_op jit(solution)/shard_map/ppermute | solution.py:20
  20.8 12.5 %collective-permute-start.3 = (bf16[2,64,896]{2,1,0:T(8,128)(2,1)S(1)}, bf16[2,64,896]{2,1,0:T(8,128)(2,1)S(1)}, u32[]{:S(2)}, u32[]{:S(2)}) collective-permute-start(bf16[2,64,896]{2,1,0:T(8,128)(2,1)S(1)} %get-tuple-element.43), channel_id=1, source_target_pairs={{0,4},{2,6},{4,0},{6,2},{1,5},{3,7},{5,1},{7,3},{8,12},{10,14},{12... | collective-permute-start | bytes 688136 | tf_op jit(solution)/shard_map/ppermute | solution.py:20
  24.6 10.6 %collective-permute-start.4 = (bf16[2,64,896]{2,1,0:T(8,128)(2,1)S(1)}, bf16[2,64,896]{2,1,0:T(8,128)(2,1)S(1)}, u32[]{:S(2)}, u32[]{:S(2)}) collective-permute-start(bf16[2,64,896]{2,1,0:T(8,128)(2,1)S(1)} %get-tuple-element.44), channel_id=1, source_target_pairs={{0,6},{2,4},{4,2},{6,0},{1,7},{3,5},{5,3},{7,1},{8,14},{10,12},{12... | collective-permute-start | bytes 688136 | tf_op jit(solution)/shard_map/ppermute | solution.py:20
  25.5 18.9 %collective-permute-start.9 = (bf16[2,64,1024]{2,1,0:T(8,128)(2,1)S(1)}, bf16[2,64,1024]{2,1,0:T(8,128)(2,1)S(1)}, u32[]{:S(2)}, u32[]{:S(2)}) collective-permute-start(bf16[2,64,1024]{2,1,0:T(8,128)(2,1)S(1)} %share.5.refs_4_), channel_id=1, source_target_pairs={{0,24},{8,16},{16,8},{24,0},{1,25},{9,17},{17,9},{25,1},{2,26},{10... | collective-permute-start | bytes 786440 | tf_op jit(solution)/shard_map/ppermute | solution.py:25
  29.8 10.2 %collective-permute-start.11 = (bf16[2,64,896]{2,1,0:T(8,128)(2,1)S(1)}, bf16[2,64,896]{2,1,0:T(8,128)(2,1)S(1)}, u32[]{:S(2)}, u32[]{:S(2)}) collective-permute-start(bf16[2,64,896]{2,1,0:T(8,128)(2,1)S(1)} %get-tuple-element.52), channel_id=1, source_target_pairs={{0,2},{2,0},{4,6},{6,4},{1,3},{3,1},{5,7},{7,5},{8,10},{10,8},{12,... | collective-permute-start | bytes 688136 | tf_op jit(solution)/shard_map/ppermute | solution.py:20
  33.3 12.6 %collective-permute-start.16 = (bf16[2,64,896]{2,1,0:T(8,128)(2,1)S(1)}, bf16[2,64,896]{2,1,0:T(8,128)(2,1)S(1)}, u32[]{:S(2)}, u32[]{:S(2)}) collective-permute-start(bf16[2,64,896]{2,1,0:T(8,128)(2,1)S(1)} %get-tuple-element.58), channel_id=1, source_target_pairs={{0,4},{2,6},{4,0},{6,2},{1,5},{3,7},{5,1},{7,3},{8,12},{10,14},{12... | collective-permute-start | bytes 688136 | tf_op jit(solution)/shard_map/ppermute | solution.py:20
  35.2 12.1 %collective-permute-start.17 = (bf16[2,64,896]{2,1,0:T(8,128)(2,1)S(1)}, bf16[2,64,896]{2,1,0:T(8,128)(2,1)S(1)}, u32[]{:S(2)}, u32[]{:S(2)}) collective-permute-start(bf16[2,64,896]{2,1,0:T(8,128)(2,1)S(1)} %get-tuple-element.59), channel_id=1, source_target_pairs={{0,6},{2,4},{4,2},{6,0},{1,7},{3,5},{5,3},{7,1},{8,14},{10,12},{12... | collective-permute-start | bytes 688136 | tf_op jit(solution)/shard_map/ppermute | solution.py:20
  36.6 19.2 %copy-start = (f32[2,1,64,3584]{3,2,1,0:T(8,128)S(1)}, f32[2,1,64,3584]{3,2,1,0:T(8,128)}, u32[]{:S(2)}) copy-start(f32[2,1,64,3584]{3,2,1,0:T(8,128)} %refs_1_.9) | copy-start | bytes 5505028
  36.6 19.2 %copy-start.1 = (bf16[2,1,64,3584]{3,2,1,0:T(8,128)(2,1)S(1)}, bf16[2,1,64,3584]{3,2,1,0:T(8,128)(2,1)}, u32[]{:S(2)}) copy-start(bf16[2,1,64,3584]{3,2,1,0:T(8,128)(2,1)} %refs_2_.9) | copy-start | bytes 2752516
  36.6 19.2 %copy-start.2 = (bf16[2,1,64,3584]{3,2,1,0:T(8,128)(2,1)S(1)}, bf16[2,1,64,3584]{3,2,1,0:T(8,128)(2,1)}, u32[]{:S(2)}) copy-start(bf16[2,1,64,3584]{3,2,1,0:T(8,128)(2,1)} %refs_3_.9) | copy-start | bytes 2752516
  36.8 18.5 %collective-permute-start.6 = (bf16[2,64,896]{2,1,0:T(8,128)(2,1)S(1)}, bf16[2,64,896]{2,1,0:T(8,128)(2,1)S(1)}, u32[]{:S(2)}, u32[]{:S(2)}) collective-permute-start(bf16[2,64,896]{2,1,0:T(8,128)(2,1)S(1)} %share.4.refs_4_), channel_id=1, source_target_pairs={{0,24},{8,16},{16,8},{24,0},{1,25},{9,17},{17,9},{25,1},{2,26},{10... | collective-permute-start | bytes 688136 | tf_op jit(solution)/shard_map/ppermute | solution.py:25
  40.4 8.5 %collective-permute-start.12 = (bf16[2,64,768]{2,1,0:T(8,128)(2,1)S(1)}, bf16[2,64,768]{2,1,0:T(8,128)(2,1)S(1)}, u32[]{:S(2)}, u32[]{:S(2)}) collective-permute-start(bf16[2,64,768]{2,1,0:T(8,128)(2,1)S(1)} %get-tuple-element.54), channel_id=1, source_target_pairs={{0,2},{2,0},{4,6},{6,4},{1,3},{3,1},{5,7},{7,5},{8,10},{10,8},{12,... | collective-permute-start | bytes 589832 | tf_op jit(solution)/shard_map/ppermute | solution.py:20
  44.4 10.9 %collective-permute-start.13 = (bf16[2,64,768]{2,1,0:T(8,128)(2,1)S(1)}, bf16[2,64,768]{2,1,0:T(8,128)(2,1)S(1)}, u32[]{:S(2)}, u32[]{:S(2)}) collective-permute-start(bf16[2,64,768]{2,1,0:T(8,128)(2,1)S(1)} %get-tuple-element.55), channel_id=1, source_target_pairs={{0,4},{2,6},{4,0},{6,2},{1,5},{3,7},{5,1},{7,3},{8,12},{10,14},{12... | collective-permute-start | bytes 589832 | tf_op jit(solution)/shard_map/ppermute | solution.py:20
  45.9 9.4 %collective-permute-start.14 = (bf16[2,64,768]{2,1,0:T(8,128)(2,1)S(1)}, bf16[2,64,768]{2,1,0:T(8,128)(2,1)S(1)}, u32[]{:S(2)}, u32[]{:S(2)}) collective-permute-start(bf16[2,64,768]{2,1,0:T(8,128)(2,1)S(1)} %get-tuple-element.56), channel_id=1, source_target_pairs={{0,6},{2,4},{4,2},{6,0},{1,7},{3,5},{5,3},{7,1},{8,14},{10,12},{12... | collective-permute-start | bytes 589832 | tf_op jit(solution)/shard_map/ppermute | solution.py:20
  47.5 15.9 %collective-permute-start.18 = (bf16[2,64,896]{2,1,0:T(8,128)(2,1)S(1)}, bf16[2,64,896]{2,1,0:T(8,128)(2,1)S(1)}, u32[]{:S(2)}, u32[]{:S(2)}) collective-permute-start(bf16[2,64,896]{2,1,0:T(8,128)(2,1)S(1)} %share.7), channel_id=1, source_target_pairs={{0,24},{8,16},{16,8},{24,0},{1,25},{9,17},{17,9},{25,1},{2,26},{10... | collective-permute-start | bytes 688136 | tf_op jit(solution)/shard_map/ppermute | solution.py:25
  55.4 12.0 %collective-permute-start.15 = (bf16[2,64,768]{2,1,0:T(8,128)(2,1)S(1)}, bf16[2,64,768]{2,1,0:T(8,128)(2,1)S(1)}, u32[]{:S(2)}, u32[]{:S(2)}) collective-permute-start(bf16[2,64,768]{2,1,0:T(8,128)(2,1)S(1)} %share.6), channel_id=1, source_target_pairs={{0,24},{8,16},{16,8},{24,0},{1,25},{9,17},{17,9},{25,1},{2,26},{10... | collective-permute-start | bytes 589832 | tf_op jit(solution)/shard_map/ppermute | solution.py:25
  58.3 14.5 %collective-permute-start.10 = (bf16[16,3584]{1,0:T(8,128)(2,1)S(1)}, bf16[16,3584]{1,0:T(8,128)(2,1)S(1)}, u32[]{:S(2)}, u32[]{:S(2)}) collective-permute-start(bf16[16,3584]{1,0:T(8,128)(2,1)S(1)} %leaving.3), channel_id=1, source_target_pairs={{0,8},{8,16},{16,24},{1,9},{9,17},{17,25},{2,10},{10,18},{18,26},{... | collective-permute-start | bytes 344072 | tf_op jit(solution)/shard_map/ppermute | solution.py:35
  67.9 3.7 %collective-permute-start.19 = (f32[8,128]{1,0:T(8,128)S(1)}, f32[8,128]{1,0:T(8,128)S(1)}, u32[]{:S(2)}, u32[]{:S(2)}) collective-permute-start(f32[8,128]{1,0:T(8,128)S(1)} %get-tuple-element.61.refs_0_), channel_id=1, source_target_pairs={{0,2},{2,0},{4,6},{6,4},{1,3},{3,1},{5,7},{7,5},{8,10},{10,8},{12,... | collective-permute-start | bytes 12296 | tf_op jit(solution)/shard_map/ppermute | solution.py:20
  69.5 4.6 %collective-permute-start.20 = (f32[8,128]{1,0:T(8,128)S(1)}, f32[8,128]{1,0:T(8,128)S(1)}, u32[]{:S(2)}, u32[]{:S(2)}) collective-permute-start(f32[8,128]{1,0:T(8,128)S(1)} %get-tuple-element.61.refs_0_), channel_id=1, source_target_pairs={{0,4},{2,6},{4,0},{6,2},{1,5},{3,7},{5,1},{7,3},{8,12},{10,14},{12... | collective-permute-start | bytes 12296 | tf_op jit(solution)/shard_map/ppermute | solution.py:20
  71.0 4.5 %collective-permute-start.21 = (f32[8,128]{1,0:T(8,128)S(1)}, f32[8,128]{1,0:T(8,128)S(1)}, u32[]{:S(2)}, u32[]{:S(2)}) collective-permute-start(f32[8,128]{1,0:T(8,128)S(1)} %get-tuple-element.61.refs_0_), channel_id=1, source_target_pairs={{0,6},{2,4},{4,2},{6,0},{1,7},{3,5},{5,3},{7,1},{8,14},{10,12},{12... | collective-permute-start | bytes 12296 | tf_op jit(solution)/shard_map/ppermute | solution.py:20

commit v13 on v12

--- a/solution.py
+++ b/solution.py
@@ -227,19 +227,26 @@
                 block += 1
 
 
-def scale_kernel(group, experts, *refs):
-    peak_refs, scale_ref = refs[:experts], refs[-1]
+def finish_kernel(start, group, count, *refs):
+    tail_refs, peak_refs, (left_ref, scale_ref, sems) = refs[:count], refs[count + 2 : -3], refs[-3:]
+    copies = []
+    for k, ref in enumerate(tail_refs):
+        rows = pl.ds(start + k * ref.shape[0], ref.shape[0])
+        copies.append(pltpu.make_async_copy(ref, left_ref.at[0, rows], sems.at[k]))
+    for copy in copies:
+        copy.start()
     blocks = scale_ref.shape[3]
     mine = lax.axis_index("expert") // group
     for far in range(len(peak_refs) // group):
         top = merged(peak_refs[far * group : (far + 1) * group])
         for side in range(2):
             scale_ref[side, 0, pl.ds(mine ^ far, 1), :] = top[side : side + 1, :blocks]
-
-
-def place_kernel(start, in_ref, *rest):
-    out_ref, token_ref, sem = rest[-3:]
-    copy = pltpu.make_async_copy(in_ref, out_ref.at[0, pl.ds(start, in_ref.shape[0])], sem)
+    for copy in copies:
+        copy.wait()
+
+
+def place_kernel(in_ref, out_ref, token_ref, sem):
+    copy = pltpu.make_async_copy(in_ref, out_ref.at[0, pl.ds(0, in_ref.shape[0])], sem)
     copy.start()
     token_ref[...] = jnp.zeros_like(token_ref)
     copy.wait()
@@ -320,7 +327,7 @@
             flops=4 * tokens * latent * (stop - start),
         )
 
-    head = 112
+    head = 96
     first_rows = leaving(0, head)
     left_head = turned(first_rows, "pipe")
     first = grads(0, first_rows)
@@ -336,26 +343,23 @@
                 shape(own.shape, BF16),
                 own,
                 *others[-1],
+                *shares[-1:],
                 *after,
                 read=experts,
             )
         )
         arrived.append(mirrored(shares[-1], "pipe"))
 
-    def place(start, rows, kept=(), after=()):
-        return pl.pallas_call(
-            lambda *refs: place_kernel(start, *refs),
-            in_specs=[ANY] * (1 + len(kept) + len(after)),
-            out_specs=[ANY, VMEM],
-            out_shape=[shape((1, tokens, width), BF16), shape((8, LANES), F32)],
-            scratch_shapes=[pltpu.SemaphoreType.DMA],
-            input_output_aliases={1 + k: k for k in range(len(kept))},
-            compiler_params=ROOM,
-            cost_estimate=pl.CostEstimate(flops=0, bytes_accessed=4 * rows.shape[0] * width, transcendentals=0),
-            name="place",
-        )(rows, *kept, *after)
-
-    placed, token = place(0, left_head)
+    placed, token = pl.pallas_call(
+        place_kernel,
+        in_specs=[ANY],
+        out_specs=[ANY, VMEM],
+        out_shape=[shape((1, tokens, width), BF16), shape((8, LANES), F32)],
+        scratch_shapes=[pltpu.SemaphoreType.DMA],
+        compiler_params=ROOM,
+        cost_estimate=pl.CostEstimate(flops=0, bytes_accessed=4 * head * width, transcendentals=0),
+        name="place",
+    )(left_head)
 
     fresh, peaks, steps = [], None, []
     for chunk, (start, stop) in enumerate(chunks):
@@ -378,7 +382,9 @@
         fresh.append(some)
         steps.append(peaks)
 
-    left_tail = shifted(leaving(head, tokens - head, steps[-3]), "pipe")
+    half = (tokens - head) // 2
+    tail_rows = leaving(head, half, steps[-3])
+    left_tails = [shifted(tail_rows, "pipe"), shifted(leaving(head + half, half, steps[-3]), "pipe")]
 
     group = LANES // depth
     peak_rows = [peaks] + [exchange(peaks, "expert", k) for k in range(1, experts)]
@@ -391,15 +397,18 @@
         read=group + len(fresh),
         flops=4 * depth * width,
     )
-    scales = call(
-        lambda *refs: scale_kernel(group, experts, *refs),
-        "scales",
-        shape((2, 1, experts // group, blocks), F32),
-        *peak_rows,
-        token,
-        read=experts,
-    )
-    left, _ = place(head, left_tail, (placed,), (token,))
+    count = len(left_tails)
+    left, scales = pl.pallas_call(
+        lambda *refs: finish_kernel(head, group, count, *refs),
+        in_specs=[ANY] * (count + 2) + [VMEM] * experts,
+        out_specs=[ANY, VMEM],
+        out_shape=[shape((1, tokens, width), BF16), shape((2, 1, experts // group, blocks), F32)],
+        scratch_shapes=[pltpu.SemaphoreType.DMA((count,))],
+        input_output_aliases={count: 0},
+        compiler_params=ROOM,
+        cost_estimate=pl.CostEstimate(flops=0, bytes_accessed=4 * (tokens - head) * width, transcendentals=0),
+        name="finish",
+    )(*left_tails, placed, token, *peak_rows)
     return (left, coded, scales)
 
 

time: 76.3 us -> 76.2 us (level); the launches traced: 76.1 us -> 75.1 us
  waiting for transfers between devices: 30.3 us -> 26.3 us
  starting transfers between devices: 29.9 us -> 33.1 us
    ppermute x16, waiting for transfers between devices: 22.1 us -> 17.1 us  [exchange(): return lax.ppermute(block, axis, [(i, i ^ offset) for i in range(count)])]
    ppermute x1 -> x2, starting transfers between devices: 3.61 us -> 5.66 us  [shifted(): return lax.ppermute(block, axis, [(i, i + 1) for i in range(count - 1)])]
    ppermute x4, starting transfers between devices: 5.17 us -> 6.5 us  [mirrored(): return lax.ppermute(block, axis, [(i, count - 1 - i) for i in range(count)])]
    ppermute x4, waiting for transfers between devices: 8.21 us -> 9.19 us  [mirrored(): return lax.ppermute(block, axis, [(i, count - 1 - i) for i in range(count)])]
  transfers between devices with their start and end apart: 22 -> 23, of which waited for: 13 -> 14; matrix products, arithmetic and copies ran while one was open for 0% -> 0% of each run, Pallas kernels for 13% -> 11%
where the time goes in v13:
time: 76.2 us; the launch traced here: 75.1 us
  starting transfers between devices  33.1 us (43%)
  waiting for transfers between devices  26.3 us (35%)
  Pallas kernels  14.8 us (19%)
  between operations  0.81 us (1%)
    ppermute x16, starting transfers between devices, exchange(): return lax.ppermute(block, axis, [(i, i ^ offset) for i in range(count)])  19.4 us
    ppermute x16, waiting for transfers between devices, exchange(): return lax.ppermute(block, axis, [(i, i ^ offset) for i in range(count)])  17.1 us
    ppermute x4, waiting for transfers between devices, mirrored(): return lax.ppermute(block, axis, [(i, count - 1 - i) for i in range(count)])  9.19 us
    pallas_call x16, Pallas kernels, call(): pl.pallas_call(kernel, in_specs=[VMEM] * read + [ANY] * (len(operands) -...  7.06 us
    ppermute x4, starting transfers between devices, mirrored(): return lax.ppermute(block, axis, [(i, count - 1 - i) for i in range(count)])  6.5 us
    ppermute x2, starting transfers between devices, shifted(): return lax.ppermute(block, axis, [(i, i + 1) for i in range(count - 1)])  5.66 us
    pallas_call x1, Pallas kernels, shards(): pl.pallas_call(lambda *refs: latent_kernel(tiles, *refs), in_specs=[ANY]...  4.12 us
    ppermute x1, starting transfers between devices, turned(): lax.ppermute(block, axis, [(i, (i + 1) % count) for i in range(count)])  1.58 us
  transfers between devices with their start and end apart: 23, of which 14 were waited for; matrix products, arithmetic and copies ran while one was open for 0% of the time, Pallas kernels for 11%

profile of v13, /device:TPU:8, one launch (start us, length us, event | category | flops | bytes accessed | tf_op | source)
XLA Modules:
  0.0 75.1 jit_solution(10918971119114671982)
XLA Ops:
  0.6 4.1 %latents.1 = (f32[1024,128]{1,0:T(8,128)S(1)}, bf16[128,3584]{1,0:T(8,128)(2,1)S(1)}, bf16[128,3584]{1,0:T(8,128)(2,1)S(1)}, bf16[128,3584]{1,0:T(8,128)(2,1)S(1)}) custom-call(bf16[1,128,3584]{2,1,0:T(8,128)(2,1)} %refs_0_.1, bf16[1,128,3584]{2,1,0:T(8,128)(2,1)} %refs_1_.5, bf16[1,128,3584]{2,1,0:T(8,128)(2,1)} %refs_2_.5, ...), custom_call_target="tpu_custom_call" | custom-call | flops 704643072 | bytes 8257536 | tf_op jit(solution)/shard_map/latents/pallas_call | solution.py:271
  4.8 1.5 %fetch.1.refs_3_ = bf16[256,3584]{1,0:T(8,128)(2,1)S(1)} custom-call(bf16[2,1,256,3584]{3,2,1,0:T(8,128)(2,1)} %in_ref.1, f32[1024,128]{1,0:T(8,128)S(1)} %get-tuple-element.37.rest_0_.refs_0_), custom_call_target="tpu_custom_call" | custom-call | bytes 1835008 | tf_op jit(solution)/shard_map/fetch/pallas_call | solution.py:290
  7.8 1.6 %collective-permute-start.1 = (bf16[2,64,1024]{2,1,0:T(8,128)(2,1)S(1)}, bf16[2,64,1024]{2,1,0:T(8,128)(2,1)S(1)}, u32[]{:S(2)}, u32[]{:S(2)}) collective-permute-start(bf16[2,64,1024]{2,1,0:T(8,128)(2,1)S(1)} %get-tuple-element.41), channel_id=1, source_target_pairs={{0,2},{2,0},{4,6},{6,4},{1,3},{3,1},{5,7},{7,5},{8,10},{10,8},{12,... | collective-permute-start | bytes 786440 | tf_op jit(solution)/shard_map/ppermute | solution.py:20
  9.3 1.6 %collective-permute-start.7 = (bf16[96,3584]{1,0:T(8,128)(2,1)S(1)}, bf16[96,3584]{1,0:T(8,128)(2,1)S(1)}, u32[]{:S(2)}, u32[]{:S(2)}) collective-permute-start(bf16[96,3584]{1,0:T(8,128)(2,1)S(1)} %leaving.3.refs_4_), channel_id=1, source_target_pairs={{0,8},{8,16},{16,24},{24,0},{1,9},{9,17},{17,25},{25,1},{2,10},{10... | collective-permute-start | bytes 2064392 | tf_op jit(solution)/shard_map/ppermute | solution.py:30
  10.9 1.5 %collective-permute-start.5 = (bf16[2,64,1024]{2,1,0:T(8,128)(2,1)S(1)}, bf16[2,64,1024]{2,1,0:T(8,128)(2,1)S(1)}, u32[]{:S(2)}, u32[]{:S(2)}) collective-permute-start(bf16[2,64,1024]{2,1,0:T(8,128)(2,1)S(1)} %get-tuple-element.47), channel_id=1, source_target_pairs={{0,4},{2,6},{4,0},{6,2},{1,5},{3,7},{5,1},{7,3},{8,12},{10,14},{12... | collective-permute-start | bytes 786440 | tf_op jit(solution)/shard_map/ppermute | solution.py:20
  12.9 4.1 %collective-permute-done.1.refs_4_.refs_1_ = bf16[2,64,1024]{2,1,0:T(8,128)(2,1)S(1)} collective-permute-done((bf16[2,64,1024]{2,1,0:T(8,128)(2,1)S(1)}, bf16[2,64,1024]{2,1,0:T(8,128)(2,1)S(1)}, u32[]{:S(2)}, u32[]{:S(2)}) %collective-permute-start.1) | collective-permute-done | bytes 262176 | tf_op jit(solution)/shard_map/ppermute | solution.py:20
  17.5 1.6 %collective-permute-start.2 = (bf16[2,64,896]{2,1,0:T(8,128)(2,1)S(1)}, bf16[2,64,896]{2,1,0:T(8,128)(2,1)S(1)}, u32[]{:S(2)}, u32[]{:S(2)}) collective-permute-start(bf16[2,64,896]{2,1,0:T(8,128)(2,1)S(1)} %get-tuple-element.43), channel_id=1, source_target_pairs={{0,2},{2,0},{4,6},{6,4},{1,3},{3,1},{5,7},{7,5},{8,10},{10,8},{12,... | collective-permute-start | bytes 688136 | tf_op jit(solution)/shard_map/ppermute | solution.py:20
  19.1 1.5 %collective-permute-start.3 = (bf16[2,64,896]{2,1,0:T(8,128)(2,1)S(1)}, bf16[2,64,896]{2,1,0:T(8,128)(2,1)S(1)}, u32[]{:S(2)}, u32[]{:S(2)}) collective-permute-start(bf16[2,64,896]{2,1,0:T(8,128)(2,1)S(1)} %get-tuple-element.44), channel_id=1, source_target_pairs={{0,4},{2,6},{4,0},{6,2},{1,5},{3,7},{5,1},{7,3},{8,12},{10,14},{12... | collective-permute-start | bytes 688136 | tf_op jit(solution)/shard_map/ppermute | solution.py:20
  20.6 5.1 %collective-permute-done.5.refs_2_ = bf16[2,64,1024]{2,1,0:T(8,128)(2,1)S(1)} collective-permute-done((bf16[2,64,1024]{2,1,0:T(8,128)(2,1)S(1)}, bf16[2,64,1024]{2,1,0:T(8,128)(2,1)S(1)}, u32[]{:S(2)}, u32[]{:S(2)}) %collective-permute-start.5) | collective-permute-done | bytes 262176 | tf_op jit(solution)/shard_map/ppermute | solution.py:20
  25.7 1.6 %collective-permute-start.4 = (bf16[2,64,896]{2,1,0:T(8,128)(2,1)S(1)}, bf16[2,64,896]{2,1,0:T(8,128)(2,1)S(1)}, u32[]{:S(2)}, u32[]{:S(2)}) collective-permute-start(bf16[2,64,896]{2,1,0:T(8,128)(2,1)S(1)} %get-tuple-element.45), channel_id=1, source_target_pairs={{0,6},{2,4},{4,2},{6,0},{1,7},{3,5},{5,3},{7,1},{8,14},{10,12},{12... | collective-permute-start | bytes 688136 | tf_op jit(solution)/shard_map/ppermute | solution.py:20
  27.4 1.6 %collective-permute-start.9 = (bf16[2,64,1024]{2,1,0:T(8,128)(2,1)S(1)}, bf16[2,64,1024]{2,1,0:T(8,128)(2,1)S(1)}, u32[]{:S(2)}, u32[]{:S(2)}) collective-permute-start(bf16[2,64,1024]{2,1,0:T(8,128)(2,1)S(1)} %share.4.refs_4_), channel_id=1, source_target_pairs={{0,24},{8,16},{16,8},{24,0},{1,25},{9,17},{17,9},{25,1},{2,26},{10... | collective-permute-start | bytes 786440 | tf_op jit(solution)/shard_map/ppermute | solution.py:25
  29.6 1.6 %collective-permute-start.12 = (bf16[2,64,896]{2,1,0:T(8,128)(2,1)S(1)}, bf16[2,64,896]{2,1,0:T(8,128)(2,1)S(1)}, u32[]{:S(2)}, u32[]{:S(2)}) collective-permute-start(bf16[2,64,896]{2,1,0:T(8,128)(2,1)S(1)} %get-tuple-element.53), channel_id=1, source_target_pairs={{0,2},{2,0},{4,6},{6,4},{1,3},{3,1},{5,7},{7,5},{8,10},{10,8},{12,... | collective-permute-start | bytes 688136 | tf_op jit(solution)/shard_map/ppermute | solution.py:20
  31.1 2.0 %collective-permute-done.3.refs_2_ = bf16[2,64,896]{2,1,0:T(8,128)(2,1)S(1)} collective-permute-done((bf16[2,64,896]{2,1,0:T(8,128)(2,1)S(1)}, bf16[2,64,896]{2,1,0:T(8,128)(2,1)S(1)}, u32[]{:S(2)}, u32[]{:S(2)}) %collective-permute-start.3) | collective-permute-done | bytes 229408 | tf_op jit(solution)/shard_map/ppermute | solution.py:20
  33.1 1.4 %collective-permute-start.16 = (bf16[2,64,896]{2,1,0:T(8,128)(2,1)S(1)}, bf16[2,64,896]{2,1,0:T(8,128)(2,1)S(1)}, u32[]{:S(2)}, u32[]{:S(2)}) collective-permute-start(bf16[2,64,896]{2,1,0:T(8,128)(2,1)S(1)} %get-tuple-element.59), channel_id=1, source_target_pairs={{0,4},{2,6},{4,0},{6,2},{1,5},{3,7},{5,1},{7,3},{8,12},{10,14},{12... | collective-permute-start | bytes 688136 | tf_op jit(solution)/shard_map/ppermute | solution.py:20
  35.1 1.5 %collective-permute-start.17 = (bf16[2,64,896]{2,1,0:T(8,128)(2,1)S(1)}, bf16[2,64,896]{2,1,0:T(8,128)(2,1)S(1)}, u32[]{:S(2)}, u32[]{:S(2)}) collective-permute-start(bf16[2,64,896]{2,1,0:T(8,128)(2,1)S(1)} %get-tuple-element.60), channel_id=1, source_target_pairs={{0,6},{2,4},{4,2},{6,0},{1,7},{3,5},{5,3},{7,1},{8,14},{10,12},{12... | collective-permute-start | bytes 688136 | tf_op jit(solution)/shard_map/ppermute | solution.py:20
  36.8 1.6 %collective-permute-start.8 = (bf16[2,64,896]{2,1,0:T(8,128)(2,1)S(1)}, bf16[2,64,896]{2,1,0:T(8,128)(2,1)S(1)}, u32[]{:S(2)}, u32[]{:S(2)}) collective-permute-start(bf16[2,64,896]{2,1,0:T(8,128)(2,1)S(1)} %share.5.refs_4_), channel_id=1, source_target_pairs={{0,24},{8,16},{16,8},{24,0},{1,25},{9,17},{17,9},{25,1},{2,26},{10... | collective-permute-start | bytes 688136 | tf_op jit(solution)/shard_map/ppermute | solution.py:25
  38.4 0.7 collective-permute-done.12.refs_5_.refs_1_
  39.7 4.8 %collective-permute-done.9.refs_0_.refs_5_ = bf16[2,64,1024]{2,1,0:T(8,128)(2,1)S(1)} collective-permute-done((bf16[2,64,1024]{2,1,0:T(8,128)(2,1)S(1)}, bf16[2,64,1024]{2,1,0:T(8,128)(2,1)S(1)}, u32[]{:S(2)}, u32[]{:S(2)}) %collective-permute-start.9) | collective-permute-done | bytes 262176 | tf_op jit(solution)/shard_map/ppermute | solution.py:25
  44.4 0.7 collective-permute-start.14
  45.1 2.2 %collective-permute-start.15 = (bf16[2,64,768]{2,1,0:T(8,128)(2,1)S(1)}, bf16[2,64,768]{2,1,0:T(8,128)(2,1)S(1)}, u32[]{:S(2)}, u32[]{:S(2)}) collective-permute-start(bf16[2,64,768]{2,1,0:T(8,128)(2,1)S(1)} %get-tuple-element.57), channel_id=1, source_target_pairs={{0,6},{2,4},{4,2},{6,0},{1,7},{3,5},{5,3},{7,1},{8,14},{10,12},{12... | collective-permute-start | bytes 589832 | tf_op jit(solution)/shard_map/ppermute | solution.py:20
  47.5 3.0 %collective-permute-start.19 = (bf16[2,64,896]{2,1,0:T(8,128)(2,1)S(1)}, bf16[2,64,896]{2,1,0:T(8,128)(2,1)S(1)}, u32[]{:S(2)}, u32[]{:S(2)}) collective-permute-start(bf16[2,64,896]{2,1,0:T(8,128)(2,1)S(1)} %share.6.refs_4_), channel_id=1, source_target_pairs={{0,24},{8,16},{16,8},{24,0},{1,25},{9,17},{17,9},{25,1},{2,26},{10... | collective-permute-start | bytes 688136 | tf_op jit(solution)/shard_map/ppermute | solution.py:25
  50.5 1.2 %collective-permute-done.8.refs_0_.refs_5_ = bf16[2,64,896]{2,1,0:T(8,128)(2,1)S(1)} collective-permute-done((bf16[2,64,896]{2,1,0:T(8,128)(2,1)S(1)}, bf16[2,64,896]{2,1,0:T(8,128)(2,1)S(1)}, u32[]{:S(2)}, u32[]{:S(2)}) %collective-permute-start.8) | collective-permute-done | bytes 229408 | tf_op jit(solution)/shard_map/ppermute | solution.py:25
  51.7 2.6 %collective-permute-done.14.refs_2_ = bf16[2,64,768]{2,1,0:T(8,128)(2,1)S(1)} collective-permute-done((bf16[2,64,768]{2,1,0:T(8,128)(2,1)S(1)}, bf16[2,64,768]{2,1,0:T(8,128)(2,1)S(1)}, u32[]{:S(2)}, u32[]{:S(2)}) %collective-permute-start.14) | collective-permute-done | bytes 196640 | tf_op jit(solution)/shard_map/ppermute | solution.py:20
  55.3 0.9 %place.1 = (bf16[1,128,3584]{2,1,0:T(8,128)(2,1)}, f32[8,128]{1,0:T(8,128)S(1)}) custom-call(bf16[96,3584]{1,0:T(8,128)(2,1)S(1)} %collective-permute-done.7.refs_5_.in_ref), custom_call_target="tpu_custom_call" | custom-call | bytes 1376256 | tf_op jit(solution)/shard_map/place/pallas_call | solution.py:353
  57.1 3.7 %collective-permute-start.10 = (bf16[16,3584]{1,0:T(8,128)(2,1)S(1)}, bf16[16,3584]{1,0:T(8,128)(2,1)S(1)}, u32[]{:S(2)}, u32[]{:S(2)}) collective-permute-start(bf16[16,3584]{1,0:T(8,128)(2,1)S(1)} %leaving.4), channel_id=1, source_target_pairs={{0,8},{8,16},{16,24},{1,9},{9,17},{17,25},{2,10},{10,18},{18,26},{... | collective-permute-start | bytes 344072 | tf_op jit(solution)/shard_map/ppermute | solution.py:35
  61.3 1.9 %collective-permute-start.11 = (bf16[16,3584]{1,0:T(8,128)(2,1)S(1)}, bf16[16,3584]{1,0:T(8,128)(2,1)S(1)}, u32[]{:S(2)}, u32[]{:S(2)}) collective-permute-start(bf16[16,3584]{1,0:T(8,128)(2,1)S(1)} %leaving.5), channel_id=1, source_target_pairs={{0,8},{8,16},{16,24},{1,9},{9,17},{17,25},{2,10},{10,18},{18,26},{... | collective-permute-start | bytes 344072 | tf_op jit(solution)/shard_map/ppermute | solution.py:35
  64.2 2.7 %collective-permute-done.18.refs_0_ = bf16[2,64,768]{2,1,0:T(8,128)(2,1)S(1)} collective-permute-done((bf16[2,64,768]{2,1,0:T(8,128)(2,1)S(1)}, bf16[2,64,768]{2,1,0:T(8,128)(2,1)S(1)}, u32[]{:S(2)}, u32[]{:S(2)}) %collective-permute-start.18) | collective-permute-done | bytes 196640 | tf_op jit(solution)/shard_map/ppermute | solution.py:25
  67.4 1.3 %collective-permute-start.20 = (f32[8,128]{1,0:T(8,128)S(1)}, f32[8,128]{1,0:T(8,128)S(1)}, u32[]{:S(2)}, u32[]{:S(2)}) collective-permute-start(f32[8,128]{1,0:T(8,128)S(1)} %get-tuple-element.62.refs_0_.refs_4_), channel_id=1, source_target_pairs={{0,2},{2,0},{4,6},{6,4},{1,3},{3,1},{5,7},{7,5},{8,10},{10,8},{12,... | collective-permute-start | bytes 12296 | tf_op jit(solution)/shard_map/ppermute | solution.py:20
  69.3 1.7 %collective-permute-start.22 = (f32[8,128]{1,0:T(8,128)S(1)}, f32[8,128]{1,0:T(8,128)S(1)}, u32[]{:S(2)}, u32[]{:S(2)}) collective-permute-start(f32[8,128]{1,0:T(8,128)S(1)} %get-tuple-element.62.refs_0_.refs_4_), channel_id=1, source_target_pairs={{0,6},{2,4},{4,2},{6,0},{1,7},{3,5},{5,3},{7,1},{8,14},{10,12},{12... | collective-permute-start | bytes 12296 | tf_op jit(solution)/shard_map/ppermute | solution.py:20
  71.1 1.2 %codes.1 = (bf16[2,1,64,3584]{3,2,1,0:T(8,128)(2,1)}, f32[8,128]{1,0:T(8,128)S(1)}) custom-call(f32[8,128]{1,0:T(8,128)S(1)} %get-tuple-element.62.refs_0_.refs_4_, f32[8,128]{1,0:T(8,128)S(1)} %collective-permute-done.20.refs_1_.refs_5_, f32[2,64,1024]{2,1,0:T(8,128)S(1)} %get-tuple-element.63.refs_2_, f32[2,64,896]{2,1,0:T(8,128)S(1)} %get-tuple-element.64.refs_3_, ...), custom_call_target="tpu_custom_call" | custom-call | flops 917504 | bytes 1843200 | tf_op jit(solution)/shard_map/codes/pallas_call | solution.py:56
  72.3 1.5 %collective-permute-done.22.refs_7_ = f32[8,128]{1,0:T(8,128)S(1)} collective-permute-done((f32[8,128]{1,0:T(8,128)S(1)}, f32[8,128]{1,0:T(8,128)S(1)}, u32[]{:S(2)}, u32[]{:S(2)}) %collective-permute-start.22) | collective-permute-done | bytes 4128 | tf_op jit(solution)/shard_map/ppermute | solution.py:20
  73.8 1.3 %finish.1 = (bf16[1,128,3584]{2,1,0:T(8,128)(2,1)}, f32[2,1,2,28]{3,2,1,0:T(2,128)}) custom-call(bf16[16,3584]{1,0:T(8,128)(2,1)S(1)} %collective-permute-done.10.refs_0_, bf16[16,3584]{1,0:T(8,128)(2,1)S(1)} %collective-permute-done.11.refs_1_, bf16[1,128,3584]{2,1,0:T(8,128)(2,1)} %get-tuple-element.52.refs_2_, ...), custom_call_target="tpu_custom_call", output_to_operand_aliasing={{0}: (2, {})} | custom-call | bytes 458752 | tf_op jit(solution)/shard_map/finish/pallas_call | solution.py:401
  (40 shorter events, 9.0 us)
Async XLA Ops:
  4.8 2.0 %collective-permute-start = (f32[1024,128]{1,0:T(8,128)S(1)}, f32[1024,128]{1,0:T(8,128)S(1)}, u32[]{:S(2)}, u32[]{:S(2)}) collective-permute-start(f32[1024,128]{1,0:T(8,128)S(1)} %get-tuple-element.37.rest_0_.refs_0_), channel_id=1, source_target_pairs={{0,1},{1,0},{2,3},{3,2},{4,5},{5,4},{6,7},{7,6},{8,9},{9,8},{10,11... | collective-permute-start | bytes 1572872 | tf_op jit(solution)/shard_map/ppermute | solution.py:20
  7.8 9.2 %collective-permute-start.1 = (bf16[2,64,1024]{2,1,0:T(8,128)(2,1)S(1)}, bf16[2,64,1024]{2,1,0:T(8,128)(2,1)S(1)}, u32[]{:S(2)}, u32[]{:S(2)}) collective-permute-start(bf16[2,64,1024]{2,1,0:T(8,128)(2,1)S(1)} %get-tuple-element.41), channel_id=1, source_target_pairs={{0,2},{2,0},{4,6},{6,4},{1,3},{3,1},{5,7},{7,5},{8,10},{10,8},{12,... | collective-permute-start | bytes 786440 | tf_op jit(solution)/shard_map/ppermute | solution.py:20
  9.3 27.2 %collective-permute-start.7 = (bf16[96,3584]{1,0:T(8,128)(2,1)S(1)}, bf16[96,3584]{1,0:T(8,128)(2,1)S(1)}, u32[]{:S(2)}, u32[]{:S(2)}) collective-permute-start(bf16[96,3584]{1,0:T(8,128)(2,1)S(1)} %leaving.3.refs_4_), channel_id=1, source_target_pairs={{0,8},{8,16},{16,24},{24,0},{1,9},{9,17},{17,25},{25,1},{2,10},{10... | collective-permute-start | bytes 2064392 | tf_op jit(solution)/shard_map/ppermute | solution.py:30
  10.9 14.8 %collective-permute-start.5 = (bf16[2,64,1024]{2,1,0:T(8,128)(2,1)S(1)}, bf16[2,64,1024]{2,1,0:T(8,128)(2,1)S(1)}, u32[]{:S(2)}, u32[]{:S(2)}) collective-permute-start(bf16[2,64,1024]{2,1,0:T(8,128)(2,1)S(1)} %get-tuple-element.47), channel_id=1, source_target_pairs={{0,4},{2,6},{4,0},{6,2},{1,5},{3,7},{5,1},{7,3},{8,12},{10,14},{12... | collective-permute-start | bytes 786440 | tf_op jit(solution)/shard_map/ppermute | solution.py:20
  12.4 14.8 %collective-permute-start.6 = (bf16[2,64,1024]{2,1,0:T(8,128)(2,1)S(1)}, bf16[2,64,1024]{2,1,0:T(8,128)(2,1)S(1)}, u32[]{:S(2)}, u32[]{:S(2)}) collective-permute-start(bf16[2,64,1024]{2,1,0:T(8,128)(2,1)S(1)} %get-tuple-element.48), channel_id=1, source_target_pairs={{0,6},{2,4},{4,2},{6,0},{1,7},{3,5},{5,3},{7,1},{8,14},{10,12},{12... | collective-permute-start | bytes 786440 | tf_op jit(solution)/shard_map/ppermute | solution.py:20
  17.5 11.5 %collective-permute-start.2 = (bf16[2,64,896]{2,1,0:T(8,128)(2,1)S(1)}, bf16[2,64,896]{2,1,0:T(8,128)(2,1)S(1)}, u32[]{:S(2)}, u32[]{:S(2)}) collective-permute-start(bf16[2,64,896]{2,1,0:T(8,128)(2,1)S(1)} %get-tuple-element.43), channel_id=1, source_target_pairs={{0,2},{2,0},{4,6},{6,4},{1,3},{3,1},{5,7},{7,5},{8,10},{10,8},{12,... | collective-permute-start | bytes 688136 | tf_op jit(solution)/shard_map/ppermute | solution.py:20
  19.1 14.1 %collective-permute-start.3 = (bf16[2,64,896]{2,1,0:T(8,128)(2,1)S(1)}, bf16[2,64,896]{2,1,0:T(8,128)(2,1)S(1)}, u32[]{:S(2)}, u32[]{:S(2)}) collective-permute-start(bf16[2,64,896]{2,1,0:T(8,128)(2,1)S(1)} %get-tuple-element.44), channel_id=1, source_target_pairs={{0,4},{2,6},{4,0},{6,2},{1,5},{3,7},{5,1},{7,3},{8,12},{10,14},{12... | collective-permute-start | bytes 688136 | tf_op jit(solution)/shard_map/ppermute | solution.py:20
  25.7 9.4 %collective-permute-start.4 = (bf16[2,64,896]{2,1,0:T(8,128)(2,1)S(1)}, bf16[2,64,896]{2,1,0:T(8,128)(2,1)S(1)}, u32[]{:S(2)}, u32[]{:S(2)}) collective-permute-start(bf16[2,64,896]{2,1,0:T(8,128)(2,1)S(1)} %get-tuple-element.45), channel_id=1, source_target_pairs={{0,6},{2,4},{4,2},{6,0},{1,7},{3,5},{5,3},{7,1},{8,14},{10,12},{12... | collective-permute-start | bytes 688136 | tf_op jit(solution)/shard_map/ppermute | solution.py:20
  27.4 17.0 %collective-permute-start.9 = (bf16[2,64,1024]{2,1,0:T(8,128)(2,1)S(1)}, bf16[2,64,1024]{2,1,0:T(8,128)(2,1)S(1)}, u32[]{:S(2)}, u32[]{:S(2)}) collective-permute-start(bf16[2,64,1024]{2,1,0:T(8,128)(2,1)S(1)} %share.4.refs_4_), channel_id=1, source_target_pairs={{0,24},{8,16},{16,8},{24,0},{1,25},{9,17},{17,9},{25,1},{2,26},{10... | collective-permute-start | bytes 786440 | tf_op jit(solution)/shard_map/ppermute | solution.py:25
  29.6 9.5 %collective-permute-start.12 = (bf16[2,64,896]{2,1,0:T(8,128)(2,1)S(1)}, bf16[2,64,896]{2,1,0:T(8,128)(2,1)S(1)}, u32[]{:S(2)}, u32[]{:S(2)}) collective-permute-start(bf16[2,64,896]{2,1,0:T(8,128)(2,1)S(1)} %get-tuple-element.53), channel_id=1, source_target_pairs={{0,2},{2,0},{4,6},{6,4},{1,3},{3,1},{5,7},{7,5},{8,10},{10,8},{12,... | collective-permute-start | bytes 688136 | tf_op jit(solution)/shard_map/ppermute | solution.py:20
  33.1 12.0 %collective-permute-start.16 = (bf16[2,64,896]{2,1,0:T(8,128)(2,1)S(1)}, bf16[2,64,896]{2,1,0:T(8,128)(2,1)S(1)}, u32[]{:S(2)}, u32[]{:S(2)}) collective-permute-start(bf16[2,64,896]{2,1,0:T(8,128)(2,1)S(1)} %get-tuple-element.59), channel_id=1, source_target_pairs={{0,4},{2,6},{4,0},{6,2},{1,5},{3,7},{5,1},{7,3},{8,12},{10,14},{12... | collective-permute-start | bytes 688136 | tf_op jit(solution)/shard_map/ppermute | solution.py:20
  35.1 12.3 %collective-permute-start.17 = (bf16[2,64,896]{2,1,0:T(8,128)(2,1)S(1)}, bf16[2,64,896]{2,1,0:T(8,128)(2,1)S(1)}, u32[]{:S(2)}, u32[]{:S(2)}) collective-permute-start(bf16[2,64,896]{2,1,0:T(8,128)(2,1)S(1)} %get-tuple-element.60), channel_id=1, source_target_pairs={{0,6},{2,4},{4,2},{6,0},{1,7},{3,5},{5,3},{7,1},{8,14},{10,12},{12... | collective-permute-start | bytes 688136 | tf_op jit(solution)/shard_map/ppermute | solution.py:20
  36.7 18.0 %copy-start = (f32[2,1,64,3584]{3,2,1,0:T(8,128)S(1)}, f32[2,1,64,3584]{3,2,1,0:T(8,128)}, u32[]{:S(2)}) copy-start(f32[2,1,64,3584]{3,2,1,0:T(8,128)} %refs_1_.9) | copy-start | bytes 5505028
  36.7 18.0 %copy-start.1 = (bf16[2,1,64,3584]{3,2,1,0:T(8,128)(2,1)S(1)}, bf16[2,1,64,3584]{3,2,1,0:T(8,128)(2,1)}, u32[]{:S(2)}) copy-start(bf16[2,1,64,3584]{3,2,1,0:T(8,128)(2,1)} %refs_2_.9) | copy-start | bytes 2752516
  36.7 18.0 %copy-start.2 = (bf16[2,1,64,3584]{3,2,1,0:T(8,128)(2,1)S(1)}, bf16[2,1,64,3584]{3,2,1,0:T(8,128)(2,1)}, u32[]{:S(2)}) copy-start(bf16[2,1,64,3584]{3,2,1,0:T(8,128)(2,1)} %refs_3_.9) | copy-start | bytes 2752516
  36.8 14.9 %collective-permute-start.8 = (bf16[2,64,896]{2,1,0:T(8,128)(2,1)S(1)}, bf16[2,64,896]{2,1,0:T(8,128)(2,1)S(1)}, u32[]{:S(2)}, u32[]{:S(2)}) collective-permute-start(bf16[2,64,896]{2,1,0:T(8,128)(2,1)S(1)} %share.5.refs_4_), channel_id=1, source_target_pairs={{0,24},{8,16},{16,8},{24,0},{1,25},{9,17},{17,9},{25,1},{2,26},{10... | collective-permute-start | bytes 688136 | tf_op jit(solution)/shard_map/ppermute | solution.py:25
  39.5 12.2 %collective-permute-start.13 = (bf16[2,64,768]{2,1,0:T(8,128)(2,1)S(1)}, bf16[2,64,768]{2,1,0:T(8,128)(2,1)S(1)}, u32[]{:S(2)}, u32[]{:S(2)}) collective-permute-start(bf16[2,64,768]{2,1,0:T(8,128)(2,1)S(1)} %get-tuple-element.55), channel_id=1, source_target_pairs={{0,2},{2,0},{4,6},{6,4},{1,3},{3,1},{5,7},{7,5},{8,10},{10,8},{12,... | collective-permute-start | bytes 589832 | tf_op jit(solution)/shard_map/ppermute | solution.py:20
  44.4 9.9 %collective-permute-start.14 = (bf16[2,64,768]{2,1,0:T(8,128)(2,1)S(1)}, bf16[2,64,768]{2,1,0:T(8,128)(2,1)S(1)}, u32[]{:S(2)}, u32[]{:S(2)}) collective-permute-start(bf16[2,64,768]{2,1,0:T(8,128)(2,1)S(1)} %get-tuple-element.56), channel_id=1, source_target_pairs={{0,4},{2,6},{4,0},{6,2},{1,5},{3,7},{5,1},{7,3},{8,12},{10,14},{12... | collective-permute-start | bytes 589832 | tf_op jit(solution)/shard_map/ppermute | solution.py:20
  45.1 9.2 %collective-permute-start.15 = (bf16[2,64,768]{2,1,0:T(8,128)(2,1)S(1)}, bf16[2,64,768]{2,1,0:T(8,128)(2,1)S(1)}, u32[]{:S(2)}, u32[]{:S(2)}) collective-permute-start(bf16[2,64,768]{2,1,0:T(8,128)(2,1)S(1)} %get-tuple-element.57), channel_id=1, source_target_pairs={{0,6},{2,4},{4,2},{6,0},{1,7},{3,5},{5,3},{7,1},{8,14},{10,12},{12... | collective-permute-start | bytes 589832 | tf_op jit(solution)/shard_map/ppermute | solution.py:20
  47.5 16.2 %collective-permute-start.19 = (bf16[2,64,896]{2,1,0:T(8,128)(2,1)S(1)}, bf16[2,64,896]{2,1,0:T(8,128)(2,1)S(1)}, u32[]{:S(2)}, u32[]{:S(2)}) collective-permute-start(bf16[2,64,896]{2,1,0:T(8,128)(2,1)S(1)} %share.6.refs_4_), channel_id=1, source_target_pairs={{0,24},{8,16},{16,8},{24,0},{1,25},{9,17},{17,9},{25,1},{2,26},{10... | collective-permute-start | bytes 688136 | tf_op jit(solution)/shard_map/ppermute | solution.py:25
  54.4 12.5 %collective-permute-start.18 = (bf16[2,64,768]{2,1,0:T(8,128)(2,1)S(1)}, bf16[2,64,768]{2,1,0:T(8,128)(2,1)S(1)}, u32[]{:S(2)}, u32[]{:S(2)}) collective-permute-start(bf16[2,64,768]{2,1,0:T(8,128)(2,1)S(1)} %share.7), channel_id=1, source_target_pairs={{0,24},{8,16},{16,8},{24,0},{1,25},{9,17},{17,9},{25,1},{2,26},{10... | collective-permute-start | bytes 589832 | tf_op jit(solution)/shard_map/ppermute | solution.py:25
  57.1 15.2 %collective-permute-start.10 = (bf16[16,3584]{1,0:T(8,128)(2,1)S(1)}, bf16[16,3584]{1,0:T(8,128)(2,1)S(1)}, u32[]{:S(2)}, u32[]{:S(2)}) collective-permute-start(bf16[16,3584]{1,0:T(8,128)(2,1)S(1)} %leaving.4), channel_id=1, source_target_pairs={{0,8},{8,16},{16,24},{1,9},{9,17},{17,25},{2,10},{10,18},{18,26},{... | collective-permute-start | bytes 344072 | tf_op jit(solution)/shard_map/ppermute | solution.py:35
  61.3 11.0 %collective-permute-start.11 = (bf16[16,3584]{1,0:T(8,128)(2,1)S(1)}, bf16[16,3584]{1,0:T(8,128)(2,1)S(1)}, u32[]{:S(2)}, u32[]{:S(2)}) collective-permute-start(bf16[16,3584]{1,0:T(8,128)(2,1)S(1)} %leaving.5), channel_id=1, source_target_pairs={{0,8},{8,16},{16,24},{1,9},{9,17},{17,25},{2,10},{10,18},{18,26},{... | collective-permute-start | bytes 344072 | tf_op jit(solution)/shard_map/ppermute | solution.py:35
  67.4 3.7 %collective-permute-start.20 = (f32[8,128]{1,0:T(8,128)S(1)}, f32[8,128]{1,0:T(8,128)S(1)}, u32[]{:S(2)}, u32[]{:S(2)}) collective-permute-start(f32[8,128]{1,0:T(8,128)S(1)} %get-tuple-element.62.refs_0_.refs_4_), channel_id=1, source_target_pairs={{0,2},{2,0},{4,6},{6,4},{1,3},{3,1},{5,7},{7,5},{8,10},{10,8},{12,... | collective-permute-start | bytes 12296 | tf_op jit(solution)/shard_map/ppermute | solution.py:20
  68.7 3.6 %collective-permute-start.21 = (f32[8,128]{1,0:T(8,128)S(1)}, f32[8,128]{1,0:T(8,128)S(1)}, u32[]{:S(2)}, u32[]{:S(2)}) collective-permute-start(f32[8,128]{1,0:T(8,128)S(1)} %get-tuple-element.62.refs_0_.refs_4_), channel_id=1, source_target_pairs={{0,4},{2,6},{4,0},{6,2},{1,5},{3,7},{5,1},{7,3},{8,12},{10,14},{12... | collective-permute-start | bytes 12296 | tf_op jit(solution)/shard_map/ppermute | solution.py:20
  69.3 4.5 %collective-permute-start.22 = (f32[8,128]{1,0:T(8,128)S(1)}, f32[8,128]{1,0:T(8,128)S(1)}, u32[]{:S(2)}, u32[]{:S(2)}) collective-permute-start(f32[8,128]{1,0:T(8,128)S(1)} %get-tuple-element.62.refs_0_.refs_4_), channel_id=1, source_target_pairs={{0,6},{2,4},{4,2},{6,0},{1,7},{3,5},{5,3},{7,1},{8,14},{10,12},{12... | collective-permute-start | bytes 12296 | tf_op jit(solution)/shard_map/ppermute | solution.py:20

commit v14 on v12

--- a/solution.py
+++ b/solution.py
@@ -237,12 +237,17 @@
             scale_ref[side, 0, pl.ds(mine ^ far, 1), :] = top[side : side + 1, :blocks]
 
 
-def place_kernel(start, in_ref, *rest):
-    out_ref, token_ref, sem = rest[-3:]
-    copy = pltpu.make_async_copy(in_ref, out_ref.at[0, pl.ds(start, in_ref.shape[0])], sem)
-    copy.start()
+def place_kernel(start, count, *refs):
+    out_ref, token_ref, sems = refs[-3:]
+    copies = []
+    for k, ref in enumerate(refs[:count]):
+        rows = pl.ds(start + k * ref.shape[0], ref.shape[0])
+        copies.append(pltpu.make_async_copy(ref, out_ref.at[0, rows], sems.at[k]))
+    for copy in copies:
+        copy.start()
     token_ref[...] = jnp.zeros_like(token_ref)
-    copy.wait()
+    for copy in copies:
+        copy.wait()
 
 
 def shards(enter_fwd, enter_rev, cot_rev, gain, proj_down, proj_up, master, moment, second):
@@ -320,7 +325,7 @@
             flops=4 * tokens * latent * (stop - start),
         )
 
-    head = 112
+    head = 96
     first_rows = leaving(0, head)
     left_head = turned(first_rows, "pipe")
     first = grads(0, first_rows)
@@ -342,20 +347,23 @@
         )
         arrived.append(mirrored(shares[-1], "pipe"))
 
-    def place(start, rows, kept=(), after=()):
+    def place(start, some, kept=(), after=()):
+        count = len(some)
         return pl.pallas_call(
-            lambda *refs: place_kernel(start, *refs),
-            in_specs=[ANY] * (1 + len(kept) + len(after)),
+            lambda *refs: place_kernel(start, count, *refs),
+            in_specs=[ANY] * (count + len(kept) + len(after)),
             out_specs=[ANY, VMEM],
             out_shape=[shape((1, tokens, width), BF16), shape((8, LANES), F32)],
-            scratch_shapes=[pltpu.SemaphoreType.DMA],
-            input_output_aliases={1 + k: k for k in range(len(kept))},
+            scratch_shapes=[pltpu.SemaphoreType.DMA((count,))],
+            input_output_aliases={count + k: k for k in range(len(kept))},
             compiler_params=ROOM,
-            cost_estimate=pl.CostEstimate(flops=0, bytes_accessed=4 * rows.shape[0] * width, transcendentals=0),
+            cost_estimate=pl.CostEstimate(
+                flops=0, bytes_accessed=4 * count * some[0].shape[0] * width, transcendentals=0
+            ),
             name="place",
-        )(rows, *kept, *after)
-
-    placed, token = place(0, left_head)
+        )(*some, *kept, *after)
+
+    placed, token = place(0, [left_head])
 
     fresh, peaks, steps = [], None, []
     for chunk, (start, stop) in enumerate(chunks):
@@ -378,7 +386,9 @@
         fresh.append(some)
         steps.append(peaks)
 
-    left_tail = shifted(leaving(head, tokens - head, steps[-3]), "pipe")
+    half = (tokens - head) // 2
+    tail_rows = leaving(head, half, steps[-3])
+    left_tails = [shifted(tail_rows, "pipe"), shifted(leaving(head + half, half, steps[-3]), "pipe")]
 
     group = LANES // depth
     peak_rows = [peaks] + [exchange(peaks, "expert", k) for k in range(1, experts)]
@@ -391,6 +401,7 @@
         read=group + len(fresh),
         flops=4 * depth * width,
     )
+    placed, token = place(head, left_tails, (placed,), (token,))
     scales = call(
         lambda *refs: scale_kernel(group, experts, *refs),
         "scales",
@@ -399,8 +410,7 @@
         token,
         read=experts,
     )
-    left, _ = place(head, left_tail, (placed,), (token,))
-    return (left, coded, scales)
+    return (placed, coded, scales)
 
 
 def solution(mesh):

time: 76.3 us -> 75.5 us (0.990); the launches traced: 76.1 us -> 74.4 us
  waiting for transfers between devices: 30.3 us -> 25.6 us
  starting transfers between devices: 29.9 us -> 33.1 us
    ppermute x16, waiting for transfers between devices: 22.1 us -> 16.4 us  [exchange(): return lax.ppermute(block, axis, [(i, i ^ offset) for i in range(count)])]
    ppermute x1 -> x2, starting transfers between devices: 3.61 us -> 5.66 us  [shifted(): return lax.ppermute(block, axis, [(i, i + 1) for i in range(count - 1)])]
    ppermute x4, starting transfers between devices: 5.17 us -> 6.5 us  [mirrored(): return lax.ppermute(block, axis, [(i, count - 1 - i) for i in range(count)])]
    ppermute x4, waiting for transfers between devices: 8.21 us -> 9.18 us  [mirrored(): return lax.ppermute(block, axis, [(i, count - 1 - i) for i in range(count)])]
    pallas_call x16 -> x17, Pallas kernels: 7.27 us -> 7.65 us  [call(): pl.pallas_call(kernel, in_specs=[VMEM] * read + [ANY] * (len(operands) -...]
  transfers between devices with their start and end apart: 22 -> 23, of which waited for: 13 -> 13; matrix products, arithmetic and copies ran while one was open for 0% -> 0% of each run, Pallas kernels for 13% -> 12%
where the time goes in v14:
time: 75.5 us; the launch traced here: 74.4 us
  starting transfers between devices  33.1 us (44%)
  waiting for transfers between devices  25.6 us (34%)
  Pallas kernels  14.8 us (20%)
  between operations  0.81 us (1%)
    ppermute x16, starting transfers between devices, exchange(): return lax.ppermute(block, axis, [(i, i ^ offset) for i in range(count)])  19.4 us
    ppermute x16, waiting for transfers between devices, exchange(): return lax.ppermute(block, axis, [(i, i ^ offset) for i in range(count)])  16.4 us
    ppermute x4, waiting for transfers between devices, mirrored(): return lax.ppermute(block, axis, [(i, count - 1 - i) for i in range(count)])  9.18 us
    pallas_call x17, Pallas kernels, call(): pl.pallas_call(kernel, in_specs=[VMEM] * read + [ANY] * (len(operands) -...  7.65 us
    ppermute x4, starting transfers between devices, mirrored(): return lax.ppermute(block, axis, [(i, count - 1 - i) for i in range(count)])  6.5 us
    ppermute x2, starting transfers between devices, shifted(): return lax.ppermute(block, axis, [(i, i + 1) for i in range(count - 1)])  5.66 us
    pallas_call x1, Pallas kernels, shards(): pl.pallas_call(lambda *refs: latent_kernel(tiles, *refs), in_specs=[ANY]...  4.12 us
    ppermute x1, starting transfers between devices, turned(): lax.ppermute(block, axis, [(i, (i + 1) % count) for i in range(count)])  1.58 us
  transfers between devices with their start and end apart: 23, of which 13 were waited for; matrix products, arithmetic and copies ran while one was open for 0% of the time, Pallas kernels for 12%

profile of v14, /device:TPU:8, one launch (start us, length us, event | category | flops | bytes accessed | tf_op | source)
XLA Modules:
  0.0 74.4 jit_solution(4309732298527790092)
XLA Ops:
  0.6 4.1 %latents.1 = (f32[1024,128]{1,0:T(8,128)S(1)}, bf16[128,3584]{1,0:T(8,128)(2,1)S(1)}, bf16[128,3584]{1,0:T(8,128)(2,1)S(1)}, bf16[128,3584]{1,0:T(8,128)(2,1)S(1)}) custom-call(bf16[1,128,3584]{2,1,0:T(8,128)(2,1)} %refs_0_.1, bf16[1,128,3584]{2,1,0:T(8,128)(2,1)} %refs_1_.5, bf16[1,128,3584]{2,1,0:T(8,128)(2,1)} %refs_2_.5, ...), custom_call_target="tpu_custom_call" | custom-call | flops 704643072 | bytes 8257536 | tf_op jit(solution)/shard_map/latents/pallas_call | solution.py:269
  4.8 1.5 %fetch.1.refs_3_ = bf16[256,3584]{1,0:T(8,128)(2,1)S(1)} custom-call(bf16[2,1,256,3584]{3,2,1,0:T(8,128)(2,1)} %in_ref.1, f32[1024,128]{1,0:T(8,128)S(1)} %get-tuple-element.37.rest_0_.refs_0_), custom_call_target="tpu_custom_call" | custom-call | bytes 1835008 | tf_op jit(solution)/shard_map/fetch/pallas_call | solution.py:288
  7.8 1.6 %collective-permute-start.1 = (bf16[2,64,1024]{2,1,0:T(8,128)(2,1)S(1)}, bf16[2,64,1024]{2,1,0:T(8,128)(2,1)S(1)}, u32[]{:S(2)}, u32[]{:S(2)}) collective-permute-start(bf16[2,64,1024]{2,1,0:T(8,128)(2,1)S(1)} %get-tuple-element.41), channel_id=1, source_target_pairs={{0,2},{2,0},{4,6},{6,4},{1,3},{3,1},{5,7},{7,5},{8,10},{10,8},{12,... | collective-permute-start | bytes 786440 | tf_op jit(solution)/shard_map/ppermute | solution.py:20
  9.3 1.6 %collective-permute-start.5 = (bf16[96,3584]{1,0:T(8,128)(2,1)S(1)}, bf16[96,3584]{1,0:T(8,128)(2,1)S(1)}, u32[]{:S(2)}, u32[]{:S(2)}) collective-permute-start(bf16[96,3584]{1,0:T(8,128)(2,1)S(1)} %leaving.3.refs_4_), channel_id=1, source_target_pairs={{0,8},{8,16},{16,24},{24,0},{1,9},{9,17},{17,25},{25,1},{2,10},{10... | collective-permute-start | bytes 2064392 | tf_op jit(solution)/shard_map/ppermute | solution.py:30
  10.9 1.5 %collective-permute-start.7 = (bf16[2,64,1024]{2,1,0:T(8,128)(2,1)S(1)}, bf16[2,64,1024]{2,1,0:T(8,128)(2,1)S(1)}, u32[]{:S(2)}, u32[]{:S(2)}) collective-permute-start(bf16[2,64,1024]{2,1,0:T(8,128)(2,1)S(1)} %get-tuple-element.47), channel_id=1, source_target_pairs={{0,4},{2,6},{4,0},{6,2},{1,5},{3,7},{5,1},{7,3},{8,12},{10,14},{12... | collective-permute-start | bytes 786440 | tf_op jit(solution)/shard_map/ppermute | solution.py:20
  12.9 4.1 %collective-permute-done.1.refs_4_.refs_1_ = bf16[2,64,1024]{2,1,0:T(8,128)(2,1)S(1)} collective-permute-done((bf16[2,64,1024]{2,1,0:T(8,128)(2,1)S(1)}, bf16[2,64,1024]{2,1,0:T(8,128)(2,1)S(1)}, u32[]{:S(2)}, u32[]{:S(2)}) %collective-permute-start.1) | collective-permute-done | bytes 262176 | tf_op jit(solution)/shard_map/ppermute | solution.py:20
  17.5 1.6 %collective-permute-start.2 = (bf16[2,64,896]{2,1,0:T(8,128)(2,1)S(1)}, bf16[2,64,896]{2,1,0:T(8,128)(2,1)S(1)}, u32[]{:S(2)}, u32[]{:S(2)}) collective-permute-start(bf16[2,64,896]{2,1,0:T(8,128)(2,1)S(1)} %get-tuple-element.43), channel_id=1, source_target_pairs={{0,2},{2,0},{4,6},{6,4},{1,3},{3,1},{5,7},{7,5},{8,10},{10,8},{12,... | collective-permute-start | bytes 688136 | tf_op jit(solution)/shard_map/ppermute | solution.py:20
  19.1 1.5 %collective-permute-start.3 = (bf16[2,64,896]{2,1,0:T(8,128)(2,1)S(1)}, bf16[2,64,896]{2,1,0:T(8,128)(2,1)S(1)}, u32[]{:S(2)}, u32[]{:S(2)}) collective-permute-start(bf16[2,64,896]{2,1,0:T(8,128)(2,1)S(1)} %get-tuple-element.44), channel_id=1, source_target_pairs={{0,4},{2,6},{4,0},{6,2},{1,5},{3,7},{5,1},{7,3},{8,12},{10,14},{12... | collective-permute-start | bytes 688136 | tf_op jit(solution)/shard_map/ppermute | solution.py:20
  20.6 5.1 %collective-permute-done.7.refs_2_ = bf16[2,64,1024]{2,1,0:T(8,128)(2,1)S(1)} collective-permute-done((bf16[2,64,1024]{2,1,0:T(8,128)(2,1)S(1)}, bf16[2,64,1024]{2,1,0:T(8,128)(2,1)S(1)}, u32[]{:S(2)}, u32[]{:S(2)}) %collective-permute-start.7) | collective-permute-done | bytes 262176 | tf_op jit(solution)/shard_map/ppermute | solution.py:20
  25.7 1.6 %collective-permute-start.4 = (bf16[2,64,896]{2,1,0:T(8,128)(2,1)S(1)}, bf16[2,64,896]{2,1,0:T(8,128)(2,1)S(1)}, u32[]{:S(2)}, u32[]{:S(2)}) collective-permute-start(bf16[2,64,896]{2,1,0:T(8,128)(2,1)S(1)} %get-tuple-element.45), channel_id=1, source_target_pairs={{0,6},{2,4},{4,2},{6,0},{1,7},{3,5},{5,3},{7,1},{8,14},{10,12},{12... | collective-permute-start | bytes 688136 | tf_op jit(solution)/shard_map/ppermute | solution.py:20
  27.4 1.6 %collective-permute-start.9 = (bf16[2,64,1024]{2,1,0:T(8,128)(2,1)S(1)}, bf16[2,64,1024]{2,1,0:T(8,128)(2,1)S(1)}, u32[]{:S(2)}, u32[]{:S(2)}) collective-permute-start(bf16[2,64,1024]{2,1,0:T(8,128)(2,1)S(1)} %share.5.refs_4_), channel_id=1, source_target_pairs={{0,24},{8,16},{16,8},{24,0},{1,25},{9,17},{17,9},{25,1},{2,26},{10... | collective-permute-start | bytes 786440 | tf_op jit(solution)/shard_map/ppermute | solution.py:25
  29.6 1.6 %collective-permute-start.12 = (bf16[2,64,896]{2,1,0:T(8,128)(2,1)S(1)}, bf16[2,64,896]{2,1,0:T(8,128)(2,1)S(1)}, u32[]{:S(2)}, u32[]{:S(2)}) collective-permute-start(bf16[2,64,896]{2,1,0:T(8,128)(2,1)S(1)} %get-tuple-element.53), channel_id=1, source_target_pairs={{0,2},{2,0},{4,6},{6,4},{1,3},{3,1},{5,7},{7,5},{8,10},{10,8},{12,... | collective-permute-start | bytes 688136 | tf_op jit(solution)/shard_map/ppermute | solution.py:20
  31.1 2.0 %collective-permute-done.3.refs_2_ = bf16[2,64,896]{2,1,0:T(8,128)(2,1)S(1)} collective-permute-done((bf16[2,64,896]{2,1,0:T(8,128)(2,1)S(1)}, bf16[2,64,896]{2,1,0:T(8,128)(2,1)S(1)}, u32[]{:S(2)}, u32[]{:S(2)}) %collective-permute-start.3) | collective-permute-done | bytes 229408 | tf_op jit(solution)/shard_map/ppermute | solution.py:20
  33.1 1.4 %collective-permute-start.17 = (bf16[2,64,896]{2,1,0:T(8,128)(2,1)S(1)}, bf16[2,64,896]{2,1,0:T(8,128)(2,1)S(1)}, u32[]{:S(2)}, u32[]{:S(2)}) collective-permute-start(bf16[2,64,896]{2,1,0:T(8,128)(2,1)S(1)} %get-tuple-element.59), channel_id=1, source_target_pairs={{0,4},{2,6},{4,0},{6,2},{1,5},{3,7},{5,1},{7,3},{8,12},{10,14},{12... | collective-permute-start | bytes 688136 | tf_op jit(solution)/shard_map/ppermute | solution.py:20
  35.1 1.5 %collective-permute-start.18 = (bf16[2,64,896]{2,1,0:T(8,128)(2,1)S(1)}, bf16[2,64,896]{2,1,0:T(8,128)(2,1)S(1)}, u32[]{:S(2)}, u32[]{:S(2)}) collective-permute-start(bf16[2,64,896]{2,1,0:T(8,128)(2,1)S(1)} %get-tuple-element.60), channel_id=1, source_target_pairs={{0,6},{2,4},{4,2},{6,0},{1,7},{3,5},{5,3},{7,1},{8,14},{10,12},{12... | collective-permute-start | bytes 688136 | tf_op jit(solution)/shard_map/ppermute | solution.py:20
  36.7 1.6 %collective-permute-start.6 = (bf16[2,64,896]{2,1,0:T(8,128)(2,1)S(1)}, bf16[2,64,896]{2,1,0:T(8,128)(2,1)S(1)}, u32[]{:S(2)}, u32[]{:S(2)}) collective-permute-start(bf16[2,64,896]{2,1,0:T(8,128)(2,1)S(1)} %share.4.refs_4_), channel_id=1, source_target_pairs={{0,24},{8,16},{16,8},{24,0},{1,25},{9,17},{17,9},{25,1},{2,26},{10... | collective-permute-start | bytes 688136 | tf_op jit(solution)/shard_map/ppermute | solution.py:25
  38.4 0.7 collective-permute-done.12.refs_5_.refs_1_
  39.7 4.8 %collective-permute-done.9.refs_0_.refs_4_ = bf16[2,64,1024]{2,1,0:T(8,128)(2,1)S(1)} collective-permute-done((bf16[2,64,1024]{2,1,0:T(8,128)(2,1)S(1)}, bf16[2,64,1024]{2,1,0:T(8,128)(2,1)S(1)}, u32[]{:S(2)}, u32[]{:S(2)}) %collective-permute-start.9) | collective-permute-done | bytes 262176 | tf_op jit(solution)/shard_map/ppermute | solution.py:25
  44.4 0.7 collective-permute-start.14
  45.1 2.2 %collective-permute-start.15 = (bf16[2,64,768]{2,1,0:T(8,128)(2,1)S(1)}, bf16[2,64,768]{2,1,0:T(8,128)(2,1)S(1)}, u32[]{:S(2)}, u32[]{:S(2)}) collective-permute-start(bf16[2,64,768]{2,1,0:T(8,128)(2,1)S(1)} %get-tuple-element.57), channel_id=1, source_target_pairs={{0,6},{2,4},{4,2},{6,0},{1,7},{3,5},{5,3},{7,1},{8,14},{10,12},{12... | collective-permute-start | bytes 589832 | tf_op jit(solution)/shard_map/ppermute | solution.py:20
  47.5 3.0 %collective-permute-start.19 = (bf16[2,64,896]{2,1,0:T(8,128)(2,1)S(1)}, bf16[2,64,896]{2,1,0:T(8,128)(2,1)S(1)}, u32[]{:S(2)}, u32[]{:S(2)}) collective-permute-start(bf16[2,64,896]{2,1,0:T(8,128)(2,1)S(1)} %share.7), channel_id=1, source_target_pairs={{0,24},{8,16},{16,8},{24,0},{1,25},{9,17},{17,9},{25,1},{2,26},{10... | collective-permute-start | bytes 688136 | tf_op jit(solution)/shard_map/ppermute | solution.py:25
  50.5 1.2 %collective-permute-done.6.refs_0_.refs_4_ = bf16[2,64,896]{2,1,0:T(8,128)(2,1)S(1)} collective-permute-done((bf16[2,64,896]{2,1,0:T(8,128)(2,1)S(1)}, bf16[2,64,896]{2,1,0:T(8,128)(2,1)S(1)}, u32[]{:S(2)}, u32[]{:S(2)}) %collective-permute-start.6) | collective-permute-done | bytes 229408 | tf_op jit(solution)/shard_map/ppermute | solution.py:25
  51.7 2.6 %collective-permute-done.14.refs_2_ = bf16[2,64,768]{2,1,0:T(8,128)(2,1)S(1)} collective-permute-done((bf16[2,64,768]{2,1,0:T(8,128)(2,1)S(1)}, bf16[2,64,768]{2,1,0:T(8,128)(2,1)S(1)}, u32[]{:S(2)}, u32[]{:S(2)}) %collective-permute-start.14) | collective-permute-done | bytes 196640 | tf_op jit(solution)/shard_map/ppermute | solution.py:20
  55.3 0.9 %place.2 = (bf16[1,128,3584]{2,1,0:T(8,128)(2,1)}, f32[8,128]{1,0:T(8,128)S(1)}) custom-call(bf16[96,3584]{1,0:T(8,128)(2,1)S(1)} %collective-permute-done.5.refs_4_.refs_0_), custom_call_target="tpu_custom_call" | custom-call | bytes 1376256 | tf_op jit(solution)/shard_map/place/pallas_call | solution.py:352
  57.1 3.7 %collective-permute-start.10 = (bf16[16,3584]{1,0:T(8,128)(2,1)S(1)}, bf16[16,3584]{1,0:T(8,128)(2,1)S(1)}, u32[]{:S(2)}, u32[]{:S(2)}) collective-permute-start(bf16[16,3584]{1,0:T(8,128)(2,1)S(1)} %leaving.4), channel_id=1, source_target_pairs={{0,8},{8,16},{16,24},{1,9},{9,17},{17,25},{2,10},{10,18},{18,26},{... | collective-permute-start | bytes 344072 | tf_op jit(solution)/shard_map/ppermute | solution.py:35
  61.3 1.9 %collective-permute-start.11 = (bf16[16,3584]{1,0:T(8,128)(2,1)S(1)}, bf16[16,3584]{1,0:T(8,128)(2,1)S(1)}, u32[]{:S(2)}, u32[]{:S(2)}) collective-permute-start(bf16[16,3584]{1,0:T(8,128)(2,1)S(1)} %leaving.5), channel_id=1, source_target_pairs={{0,8},{8,16},{16,24},{1,9},{9,17},{17,25},{2,10},{10,18},{18,26},{... | collective-permute-start | bytes 344072 | tf_op jit(solution)/shard_map/ppermute | solution.py:35
  64.2 2.7 %collective-permute-done.16.refs_0_ = bf16[2,64,768]{2,1,0:T(8,128)(2,1)S(1)} collective-permute-done((bf16[2,64,768]{2,1,0:T(8,128)(2,1)S(1)}, bf16[2,64,768]{2,1,0:T(8,128)(2,1)S(1)}, u32[]{:S(2)}, u32[]{:S(2)}) %collective-permute-start.16) | collective-permute-done | bytes 196640 | tf_op jit(solution)/shard_map/ppermute | solution.py:25
  67.4 1.3 %collective-permute-start.20 = (f32[8,128]{1,0:T(8,128)S(1)}, f32[8,128]{1,0:T(8,128)S(1)}, u32[]{:S(2)}, u32[]{:S(2)}) collective-permute-start(f32[8,128]{1,0:T(8,128)S(1)} %get-tuple-element.62.refs_0_), channel_id=1, source_target_pairs={{0,2},{2,0},{4,6},{6,4},{1,3},{3,1},{5,7},{7,5},{8,10},{10,8},{12,... | collective-permute-start | bytes 12296 | tf_op jit(solution)/shard_map/ppermute | solution.py:20
  69.3 1.7 %collective-permute-start.22 = (f32[8,128]{1,0:T(8,128)S(1)}, f32[8,128]{1,0:T(8,128)S(1)}, u32[]{:S(2)}, u32[]{:S(2)}) collective-permute-start(f32[8,128]{1,0:T(8,128)S(1)} %get-tuple-element.62.refs_0_), channel_id=1, source_target_pairs={{0,6},{2,4},{4,2},{6,0},{1,7},{3,5},{5,3},{7,1},{8,14},{10,12},{12... | collective-permute-start | bytes 12296 | tf_op jit(solution)/shard_map/ppermute | solution.py:20
  71.1 1.2 %codes.1 = (bf16[2,1,64,3584]{3,2,1,0:T(8,128)(2,1)}, f32[8,128]{1,0:T(8,128)S(1)}) custom-call(f32[8,128]{1,0:T(8,128)S(1)} %get-tuple-element.62.refs_0_, f32[8,128]{1,0:T(8,128)S(1)} %collective-permute-done.20.refs_1_, f32[2,64,1024]{2,1,0:T(8,128)S(1)} %get-tuple-element.63.refs_2_, f32[2,64,896]{2,1,0:T(8,128)S(1)} %get-tuple-element.64.refs_3_, ...), custom_call_target="tpu_custom_call" | custom-call | flops 917504 | bytes 1843200 | tf_op jit(solution)/shard_map/codes/pallas_call | solution.py:56
  72.3 0.7 place.3
  73.0 0.8 %collective-permute-done.22.refs_3_ = f32[8,128]{1,0:T(8,128)S(1)} collective-permute-done((f32[8,128]{1,0:T(8,128)S(1)}, f32[8,128]{1,0:T(8,128)S(1)}, u32[]{:S(2)}, u32[]{:S(2)}) %collective-permute-start.22) | collective-permute-done | bytes 4128 | tf_op jit(solution)/shard_map/ppermute | solution.py:20
  (41 shorter events, 9.5 us)
Async XLA Ops:
  4.8 2.0 %collective-permute-start = (f32[1024,128]{1,0:T(8,128)S(1)}, f32[1024,128]{1,0:T(8,128)S(1)}, u32[]{:S(2)}, u32[]{:S(2)}) collective-permute-start(f32[1024,128]{1,0:T(8,128)S(1)} %get-tuple-element.37.rest_0_.refs_0_), channel_id=1, source_target_pairs={{0,1},{1,0},{2,3},{3,2},{4,5},{5,4},{6,7},{7,6},{8,9},{9,8},{10,11... | collective-permute-start | bytes 1572872 | tf_op jit(solution)/shard_map/ppermute | solution.py:20
  7.8 9.2 %collective-permute-start.1 = (bf16[2,64,1024]{2,1,0:T(8,128)(2,1)S(1)}, bf16[2,64,1024]{2,1,0:T(8,128)(2,1)S(1)}, u32[]{:S(2)}, u32[]{:S(2)}) collective-permute-start(bf16[2,64,1024]{2,1,0:T(8,128)(2,1)S(1)} %get-tuple-element.41), channel_id=1, source_target_pairs={{0,2},{2,0},{4,6},{6,4},{1,3},{3,1},{5,7},{7,5},{8,10},{10,8},{12,... | collective-permute-start | bytes 786440 | tf_op jit(solution)/shard_map/ppermute | solution.py:20
  9.3 27.2 %collective-permute-start.5 = (bf16[96,3584]{1,0:T(8,128)(2,1)S(1)}, bf16[96,3584]{1,0:T(8,128)(2,1)S(1)}, u32[]{:S(2)}, u32[]{:S(2)}) collective-permute-start(bf16[96,3584]{1,0:T(8,128)(2,1)S(1)} %leaving.3.refs_4_), channel_id=1, source_target_pairs={{0,8},{8,16},{16,24},{24,0},{1,9},{9,17},{17,25},{25,1},{2,10},{10... | collective-permute-start | bytes 2064392 | tf_op jit(solution)/shard_map/ppermute | solution.py:30
  10.9 14.8 %collective-permute-start.7 = (bf16[2,64,1024]{2,1,0:T(8,128)(2,1)S(1)}, bf16[2,64,1024]{2,1,0:T(8,128)(2,1)S(1)}, u32[]{:S(2)}, u32[]{:S(2)}) collective-permute-start(bf16[2,64,1024]{2,1,0:T(8,128)(2,1)S(1)} %get-tuple-element.47), channel_id=1, source_target_pairs={{0,4},{2,6},{4,0},{6,2},{1,5},{3,7},{5,1},{7,3},{8,12},{10,14},{12... | collective-permute-start | bytes 786440 | tf_op jit(solution)/shard_map/ppermute | solution.py:20
  12.4 14.8 %collective-permute-start.8 = (bf16[2,64,1024]{2,1,0:T(8,128)(2,1)S(1)}, bf16[2,64,1024]{2,1,0:T(8,128)(2,1)S(1)}, u32[]{:S(2)}, u32[]{:S(2)}) collective-permute-start(bf16[2,64,1024]{2,1,0:T(8,128)(2,1)S(1)} %get-tuple-element.48), channel_id=1, source_target_pairs={{0,6},{2,4},{4,2},{6,0},{1,7},{3,5},{5,3},{7,1},{8,14},{10,12},{12... | collective-permute-start | bytes 786440 | tf_op jit(solution)/shard_map/ppermute | solution.py:20
  17.5 11.5 %collective-permute-start.2 = (bf16[2,64,896]{2,1,0:T(8,128)(2,1)S(1)}, bf16[2,64,896]{2,1,0:T(8,128)(2,1)S(1)}, u32[]{:S(2)}, u32[]{:S(2)}) collective-permute-start(bf16[2,64,896]{2,1,0:T(8,128)(2,1)S(1)} %get-tuple-element.43), channel_id=1, source_target_pairs={{0,2},{2,0},{4,6},{6,4},{1,3},{3,1},{5,7},{7,5},{8,10},{10,8},{12,... | collective-permute-start | bytes 688136 | tf_op jit(solution)/shard_map/ppermute | solution.py:20
  19.1 14.1 %collective-permute-start.3 = (bf16[2,64,896]{2,1,0:T(8,128)(2,1)S(1)}, bf16[2,64,896]{2,1,0:T(8,128)(2,1)S(1)}, u32[]{:S(2)}, u32[]{:S(2)}) collective-permute-start(bf16[2,64,896]{2,1,0:T(8,128)(2,1)S(1)} %get-tuple-element.44), channel_id=1, source_target_pairs={{0,4},{2,6},{4,0},{6,2},{1,5},{3,7},{5,1},{7,3},{8,12},{10,14},{12... | collective-permute-start | bytes 688136 | tf_op jit(solution)/shard_map/ppermute | solution.py:20
  25.7 9.4 %collective-permute-start.4 = (bf16[2,64,896]{2,1,0:T(8,128)(2,1)S(1)}, bf16[2,64,896]{2,1,0:T(8,128)(2,1)S(1)}, u32[]{:S(2)}, u32[]{:S(2)}) collective-permute-start(bf16[2,64,896]{2,1,0:T(8,128)(2,1)S(1)} %get-tuple-element.45), channel_id=1, source_target_pairs={{0,6},{2,4},{4,2},{6,0},{1,7},{3,5},{5,3},{7,1},{8,14},{10,12},{12... | collective-permute-start | bytes 688136 | tf_op jit(solution)/shard_map/ppermute | solution.py:20
  27.4 17.0 %collective-permute-start.9 = (bf16[2,64,1024]{2,1,0:T(8,128)(2,1)S(1)}, bf16[2,64,1024]{2,1,0:T(8,128)(2,1)S(1)}, u32[]{:S(2)}, u32[]{:S(2)}) collective-permute-start(bf16[2,64,1024]{2,1,0:T(8,128)(2,1)S(1)} %share.5.refs_4_), channel_id=1, source_target_pairs={{0,24},{8,16},{16,8},{24,0},{1,25},{9,17},{17,9},{25,1},{2,26},{10... | collective-permute-start | bytes 786440 | tf_op jit(solution)/shard_map/ppermute | solution.py:25
  29.6 9.5 %collective-permute-start.12 = (bf16[2,64,896]{2,1,0:T(8,128)(2,1)S(1)}, bf16[2,64,896]{2,1,0:T(8,128)(2,1)S(1)}, u32[]{:S(2)}, u32[]{:S(2)}) collective-permute-start(bf16[2,64,896]{2,1,0:T(8,128)(2,1)S(1)} %get-tuple-element.53), channel_id=1, source_target_pairs={{0,2},{2,0},{4,6},{6,4},{1,3},{3,1},{5,7},{7,5},{8,10},{10,8},{12,... | collective-permute-start | bytes 688136 | tf_op jit(solution)/shard_map/ppermute | solution.py:20
  33.1 12.0 %collective-permute-start.17 = (bf16[2,64,896]{2,1,0:T(8,128)(2,1)S(1)}, bf16[2,64,896]{2,1,0:T(8,128)(2,1)S(1)}, u32[]{:S(2)}, u32[]{:S(2)}) collective-permute-start(bf16[2,64,896]{2,1,0:T(8,128)(2,1)S(1)} %get-tuple-element.59), channel_id=1, source_target_pairs={{0,4},{2,6},{4,0},{6,2},{1,5},{3,7},{5,1},{7,3},{8,12},{10,14},{12... | collective-permute-start | bytes 688136 | tf_op jit(solution)/shard_map/ppermute | solution.py:20
  35.1 12.3 %collective-permute-start.18 = (bf16[2,64,896]{2,1,0:T(8,128)(2,1)S(1)}, bf16[2,64,896]{2,1,0:T(8,128)(2,1)S(1)}, u32[]{:S(2)}, u32[]{:S(2)}) collective-permute-start(bf16[2,64,896]{2,1,0:T(8,128)(2,1)S(1)} %get-tuple-element.60), channel_id=1, source_target_pairs={{0,6},{2,4},{4,2},{6,0},{1,7},{3,5},{5,3},{7,1},{8,14},{10,12},{12... | collective-permute-start | bytes 688136 | tf_op jit(solution)/shard_map/ppermute | solution.py:20
  36.6 18.1 %copy-start = (f32[2,1,64,3584]{3,2,1,0:T(8,128)S(1)}, f32[2,1,64,3584]{3,2,1,0:T(8,128)}, u32[]{:S(2)}) copy-start(f32[2,1,64,3584]{3,2,1,0:T(8,128)} %refs_1_.9) | copy-start | bytes 5505028
  36.6 18.1 %copy-start.1 = (bf16[2,1,64,3584]{3,2,1,0:T(8,128)(2,1)S(1)}, bf16[2,1,64,3584]{3,2,1,0:T(8,128)(2,1)}, u32[]{:S(2)}) copy-start(bf16[2,1,64,3584]{3,2,1,0:T(8,128)(2,1)} %refs_2_.9) | copy-start | bytes 2752516
  36.6 18.1 %copy-start.2 = (bf16[2,1,64,3584]{3,2,1,0:T(8,128)(2,1)S(1)}, bf16[2,1,64,3584]{3,2,1,0:T(8,128)(2,1)}, u32[]{:S(2)}) copy-start(bf16[2,1,64,3584]{3,2,1,0:T(8,128)(2,1)} %refs_3_.9) | copy-start | bytes 2752516
  36.7 15.0 %collective-permute-start.6 = (bf16[2,64,896]{2,1,0:T(8,128)(2,1)S(1)}, bf16[2,64,896]{2,1,0:T(8,128)(2,1)S(1)}, u32[]{:S(2)}, u32[]{:S(2)}) collective-permute-start(bf16[2,64,896]{2,1,0:T(8,128)(2,1)S(1)} %share.4.refs_4_), channel_id=1, source_target_pairs={{0,24},{8,16},{16,8},{24,0},{1,25},{9,17},{17,9},{25,1},{2,26},{10... | collective-permute-start | bytes 688136 | tf_op jit(solution)/shard_map/ppermute | solution.py:25
  39.5 12.2 %collective-permute-start.13 = (bf16[2,64,768]{2,1,0:T(8,128)(2,1)S(1)}, bf16[2,64,768]{2,1,0:T(8,128)(2,1)S(1)}, u32[]{:S(2)}, u32[]{:S(2)}) collective-permute-start(bf16[2,64,768]{2,1,0:T(8,128)(2,1)S(1)} %get-tuple-element.55), channel_id=1, source_target_pairs={{0,2},{2,0},{4,6},{6,4},{1,3},{3,1},{5,7},{7,5},{8,10},{10,8},{12,... | collective-permute-start | bytes 589832 | tf_op jit(solution)/shard_map/ppermute | solution.py:20
  44.4 9.9 %collective-permute-start.14 = (bf16[2,64,768]{2,1,0:T(8,128)(2,1)S(1)}, bf16[2,64,768]{2,1,0:T(8,128)(2,1)S(1)}, u32[]{:S(2)}, u32[]{:S(2)}) collective-permute-start(bf16[2,64,768]{2,1,0:T(8,128)(2,1)S(1)} %get-tuple-element.56), channel_id=1, source_target_pairs={{0,4},{2,6},{4,0},{6,2},{1,5},{3,7},{5,1},{7,3},{8,12},{10,14},{12... | collective-permute-start | bytes 589832 | tf_op jit(solution)/shard_map/ppermute | solution.py:20
  45.1 9.2 %collective-permute-start.15 = (bf16[2,64,768]{2,1,0:T(8,128)(2,1)S(1)}, bf16[2,64,768]{2,1,0:T(8,128)(2,1)S(1)}, u32[]{:S(2)}, u32[]{:S(2)}) collective-permute-start(bf16[2,64,768]{2,1,0:T(8,128)(2,1)S(1)} %get-tuple-element.57), channel_id=1, source_target_pairs={{0,6},{2,4},{4,2},{6,0},{1,7},{3,5},{5,3},{7,1},{8,14},{10,12},{12... | collective-permute-start | bytes 589832 | tf_op jit(solution)/shard_map/ppermute | solution.py:20
  47.5 16.2 %collective-permute-start.19 = (bf16[2,64,896]{2,1,0:T(8,128)(2,1)S(1)}, bf16[2,64,896]{2,1,0:T(8,128)(2,1)S(1)}, u32[]{:S(2)}, u32[]{:S(2)}) collective-permute-start(bf16[2,64,896]{2,1,0:T(8,128)(2,1)S(1)} %share.7), channel_id=1, source_target_pairs={{0,24},{8,16},{16,8},{24,0},{1,25},{9,17},{17,9},{25,1},{2,26},{10... | collective-permute-start | bytes 688136 | tf_op jit(solution)/shard_map/ppermute | solution.py:25
  54.5 12.5 %collective-permute-start.16 = (bf16[2,64,768]{2,1,0:T(8,128)(2,1)S(1)}, bf16[2,64,768]{2,1,0:T(8,128)(2,1)S(1)}, u32[]{:S(2)}, u32[]{:S(2)}) collective-permute-start(bf16[2,64,768]{2,1,0:T(8,128)(2,1)S(1)} %share.6), channel_id=1, source_target_pairs={{0,24},{8,16},{16,8},{24,0},{1,25},{9,17},{17,9},{25,1},{2,26},{10... | collective-permute-start | bytes 589832 | tf_op jit(solution)/shard_map/ppermute | solution.py:25
  57.1 15.2 %collective-permute-start.10 = (bf16[16,3584]{1,0:T(8,128)(2,1)S(1)}, bf16[16,3584]{1,0:T(8,128)(2,1)S(1)}, u32[]{:S(2)}, u32[]{:S(2)}) collective-permute-start(bf16[16,3584]{1,0:T(8,128)(2,1)S(1)} %leaving.4), channel_id=1, source_target_pairs={{0,8},{8,16},{16,24},{1,9},{9,17},{17,25},{2,10},{10,18},{18,26},{... | collective-permute-start | bytes 344072 | tf_op jit(solution)/shard_map/ppermute | solution.py:35
  61.3 11.0 %collective-permute-start.11 = (bf16[16,3584]{1,0:T(8,128)(2,1)S(1)}, bf16[16,3584]{1,0:T(8,128)(2,1)S(1)}, u32[]{:S(2)}, u32[]{:S(2)}) collective-permute-start(bf16[16,3584]{1,0:T(8,128)(2,1)S(1)} %leaving.5), channel_id=1, source_target_pairs={{0,8},{8,16},{16,24},{1,9},{9,17},{17,25},{2,10},{10,18},{18,26},{... | collective-permute-start | bytes 344072 | tf_op jit(solution)/shard_map/ppermute | solution.py:35
  67.4 3.7 %collective-permute-start.20 = (f32[8,128]{1,0:T(8,128)S(1)}, f32[8,128]{1,0:T(8,128)S(1)}, u32[]{:S(2)}, u32[]{:S(2)}) collective-permute-start(f32[8,128]{1,0:T(8,128)S(1)} %get-tuple-element.62.refs_0_), channel_id=1, source_target_pairs={{0,2},{2,0},{4,6},{6,4},{1,3},{3,1},{5,7},{7,5},{8,10},{10,8},{12,... | collective-permute-start | bytes 12296 | tf_op jit(solution)/shard_map/ppermute | solution.py:20
  68.7 4.3 %collective-permute-start.21 = (f32[8,128]{1,0:T(8,128)S(1)}, f32[8,128]{1,0:T(8,128)S(1)}, u32[]{:S(2)}, u32[]{:S(2)}) collective-permute-start(f32[8,128]{1,0:T(8,128)S(1)} %get-tuple-element.62.refs_0_), channel_id=1, source_target_pairs={{0,4},{2,6},{4,0},{6,2},{1,5},{3,7},{5,1},{7,3},{8,12},{10,14},{12... | collective-permute-start | bytes 12296 | tf_op jit(solution)/shard_map/ppermute | solution.py:20
  69.3 4.5 %collective-permute-start.22 = (f32[8,128]{1,0:T(8,128)S(1)}, f32[8,128]{1,0:T(8,128)S(1)}, u32[]{:S(2)}, u32[]{:S(2)}) collective-permute-start(f32[8,128]{1,0:T(8,128)S(1)} %get-tuple-element.62.refs_0_), channel_id=1, source_target_pairs={{0,6},{2,4},{4,2},{6,0},{1,7},{3,5},{5,3},{7,1},{8,14},{10,12},{12... | collective-permute-start | bytes 12296 | tf_op jit(solution)/shard_map/ppermute | solution.py:20

commit v15 on v14

--- a/solution.py
+++ b/solution.py
@@ -257,7 +257,7 @@
     depth = latent // experts
     blocks = width // LANES
     tiles = 2
-    weights = [8, 7, 7, 6]
+    weights = [8, 8, 7, 5]
     edges = [blocks * sum(weights[:k]) // sum(weights) * LANES for k in range(len(weights) + 1)]
     chunks = list(zip(edges[:-1], edges[1:]))
 

time: 75.5 us -> 79.6 us (1.054)
  the two profiles are of different devices: /device:TPU:8 before, /device:TPU:0 now
where the time goes in v15:
time: 79.6 us; the launch traced here: 79.4 us
  starting transfers between devices  42.5 us (53%)
  waiting for transfers between devices  21.3 us (27%)
  Pallas kernels  14.8 us (19%)
  between operations  0.82 us (1%)
    ppermute x16, waiting for transfers between devices, exchange(): return lax.ppermute(block, axis, [(i, i ^ offset) for i in range(count)])  21.2 us
    ppermute x16, starting transfers between devices, exchange(): return lax.ppermute(block, axis, [(i, i ^ offset) for i in range(count)])  20.6 us
    ppermute x4, starting transfers between devices, mirrored(): return lax.ppermute(block, axis, [(i, count - 1 - i) for i in range(count)])  9.82 us
    ppermute x2, starting transfers between devices, shifted(): return lax.ppermute(block, axis, [(i, i + 1) for i in range(count - 1)])  9.07 us
    pallas_call x17, Pallas kernels, call(): pl.pallas_call(kernel, in_specs=[VMEM] * read + [ANY] * (len(operands) -...  7.64 us
    pallas_call x1, Pallas kernels, shards(): pl.pallas_call(lambda *refs: latent_kernel(tiles, *refs), in_specs=[ANY]...  4.12 us
    ppermute x1, starting transfers between devices, turned(): lax.ppermute(block, axis, [(i, (i + 1) % count) for i in range(count)])  3.01 us
  transfers between devices with their start and end apart: 23, of which 9 were waited for; matrix products, arithmetic and copies ran while one was open for 0% of the time, Pallas kernels for 12%

profile of v15, /device:TPU:0, one launch (start us, length us, event | category | flops | bytes accessed | tf_op | source)
XLA Modules:
  0.0 79.4 jit_solution(16137721937389350184)
XLA Ops:
  0.6 4.1 %latents.1 = (f32[1024,128]{1,0:T(8,128)S(1)}, bf16[128,3584]{1,0:T(8,128)(2,1)S(1)}, bf16[128,3584]{1,0:T(8,128)(2,1)S(1)}, bf16[128,3584]{1,0:T(8,128)(2,1)S(1)}) custom-call(bf16[1,128,3584]{2,1,0:T(8,128)(2,1)} %refs_0_.1, bf16[1,128,3584]{2,1,0:T(8,128)(2,1)} %refs_1_.5, bf16[1,128,3584]{2,1,0:T(8,128)(2,1)} %refs_2_.5, ...), custom_call_target="tpu_custom_call" | custom-call | flops 704643072 | bytes 8257536 | tf_op jit(solution)/shard_map/latents/pallas_call | solution.py:269
  5.3 1.5 %fetch.1.refs_3_ = bf16[256,3584]{1,0:T(8,128)(2,1)S(1)} custom-call(bf16[2,1,256,3584]{3,2,1,0:T(8,128)(2,1)} %in_ref.1, f32[1024,128]{1,0:T(8,128)S(1)} %get-tuple-element.37.rest_0_.refs_0_), custom_call_target="tpu_custom_call" | custom-call | bytes 1835008 | tf_op jit(solution)/shard_map/fetch/pallas_call | solution.py:288
  7.3 3.0 %collective-permute-start.5 = (bf16[96,3584]{1,0:T(8,128)(2,1)S(1)}, bf16[96,3584]{1,0:T(8,128)(2,1)S(1)}, u32[]{:S(2)}, u32[]{:S(2)}) collective-permute-start(bf16[96,3584]{1,0:T(8,128)(2,1)S(1)} %leaving.3.refs_4_), channel_id=1, source_target_pairs={{0,8},{8,16},{16,24},{24,0},{1,9},{9,17},{17,25},{25,1},{2,10},{10... | collective-permute-start | bytes 2064392 | tf_op jit(solution)/shard_map/ppermute | solution.py:30
  10.9 1.6 %collective-permute-start.1 = (bf16[2,64,1024]{2,1,0:T(8,128)(2,1)S(1)}, bf16[2,64,1024]{2,1,0:T(8,128)(2,1)S(1)}, u32[]{:S(2)}, u32[]{:S(2)}) collective-permute-start(bf16[2,64,1024]{2,1,0:T(8,128)(2,1)S(1)} %get-tuple-element.41), channel_id=1, source_target_pairs={{0,2},{2,0},{4,6},{6,4},{1,3},{3,1},{5,7},{7,5},{8,10},{10,8},{12,... | collective-permute-start | bytes 786440 | tf_op jit(solution)/shard_map/ppermute | solution.py:20
  12.4 1.5 %collective-permute-start.7 = (bf16[2,64,1024]{2,1,0:T(8,128)(2,1)S(1)}, bf16[2,64,1024]{2,1,0:T(8,128)(2,1)S(1)}, u32[]{:S(2)}, u32[]{:S(2)}) collective-permute-start(bf16[2,64,1024]{2,1,0:T(8,128)(2,1)S(1)} %get-tuple-element.47), channel_id=1, source_target_pairs={{0,4},{2,6},{4,0},{6,2},{1,5},{3,7},{5,1},{7,3},{8,12},{10,14},{12... | collective-permute-start | bytes 786440 | tf_op jit(solution)/shard_map/ppermute | solution.py:20
  14.4 5.7 %collective-permute-done.1.refs_4_.refs_1_ = bf16[2,64,1024]{2,1,0:T(8,128)(2,1)S(1)} collective-permute-done((bf16[2,64,1024]{2,1,0:T(8,128)(2,1)S(1)}, bf16[2,64,1024]{2,1,0:T(8,128)(2,1)S(1)}, u32[]{:S(2)}, u32[]{:S(2)}) %collective-permute-start.1) | collective-permute-done | bytes 262176 | tf_op jit(solution)/shard_map/ppermute | solution.py:20
  20.7 1.6 %collective-permute-start.2 = (bf16[2,64,1024]{2,1,0:T(8,128)(2,1)S(1)}, bf16[2,64,1024]{2,1,0:T(8,128)(2,1)S(1)}, u32[]{:S(2)}, u32[]{:S(2)}) collective-permute-start(bf16[2,64,1024]{2,1,0:T(8,128)(2,1)S(1)} %get-tuple-element.43), channel_id=1, source_target_pairs={{0,2},{2,0},{4,6},{6,4},{1,3},{3,1},{5,7},{7,5},{8,10},{10,8},{12,... | collective-permute-start | bytes 786440 | tf_op jit(solution)/shard_map/ppermute | solution.py:20
  22.2 1.5 %collective-permute-start.3 = (bf16[2,64,1024]{2,1,0:T(8,128)(2,1)S(1)}, bf16[2,64,1024]{2,1,0:T(8,128)(2,1)S(1)}, u32[]{:S(2)}, u32[]{:S(2)}) collective-permute-start(bf16[2,64,1024]{2,1,0:T(8,128)(2,1)S(1)} %get-tuple-element.44), channel_id=1, source_target_pairs={{0,4},{2,6},{4,0},{6,2},{1,5},{3,7},{5,1},{7,3},{8,12},{10,14},{12... | collective-permute-start | bytes 786440 | tf_op jit(solution)/shard_map/ppermute | solution.py:20
  23.7 2.2 %collective-permute-done.7.refs_2_ = bf16[2,64,1024]{2,1,0:T(8,128)(2,1)S(1)} collective-permute-done((bf16[2,64,1024]{2,1,0:T(8,128)(2,1)S(1)}, bf16[2,64,1024]{2,1,0:T(8,128)(2,1)S(1)}, u32[]{:S(2)}, u32[]{:S(2)}) %collective-permute-start.7) | collective-permute-done | bytes 262176 | tf_op jit(solution)/shard_map/ppermute | solution.py:20
  25.9 0.8 collective-permute-start.4
  26.9 2.5 %collective-permute-start.9 = (bf16[2,64,1024]{2,1,0:T(8,128)(2,1)S(1)}, bf16[2,64,1024]{2,1,0:T(8,128)(2,1)S(1)}, u32[]{:S(2)}, u32[]{:S(2)}) collective-permute-start(bf16[2,64,1024]{2,1,0:T(8,128)(2,1)S(1)} %share.5.refs_4_), channel_id=1, source_target_pairs={{0,24},{8,16},{16,8},{24,0},{1,25},{9,17},{17,9},{25,1},{2,26},{10... | collective-permute-start | bytes 786440 | tf_op jit(solution)/shard_map/ppermute | solution.py:25
  29.3 2.1 %collective-permute-done.2.refs_1_.refs_5_ = bf16[2,64,1024]{2,1,0:T(8,128)(2,1)S(1)} collective-permute-done((bf16[2,64,1024]{2,1,0:T(8,128)(2,1)S(1)}, bf16[2,64,1024]{2,1,0:T(8,128)(2,1)S(1)}, u32[]{:S(2)}, u32[]{:S(2)}) %collective-permute-start.2) | collective-permute-done | bytes 262176 | tf_op jit(solution)/shard_map/ppermute | solution.py:20
  31.9 1.6 %collective-permute-start.12 = (bf16[2,64,896]{2,1,0:T(8,128)(2,1)S(1)}, bf16[2,64,896]{2,1,0:T(8,128)(2,1)S(1)}, u32[]{:S(2)}, u32[]{:S(2)}) collective-permute-start(bf16[2,64,896]{2,1,0:T(8,128)(2,1)S(1)} %get-tuple-element.53), channel_id=1, source_target_pairs={{0,2},{2,0},{4,6},{6,4},{1,3},{3,1},{5,7},{7,5},{8,10},{10,8},{12,... | collective-permute-start | bytes 688136 | tf_op jit(solution)/shard_map/ppermute | solution.py:20
  33.5 2.6 %collective-permute-done.3.refs_2_ = bf16[2,64,1024]{2,1,0:T(8,128)(2,1)S(1)} collective-permute-done((bf16[2,64,1024]{2,1,0:T(8,128)(2,1)S(1)}, bf16[2,64,1024]{2,1,0:T(8,128)(2,1)S(1)}, u32[]{:S(2)}, u32[]{:S(2)}) %collective-permute-start.3) | collective-permute-done | bytes 262176 | tf_op jit(solution)/shard_map/ppermute | solution.py:20
  36.1 2.4 %collective-permute-start.17 = (bf16[2,64,896]{2,1,0:T(8,128)(2,1)S(1)}, bf16[2,64,896]{2,1,0:T(8,128)(2,1)S(1)}, u32[]{:S(2)}, u32[]{:S(2)}) collective-permute-start(bf16[2,64,896]{2,1,0:T(8,128)(2,1)S(1)} %get-tuple-element.59), channel_id=1, source_target_pairs={{0,4},{2,6},{4,0},{6,2},{1,5},{3,7},{5,1},{7,3},{8,12},{10,14},{12... | collective-permute-start | bytes 688136 | tf_op jit(solution)/shard_map/ppermute | solution.py:20
  38.5 0.9 %collective-permute-start.18 = (bf16[2,64,896]{2,1,0:T(8,128)(2,1)S(1)}, bf16[2,64,896]{2,1,0:T(8,128)(2,1)S(1)}, u32[]{:S(2)}, u32[]{:S(2)}) collective-permute-start(bf16[2,64,896]{2,1,0:T(8,128)(2,1)S(1)} %get-tuple-element.60), channel_id=1, source_target_pairs={{0,6},{2,4},{4,2},{6,0},{1,7},{3,5},{5,3},{7,1},{8,14},{10,12},{12... | collective-permute-start | bytes 688136 | tf_op jit(solution)/shard_map/ppermute | solution.py:20
  39.6 2.3 %collective-permute-start.6 = (bf16[2,64,1024]{2,1,0:T(8,128)(2,1)S(1)}, bf16[2,64,1024]{2,1,0:T(8,128)(2,1)S(1)}, u32[]{:S(2)}, u32[]{:S(2)}) collective-permute-start(bf16[2,64,1024]{2,1,0:T(8,128)(2,1)S(1)} %share.4.refs_4_), channel_id=1, source_target_pairs={{0,24},{8,16},{16,8},{24,0},{1,25},{9,17},{17,9},{25,1},{2,26},{10... | collective-permute-start | bytes 786440 | tf_op jit(solution)/shard_map/ppermute | solution.py:25
  42.5 1.5 %collective-permute-start.13 = (bf16[2,64,640]{2,1,0:T(8,128)(2,1)S(1)}, bf16[2,64,640]{2,1,0:T(8,128)(2,1)S(1)}, u32[]{:S(2)}, u32[]{:S(2)}) collective-permute-start(bf16[2,64,640]{2,1,0:T(8,128)(2,1)S(1)} %get-tuple-element.55), channel_id=1, source_target_pairs={{0,2},{2,0},{4,6},{6,4},{1,3},{3,1},{5,7},{7,5},{8,10},{10,8},{12,... | collective-permute-start | bytes 491528 | tf_op jit(solution)/shard_map/ppermute | solution.py:20
  44.0 1.5 %collective-permute-start.14 = (bf16[2,64,640]{2,1,0:T(8,128)(2,1)S(1)}, bf16[2,64,640]{2,1,0:T(8,128)(2,1)S(1)}, u32[]{:S(2)}, u32[]{:S(2)}) collective-permute-start(bf16[2,64,640]{2,1,0:T(8,128)(2,1)S(1)} %get-tuple-element.56), channel_id=1, source_target_pairs={{0,4},{2,6},{4,0},{6,2},{1,5},{3,7},{5,1},{7,3},{8,12},{10,14},{12... | collective-permute-start | bytes 491528 | tf_op jit(solution)/shard_map/ppermute | solution.py:20
  45.4 3.1 %collective-permute-done.17.refs_2_ = bf16[2,64,896]{2,1,0:T(8,128)(2,1)S(1)} collective-permute-done((bf16[2,64,896]{2,1,0:T(8,128)(2,1)S(1)}, bf16[2,64,896]{2,1,0:T(8,128)(2,1)S(1)}, u32[]{:S(2)}, u32[]{:S(2)}) %collective-permute-start.17) | collective-permute-done | bytes 229408 | tf_op jit(solution)/shard_map/ppermute | solution.py:20
  48.5 0.6 collective-permute-start.15
  49.2 2.7 %collective-permute-start.19 = (bf16[2,64,896]{2,1,0:T(8,128)(2,1)S(1)}, bf16[2,64,896]{2,1,0:T(8,128)(2,1)S(1)}, u32[]{:S(2)}, u32[]{:S(2)}) collective-permute-start(bf16[2,64,896]{2,1,0:T(8,128)(2,1)S(1)} %share.7), channel_id=1, source_target_pairs={{0,24},{8,16},{16,8},{24,0},{1,25},{9,17},{17,9},{25,1},{2,26},{10... | collective-permute-start | bytes 688136 | tf_op jit(solution)/shard_map/ppermute | solution.py:25
  51.9 0.8 %collective-permute-done.14.refs_2_ = bf16[2,64,640]{2,1,0:T(8,128)(2,1)S(1)} collective-permute-done((bf16[2,64,640]{2,1,0:T(8,128)(2,1)S(1)}, bf16[2,64,640]{2,1,0:T(8,128)(2,1)S(1)}, u32[]{:S(2)}, u32[]{:S(2)}) %collective-permute-start.14) | collective-permute-done | bytes 163872 | tf_op jit(solution)/shard_map/ppermute | solution.py:20
  52.7 2.0 %collective-permute-done.15.refs_3_ = bf16[2,64,640]{2,1,0:T(8,128)(2,1)S(1)} collective-permute-done((bf16[2,64,640]{2,1,0:T(8,128)(2,1)S(1)}, bf16[2,64,640]{2,1,0:T(8,128)(2,1)S(1)}, u32[]{:S(2)}, u32[]{:S(2)}) %collective-permute-start.15) | collective-permute-done | bytes 163872 | tf_op jit(solution)/shard_map/ppermute | solution.py:20
  54.8 2.4 %collective-permute-start.16 = (bf16[2,64,640]{2,1,0:T(8,128)(2,1)S(1)}, bf16[2,64,640]{2,1,0:T(8,128)(2,1)S(1)}, u32[]{:S(2)}, u32[]{:S(2)}) collective-permute-start(bf16[2,64,640]{2,1,0:T(8,128)(2,1)S(1)} %share.6), channel_id=1, source_target_pairs={{0,24},{8,16},{16,8},{24,0},{1,25},{9,17},{17,9},{25,1},{2,26},{10... | collective-permute-start | bytes 491528 | tf_op jit(solution)/shard_map/ppermute | solution.py:25
  57.8 0.9 %place.2 = (bf16[1,128,3584]{2,1,0:T(8,128)(2,1)}, f32[8,128]{1,0:T(8,128)S(1)}) custom-call(bf16[96,3584]{1,0:T(8,128)(2,1)S(1)} %collective-permute-done.5.refs_4_.refs_0_), custom_call_target="tpu_custom_call" | custom-call | bytes 1376256 | tf_op jit(solution)/shard_map/place/pallas_call | solution.py:352
  59.6 6.7 %collective-permute-start.10 = (bf16[16,3584]{1,0:T(8,128)(2,1)S(1)}, bf16[16,3584]{1,0:T(8,128)(2,1)S(1)}, u32[]{:S(2)}, u32[]{:S(2)}) collective-permute-start(bf16[16,3584]{1,0:T(8,128)(2,1)S(1)} %leaving.4), channel_id=1, source_target_pairs={{0,8},{8,16},{16,24},{1,9},{9,17},{17,25},{2,10},{10,18},{18,26},{... | collective-permute-start | bytes 344072 | tf_op jit(solution)/shard_map/ppermute | solution.py:35
  66.7 2.4 %collective-permute-start.11 = (bf16[16,3584]{1,0:T(8,128)(2,1)S(1)}, bf16[16,3584]{1,0:T(8,128)(2,1)S(1)}, u32[]{:S(2)}, u32[]{:S(2)}) collective-permute-start(bf16[16,3584]{1,0:T(8,128)(2,1)S(1)} %leaving.5), channel_id=1, source_target_pairs={{0,8},{8,16},{16,24},{1,9},{9,17},{17,25},{2,10},{10,18},{18,26},{... | collective-permute-start | bytes 344072 | tf_op jit(solution)/shard_map/ppermute | solution.py:35
  70.2 4.1 %collective-permute-start.21 = (f32[8,128]{1,0:T(8,128)S(1)}, f32[8,128]{1,0:T(8,128)S(1)}, u32[]{:S(2)}, u32[]{:S(2)}) collective-permute-start(f32[8,128]{1,0:T(8,128)S(1)} %get-tuple-element.62.refs_0_), channel_id=1, source_target_pairs={{0,4},{2,6},{4,0},{6,2},{1,5},{3,7},{5,1},{7,3},{8,12},{10,14},{12... | collective-permute-start | bytes 12296 | tf_op jit(solution)/shard_map/ppermute | solution.py:20
  74.3 1.2 %codes.1 = (bf16[2,1,64,3584]{3,2,1,0:T(8,128)(2,1)}, f32[8,128]{1,0:T(8,128)S(1)}) custom-call(f32[8,128]{1,0:T(8,128)S(1)} %get-tuple-element.62.refs_0_, f32[8,128]{1,0:T(8,128)S(1)} %collective-permute-done.20.refs_1_, f32[2,64,1024]{2,1,0:T(8,128)S(1)} %get-tuple-element.63.refs_2_, f32[2,64,1024]{2,1,0:T(8,128)S(1)} %get-tuple-element.64.refs_3_, ...), custom_call_target="tpu_custom_call" | custom-call | flops 917504 | bytes 1843200 | tf_op jit(solution)/shard_map/codes/pallas_call | solution.py:56
  75.5 0.7 place.3
  76.2 2.6 %collective-permute-done.22.refs_3_ = f32[8,128]{1,0:T(8,128)S(1)} collective-permute-done((f32[8,128]{1,0:T(8,128)S(1)}, f32[8,128]{1,0:T(8,128)S(1)}, u32[]{:S(2)}, u32[]{:S(2)}) %collective-permute-start.22) | collective-permute-done | bytes 4128 | tf_op jit(solution)/shard_map/ppermute | solution.py:20
  (41 shorter events, 7.8 us)
Async XLA Ops:
  4.8 2.1 %collective-permute-start = (f32[1024,128]{1,0:T(8,128)S(1)}, f32[1024,128]{1,0:T(8,128)S(1)}, u32[]{:S(2)}, u32[]{:S(2)}) collective-permute-start(f32[1024,128]{1,0:T(8,128)S(1)} %get-tuple-element.37.rest_0_.refs_0_), channel_id=1, source_target_pairs={{0,1},{1,0},{2,3},{3,2},{4,5},{5,4},{6,7},{7,6},{8,9},{9,8},{10,11... | collective-permute-start | bytes 1572872 | tf_op jit(solution)/shard_map/ppermute | solution.py:20
  7.3 32.1 %collective-permute-start.5 = (bf16[96,3584]{1,0:T(8,128)(2,1)S(1)}, bf16[96,3584]{1,0:T(8,128)(2,1)S(1)}, u32[]{:S(2)}, u32[]{:S(2)}) collective-permute-start(bf16[96,3584]{1,0:T(8,128)(2,1)S(1)} %leaving.3.refs_4_), channel_id=1, source_target_pairs={{0,8},{8,16},{16,24},{24,0},{1,9},{9,17},{17,25},{25,1},{2,10},{10... | collective-permute-start | bytes 2064392 | tf_op jit(solution)/shard_map/ppermute | solution.py:30
  10.9 9.3 %collective-permute-start.1 = (bf16[2,64,1024]{2,1,0:T(8,128)(2,1)S(1)}, bf16[2,64,1024]{2,1,0:T(8,128)(2,1)S(1)}, u32[]{:S(2)}, u32[]{:S(2)}) collective-permute-start(bf16[2,64,1024]{2,1,0:T(8,128)(2,1)S(1)} %get-tuple-element.41), channel_id=1, source_target_pairs={{0,2},{2,0},{4,6},{6,4},{1,3},{3,1},{5,7},{7,5},{8,10},{10,8},{12,... | collective-permute-start | bytes 786440 | tf_op jit(solution)/shard_map/ppermute | solution.py:20
  12.4 13.5 %collective-permute-start.7 = (bf16[2,64,1024]{2,1,0:T(8,128)(2,1)S(1)}, bf16[2,64,1024]{2,1,0:T(8,128)(2,1)S(1)}, u32[]{:S(2)}, u32[]{:S(2)}) collective-permute-start(bf16[2,64,1024]{2,1,0:T(8,128)(2,1)S(1)} %get-tuple-element.47), channel_id=1, source_target_pairs={{0,4},{2,6},{4,0},{6,2},{1,5},{3,7},{5,1},{7,3},{8,12},{10,14},{12... | collective-permute-start | bytes 786440 | tf_op jit(solution)/shard_map/ppermute | solution.py:20
  13.9 12.8 %collective-permute-start.8 = (bf16[2,64,1024]{2,1,0:T(8,128)(2,1)S(1)}, bf16[2,64,1024]{2,1,0:T(8,128)(2,1)S(1)}, u32[]{:S(2)}, u32[]{:S(2)}) collective-permute-start(bf16[2,64,1024]{2,1,0:T(8,128)(2,1)S(1)} %get-tuple-element.48), channel_id=1, source_target_pairs={{0,6},{2,4},{4,2},{6,0},{1,7},{3,5},{5,3},{7,1},{8,14},{10,12},{12... | collective-permute-start | bytes 786440 | tf_op jit(solution)/shard_map/ppermute | solution.py:20
  20.7 10.7 %collective-permute-start.2 = (bf16[2,64,1024]{2,1,0:T(8,128)(2,1)S(1)}, bf16[2,64,1024]{2,1,0:T(8,128)(2,1)S(1)}, u32[]{:S(2)}, u32[]{:S(2)}) collective-permute-start(bf16[2,64,1024]{2,1,0:T(8,128)(2,1)S(1)} %get-tuple-element.43), channel_id=1, source_target_pairs={{0,2},{2,0},{4,6},{6,4},{1,3},{3,1},{5,7},{7,5},{8,10},{10,8},{12,... | collective-permute-start | bytes 786440 | tf_op jit(solution)/shard_map/ppermute | solution.py:20
  22.2 13.8 %collective-permute-start.3 = (bf16[2,64,1024]{2,1,0:T(8,128)(2,1)S(1)}, bf16[2,64,1024]{2,1,0:T(8,128)(2,1)S(1)}, u32[]{:S(2)}, u32[]{:S(2)}) collective-permute-start(bf16[2,64,1024]{2,1,0:T(8,128)(2,1)S(1)} %get-tuple-element.44), channel_id=1, source_target_pairs={{0,4},{2,6},{4,0},{6,2},{1,5},{3,7},{5,1},{7,3},{8,12},{10,14},{12... | collective-permute-start | bytes 786440 | tf_op jit(solution)/shard_map/ppermute | solution.py:20
  25.9 12.6 %collective-permute-start.4 = (bf16[2,64,1024]{2,1,0:T(8,128)(2,1)S(1)}, bf16[2,64,1024]{2,1,0:T(8,128)(2,1)S(1)}, u32[]{:S(2)}, u32[]{:S(2)}) collective-permute-start(bf16[2,64,1024]{2,1,0:T(8,128)(2,1)S(1)} %get-tuple-element.45), channel_id=1, source_target_pairs={{0,6},{2,4},{4,2},{6,0},{1,7},{3,5},{5,3},{7,1},{8,14},{10,12},{12... | collective-permute-start | bytes 786440 | tf_op jit(solution)/shard_map/ppermute | solution.py:20
  26.9 17.1 %collective-permute-start.9 = (bf16[2,64,1024]{2,1,0:T(8,128)(2,1)S(1)}, bf16[2,64,1024]{2,1,0:T(8,128)(2,1)S(1)}, u32[]{:S(2)}, u32[]{:S(2)}) collective-permute-start(bf16[2,64,1024]{2,1,0:T(8,128)(2,1)S(1)} %share.5.refs_4_), channel_id=1, source_target_pairs={{0,24},{8,16},{16,8},{24,0},{1,25},{9,17},{17,9},{25,1},{2,26},{10... | collective-permute-start | bytes 786440 | tf_op jit(solution)/shard_map/ppermute | solution.py:25
  31.9 10.2 %collective-permute-start.12 = (bf16[2,64,896]{2,1,0:T(8,128)(2,1)S(1)}, bf16[2,64,896]{2,1,0:T(8,128)(2,1)S(1)}, u32[]{:S(2)}, u32[]{:S(2)}) collective-permute-start(bf16[2,64,896]{2,1,0:T(8,128)(2,1)S(1)} %get-tuple-element.53), channel_id=1, source_target_pairs={{0,2},{2,0},{4,6},{6,4},{1,3},{3,1},{5,7},{7,5},{8,10},{10,8},{12,... | collective-permute-start | bytes 688136 | tf_op jit(solution)/shard_map/ppermute | solution.py:20
  36.1 12.4 %collective-permute-start.17 = (bf16[2,64,896]{2,1,0:T(8,128)(2,1)S(1)}, bf16[2,64,896]{2,1,0:T(8,128)(2,1)S(1)}, u32[]{:S(2)}, u32[]{:S(2)}) collective-permute-start(bf16[2,64,896]{2,1,0:T(8,128)(2,1)S(1)} %get-tuple-element.59), channel_id=1, source_target_pairs={{0,4},{2,6},{4,0},{6,2},{1,5},{3,7},{5,1},{7,3},{8,12},{10,14},{12... | collective-permute-start | bytes 688136 | tf_op jit(solution)/shard_map/ppermute | solution.py:20
  38.5 10.6 %collective-permute-start.18 = (bf16[2,64,896]{2,1,0:T(8,128)(2,1)S(1)}, bf16[2,64,896]{2,1,0:T(8,128)(2,1)S(1)}, u32[]{:S(2)}, u32[]{:S(2)}) collective-permute-start(bf16[2,64,896]{2,1,0:T(8,128)(2,1)S(1)} %get-tuple-element.60), channel_id=1, source_target_pairs={{0,6},{2,4},{4,2},{6,0},{1,7},{3,5},{5,3},{7,1},{8,14},{10,12},{12... | collective-permute-start | bytes 688136 | tf_op jit(solution)/shard_map/ppermute | solution.py:20
  39.5 17.7 %copy-start = (f32[2,1,64,3584]{3,2,1,0:T(8,128)S(1)}, f32[2,1,64,3584]{3,2,1,0:T(8,128)}, u32[]{:S(2)}) copy-start(f32[2,1,64,3584]{3,2,1,0:T(8,128)} %refs_1_.9) | copy-start | bytes 5505028
  39.5 17.7 %copy-start.1 = (bf16[2,1,64,3584]{3,2,1,0:T(8,128)(2,1)S(1)}, bf16[2,1,64,3584]{3,2,1,0:T(8,128)(2,1)}, u32[]{:S(2)}) copy-start(bf16[2,1,64,3584]{3,2,1,0:T(8,128)(2,1)} %refs_2_.9) | copy-start | bytes 2752516
  39.5 17.7 %copy-start.2 = (bf16[2,1,64,3584]{3,2,1,0:T(8,128)(2,1)S(1)}, bf16[2,1,64,3584]{3,2,1,0:T(8,128)(2,1)}, u32[]{:S(2)}) copy-start(bf16[2,1,64,3584]{3,2,1,0:T(8,128)(2,1)} %refs_3_.9) | copy-start | bytes 2752516
  39.6 15.1 %collective-permute-start.6 = (bf16[2,64,1024]{2,1,0:T(8,128)(2,1)S(1)}, bf16[2,64,1024]{2,1,0:T(8,128)(2,1)S(1)}, u32[]{:S(2)}, u32[]{:S(2)}) collective-permute-start(bf16[2,64,1024]{2,1,0:T(8,128)(2,1)S(1)} %share.4.refs_4_), channel_id=1, source_target_pairs={{0,24},{8,16},{16,8},{24,0},{1,25},{9,17},{17,9},{25,1},{2,26},{10... | collective-permute-start | bytes 786440 | tf_op jit(solution)/shard_map/ppermute | solution.py:25
  42.5 9.4 %collective-permute-start.13 = (bf16[2,64,640]{2,1,0:T(8,128)(2,1)S(1)}, bf16[2,64,640]{2,1,0:T(8,128)(2,1)S(1)}, u32[]{:S(2)}, u32[]{:S(2)}) collective-permute-start(bf16[2,64,640]{2,1,0:T(8,128)(2,1)S(1)} %get-tuple-element.55), channel_id=1, source_target_pairs={{0,2},{2,0},{4,6},{6,4},{1,3},{3,1},{5,7},{7,5},{8,10},{10,8},{12,... | collective-permute-start | bytes 491528 | tf_op jit(solution)/shard_map/ppermute | solution.py:20
  44.0 8.8 %collective-permute-start.14 = (bf16[2,64,640]{2,1,0:T(8,128)(2,1)S(1)}, bf16[2,64,640]{2,1,0:T(8,128)(2,1)S(1)}, u32[]{:S(2)}, u32[]{:S(2)}) collective-permute-start(bf16[2,64,640]{2,1,0:T(8,128)(2,1)S(1)} %get-tuple-element.56), channel_id=1, source_target_pairs={{0,4},{2,6},{4,0},{6,2},{1,5},{3,7},{5,1},{7,3},{8,12},{10,14},{12... | collective-permute-start | bytes 491528 | tf_op jit(solution)/shard_map/ppermute | solution.py:20
  48.5 6.2 %collective-permute-start.15 = (bf16[2,64,640]{2,1,0:T(8,128)(2,1)S(1)}, bf16[2,64,640]{2,1,0:T(8,128)(2,1)S(1)}, u32[]{:S(2)}, u32[]{:S(2)}) collective-permute-start(bf16[2,64,640]{2,1,0:T(8,128)(2,1)S(1)} %get-tuple-element.57), channel_id=1, source_target_pairs={{0,6},{2,4},{4,2},{6,0},{1,7},{3,5},{5,3},{7,1},{8,14},{10,12},{12... | collective-permute-start | bytes 491528 | tf_op jit(solution)/shard_map/ppermute | solution.py:20
  49.2 19.9 %collective-permute-start.19 = (bf16[2,64,896]{2,1,0:T(8,128)(2,1)S(1)}, bf16[2,64,896]{2,1,0:T(8,128)(2,1)S(1)}, u32[]{:S(2)}, u32[]{:S(2)}) collective-permute-start(bf16[2,64,896]{2,1,0:T(8,128)(2,1)S(1)} %share.7), channel_id=1, source_target_pairs={{0,24},{8,16},{16,8},{24,0},{1,25},{9,17},{17,9},{25,1},{2,26},{10... | collective-permute-start | bytes 688136 | tf_op jit(solution)/shard_map/ppermute | solution.py:25
  54.8 14.9 %collective-permute-start.16 = (bf16[2,64,640]{2,1,0:T(8,128)(2,1)S(1)}, bf16[2,64,640]{2,1,0:T(8,128)(2,1)S(1)}, u32[]{:S(2)}, u32[]{:S(2)}) collective-permute-start(bf16[2,64,640]{2,1,0:T(8,128)(2,1)S(1)} %share.6), channel_id=1, source_target_pairs={{0,24},{8,16},{16,8},{24,0},{1,25},{9,17},{17,9},{25,1},{2,26},{10... | collective-permute-start | bytes 491528 | tf_op jit(solution)/shard_map/ppermute | solution.py:25
  59.6 15.9 %collective-permute-start.10 = (bf16[16,3584]{1,0:T(8,128)(2,1)S(1)}, bf16[16,3584]{1,0:T(8,128)(2,1)S(1)}, u32[]{:S(2)}, u32[]{:S(2)}) collective-permute-start(bf16[16,3584]{1,0:T(8,128)(2,1)S(1)} %leaving.4), channel_id=1, source_target_pairs={{0,8},{8,16},{16,24},{1,9},{9,17},{17,25},{2,10},{10,18},{18,26},{... | collective-permute-start | bytes 344072 | tf_op jit(solution)/shard_map/ppermute | solution.py:35
  66.7 8.8 %collective-permute-start.11 = (bf16[16,3584]{1,0:T(8,128)(2,1)S(1)}, bf16[16,3584]{1,0:T(8,128)(2,1)S(1)}, u32[]{:S(2)}, u32[]{:S(2)}) collective-permute-start(bf16[16,3584]{1,0:T(8,128)(2,1)S(1)} %leaving.5), channel_id=1, source_target_pairs={{0,8},{8,16},{16,24},{1,9},{9,17},{17,25},{2,10},{10,18},{18,26},{... | collective-permute-start | bytes 344072 | tf_op jit(solution)/shard_map/ppermute | solution.py:35
  70.1 4.2 %collective-permute-start.20 = (f32[8,128]{1,0:T(8,128)S(1)}, f32[8,128]{1,0:T(8,128)S(1)}, u32[]{:S(2)}, u32[]{:S(2)}) collective-permute-start(f32[8,128]{1,0:T(8,128)S(1)} %get-tuple-element.62.refs_0_), channel_id=1, source_target_pairs={{0,2},{2,0},{4,6},{6,4},{1,3},{3,1},{5,7},{7,5},{8,10},{10,8},{12,... | collective-permute-start | bytes 12296 | tf_op jit(solution)/shard_map/ppermute | solution.py:20
  70.2 6.0 %collective-permute-start.21 = (f32[8,128]{1,0:T(8,128)S(1)}, f32[8,128]{1,0:T(8,128)S(1)}, u32[]{:S(2)}, u32[]{:S(2)}) collective-permute-start(f32[8,128]{1,0:T(8,128)S(1)} %get-tuple-element.62.refs_0_), channel_id=1, source_target_pairs={{0,4},{2,6},{4,0},{6,2},{1,5},{3,7},{5,1},{7,3},{8,12},{10,14},{12... | collective-permute-start | bytes 12296 | tf_op jit(solution)/shard_map/ppermute | solution.py:20
  74.3 4.5 %collective-permute-start.22 = (f32[8,128]{1,0:T(8,128)S(1)}, f32[8,128]{1,0:T(8,128)S(1)}, u32[]{:S(2)}, u32[]{:S(2)}) collective-permute-start(f32[8,128]{1,0:T(8,128)S(1)} %get-tuple-element.62.refs_0_), channel_id=1, source_target_pairs={{0,6},{2,4},{4,2},{6,0},{1,7},{3,5},{5,3},{7,1},{8,14},{10,12},{12... | collective-permute-start | bytes 12296 | tf_op jit(solution)/shard_map/ppermute | solution.py:20

commit v16 on v14

--- a/solution.py
+++ b/solution.py
@@ -74,7 +74,7 @@
     return total
 
 
-def latent_kernel(tiles, x1, x2, c2, down, up, gain, out_ref, vx1, scaled2, vc2, va1, vx2, va2, vb2, vgain, sems):
+def latent_kernel(tiles, x1, x2, c2, down, up, gain_ref, out_ref, vx1, scaled2, vc2, va1, vx2, va2, vb2, sems):
     tokens, width = vx1.shape
     latent = va1.shape[0]
     tile = width // tiles
@@ -91,15 +91,12 @@
             for k, (src, dst) in enumerate(groups[job])
         ]
 
-    whole_gain = pltpu.make_async_copy(gain, vgain, sems.at[len(groups), 0, 0])
-    whole_gain.start()
     for job in range(len(groups)):
         for at in range(tiles):
             for copy in copies(job, at):
                 copy.start()
     base = 2 * latent + tokens
     out_ref[...] = jnp.zeros_like(out_ref)
-    whole_gain.wait()
 
     def step(job, at):
         for copy in copies(job, at):
@@ -107,7 +104,7 @@
         cols = pl.ds(pl.multiple_of(at * tile, LANES), tile)
         if job < 2:
             rows = (vx1, vx2)[job][:, cols].astype(F32)
-            right = (rows * vgain[job : job + 1, cols].astype(F32)).astype(BF16)
+            right = (rows * gain_ref[job : job + 1, cols]).astype(BF16)
             squares = folded_squares(rows)
         if job == 0:
             raw = lax.dot_general(right, va1[:, cols], BOTH_LAST, preferred_element_type=F32)
@@ -268,7 +265,7 @@
     held = pltpu.VMEM((tokens, width), BF16)
     packed, rows1, scaled2, cot2 = pl.pallas_call(
         lambda *refs: latent_kernel(tiles, *refs),
-        in_specs=[ANY] * 6,
+        in_specs=[ANY] * 5 + [VMEM],
         out_specs=[VMEM] * 4,
         out_shape=[pltpu.VMEM((pack_rows, LANES), F32), held, held, held],
         scratch_shapes=[
@@ -276,15 +273,17 @@
             pltpu.VMEM((tokens, width), BF16),
             pltpu.VMEM((latent, width), BF16),
             pltpu.VMEM((latent, width), BF16),
-            pltpu.VMEM((2, width), BF16),
-            pltpu.SemaphoreType.DMA((4, 2, tiles)),
+            pltpu.SemaphoreType.DMA((3, 2, tiles)),
         ],
         compiler_params=ROOM,
         cost_estimate=pl.CostEstimate(
             flops=6 * tokens * latent * width, bytes_accessed=6 * (tokens + latent) * width, transcendentals=0
         ),
         name="latents",
-    )(*(streamed(a) for a in (enter_fwd, enter_rev, cot_rev, proj_down, proj_up, gain.reshape(2, width))))
+    )(
+        *(streamed(a) for a in (enter_fwd, enter_rev, cot_rev, proj_down, proj_up)),
+        gain.reshape(2, width).astype(F32),
+    )
     own_up = pl.pallas_call(
         fetch_kernel,
         in_specs=[ANY] * 2,

time: 75.5 us -> 76.5 us (1.013)
  no operation moved by 1% of the time
where the time goes in v16:
time: 76.5 us; the launch traced here: 75.4 us
  starting transfers between devices  32.9 us (43%)
  waiting for transfers between devices  26 us (34%)
  Pallas kernels  14.8 us (19%)
  between operations  0.82 us (1%)
    ppermute x16, starting transfers between devices, exchange(): return lax.ppermute(block, axis, [(i, i ^ offset) for i in range(count)])  19 us
    ppermute x16, waiting for transfers between devices, exchange(): return lax.ppermute(block, axis, [(i, i ^ offset) for i in range(count)])  16.8 us
    ppermute x4, waiting for transfers between devices, mirrored(): return lax.ppermute(block, axis, [(i, count - 1 - i) for i in range(count)])  9.26 us
    pallas_call x17, Pallas kernels, call(): pl.pallas_call(kernel, in_specs=[VMEM] * read + [ANY] * (len(operands) -...  7.63 us
    ppermute x4, starting transfers between devices, mirrored(): return lax.ppermute(block, axis, [(i, count - 1 - i) for i in range(count)])  6.69 us
    ppermute x2, starting transfers between devices, shifted(): return lax.ppermute(block, axis, [(i, i + 1) for i in range(count - 1)])  5.66 us
    pallas_call x1, Pallas kernels, shards(): pl.pallas_call(lambda *refs: latent_kernel(tiles, *refs), in_specs=[ANY]...  4.12 us
    ppermute x1, starting transfers between devices, turned(): lax.ppermute(block, axis, [(i, (i + 1) % count) for i in range(count)])  1.59 us
  transfers between devices with their start and end apart: 23, of which 13 were waited for; matrix products, arithmetic and copies ran while one was open for 0% of the time, Pallas kernels for 12%

profile of v16, /device:TPU:8, one launch (start us, length us, event | category | flops | bytes accessed | tf_op | source)
XLA Modules:
  0.0 75.4 jit_solution(6397592114156207415)
XLA Ops:
  0.6 0.7 bitcast_convert_fusion.refs_5_
  1.4 4.1 %latents.1 = (f32[1024,128]{1,0:T(8,128)S(1)}, bf16[128,3584]{1,0:T(8,128)(2,1)S(1)}, bf16[128,3584]{1,0:T(8,128)(2,1)S(1)}, bf16[128,3584]{1,0:T(8,128)(2,1)S(1)}) custom-call(bf16[1,128,3584]{2,1,0:T(8,128)(2,1)} %refs_0_.1, bf16[1,128,3584]{2,1,0:T(8,128)(2,1)} %refs_1_.5, bf16[1,128,3584]{2,1,0:T(8,128)(2,1)} %refs_2_.5, ...), custom_call_target="tpu_custom_call" | custom-call | flops 704643072 | bytes 8257536 | tf_op jit(solution)/shard_map/latents/pallas_call | solution.py:266
  5.6 1.5 %fetch.1.refs_3_ = bf16[256,3584]{1,0:T(8,128)(2,1)S(1)} custom-call(bf16[2,1,256,3584]{3,2,1,0:T(8,128)(2,1)} %in_ref.1, f32[1024,128]{1,0:T(8,128)S(1)} %get-tuple-element.37.rest_0_.refs_0_), custom_call_target="tpu_custom_call" | custom-call | bytes 1835008 | tf_op jit(solution)/shard_map/fetch/pallas_call | solution.py:287
  8.5 1.5 %collective-permute-start.1 = (bf16[2,64,1024]{2,1,0:T(8,128)(2,1)S(1)}, bf16[2,64,1024]{2,1,0:T(8,128)(2,1)S(1)}, u32[]{:S(2)}, u32[]{:S(2)}) collective-permute-start(bf16[2,64,1024]{2,1,0:T(8,128)(2,1)S(1)} %get-tuple-element.41), channel_id=1, source_target_pairs={{0,2},{2,0},{4,6},{6,4},{1,3},{3,1},{5,7},{7,5},{8,10},{10,8},{12,... | collective-permute-start | bytes 786440 | tf_op jit(solution)/shard_map/ppermute | solution.py:20
  10.1 1.6 %collective-permute-start.5 = (bf16[96,3584]{1,0:T(8,128)(2,1)S(1)}, bf16[96,3584]{1,0:T(8,128)(2,1)S(1)}, u32[]{:S(2)}, u32[]{:S(2)}) collective-permute-start(bf16[96,3584]{1,0:T(8,128)(2,1)S(1)} %leaving.3.refs_4_), channel_id=1, source_target_pairs={{0,8},{8,16},{16,24},{24,0},{1,9},{9,17},{17,25},{25,1},{2,10},{10... | collective-permute-start | bytes 2064392 | tf_op jit(solution)/shard_map/ppermute | solution.py:30
  11.6 1.5 %collective-permute-start.7 = (bf16[2,64,1024]{2,1,0:T(8,128)(2,1)S(1)}, bf16[2,64,1024]{2,1,0:T(8,128)(2,1)S(1)}, u32[]{:S(2)}, u32[]{:S(2)}) collective-permute-start(bf16[2,64,1024]{2,1,0:T(8,128)(2,1)S(1)} %get-tuple-element.47), channel_id=1, source_target_pairs={{0,4},{2,6},{4,0},{6,2},{1,5},{3,7},{5,1},{7,3},{8,12},{10,14},{12... | collective-permute-start | bytes 786440 | tf_op jit(solution)/shard_map/ppermute | solution.py:20
  13.6 4.1 %collective-permute-done.1.refs_4_.refs_1_ = bf16[2,64,1024]{2,1,0:T(8,128)(2,1)S(1)} collective-permute-done((bf16[2,64,1024]{2,1,0:T(8,128)(2,1)S(1)}, bf16[2,64,1024]{2,1,0:T(8,128)(2,1)S(1)}, u32[]{:S(2)}, u32[]{:S(2)}) %collective-permute-start.1) | collective-permute-done | bytes 262176 | tf_op jit(solution)/shard_map/ppermute | solution.py:20
  18.2 1.5 %collective-permute-start.2 = (bf16[2,64,896]{2,1,0:T(8,128)(2,1)S(1)}, bf16[2,64,896]{2,1,0:T(8,128)(2,1)S(1)}, u32[]{:S(2)}, u32[]{:S(2)}) collective-permute-start(bf16[2,64,896]{2,1,0:T(8,128)(2,1)S(1)} %get-tuple-element.43), channel_id=1, source_target_pairs={{0,2},{2,0},{4,6},{6,4},{1,3},{3,1},{5,7},{7,5},{8,10},{10,8},{12,... | collective-permute-start | bytes 688136 | tf_op jit(solution)/shard_map/ppermute | solution.py:20
  19.8 1.5 %collective-permute-start.3 = (bf16[2,64,896]{2,1,0:T(8,128)(2,1)S(1)}, bf16[2,64,896]{2,1,0:T(8,128)(2,1)S(1)}, u32[]{:S(2)}, u32[]{:S(2)}) collective-permute-start(bf16[2,64,896]{2,1,0:T(8,128)(2,1)S(1)} %get-tuple-element.44), channel_id=1, source_target_pairs={{0,4},{2,6},{4,0},{6,2},{1,5},{3,7},{5,1},{7,3},{8,12},{10,14},{12... | collective-permute-start | bytes 688136 | tf_op jit(solution)/shard_map/ppermute | solution.py:20
  21.3 5.2 %collective-permute-done.7.refs_2_ = bf16[2,64,1024]{2,1,0:T(8,128)(2,1)S(1)} collective-permute-done((bf16[2,64,1024]{2,1,0:T(8,128)(2,1)S(1)}, bf16[2,64,1024]{2,1,0:T(8,128)(2,1)S(1)}, u32[]{:S(2)}, u32[]{:S(2)}) %collective-permute-start.7) | collective-permute-done | bytes 262176 | tf_op jit(solution)/shard_map/ppermute | solution.py:20
  26.5 1.5 %collective-permute-start.4 = (bf16[2,64,896]{2,1,0:T(8,128)(2,1)S(1)}, bf16[2,64,896]{2,1,0:T(8,128)(2,1)S(1)}, u32[]{:S(2)}, u32[]{:S(2)}) collective-permute-start(bf16[2,64,896]{2,1,0:T(8,128)(2,1)S(1)} %get-tuple-element.45), channel_id=1, source_target_pairs={{0,6},{2,4},{4,2},{6,0},{1,7},{3,5},{5,3},{7,1},{8,14},{10,12},{12... | collective-permute-start | bytes 688136 | tf_op jit(solution)/shard_map/ppermute | solution.py:20
  28.1 1.6 %collective-permute-start.9 = (bf16[2,64,1024]{2,1,0:T(8,128)(2,1)S(1)}, bf16[2,64,1024]{2,1,0:T(8,128)(2,1)S(1)}, u32[]{:S(2)}, u32[]{:S(2)}) collective-permute-start(bf16[2,64,1024]{2,1,0:T(8,128)(2,1)S(1)} %share.5.refs_4_), channel_id=1, source_target_pairs={{0,24},{8,16},{16,8},{24,0},{1,25},{9,17},{17,9},{25,1},{2,26},{10... | collective-permute-start | bytes 786440 | tf_op jit(solution)/shard_map/ppermute | solution.py:25
  30.3 1.6 %collective-permute-start.12 = (bf16[2,64,896]{2,1,0:T(8,128)(2,1)S(1)}, bf16[2,64,896]{2,1,0:T(8,128)(2,1)S(1)}, u32[]{:S(2)}, u32[]{:S(2)}) collective-permute-start(bf16[2,64,896]{2,1,0:T(8,128)(2,1)S(1)} %get-tuple-element.53), channel_id=1, source_target_pairs={{0,2},{2,0},{4,6},{6,4},{1,3},{3,1},{5,7},{7,5},{8,10},{10,8},{12,... | collective-permute-start | bytes 688136 | tf_op jit(solution)/shard_map/ppermute | solution.py:20
  31.8 2.2 %collective-permute-done.3.refs_2_ = bf16[2,64,896]{2,1,0:T(8,128)(2,1)S(1)} collective-permute-done((bf16[2,64,896]{2,1,0:T(8,128)(2,1)S(1)}, bf16[2,64,896]{2,1,0:T(8,128)(2,1)S(1)}, u32[]{:S(2)}, u32[]{:S(2)}) %collective-permute-start.3) | collective-permute-done | bytes 229408 | tf_op jit(solution)/shard_map/ppermute | solution.py:20
  34.1 1.3 %collective-permute-start.17 = (bf16[2,64,896]{2,1,0:T(8,128)(2,1)S(1)}, bf16[2,64,896]{2,1,0:T(8,128)(2,1)S(1)}, u32[]{:S(2)}, u32[]{:S(2)}) collective-permute-start(bf16[2,64,896]{2,1,0:T(8,128)(2,1)S(1)} %get-tuple-element.59), channel_id=1, source_target_pairs={{0,4},{2,6},{4,0},{6,2},{1,5},{3,7},{5,1},{7,3},{8,12},{10,14},{12... | collective-permute-start | bytes 688136 | tf_op jit(solution)/shard_map/ppermute | solution.py:20
  35.9 1.4 %collective-permute-start.18 = (bf16[2,64,896]{2,1,0:T(8,128)(2,1)S(1)}, bf16[2,64,896]{2,1,0:T(8,128)(2,1)S(1)}, u32[]{:S(2)}, u32[]{:S(2)}) collective-permute-start(bf16[2,64,896]{2,1,0:T(8,128)(2,1)S(1)} %get-tuple-element.60), channel_id=1, source_target_pairs={{0,6},{2,4},{4,2},{6,0},{1,7},{3,5},{5,3},{7,1},{8,14},{10,12},{12... | collective-permute-start | bytes 688136 | tf_op jit(solution)/shard_map/ppermute | solution.py:20
  37.4 1.7 %collective-permute-start.6 = (bf16[2,64,896]{2,1,0:T(8,128)(2,1)S(1)}, bf16[2,64,896]{2,1,0:T(8,128)(2,1)S(1)}, u32[]{:S(2)}, u32[]{:S(2)}) collective-permute-start(bf16[2,64,896]{2,1,0:T(8,128)(2,1)S(1)} %share.4.refs_4_), channel_id=1, source_target_pairs={{0,24},{8,16},{16,8},{24,0},{1,25},{9,17},{17,9},{25,1},{2,26},{10... | collective-permute-start | bytes 688136 | tf_op jit(solution)/shard_map/ppermute | solution.py:25
  39.1 0.8 %collective-permute-done.12.refs_5_.refs_1_ = bf16[2,64,896]{2,1,0:T(8,128)(2,1)S(1)} collective-permute-done((bf16[2,64,896]{2,1,0:T(8,128)(2,1)S(1)}, bf16[2,64,896]{2,1,0:T(8,128)(2,1)S(1)}, u32[]{:S(2)}, u32[]{:S(2)}) %collective-permute-start.12) | collective-permute-done | bytes 229408 | tf_op jit(solution)/shard_map/ppermute | solution.py:20
  40.4 4.7 %collective-permute-done.9.refs_0_.refs_4_ = bf16[2,64,1024]{2,1,0:T(8,128)(2,1)S(1)} collective-permute-done((bf16[2,64,1024]{2,1,0:T(8,128)(2,1)S(1)}, bf16[2,64,1024]{2,1,0:T(8,128)(2,1)S(1)}, u32[]{:S(2)}, u32[]{:S(2)}) %collective-permute-start.9) | collective-permute-done | bytes 262176 | tf_op jit(solution)/shard_map/ppermute | solution.py:25
  45.9 2.2 %collective-permute-start.15 = (bf16[2,64,768]{2,1,0:T(8,128)(2,1)S(1)}, bf16[2,64,768]{2,1,0:T(8,128)(2,1)S(1)}, u32[]{:S(2)}, u32[]{:S(2)}) collective-permute-start(bf16[2,64,768]{2,1,0:T(8,128)(2,1)S(1)} %get-tuple-element.57), channel_id=1, source_target_pairs={{0,6},{2,4},{4,2},{6,0},{1,7},{3,5},{5,3},{7,1},{8,14},{10,12},{12... | collective-permute-start | bytes 589832 | tf_op jit(solution)/shard_map/ppermute | solution.py:20
  48.2 3.1 %collective-permute-start.19 = (bf16[2,64,896]{2,1,0:T(8,128)(2,1)S(1)}, bf16[2,64,896]{2,1,0:T(8,128)(2,1)S(1)}, u32[]{:S(2)}, u32[]{:S(2)}) collective-permute-start(bf16[2,64,896]{2,1,0:T(8,128)(2,1)S(1)} %share.7), channel_id=1, source_target_pairs={{0,24},{8,16},{16,8},{24,0},{1,25},{9,17},{17,9},{25,1},{2,26},{10... | collective-permute-start | bytes 688136 | tf_op jit(solution)/shard_map/ppermute | solution.py:25
  51.4 1.1 %collective-permute-done.6.refs_0_.refs_4_ = bf16[2,64,896]{2,1,0:T(8,128)(2,1)S(1)} collective-permute-done((bf16[2,64,896]{2,1,0:T(8,128)(2,1)S(1)}, bf16[2,64,896]{2,1,0:T(8,128)(2,1)S(1)}, u32[]{:S(2)}, u32[]{:S(2)}) %collective-permute-start.6) | collective-permute-done | bytes 229408 | tf_op jit(solution)/shard_map/ppermute | solution.py:25
  52.4 2.6 %collective-permute-done.14.refs_2_ = bf16[2,64,768]{2,1,0:T(8,128)(2,1)S(1)} collective-permute-done((bf16[2,64,768]{2,1,0:T(8,128)(2,1)S(1)}, bf16[2,64,768]{2,1,0:T(8,128)(2,1)S(1)}, u32[]{:S(2)}, u32[]{:S(2)}) %collective-permute-start.14) | collective-permute-done | bytes 196640 | tf_op jit(solution)/shard_map/ppermute | solution.py:20
  56.0 0.9 %place.2 = (bf16[1,128,3584]{2,1,0:T(8,128)(2,1)}, f32[8,128]{1,0:T(8,128)S(1)}) custom-call(bf16[96,3584]{1,0:T(8,128)(2,1)S(1)} %collective-permute-done.5.refs_4_.refs_0_), custom_call_target="tpu_custom_call" | custom-call | bytes 1376256 | tf_op jit(solution)/shard_map/place/pallas_call | solution.py:351
  57.9 3.7 %collective-permute-start.10 = (bf16[16,3584]{1,0:T(8,128)(2,1)S(1)}, bf16[16,3584]{1,0:T(8,128)(2,1)S(1)}, u32[]{:S(2)}, u32[]{:S(2)}) collective-permute-start(bf16[16,3584]{1,0:T(8,128)(2,1)S(1)} %leaving.4), channel_id=1, source_target_pairs={{0,8},{8,16},{16,24},{1,9},{9,17},{17,25},{2,10},{10,18},{18,26},{... | collective-permute-start | bytes 344072 | tf_op jit(solution)/shard_map/ppermute | solution.py:35
  62.0 1.9 %collective-permute-start.11 = (bf16[16,3584]{1,0:T(8,128)(2,1)S(1)}, bf16[16,3584]{1,0:T(8,128)(2,1)S(1)}, u32[]{:S(2)}, u32[]{:S(2)}) collective-permute-start(bf16[16,3584]{1,0:T(8,128)(2,1)S(1)} %leaving.5), channel_id=1, source_target_pairs={{0,8},{8,16},{16,24},{1,9},{9,17},{17,25},{2,10},{10,18},{18,26},{... | collective-permute-start | bytes 344072 | tf_op jit(solution)/shard_map/ppermute | solution.py:35
  65.1 2.9 %collective-permute-done.16.refs_0_ = bf16[2,64,768]{2,1,0:T(8,128)(2,1)S(1)} collective-permute-done((bf16[2,64,768]{2,1,0:T(8,128)(2,1)S(1)}, bf16[2,64,768]{2,1,0:T(8,128)(2,1)S(1)}, u32[]{:S(2)}, u32[]{:S(2)}) %collective-permute-start.16) | collective-permute-done | bytes 196640 | tf_op jit(solution)/shard_map/ppermute | solution.py:25
  68.4 1.0 %collective-permute-start.20 = (f32[8,128]{1,0:T(8,128)S(1)}, f32[8,128]{1,0:T(8,128)S(1)}, u32[]{:S(2)}, u32[]{:S(2)}) collective-permute-start(f32[8,128]{1,0:T(8,128)S(1)} %get-tuple-element.62.refs_0_), channel_id=1, source_target_pairs={{0,2},{2,0},{4,6},{6,4},{1,3},{3,1},{5,7},{7,5},{8,10},{10,8},{12,... | collective-permute-start | bytes 12296 | tf_op jit(solution)/shard_map/ppermute | solution.py:20
  69.4 0.8 %collective-permute-start.21 = (f32[8,128]{1,0:T(8,128)S(1)}, f32[8,128]{1,0:T(8,128)S(1)}, u32[]{:S(2)}, u32[]{:S(2)}) collective-permute-start(f32[8,128]{1,0:T(8,128)S(1)} %get-tuple-element.62.refs_0_), channel_id=1, source_target_pairs={{0,4},{2,6},{4,0},{6,2},{1,5},{3,7},{5,1},{7,3},{8,12},{10,14},{12... | collective-permute-start | bytes 12296 | tf_op jit(solution)/shard_map/ppermute | solution.py:20
  70.3 1.7 %collective-permute-start.22 = (f32[8,128]{1,0:T(8,128)S(1)}, f32[8,128]{1,0:T(8,128)S(1)}, u32[]{:S(2)}, u32[]{:S(2)}) collective-permute-start(f32[8,128]{1,0:T(8,128)S(1)} %get-tuple-element.62.refs_0_), channel_id=1, source_target_pairs={{0,6},{2,4},{4,2},{6,0},{1,7},{3,5},{5,3},{7,1},{8,14},{10,12},{12... | collective-permute-start | bytes 12296 | tf_op jit(solution)/shard_map/ppermute | solution.py:20
  72.1 1.2 %codes.1 = (bf16[2,1,64,3584]{3,2,1,0:T(8,128)(2,1)}, f32[8,128]{1,0:T(8,128)S(1)}) custom-call(f32[8,128]{1,0:T(8,128)S(1)} %get-tuple-element.62.refs_0_, f32[8,128]{1,0:T(8,128)S(1)} %collective-permute-done.20.refs_1_, f32[2,64,1024]{2,1,0:T(8,128)S(1)} %get-tuple-element.63.refs_2_, f32[2,64,896]{2,1,0:T(8,128)S(1)} %get-tuple-element.64.refs_3_, ...), custom_call_target="tpu_custom_call" | custom-call | flops 917504 | bytes 1843200 | tf_op jit(solution)/shard_map/codes/pallas_call | solution.py:56
  74.0 0.8 %collective-permute-done.22.refs_3_ = f32[8,128]{1,0:T(8,128)S(1)} collective-permute-done((f32[8,128]{1,0:T(8,128)S(1)}, f32[8,128]{1,0:T(8,128)S(1)}, u32[]{:S(2)}, u32[]{:S(2)}) %collective-permute-start.22) | collective-permute-done | bytes 4128 | tf_op jit(solution)/shard_map/ppermute | solution.py:20
  (42 shorter events, 10.4 us)
Async XLA Ops:
  5.5 2.0 %collective-permute-start = (f32[1024,128]{1,0:T(8,128)S(1)}, f32[1024,128]{1,0:T(8,128)S(1)}, u32[]{:S(2)}, u32[]{:S(2)}) collective-permute-start(f32[1024,128]{1,0:T(8,128)S(1)} %get-tuple-element.37.rest_0_.refs_0_), channel_id=1, source_target_pairs={{0,1},{1,0},{2,3},{3,2},{4,5},{5,4},{6,7},{7,6},{8,9},{9,8},{10,11... | collective-permute-start | bytes 1572872 | tf_op jit(solution)/shard_map/ppermute | solution.py:20
  8.5 9.2 %collective-permute-start.1 = (bf16[2,64,1024]{2,1,0:T(8,128)(2,1)S(1)}, bf16[2,64,1024]{2,1,0:T(8,128)(2,1)S(1)}, u32[]{:S(2)}, u32[]{:S(2)}) collective-permute-start(bf16[2,64,1024]{2,1,0:T(8,128)(2,1)S(1)} %get-tuple-element.41), channel_id=1, source_target_pairs={{0,2},{2,0},{4,6},{6,4},{1,3},{3,1},{5,7},{7,5},{8,10},{10,8},{12,... | collective-permute-start | bytes 786440 | tf_op jit(solution)/shard_map/ppermute | solution.py:20
  10.1 27.3 %collective-permute-start.5 = (bf16[96,3584]{1,0:T(8,128)(2,1)S(1)}, bf16[96,3584]{1,0:T(8,128)(2,1)S(1)}, u32[]{:S(2)}, u32[]{:S(2)}) collective-permute-start(bf16[96,3584]{1,0:T(8,128)(2,1)S(1)} %leaving.3.refs_4_), channel_id=1, source_target_pairs={{0,8},{8,16},{16,24},{24,0},{1,9},{9,17},{17,25},{25,1},{2,10},{10... | collective-permute-start | bytes 2064392 | tf_op jit(solution)/shard_map/ppermute | solution.py:30
  11.6 14.9 %collective-permute-start.7 = (bf16[2,64,1024]{2,1,0:T(8,128)(2,1)S(1)}, bf16[2,64,1024]{2,1,0:T(8,128)(2,1)S(1)}, u32[]{:S(2)}, u32[]{:S(2)}) collective-permute-start(bf16[2,64,1024]{2,1,0:T(8,128)(2,1)S(1)} %get-tuple-element.47), channel_id=1, source_target_pairs={{0,4},{2,6},{4,0},{6,2},{1,5},{3,7},{5,1},{7,3},{8,12},{10,14},{12... | collective-permute-start | bytes 786440 | tf_op jit(solution)/shard_map/ppermute | solution.py:20
  13.1 14.8 %collective-permute-start.8 = (bf16[2,64,1024]{2,1,0:T(8,128)(2,1)S(1)}, bf16[2,64,1024]{2,1,0:T(8,128)(2,1)S(1)}, u32[]{:S(2)}, u32[]{:S(2)}) collective-permute-start(bf16[2,64,1024]{2,1,0:T(8,128)(2,1)S(1)} %get-tuple-element.48), channel_id=1, source_target_pairs={{0,6},{2,4},{4,2},{6,0},{1,7},{3,5},{5,3},{7,1},{8,14},{10,12},{12... | collective-permute-start | bytes 786440 | tf_op jit(solution)/shard_map/ppermute | solution.py:20
  18.2 11.5 %collective-permute-start.2 = (bf16[2,64,896]{2,1,0:T(8,128)(2,1)S(1)}, bf16[2,64,896]{2,1,0:T(8,128)(2,1)S(1)}, u32[]{:S(2)}, u32[]{:S(2)}) collective-permute-start(bf16[2,64,896]{2,1,0:T(8,128)(2,1)S(1)} %get-tuple-element.43), channel_id=1, source_target_pairs={{0,2},{2,0},{4,6},{6,4},{1,3},{3,1},{5,7},{7,5},{8,10},{10,8},{12,... | collective-permute-start | bytes 688136 | tf_op jit(solution)/shard_map/ppermute | solution.py:20
  19.8 14.3 %collective-permute-start.3 = (bf16[2,64,896]{2,1,0:T(8,128)(2,1)S(1)}, bf16[2,64,896]{2,1,0:T(8,128)(2,1)S(1)}, u32[]{:S(2)}, u32[]{:S(2)}) collective-permute-start(bf16[2,64,896]{2,1,0:T(8,128)(2,1)S(1)} %get-tuple-element.44), channel_id=1, source_target_pairs={{0,4},{2,6},{4,0},{6,2},{1,5},{3,7},{5,1},{7,3},{8,12},{10,14},{12... | collective-permute-start | bytes 688136 | tf_op jit(solution)/shard_map/ppermute | solution.py:20
  26.5 9.4 %collective-permute-start.4 = (bf16[2,64,896]{2,1,0:T(8,128)(2,1)S(1)}, bf16[2,64,896]{2,1,0:T(8,128)(2,1)S(1)}, u32[]{:S(2)}, u32[]{:S(2)}) collective-permute-start(bf16[2,64,896]{2,1,0:T(8,128)(2,1)S(1)} %get-tuple-element.45), channel_id=1, source_target_pairs={{0,6},{2,4},{4,2},{6,0},{1,7},{3,5},{5,3},{7,1},{8,14},{10,12},{12... | collective-permute-start | bytes 688136 | tf_op jit(solution)/shard_map/ppermute | solution.py:20
  28.1 17.0 %collective-permute-start.9 = (bf16[2,64,1024]{2,1,0:T(8,128)(2,1)S(1)}, bf16[2,64,1024]{2,1,0:T(8,128)(2,1)S(1)}, u32[]{:S(2)}, u32[]{:S(2)}) collective-permute-start(bf16[2,64,1024]{2,1,0:T(8,128)(2,1)S(1)} %share.5.refs_4_), channel_id=1, source_target_pairs={{0,24},{8,16},{16,8},{24,0},{1,25},{9,17},{17,9},{25,1},{2,26},{10... | collective-permute-start | bytes 786440 | tf_op jit(solution)/shard_map/ppermute | solution.py:25
  30.3 9.6 %collective-permute-start.12 = (bf16[2,64,896]{2,1,0:T(8,128)(2,1)S(1)}, bf16[2,64,896]{2,1,0:T(8,128)(2,1)S(1)}, u32[]{:S(2)}, u32[]{:S(2)}) collective-permute-start(bf16[2,64,896]{2,1,0:T(8,128)(2,1)S(1)} %get-tuple-element.53), channel_id=1, source_target_pairs={{0,2},{2,0},{4,6},{6,4},{1,3},{3,1},{5,7},{7,5},{8,10},{10,8},{12,... | collective-permute-start | bytes 688136 | tf_op jit(solution)/shard_map/ppermute | solution.py:20
  34.1 11.8 %collective-permute-start.17 = (bf16[2,64,896]{2,1,0:T(8,128)(2,1)S(1)}, bf16[2,64,896]{2,1,0:T(8,128)(2,1)S(1)}, u32[]{:S(2)}, u32[]{:S(2)}) collective-permute-start(bf16[2,64,896]{2,1,0:T(8,128)(2,1)S(1)} %get-tuple-element.59), channel_id=1, source_target_pairs={{0,4},{2,6},{4,0},{6,2},{1,5},{3,7},{5,1},{7,3},{8,12},{10,14},{12... | collective-permute-start | bytes 688136 | tf_op jit(solution)/shard_map/ppermute | solution.py:20
  35.9 12.2 %collective-permute-start.18 = (bf16[2,64,896]{2,1,0:T(8,128)(2,1)S(1)}, bf16[2,64,896]{2,1,0:T(8,128)(2,1)S(1)}, u32[]{:S(2)}, u32[]{:S(2)}) collective-permute-start(bf16[2,64,896]{2,1,0:T(8,128)(2,1)S(1)} %get-tuple-element.60), channel_id=1, source_target_pairs={{0,6},{2,4},{4,2},{6,0},{1,7},{3,5},{5,3},{7,1},{8,14},{10,12},{12... | collective-permute-start | bytes 688136 | tf_op jit(solution)/shard_map/ppermute | solution.py:20
  37.3 18.1 %copy-start = (f32[2,1,64,3584]{3,2,1,0:T(8,128)S(1)}, f32[2,1,64,3584]{3,2,1,0:T(8,128)}, u32[]{:S(2)}) copy-start(f32[2,1,64,3584]{3,2,1,0:T(8,128)} %refs_1_.9) | copy-start | bytes 5505028
  37.3 18.1 %copy-start.1 = (bf16[2,1,64,3584]{3,2,1,0:T(8,128)(2,1)S(1)}, bf16[2,1,64,3584]{3,2,1,0:T(8,128)(2,1)}, u32[]{:S(2)}) copy-start(bf16[2,1,64,3584]{3,2,1,0:T(8,128)(2,1)} %refs_2_.9) | copy-start | bytes 2752516
  37.3 18.1 %copy-start.2 = (bf16[2,1,64,3584]{3,2,1,0:T(8,128)(2,1)S(1)}, bf16[2,1,64,3584]{3,2,1,0:T(8,128)(2,1)}, u32[]{:S(2)}) copy-start(bf16[2,1,64,3584]{3,2,1,0:T(8,128)(2,1)} %refs_3_.9) | copy-start | bytes 2752516
  37.4 15.0 %collective-permute-start.6 = (bf16[2,64,896]{2,1,0:T(8,128)(2,1)S(1)}, bf16[2,64,896]{2,1,0:T(8,128)(2,1)S(1)}, u32[]{:S(2)}, u32[]{:S(2)}) collective-permute-start(bf16[2,64,896]{2,1,0:T(8,128)(2,1)S(1)} %share.4.refs_4_), channel_id=1, source_target_pairs={{0,24},{8,16},{16,8},{24,0},{1,25},{9,17},{17,9},{25,1},{2,26},{10... | collective-permute-start | bytes 688136 | tf_op jit(solution)/shard_map/ppermute | solution.py:25
  40.4 12.1 %collective-permute-start.13 = (bf16[2,64,768]{2,1,0:T(8,128)(2,1)S(1)}, bf16[2,64,768]{2,1,0:T(8,128)(2,1)S(1)}, u32[]{:S(2)}, u32[]{:S(2)}) collective-permute-start(bf16[2,64,768]{2,1,0:T(8,128)(2,1)S(1)} %get-tuple-element.55), channel_id=1, source_target_pairs={{0,2},{2,0},{4,6},{6,4},{1,3},{3,1},{5,7},{7,5},{8,10},{10,8},{12,... | collective-permute-start | bytes 589832 | tf_op jit(solution)/shard_map/ppermute | solution.py:20
  45.2 9.9 %collective-permute-start.14 = (bf16[2,64,768]{2,1,0:T(8,128)(2,1)S(1)}, bf16[2,64,768]{2,1,0:T(8,128)(2,1)S(1)}, u32[]{:S(2)}, u32[]{:S(2)}) collective-permute-start(bf16[2,64,768]{2,1,0:T(8,128)(2,1)S(1)} %get-tuple-element.56), channel_id=1, source_target_pairs={{0,4},{2,6},{4,0},{6,2},{1,5},{3,7},{5,1},{7,3},{8,12},{10,14},{12... | collective-permute-start | bytes 589832 | tf_op jit(solution)/shard_map/ppermute | solution.py:20
  45.9 9.2 %collective-permute-start.15 = (bf16[2,64,768]{2,1,0:T(8,128)(2,1)S(1)}, bf16[2,64,768]{2,1,0:T(8,128)(2,1)S(1)}, u32[]{:S(2)}, u32[]{:S(2)}) collective-permute-start(bf16[2,64,768]{2,1,0:T(8,128)(2,1)S(1)} %get-tuple-element.57), channel_id=1, source_target_pairs={{0,6},{2,4},{4,2},{6,0},{1,7},{3,5},{5,3},{7,1},{8,14},{10,12},{12... | collective-permute-start | bytes 589832 | tf_op jit(solution)/shard_map/ppermute | solution.py:20
  48.2 16.3 %collective-permute-start.19 = (bf16[2,64,896]{2,1,0:T(8,128)(2,1)S(1)}, bf16[2,64,896]{2,1,0:T(8,128)(2,1)S(1)}, u32[]{:S(2)}, u32[]{:S(2)}) collective-permute-start(bf16[2,64,896]{2,1,0:T(8,128)(2,1)S(1)} %share.7), channel_id=1, source_target_pairs={{0,24},{8,16},{16,8},{24,0},{1,25},{9,17},{17,9},{25,1},{2,26},{10... | collective-permute-start | bytes 688136 | tf_op jit(solution)/shard_map/ppermute | solution.py:25
  55.2 12.8 %collective-permute-start.16 = (bf16[2,64,768]{2,1,0:T(8,128)(2,1)S(1)}, bf16[2,64,768]{2,1,0:T(8,128)(2,1)S(1)}, u32[]{:S(2)}, u32[]{:S(2)}) collective-permute-start(bf16[2,64,768]{2,1,0:T(8,128)(2,1)S(1)} %share.6), channel_id=1, source_target_pairs={{0,24},{8,16},{16,8},{24,0},{1,25},{9,17},{17,9},{25,1},{2,26},{10... | collective-permute-start | bytes 589832 | tf_op jit(solution)/shard_map/ppermute | solution.py:25
  57.9 15.4 %collective-permute-start.10 = (bf16[16,3584]{1,0:T(8,128)(2,1)S(1)}, bf16[16,3584]{1,0:T(8,128)(2,1)S(1)}, u32[]{:S(2)}, u32[]{:S(2)}) collective-permute-start(bf16[16,3584]{1,0:T(8,128)(2,1)S(1)} %leaving.4), channel_id=1, source_target_pairs={{0,8},{8,16},{16,24},{1,9},{9,17},{17,25},{2,10},{10,18},{18,26},{... | collective-permute-start | bytes 344072 | tf_op jit(solution)/shard_map/ppermute | solution.py:35
  62.0 11.3 %collective-permute-start.11 = (bf16[16,3584]{1,0:T(8,128)(2,1)S(1)}, bf16[16,3584]{1,0:T(8,128)(2,1)S(1)}, u32[]{:S(2)}, u32[]{:S(2)}) collective-permute-start(bf16[16,3584]{1,0:T(8,128)(2,1)S(1)} %leaving.5), channel_id=1, source_target_pairs={{0,8},{8,16},{16,24},{1,9},{9,17},{17,25},{2,10},{10,18},{18,26},{... | collective-permute-start | bytes 344072 | tf_op jit(solution)/shard_map/ppermute | solution.py:35
  68.4 3.7 %collective-permute-start.20 = (f32[8,128]{1,0:T(8,128)S(1)}, f32[8,128]{1,0:T(8,128)S(1)}, u32[]{:S(2)}, u32[]{:S(2)}) collective-permute-start(f32[8,128]{1,0:T(8,128)S(1)} %get-tuple-element.62.refs_0_), channel_id=1, source_target_pairs={{0,2},{2,0},{4,6},{6,4},{1,3},{3,1},{5,7},{7,5},{8,10},{10,8},{12,... | collective-permute-start | bytes 12296 | tf_op jit(solution)/shard_map/ppermute | solution.py:20
  69.4 4.6 %collective-permute-start.21 = (f32[8,128]{1,0:T(8,128)S(1)}, f32[8,128]{1,0:T(8,128)S(1)}, u32[]{:S(2)}, u32[]{:S(2)}) collective-permute-start(f32[8,128]{1,0:T(8,128)S(1)} %get-tuple-element.62.refs_0_), channel_id=1, source_target_pairs={{0,4},{2,6},{4,0},{6,2},{1,5},{3,7},{5,1},{7,3},{8,12},{10,14},{12... | collective-permute-start | bytes 12296 | tf_op jit(solution)/shard_map/ppermute | solution.py:20
  70.3 4.5 %collective-permute-start.22 = (f32[8,128]{1,0:T(8,128)S(1)}, f32[8,128]{1,0:T(8,128)S(1)}, u32[]{:S(2)}, u32[]{:S(2)}) collective-permute-start(f32[8,128]{1,0:T(8,128)S(1)} %get-tuple-element.62.refs_0_), channel_id=1, source_target_pairs={{0,6},{2,4},{4,2},{6,0},{1,7},{3,5},{5,3},{7,1},{8,14},{10,12},{12... | collective-permute-start | bytes 12296 | tf_op jit(solution)/shard_map/ppermute | solution.py:20
